TPU v7x, 32 devices: a whole 2x2x4 slice. The times are simulated.
32 devices in a mesh: dp: 2 (over y), ctx: 16 (over z, x, core).
Axes of the slice: x: 2, y: 2, z: 4, core: 2. Of those that a mesh axis runs over, the one named last changes fastest.
Arguments:
- events: bfloat16 [2, 4096, 1024], P('dp', 'ctx'), may hold values from -6 to 6
- w_query: bfloat16 [1024, 512], replicated, may hold values from -0.1875 to 0.1875
- w_key: bfloat16 [1024, 512], replicated, may hold values from -0.1875 to 0.1875
- values: bfloat16 [2, 4096, 512], P('dp', 'ctx'), may hold values from -6 to 6
- grad_out: bfloat16 [2, 4096, 512], P('dp', 'ctx'), may hold values from -6 to 6
- lengths: int32 [2, 8], P('dp'), may hold values from 1 to 768, 4096 in all within a row
- stream_shift: int32 [2], P('dp'), may hold values from 0 to 4095
- block_keep: int32 [2, 32], P('dp'), may hold values 0 or 1
Outputs:
- attended: bfloat16 [2, 4096, 512], P('dp', 'ctx')
- grad_values: bfloat16 [2, 4096, 512], P('dp', 'ctx')
- grad_wq: bfloat16 [1024, 512], P('ctx')
- grad_wk: bfloat16 [1024, 512], P('ctx')
Inputs may be any that keep to these rules, and one draw needn't show every extreme that they name: The lengths of a stream sum to 4096; the longest is exactly 768.
All inputs are finite; a program needn't handle non-finite values. No bound on the sum of `block_keep` on one device may be relied on, other than what follows from the above.
Results may differ from a plain program's by a relative error of at most 0.011.
Values may be sent and summed in bfloat16 or wider, within the bound.
No kernel may reach another device: no remote copies, remote signals or barrier semaphores. Data moves between devices by JAX's collectives and lax.ppermute only.
A program may use at most 64 MiB of HBM per device.

v0:
```python
import jax
import jax.numpy as jnp
from jax import lax
from jax.sharding import PartitionSpec as P

HD = 128
SPAN = 3
BLOCK = 128
MAXLEN = 768


def from_behind(value, axis, steps):
    count = lax.axis_size(axis)
    pairs = [(source, (source + steps) % count) for source in range(count)]
    return lax.ppermute(value, axis, pairs)


def tile_terms(query, grad, key, value, valid, scale, alpha):
    z = jnp.einsum("qhd,khd->hqk", query, key, preferred_element_type=jnp.float32) * alpha
    sig = jax.nn.sigmoid(z)
    weight = valid[None, :, :].astype(jnp.float32) * scale
    att = (z * sig * weight).astype(jnp.bfloat16)
    out = jnp.einsum("hqk,khd->qhd", att, value, preferred_element_type=jnp.float32)
    dprod = jnp.einsum("qhd,khd->hqk", grad, value, preferred_element_type=jnp.float32)
    dsc = (dprod * sig * (1.0 + z * (1.0 - sig)) * weight * alpha).astype(jnp.bfloat16)
    dquery = jnp.einsum("hqk,khd->qhd", dsc, key, preferred_element_type=jnp.float32)
    dkey = jnp.einsum("hqk,qhd->khd", dsc, query, preferred_element_type=jnp.float32)
    dvalue = jnp.einsum("hqk,qhd->khd", att, grad, preferred_element_type=jnp.float32)
    return (out, dquery, dkey, dvalue)


def body(events, w_query, w_key, values, grad_out, lengths, stream_shift, block_keep):
    rows = events.shape[1]
    features = w_query.shape[1]
    nheads = features // HD
    alpha = 1.0 / HD**0.5
    scale = 1.0 / MAXLEN**0.5
    local = events[0]
    queries = jnp.dot(local, w_query, preferred_element_type=jnp.float32).astype(jnp.bfloat16)
    keys = jnp.dot(local, w_key, preferred_element_type=jnp.float32).astype(jnp.bfloat16)
    queries = queries.reshape(rows, nheads, HD)
    keys = keys.reshape(rows, nheads, HD)
    vals = values[0].reshape(rows, nheads, HD)
    cotan = grad_out[0].reshape(rows, nheads, HD)
    cycle_size = lax.axis_size("ctx")
    myself = lax.axis_index("ctx")
    total = rows * cycle_size
    ends = jnp.cumsum(lengths[0])
    offset = stream_shift[0]
    keep = block_keep[0]
    blocks_all = jnp.arange(keep.shape[0], dtype=jnp.int32)
    within = jnp.arange(rows, dtype=jnp.int32)

    def describe(anchor):
        anchor = jnp.remainder(anchor, cycle_size)
        position = jnp.remainder(anchor * rows + within - offset, total)
        owner = jnp.sum((position[:, None] >= ends[None, :]).astype(jnp.int32), axis=1)
        which = position // BLOCK
        kept = (
            jnp.sum(jnp.where(which[:, None] == blocks_all[None, :], keep[None, :], 0), axis=1) > 0
        )
        return (position, owner, kept)

    zeros = jnp.zeros((rows, nheads, HD), jnp.float32)
    qinfo = describe(myself)
    moving = (keys, vals)
    carried = (zeros, zeros)
    out_acc = zeros
    dq_acc = zeros
    for step in range(SPAN + 1):
        if step > 0:
            moving = from_behind((moving[0], moving[1]), "ctx", 1)
            carried = (
                from_behind(carried[0].astype(jnp.bfloat16), "ctx", 1).astype(jnp.float32),
                from_behind(carried[1].astype(jnp.bfloat16), "ctx", 1).astype(jnp.float32),
            )
        kinfo = describe(myself - step)
        o, a, b, c = tile_terms(
            queries,
            cotan,
            moving[0],
            moving[1],
            (qinfo[1][:, None] == kinfo[1][None, :])
            & (kinfo[0][None, :] <= qinfo[0][:, None])
            & kinfo[2][None, :],
            scale,
            alpha,
        )
        out_acc = out_acc + o
        dq_acc = dq_acc + a
        carried = (carried[0] + b, carried[1] + c)
    carried = (
        from_behind(carried[0].astype(jnp.bfloat16), "ctx", -SPAN).astype(jnp.float32),
        from_behind(carried[1].astype(jnp.bfloat16), "ctx", -SPAN).astype(jnp.float32),
    )
    dk_acc, dv_acc = carried
    attended = out_acc.reshape(1, rows, features).astype(jnp.bfloat16)
    grad_values = dv_acc.reshape(1, rows, features).astype(jnp.bfloat16)
    dq_b = dq_acc.reshape(rows, features).astype(jnp.bfloat16)
    dk_b = dk_acc.reshape(rows, features).astype(jnp.bfloat16)
    joined = jnp.concatenate([dq_b, dk_b], axis=1)
    width_rows = local.shape[1]
    share = width_rows // cycle_size
    terms = jnp.einsum("rd,rf->df", local, joined, preferred_element_type=jnp.float32)
    summed = lax.psum(terms, ("dp", "ctx"))
    mine = lax.dynamic_slice_in_dim(summed, myself * share, share, 0)
    grad_wq = mine[:, :features].astype(jnp.bfloat16)
    grad_wk = mine[:, features:].astype(jnp.bfloat16)
    return (attended, grad_values, grad_wq, grad_wk)


def solution(mesh):
    placed = (
        P("dp", "ctx", None),
        P(),
        P(),
        P("dp", "ctx", None),
        P("dp", "ctx", None),
        P("dp", None),
        P("dp"),
        P("dp", None),
    )
    return jax.shard_map(
        body,
        mesh=mesh,
        in_specs=placed,
        out_specs=(P("dp", "ctx", None), P("dp", "ctx", None), P("ctx", None), P("ctx", None)),
        check_vma=False,
    )
```

profile of v0, /device:TPU:0, one launch (start us, length us, event | category | flops | bytes accessed | tf_op | source)
XLA Modules:
  0.0 174.0 jit_solution(14229098953332760679)
XLA Ops:
  0.6 1.2 copy.84
  2.3 1.5 fusion.20
  3.8 0.8 copy.154
  4.6 2.6 %collective-permute-start = (bf16[256,4,128]{2,0,1:T(8,128)(2,1)}, bf16[256,4,128]{2,0,1:T(8,128)(2,1)}, u32[]{:S(2)}, u32[]{:S(2)}) collective-permute-start(bf16[256,4,128]{2,0,1:T(8,128)(2,1)} %bitcast.89), channel_id=1, source_target_pairs={{0,1},{1,2},{2,3},{3,4},{4,5},{5,6},{6,7},{7,8},{8,9},{9,10},{10,1... | collective-permute-start | bytes 786440 | tf_op jit(solution)/shard_map/ppermute | solution.py:15
  7.8 0.8 reduce-window.8
  8.7 0.8 select_reduce_fusion
  9.5 1.0 reshape_squeeze.7
  10.6 1.8 %convolution_convert_fusion.3 = bf16[256,512]{1,0:T(8,128)(2,1)S(1)} fusion(bf16[1024,512]{1,0:T(8,128)(2,1)} %param.9, bf16[1,256,1024]{2,1,0:T(8,128)(2,1)} %param.8), kind=kOutput, calls=%fused_computation.42 | convolution fusion | flops 268566528 | bytes 1835008 | tf_op jit(solution)/shard_map/dot_general | solution.py:39
  12.6 1.2 and_select_fusion
  14.9 0.9 fusion.19
  15.9 1.1 fusion.18
  17.0 1.6 collective-permute-start.6
  19.2 1.6 multiply_convert_fusion.2
  21.4 3.3 %collective-permute-done.10 = bf16[256,4,128]{0,2,1:T(8,128)(2,1)} collective-permute-done((bf16[256,4,128]{0,2,1:T(8,128)(2,1)}, bf16[256,4,128]{0,2,1:T(8,128)(2,1)}, u32[]{:S(2)}, u32[]{:S(2)}) %collective-permute-start.10) | collective-permute-done | bytes 262176 | tf_op jit(solution)/shard_map/ppermute | solution.py:15
  24.7 1.2 add_convert_fusion.2
  25.9 1.6 collective-permute-done.6
  27.5 1.3 add_convert_fusion.5
  29.3 1.3 convolution_add_fusion.2
  30.6 12.4 %collective-permute-done.2 = bf16[256,4,128]{2,0,1:T(8,128)(2,1)S(1)} collective-permute-done((bf16[256,4,128]{2,0,1:T(8,128)(2,1)}, bf16[256,4,128]{2,0,1:T(8,128)(2,1)S(1)}, u32[]{:S(2)}, u32[]{:S(2)}) %collective-permute-start.2) | collective-permute-done | bytes 262176 | tf_op jit(solution)/shard_map/ppermute | solution.py:15
  44.8 0.7 add_convert_fusion.4
  46.2 15.2 %collective-permute-done.4 = bf16[256,4,128]{2,0,1:T(8,128)(2,1)S(1)} collective-permute-done((bf16[256,4,128]{2,0,1:T(8,128)(2,1)S(1)}, bf16[256,4,128]{2,0,1:T(8,128)(2,1)S(1)}, u32[]{:S(2)}, u32[]{:S(2)}) %collective-permute-start.4) | collective-permute-done | bytes 262176 | tf_op jit(solution)/shard_map/ppermute | solution.py:15
  62.8 1.0 fusion.16
  63.8 0.8 add_convert_fusion
  64.6 1.8 %copy.114 = bf16[1,256,512]{2,1,0:T(8,128)(2,1)} copy(bf16[1,256,512]{1,2,0:T(8,128)(2,1)} %bitcast.107) | data formatting | bytes 524288
  66.7 1.0 add_convert_fusion.3
  68.0 1.3 fusion.17
  69.3 6.7 %collective-permute-done.9 = bf16[256,4,128]{2,0,1:T(8,128)(2,1)S(1)} collective-permute-done((bf16[256,4,128]{2,0,1:T(8,128)(2,1)S(1)}, bf16[256,4,128]{2,0,1:T(8,128)(2,1)S(1)}, u32[]{:S(2)}, u32[]{:S(2)}) %collective-permute-start.9) | collective-permute-done | bytes 262176 | tf_op jit(solution)/shard_map/ppermute | solution.py:15
  76.1 0.8 copy.115
  77.0 3.6 %convolution_bitcast_fusion = f32[1024,1024]{0,1:T(8,128)} fusion(bf16[256,512]{0,1:T(8,128)(2,1)} %bitcast.19, bf16[256,512]{0,1:T(8,128)(2,1)S(1)} %bitcast.105, bf16[1,256,1024]{2,1,0:T(8,128)(2,1)S(1)} %copy-done.1), kind=kOutput, calls=%fused_computation | convolution fusion | flops 537919488 | bytes 5242880 | tf_op jit(solution)/shard_map/rd,rf->df/dot_general | solution.py:104
  80.6 91.8 %all-reduce.1 = bf16[1024,1024]{0,1:T(8,128)(2,1)S(1)} all-reduce(f32[1024,1024]{0,1:T(8,128)} %convolution_bitcast_fusion), channel_id=1, replica_groups=mesh['dp'=2,'ctx'=16] {'dp','ctx'}, use_global_device_ids=true, to_apply=%region_9.10 | all-reduce | flops 1048576 | bytes 6291456 | tf_op jit(solution)/shard_map/psum | solution.py:105
  172.6 0.7 copy.117
  173.3 0.7 copy.116
  (63 shorter events, 8.4 us)
Async XLA Ops:
  0.6 1.7 copy-start
  1.8 19.0 %collective-permute-start.1 = (bf16[256,4,128]{0,2,1:T(8,128)(2,1)S(1)}, bf16[256,4,128]{0,2,1:T(8,128)(2,1)S(1)}, u32[]{:S(2)}, u32[]{:S(2)}) collective-permute-start(bf16[256,4,128]{0,2,1:T(8,128)(2,1)S(1)} %bitcast.102), channel_id=1, source_target_pairs={{0,1},{1,2},{2,3},{3,4},{4,5},{5,6},{6,7},{7,8},{8,9},{9,10},{10,1... | collective-permute-start | bytes 786440 | tf_op jit(solution)/shard_map/ppermute | solution.py:15
  4.6 14.6 %collective-permute-start = (bf16[256,4,128]{2,0,1:T(8,128)(2,1)}, bf16[256,4,128]{2,0,1:T(8,128)(2,1)}, u32[]{:S(2)}, u32[]{:S(2)}) collective-permute-start(bf16[256,4,128]{2,0,1:T(8,128)(2,1)} %bitcast.89), channel_id=1, source_target_pairs={{0,1},{1,2},{2,3},{3,4},{4,5},{5,6},{6,7},{7,8},{8,9},{9,10},{10,1... | collective-permute-start | bytes 786440 | tf_op jit(solution)/shard_map/ppermute | solution.py:15
  15.8 8.8 %collective-permute-start.10 = (bf16[256,4,128]{0,2,1:T(8,128)(2,1)}, bf16[256,4,128]{0,2,1:T(8,128)(2,1)}, u32[]{:S(2)}, u32[]{:S(2)}) collective-permute-start(bf16[256,4,128]{0,2,1:T(8,128)(2,1)} %fusion.19), channel_id=1, source_target_pairs={{0,1},{1,2},{2,3},{3,4},{4,5},{5,6},{6,7},{7,8},{8,9},{9,10},{10,1... | collective-permute-start | bytes 786440 | tf_op jit(solution)/shard_map/ppermute | solution.py:15
  17.0 10.5 %collective-permute-start.6 = (bf16[256,4,128]{2,0,1:T(8,128)(2,1)}, bf16[256,4,128]{2,0,1:T(8,128)(2,1)}, u32[]{:S(2)}, u32[]{:S(2)}) collective-permute-start(bf16[256,4,128]{2,0,1:T(8,128)(2,1)} %fusion.18), channel_id=1, source_target_pairs={{0,1},{1,2},{2,3},{3,4},{4,5},{5,6},{6,7},{7,8},{8,9},{9,10},{10,1... | collective-permute-start | bytes 786440 | tf_op jit(solution)/shard_map/ppermute | solution.py:15
  18.9 1.9 %copy-start.4 = (f32[256,256]{1,0:T(8,128)S(1)}, f32[256,256]{1,0:T(8,128)}, u32[]{:S(2)}) copy-start(f32[256,256]{1,0:T(8,128)} %get-tuple-element.28) | copy-start | bytes 786436
  21.3 21.6 %copy-start.3 = (f32[256,256]{1,0:T(8,128)S(1)}, f32[256,256]{1,0:T(8,128)}, u32[]{:S(2)}) copy-start(f32[256,256]{1,0:T(8,128)} %get-tuple-element.27) | copy-start | bytes 786436
  25.8 18.4 %collective-permute-start.11 = (bf16[256,4,128]{0,2,1:T(8,128)(2,1)S(1)}, bf16[256,4,128]{0,2,1:T(8,128)(2,1)S(1)}, u32[]{:S(2)}, u32[]{:S(2)}) collective-permute-start(bf16[256,4,128]{0,2,1:T(8,128)(2,1)S(1)} %add_convert_fusion.2), channel_id=1, source_target_pairs={{0,1},{1,2},{2,3},{3,4},{4,5},{5,6},{6,7},{7,8},{8,9},{9,10},{10,1... | collective-permute-start | bytes 786440 | tf_op jit(solution)/shard_map/ppermute | solution.py:15
  28.8 16.0 %collective-permute-start.7 = (bf16[256,4,128]{2,0,1:T(8,128)(2,1)S(1)}, bf16[256,4,128]{2,0,1:T(8,128)(2,1)S(1)}, u32[]{:S(2)}, u32[]{:S(2)}) collective-permute-start(bf16[256,4,128]{2,0,1:T(8,128)(2,1)S(1)} %add_convert_fusion.5), channel_id=1, source_target_pairs={{0,1},{1,2},{2,3},{3,4},{4,5},{5,6},{6,7},{7,8},{8,9},{9,10},{10,1... | collective-permute-start | bytes 786440 | tf_op jit(solution)/shard_map/ppermute | solution.py:15
  28.8 14.7 %collective-permute-start.3 = (bf16[256,4,128]{0,2,1:T(8,128)(2,1)S(1)}, bf16[256,4,128]{0,2,1:T(8,128)(2,1)S(1)}, u32[]{:S(2)}, u32[]{:S(2)}) collective-permute-start(bf16[256,4,128]{0,2,1:T(8,128)(2,1)S(1)} %collective-permute-done.1), channel_id=1, source_target_pairs={{0,1},{1,2},{2,3},{3,4},{4,5},{5,6},{6,7},{7,8},{8,9},{9,10},{10,1... | collective-permute-start | bytes 786440 | tf_op jit(solution)/shard_map/ppermute | solution.py:15
  28.9 14.0 %collective-permute-start.2 = (bf16[256,4,128]{2,0,1:T(8,128)(2,1)}, bf16[256,4,128]{2,0,1:T(8,128)(2,1)S(1)}, u32[]{:S(2)}, u32[]{:S(2)}) collective-permute-start(bf16[256,4,128]{2,0,1:T(8,128)(2,1)} %collective-permute-done), channel_id=1, source_target_pairs={{0,1},{1,2},{2,3},{3,4},{4,5},{5,6},{6,7},{7,8},{8,9},{9,10},{10,1... | collective-permute-start | bytes 786440 | tf_op jit(solution)/shard_map/ppermute | solution.py:15
  44.0 17.3 %copy-start.2 = (f32[256,256]{1,0:T(8,128)S(1)}, f32[256,256]{1,0:T(8,128)}, u32[]{:S(2)}) copy-start(f32[256,256]{1,0:T(8,128)} %get-tuple-element.26) | copy-start | bytes 786436
  44.4 19.5 %collective-permute-start.12 = (bf16[256,4,128]{0,2,1:T(8,128)(2,1)S(1)}, bf16[256,4,128]{0,2,1:T(8,128)(2,1)S(1)}, u32[]{:S(2)}, u32[]{:S(2)}) collective-permute-start(bf16[256,4,128]{0,2,1:T(8,128)(2,1)S(1)} %add_convert_fusion.1), channel_id=1, source_target_pairs={{0,1},{1,2},{2,3},{3,4},{4,5},{5,6},{6,7},{7,8},{8,9},{9,10},{10,1... | collective-permute-start | bytes 786440 | tf_op jit(solution)/shard_map/ppermute | solution.py:15
  45.5 21.2 %collective-permute-start.8 = (bf16[256,4,128]{2,0,1:T(8,128)(2,1)}, bf16[256,4,128]{2,0,1:T(8,128)(2,1)}, u32[]{:S(2)}, u32[]{:S(2)}) collective-permute-start(bf16[256,4,128]{2,0,1:T(8,128)(2,1)} %add_convert_fusion.4), channel_id=1, source_target_pairs={{0,1},{1,2},{2,3},{3,4},{4,5},{5,6},{6,7},{7,8},{8,9},{9,10},{10,1... | collective-permute-start | bytes 786440 | tf_op jit(solution)/shard_map/ppermute | solution.py:15
  45.5 16.4 %collective-permute-start.5 = (bf16[256,4,128]{0,2,1:T(8,128)(2,1)S(1)}, bf16[256,4,128]{0,2,1:T(8,128)(2,1)S(1)}, u32[]{:S(2)}, u32[]{:S(2)}) collective-permute-start(bf16[256,4,128]{0,2,1:T(8,128)(2,1)S(1)} %collective-permute-done.3), channel_id=1, source_target_pairs={{0,1},{1,2},{2,3},{3,4},{4,5},{5,6},{6,7},{7,8},{8,9},{9,10},{10,1... | collective-permute-start | bytes 786440 | tf_op jit(solution)/shard_map/ppermute | solution.py:15
  45.5 15.8 %collective-permute-start.4 = (bf16[256,4,128]{2,0,1:T(8,128)(2,1)S(1)}, bf16[256,4,128]{2,0,1:T(8,128)(2,1)S(1)}, u32[]{:S(2)}, u32[]{:S(2)}) collective-permute-start(bf16[256,4,128]{2,0,1:T(8,128)(2,1)S(1)} %collective-permute-done.2), channel_id=1, source_target_pairs={{0,1},{1,2},{2,3},{3,4},{4,5},{5,6},{6,7},{7,8},{8,9},{9,10},{10,1... | collective-permute-start | bytes 786440 | tf_op jit(solution)/shard_map/ppermute | solution.py:15
  61.3 0.7 copy-start.5
  62.8 14.2 %copy-start.1 = (bf16[1,256,1024]{2,1,0:T(8,128)(2,1)S(1)}, bf16[1,256,1024]{2,1,0:T(8,128)(2,1)}, u32[]{:S(2)}) copy-start(bf16[1,256,1024]{2,1,0:T(8,128)(2,1)} %param.8) | copy-start | bytes 1572868
  66.4 10.6 %collective-permute-start.13 = (bf16[256,4,128]{0,2,1:T(8,128)(2,1)}, bf16[256,4,128]{0,2,1:T(8,128)(2,1)}, u32[]{:S(2)}, u32[]{:S(2)}) collective-permute-start(bf16[256,4,128]{0,2,1:T(8,128)(2,1)} %add_convert_fusion), channel_id=1, source_target_pairs={{0,13},{1,14},{2,15},{3,0},{4,1},{5,2},{6,3},{7,4},{8,5},{9,6},{10... | collective-permute-start | bytes 786440 | tf_op jit(solution)/shard_map/ppermute | solution.py:15
  67.8 8.2 %collective-permute-start.9 = (bf16[256,4,128]{2,0,1:T(8,128)(2,1)S(1)}, bf16[256,4,128]{2,0,1:T(8,128)(2,1)S(1)}, u32[]{:S(2)}, u32[]{:S(2)}) collective-permute-start(bf16[256,4,128]{2,0,1:T(8,128)(2,1)S(1)} %add_convert_fusion.3), channel_id=1, source_target_pairs={{0,13},{1,14},{2,15},{3,0},{4,1},{5,2},{6,3},{7,4},{8,5},{9,6},{10... | collective-permute-start | bytes 786440 | tf_op jit(solution)/shard_map/ppermute | solution.py:15
where the time goes:
time: 175 us; the launch traced here: 174 us
  blocking collectives  91.8 us (52%)
  waiting for transfers between devices  39.1 us (22%)
  matrix products  22.9 us (13%)
  local copies, waits for them, and re-layouts  7.64 us (4%)
  other arithmetic  5.53 us (3%)
  starting transfers between devices  5.3 us (3%)
    psum x1, blocking collectives, body(): summed = lax.psum(terms, ('dp', 'ctx'))  91.8 us
    ppermute x14, waiting for transfers between devices, from_behind(): return lax.ppermute(value, axis, pairs)  39.1 us
    unnamed x17, local copies, waits for them, and re-layouts  5.43 us
    ppermute x14, starting transfers between devices, from_behind(): return lax.ppermute(value, axis, pairs)  5.3 us
    dot_general x1, matrix products, body(): jnp.einsum('rd,rf->df', local, joined, preferred_element_type=jnp.float32)  3.6 us
  transfers between devices with their start and end apart: 14, of which 5 were waited for; matrix products, arithmetic and copies ran while one was open for 17% of the time, Pallas kernels for 0%

commit v1 on v0

v1 whole, which is shorter than its diff:
```python
import functools

import jax
import jax.numpy as jnp
from jax import lax
from jax.experimental import pallas as pl
from jax.experimental.pallas import tpu as pltpu
from jax.sharding import PartitionSpec as P

HD = 128
BLOCK = 128
MAXLEN = 768
GROUP = 4
FAR = 1 << 30
ALPHA = 1.0 / HD**0.5
SCALE = 1.0 / MAXLEN**0.5
VMEM = pl.BlockSpec(memory_space=pltpu.VMEM)
SMEM = pl.BlockSpec(memory_space=pltpu.SMEM)


def call(kernel, outs, args, specs=None, flops=0, scratch=()):
    moved = sum(a.size * a.dtype.itemsize for a in list(outs) + list(args))
    return pl.pallas_call(
        kernel,
        out_shape=tuple(outs),
        in_specs=specs or [VMEM] * len(args),
        out_specs=tuple([VMEM] * len(outs)),
        scratch_shapes=scratch,
        compiler_params=pltpu.CompilerParams(vmem_limit_bytes=24 * 1024 * 1024),
        cost_estimate=pl.CostEstimate(flops=flops, bytes_accessed=moved, transcendentals=0),
    )(*args)


def like(rows, cols, dtype=jnp.bfloat16):
    return jax.ShapeDtypeStruct((rows, cols), dtype)


def partner(value, steps):
    count = lax.axis_size("ctx")
    return lax.ppermute(value, "ctx", [(i, i ^ steps) for i in range(count)])


def around(value, steps):
    count = lax.axis_size("ctx")
    return lax.ppermute(value, "ctx", [(i, (i + steps) % count) for i in range(count)])


def place():
    return lax.rem(lax.axis_index("ctx"), GROUP)


def head_cols(h):
    return pl.ds(pl.multiple_of(h * HD, HD), HD)


def nt(a, b):
    return lax.dot_general(a, b, (((1,), (1,)), ((), ())), preferred_element_type=jnp.float32)


def nn(a, b):
    return jnp.dot(a, b, preferred_element_type=jnp.float32)


def split_kernel(a_ref, b_ref, *outs):
    me = place()
    for k in range(GROUP):
        cols = head_cols(me ^ k)
        outs[k][:, :HD] = a_ref[:, cols]
        outs[k][:, HD:] = b_ref[:, cols]


def project_kernel(x_ref, wk_ref, wq_ref, o0, o1, o2, o3, keys, queries):
    keys[...] = nn(x_ref[...], wk_ref[...]).astype(jnp.bfloat16)
    queries[...] = nn(x_ref[...], wq_ref[...]).astype(jnp.bfloat16)
    split_kernel(keys, queries, o0, o1, o2, o3)


def arrange_kernel(i0, i1, i2, i3, first, second, up, down):
    rows = i0.shape[0]
    span = up.shape[0] // rows
    me = place()
    for k, ref in enumerate((i0, i1, i2, i3)):
        j = me ^ k
        at = pl.ds(pl.multiple_of(j * rows, rows), rows)
        first[at, :] = ref[:, :HD]
        second[at, :] = ref[:, HD:]

        @pl.when(j >= GROUP - span)
        def _():
            up[pl.ds(pl.multiple_of((j - (GROUP - span)) * rows, rows), rows), :] = ref[:, :HD]

        @pl.when(j < span)
        def _():
            down[at, :] = ref[:, HD:]


def offset_of(row, shift, total):
    return lax.rem(row - shift + 2 * total, total)


def key_place(row, rows, shift, keep_ref, total):
    base = offset_of(row, shift, total)
    nblk = keep_ref.shape[1]
    raw = base + lax.broadcasted_iota(jnp.int32, (rows, HD), 0)
    b0 = base // BLOCK
    kept = jnp.full((rows, HD), keep_ref[0, b0], jnp.int32)
    for more in range(1, rows // BLOCK + 1):
        flag = keep_ref[0, lax.rem(b0 + more, nblk)]
        kept = jnp.where(raw >= (b0 + more) * BLOCK, flag, kept)
    where = jnp.where(raw >= total, raw - total, raw)
    return jnp.where(kept > 0, where, FAR)


def query_place(row, rows, shift, len_ref, total):
    base = offset_of(row, shift, total)
    raw = base + lax.broadcasted_iota(jnp.int32, (1, rows), 1)
    where = jnp.where(raw >= total, raw - total, raw)
    begin = jnp.zeros((1, rows), jnp.int32)
    end = jnp.int32(0)
    for u in range(len_ref.shape[1]):
        length = len_ref[0, u]
        end = end + length
        begin = begin + jnp.where(where >= end, length, 0)
    return where, begin


def tile_terms(k, v, q, o, kpos, qpos, qbegin):
    y = nt(k, q) * (0.5 * ALPHA)
    t = jnp.tanh(y)
    u = 1.0 + t
    kpos = jnp.concatenate([kpos] * (q.shape[0] // HD), axis=1)
    valid = (kpos >= qbegin) & (kpos <= qpos)
    att = jnp.where(valid, y * u, 0.0).astype(jnp.bfloat16)
    slope = u * (1.0 + y * (1.0 - t))
    ds = jnp.where(valid, nt(v, o) * slope, 0.0).astype(jnp.bfloat16)
    return att, ds


def inner_kernel(len_ref, shift_ref, keep_ref, k_ref, q_ref, v_ref, o_ref, out_t, dq_t, dk, dv):
    rows = k_ref.shape[0] // GROUP
    count = lax.axis_size("ctx")
    total = rows * count
    shift = shift_ref[0]
    base = (lax.axis_index("ctx") // GROUP) * (GROUP * rows)
    out_t[...] = jnp.zeros_like(out_t)
    dq_t[...] = jnp.zeros_like(dq_t)

    def key_step(kt, _):
        at = pl.ds(pl.multiple_of(kt * rows, rows), rows)
        k, v = k_ref[at, :], v_ref[at, :]
        k_t, v_t = k.T, v.T
        kpos = key_place(base + kt * rows, rows, shift, keep_ref, total)
        dk[at, :] = jnp.zeros((rows, HD), jnp.float32)
        dv[at, :] = jnp.zeros((rows, HD), jnp.float32)

        def query_step(qt, _):
            qs = pl.ds(pl.multiple_of(qt * rows, rows), rows)
            q, o = q_ref[qs, :], o_ref[qs, :]
            qpos, qbegin = query_place(base + qt * rows, rows, shift, len_ref, total)
            att, ds = tile_terms(k, v, q, o, kpos, qpos, qbegin)
            out_t[:, qs] += nn(v_t, att)
            dq_t[:, qs] += nn(k_t, ds)
            dv[at, :] += nn(att, o)
            dk[at, :] += nn(ds, q)
            return 0

        return lax.fori_loop(kt, GROUP, query_step, 0)

    lax.fori_loop(0, GROUP, key_step, 0)


def outer_kernel(
    len_ref, shift_ref, keep_ref, k_ref, q_ref, v_ref, o_ref, kp_ref, vp_ref, qn_ref, on_ref,
    out_in, dq_in, dk_in, dv_in, s0, s1, s2, s3, dqk, out_t, dq_t, dk, dv,
):
    rows = k_ref.shape[0] // GROUP
    span = kp_ref.shape[0] // rows
    count = lax.axis_size("ctx")
    total = rows * count
    shift = shift_ref[0]
    base = (lax.axis_index("ctx") // GROUP) * (GROUP * rows)
    me = place()
    out_t[...] = out_in[...]
    dq_t[...] = dq_in[...]
    dk[...] = dk_in[...]
    dv[...] = dv_in[...]

    def before(p, _):
        at = pl.ds(pl.multiple_of(p * rows, rows), rows)
        k, v = kp_ref[at, :], vp_ref[at, :]
        k_t, v_t = k.T, v.T
        kpos = key_place(base + (p - span) * rows, rows, shift, keep_ref, total)

        def query_step(qt, _):
            qs = pl.ds(pl.multiple_of(qt * rows, rows), rows)
            qpos, qbegin = query_place(base + qt * rows, rows, shift, len_ref, total)
            att, ds = tile_terms(k, v, q_ref[qs, :], o_ref[qs, :], kpos, qpos, qbegin)
            out_t[:, qs] += nn(v_t, att)
            dq_t[:, qs] += nn(k_t, ds)
            return 0

        return lax.fori_loop(0, p + 1, query_step, 0)

    lax.fori_loop(0, span, before, 0)

    def after(n, _):
        qs = pl.ds(pl.multiple_of(n * rows, rows), rows)
        q, o = qn_ref[qs, :], on_ref[qs, :]
        qpos, qbegin = query_place(base + (GROUP + n) * rows, rows, shift, len_ref, total)

        def key_step(kt, _):
            at = pl.ds(pl.multiple_of(kt * rows, rows), rows)
            kpos = key_place(base + kt * rows, rows, shift, keep_ref, total)
            att, ds = tile_terms(k_ref[at, :], v_ref[at, :], q, o, kpos, qpos, qbegin)
            dv[at, :] += nn(att, o)
            dk[at, :] += nn(ds, q)
            return 0

        return lax.fori_loop(n + 1, GROUP, key_step, 0)

    lax.fori_loop(0, span, after, 0)

    factor = 0.5 * SCALE * ALPHA
    dqk[:HD, :] = (dq_t[...] * factor).astype(jnp.bfloat16)
    for j in range(GROUP):
        at = slice(j * rows, (j + 1) * rows)
        dqk[HD:, at] = (dk[at, :] * factor).T.astype(jnp.bfloat16)
    for k, ref in enumerate((s0, s1, s2, s3)):
        at = pl.ds(pl.multiple_of((me ^ k) * rows, rows), rows)
        ref[:, :HD] = (out_t[:, at] * SCALE).T.astype(jnp.bfloat16)
        ref[:, HD:] = (dv[at, :] * SCALE).astype(jnp.bfloat16)


def terms_of(dqk, e0, e1, e2, e3):
    rows = e0.shape[0]
    me = place()
    total = None
    for k, ref in enumerate((e0, e1, e2, e3)):
        at = pl.ds(pl.multiple_of((me ^ k) * rows, rows), rows)
        part = nn(dqk[:, at], ref[...])
        total = part if total is None else total + part
    return total


def terms_kernel(dqk, e0, e1, e2, e3, whole):
    whole[...] = terms_of(dqk, e0, e1, e2, e3)


def block_terms_kernel(targets, dqk, e0, e1, e2, e3, *refs):
    outs, hold = refs[:-1], refs[-1]
    hold[...] = terms_of(dqk, e0, e1, e2, e3).astype(jnp.bfloat16)
    planes = lax.axis_size("ctx") // GROUP
    y = lax.axis_index("dp")
    z = lax.axis_index("ctx") // GROUP
    for (dy, dz), ref in zip(targets, outs):
        block = 2 * lax.rem(z + dz, planes) + (y ^ dy)
        width = ref.shape[1]
        ref[...] = hold[:, pl.ds(pl.multiple_of(block * width, width), width)]


def sum_kernel(*refs):
    ins, (near, far, hold) = refs[:-3], refs[-3:]
    total = ins[0][...].astype(jnp.float32)
    for ref in ins[1:]:
        total = total + ref[...].astype(jnp.float32)
    hold[...] = total.T
    share = near.shape[0]
    core = lax.rem(lax.axis_index("ctx"), 2)
    near[...] = hold[pl.ds(pl.multiple_of(core * share, share), share), :].astype(jnp.bfloat16)
    far[...] = hold[pl.ds(pl.multiple_of((1 - core) * share, share), share), :].astype(jnp.bfloat16)


def finish_kernel(r00, r01, r10, r11, gq, gk):
    y = lax.axis_index("dp")
    core = lax.rem(lax.axis_index("ctx"), 2)
    for (a, b), ref in zip(((0, 0), (0, 1), (1, 0), (1, 1)), (r00, r01, r10, r11)):
        cols = head_cols(2 * (y ^ a) + (core ^ b))
        gq[:, cols] = ref[:, :HD]
        gk[:, cols] = ref[:, HD:]


def merge_kernel(i0, i1, i2, i3, first, second):
    me = place()
    for k, ref in enumerate((i0, i1, i2, i3)):
        cols = head_cols(me ^ k)
        first[:, cols] = ref[:, :HD]
        second[:, cols] = ref[:, HD:]


def direct_reduce(dqk, gathered, share):
    streams = lax.axis_size("dp")
    count = lax.axis_size("ctx")
    planes = count // GROUP
    width = gathered[0].shape[1]
    block = width // (streams * planes)
    targets = [(dy, dz) for dz in range(planes) for dy in range(streams)]
    flops = 2 * dqk.shape[0] * dqk.shape[1] * width
    sends = call(
        functools.partial(block_terms_kernel, targets),
        [like(2 * HD, block)] * len(targets),
        (dqk, *gathered),
        flops=flops,
        scratch=[pltpu.VMEM((2 * HD, width), jnp.bfloat16)],
    )
    arrived = []
    for (dy, dz), value in zip(targets, sends):
        if (dy, dz) != (0, 0):
            pairs = []
            for y in range(streams):
                for i in range(count):
                    pairs.append((y * count + i, (y ^ dy) * count + (i + dz * GROUP) % count))
            value = lax.ppermute(value, ("dp", "ctx"), pairs)
        arrived.append(value)
    near, far = call(
        sum_kernel,
        [like(share, 2 * HD)] * 2,
        arrived,
        scratch=[pltpu.VMEM((block, 2 * HD), jnp.float32)],
    )
    received = []
    for a in range(2):
        for b in range(2):
            pairs = []
            for y in range(2):
                for i in range(count):
                    z, x, c = i // 4, (i // 2) % 2, i % 2
                    pairs.append((y * count + i, (x ^ a) * count + 4 * z + 2 * y + (c ^ b)))
            received.append(lax.ppermute((near, far)[b], ("dp", "ctx"), pairs))
    return call(finish_kernel, [like(share, GROUP * HD)] * 2, received)


def general_reduce(dqk, gathered, share):
    count = lax.axis_size("ctx")
    planes = count // GROUP
    width = gathered[0].shape[1]
    flops = 2 * dqk.shape[0] * dqk.shape[1] * width
    (whole,) = call(
        terms_kernel, [like(2 * HD, width, jnp.float32)], (dqk, *gathered), flops=flops
    )
    whole = lax.psum(whole.T, "dp")
    same_head = [[g * GROUP + j for g in range(planes)] for j in range(GROUP)]
    plane = [[g * GROUP + j for j in range(GROUP)] for g in range(planes)]
    part = lax.psum_scatter(
        whole, "ctx", scatter_dimension=0, axis_index_groups=same_head, tiled=True
    ).astype(jnp.bfloat16)
    part = lax.all_to_all(
        part.reshape(GROUP, share, 2 * HD), "ctx", 0, 0, axis_index_groups=plane, tiled=True
    )
    part = jnp.moveaxis(part.reshape(GROUP, share, 2, HD), 0, 2)
    return part[:, 0].reshape(share, GROUP * HD), part[:, 1].reshape(share, GROUP * HD)


def body(events, w_query, w_key, values, grad_out, lengths, stream_shift, block_keep):
    rows, width = events.shape[1:]
    features = w_query.shape[1]
    count = lax.axis_size("ctx")
    local = events[0]
    all_rows = GROUP * rows
    halo = MAXLEN
    pair = like(rows, 2 * HD)
    full = like(all_rows, HD)
    edge = like(halo, HD)

    vo = call(split_kernel, [pair] * GROUP, (values[0], grad_out[0]))
    vo = (vo[0],) + tuple(partner(vo[k], k) for k in range(1, GROUP))
    kq = call(
        project_kernel,
        [pair] * GROUP,
        (local, w_key, w_query),
        flops=4 * rows * width * features,
        scratch=[pltpu.VMEM((rows, features), jnp.bfloat16)] * 2,
    )
    kq = (kq[0],) + tuple(partner(kq[k], k) for k in range(1, GROUP))
    v, o, v_up, o_down = call(arrange_kernel, [full, full, edge, edge], vo)
    v_prev, o_next = around(v_up, GROUP), around(o_down, -GROUP)
    k, q, k_up, q_down = call(arrange_kernel, [full, full, edge, edge], kq)
    k_prev, q_next = around(k_up, GROUP), around(q_down, -GROUP)

    e1 = partner(local, 1)
    late, _ = lax.optimization_barrier((local, kq[2]))
    e2 = partner(late, 2)
    e3 = partner(e2, 1)
    info = (lengths, stream_shift, block_keep)
    wide, tall = like(HD, all_rows, jnp.float32), like(all_rows, HD, jnp.float32)
    sums = call(
        inner_kernel,
        [wide, wide, tall, tall],
        (*info, k, q, v, o),
        specs=[SMEM] * 3 + [VMEM] * 4,
        flops=2 * 6 * 10 * rows * rows * HD,
    )
    *parts, dqk = call(
        outer_kernel,
        [pair] * GROUP + [like(2 * HD, all_rows)],
        (*info, k, q, v, o, k_prev, v_prev, q_next, o_next, *sums),
        specs=[SMEM] * 3 + [VMEM] * 12,
        flops=2 * 8 * 6 * rows * rows * HD,
        scratch=[
            pltpu.VMEM((HD, all_rows), jnp.float32),
            pltpu.VMEM((HD, all_rows), jnp.float32),
            pltpu.VMEM((all_rows, HD), jnp.float32),
            pltpu.VMEM((all_rows, HD), jnp.float32),
        ],
    )
    share = width // count
    reduce = direct_reduce if lax.axis_size("dp") == 2 and count == 16 else general_reduce
    grad_wq, grad_wk = reduce(dqk, (local, e1, e2, e3), share)
    parts = (parts[0],) + tuple(partner(parts[k], k) for k in range(1, GROUP))
    attended, grad_values = call(merge_kernel, [like(rows, features)] * 2, parts)
    return (attended[None], grad_values[None], grad_wq, grad_wk)


def solution(mesh):
    placed = (
        P("dp", "ctx", None),
        P(),
        P(),
        P("dp", "ctx", None),
        P("dp", "ctx", None),
        P("dp", None),
        P("dp"),
        P("dp", None),
    )
    return jax.shard_map(
        body,
        mesh=mesh,
        in_specs=placed,
        out_specs=(P("dp", "ctx", None), P("dp", "ctx", None), P("ctx", None), P("ctx", None)),
        check_vma=False,
    )
```

time: 175 us -> 88.4 us (0.51)
  blocking collectives: 91.8 us -> 0 us
  starting transfers between devices: 5.3 us -> 36 us
  matrix products: 22.9 us -> 0 us
  Pallas kernels: 0 us -> 18.7 us
  waiting for transfers between devices: 39.1 us -> 28.8 us
  other arithmetic: 5.53 us -> 0 us
  local copies, waits for them, and re-layouts: 7.64 us -> 3.11 us
    psum x1 -> x0, blocking collectives: 91.8 us -> none  [body(): summed = lax.psum(terms, ('dp', 'ctx'))]
    ppermute x14 -> x27, starting transfers between devices: 5.3 us -> 36 us  [the longest x7 12.7 us: direct_reduce(): value = lax.ppermute(value, ('dp', 'ctx'), pairs)]
    dot_general x27 -> x0, matrix products: 22.9 us -> none  [the longest x1 3.6 us: body(): jnp.einsum('rd,rf->df', local, joined, preferred_element_type=jnp.float32)]
    pallas_call x0 -> x10, Pallas kernels: none -> 18.7 us  [call(): pl.pallas_call(kernel, out_shape=tuple(outs), in_specs=specs or [VMEM] *...]
    ppermute x14 -> x27, waiting for transfers between devices: 39.1 us -> 28.8 us  [the longest x12 20.2 us: partner(): return lax.ppermute(value, 'ctx', [(i, i ^ steps) for i in range(count)])]
    convert_element_type x4 -> x0, other arithmetic: 2.57 us -> none  [the longest x2 1.76 us: body(): carried[1].astype(jnp.bfloat16)]
    unnamed x17 -> x12, local copies, waits for them, and re-layouts: 5.43 us -> 3.11 us
  transfers between devices with their start and end apart: 14 -> 27, of which waited for: 5 -> 12; matrix products, arithmetic and copies ran while one was open for 17% -> 0% of each run, Pallas kernels for 0% -> 16%
where the time goes in v1:
time: 88.4 us; the launch traced here: 88.1 us
  starting transfers between devices  36 us (41%)
  waiting for transfers between devices  28.8 us (33%)
  Pallas kernels  18.7 us (21%)
  local copies, waits for them, and re-layouts  3.11 us (4%)
  between operations  1.45 us (2%)
    ppermute x12, waiting for transfers between devices, partner(): return lax.ppermute(value, 'ctx', [(i, i ^ steps) for i in range(count)])  20.2 us
    pallas_call x10, Pallas kernels, call(): pl.pallas_call(kernel, out_shape=tuple(outs), in_specs=specs or [VMEM] *...  18.7 us
    ppermute x7, starting transfers between devices, direct_reduce(): value = lax.ppermute(value, ('dp', 'ctx'), pairs)  12.7 us
    ppermute x12, starting transfers between devices, partner(): return lax.ppermute(value, 'ctx', [(i, i ^ steps) for i in range(count)])  9.48 us
    ppermute x4, starting transfers between devices, around(): lax.ppermute(value, 'ctx', [(i, (i + steps) % count) for i in range(count)])  7.84 us
    ppermute x4, starting transfers between devices, direct_reduce(): received.append(lax.ppermute((near, far)[b], ('dp', 'ctx'), pairs))  6 us
    ppermute x7, waiting for transfers between devices, direct_reduce(): value = lax.ppermute(value, ('dp', 'ctx'), pairs)  5.42 us
    unnamed x12, local copies, waits for them, and re-layouts  3.11 us
  transfers between devices with their start and end apart: 27, of which 12 were waited for; matrix products, arithmetic and copies ran while one was open for 0% of the time, Pallas kernels for 16%

profile of v1, /device:TPU:0, one launch (start us, length us, event | category | flops | bytes accessed | tf_op | source)
XLA Modules:
  0.0 88.1 jit_solution(5155616293229262130)
XLA Ops:
  0.6 1.2 %copy-done = bf16[1024,512]{1,0:T(8,128)(2,1)S(1)} copy-done((bf16[1024,512]{1,0:T(8,128)(2,1)S(1)}, bf16[1024,512]{1,0:T(8,128)(2,1)}, u32[]{:S(2)}) %copy-start) | copy-done | bytes 1048600
  1.9 1.2 %copy-done.1 = bf16[1024,512]{1,0:T(8,128)(2,1)S(1)} copy-done((bf16[1024,512]{1,0:T(8,128)(2,1)S(1)}, bf16[1024,512]{1,0:T(8,128)(2,1)}, u32[]{:S(2)}) %copy-start.1) | copy-done | bytes 1048600
  3.1 2.0 %shard_map.111 = (bf16[256,256]{1,0:T(8,128)(2,1)S(1)}, bf16[256,256]{1,0:T(8,128)(2,1)S(1)}, bf16[256,256]{1,0:T(8,128)(2,1)S(1)}, bf16[256,256]{1,0:T(8,128)(2,1)S(1)}) custom-call(bf16[256,1024]{1,0:T(8,128)(2,1)} %bitcast.x_ref.e0, bf16[1024,512]{1,0:T(8,128)(2,1)S(1)} %copy-done, bf16[1024,512]{1,0:T(8,128)(2,1)S(1)} %copy-done.1), custom_call_target="tpu_custom_call" | custom-call | flops 536870912 | bytes 3145728 | tf_op jit(solution)/shard_map/pallas_call | solution.py:23
  5.1 3.0 %collective-permute-start.1 = (bf16[256,256]{1,0:T(8,128)(2,1)S(1)}, bf16[256,256]{1,0:T(8,128)(2,1)S(1)}, u32[]{:S(2)}, u32[]{:S(2)}) collective-permute-start(bf16[256,256]{1,0:T(8,128)(2,1)S(1)} %get-tuple-element.46), channel_id=1, source_target_pairs={{0,2},{1,3},{2,0},{3,1},{4,6},{5,7},{6,4},{7,5},{8,10},{9,11},{10,... | collective-permute-start | bytes 393224 | tf_op jit(solution)/shard_map/ppermute | solution.py:40
  8.1 3.5 %collective-permute-done.1.i2 = bf16[256,256]{1,0:T(8,128)(2,1)S(1)} collective-permute-done((bf16[256,256]{1,0:T(8,128)(2,1)S(1)}, bf16[256,256]{1,0:T(8,128)(2,1)S(1)}, u32[]{:S(2)}, u32[]{:S(2)}) %collective-permute-start.1) | collective-permute-done | bytes 131104 | tf_op jit(solution)/shard_map/ppermute | solution.py:40
  11.6 1.7 %collective-permute-start.14 = (bf16[256,1024]{1,0:T(8,128)(2,1)}, bf16[256,1024]{1,0:T(8,128)(2,1)S(1)}, u32[]{:S(2)}, u32[]{:S(2)}) collective-permute-start(bf16[256,1024]{1,0:T(8,128)(2,1)} %bitcast.x_ref.e0), channel_id=1, source_target_pairs={{0,2},{1,3},{2,0},{3,1},{4,6},{5,7},{6,4},{7,5},{8,10},{9,11},{10,... | collective-permute-start | bytes 1572872 | tf_op jit(solution)/shard_map/ppermute | solution.py:40
  14.4 11.9 %collective-permute-done.14.e2 = bf16[256,1024]{1,0:T(8,128)(2,1)S(1)} collective-permute-done((bf16[256,1024]{1,0:T(8,128)(2,1)}, bf16[256,1024]{1,0:T(8,128)(2,1)S(1)}, u32[]{:S(2)}, u32[]{:S(2)}) %collective-permute-start.14) | collective-permute-done | bytes 524320 | tf_op jit(solution)/shard_map/ppermute | solution.py:40
  26.8 1.6 %collective-permute-start.6 = (bf16[768,128]{1,0:T(8,128)(2,1)S(1)}, bf16[768,128]{1,0:T(8,128)(2,1)S(1)}, u32[]{:S(2)}, u32[]{:S(2)}) collective-permute-start(bf16[768,128]{1,0:T(8,128)(2,1)S(1)} %get-tuple-element.56), channel_id=1, source_target_pairs={{0,4},{1,5},{2,6},{3,7},{4,8},{5,9},{6,10},{7,11},{8,12},{9,13},{1... | collective-permute-start | bytes 589832 | tf_op jit(solution)/shard_map/ppermute | solution.py:45
  28.5 1.1 %collective-permute-start.4 = (bf16[256,256]{1,0:T(8,128)(2,1)S(1)}, bf16[256,256]{1,0:T(8,128)(2,1)S(1)}, u32[]{:S(2)}, u32[]{:S(2)}) collective-permute-start(bf16[256,256]{1,0:T(8,128)(2,1)S(1)} %get-tuple-element.52), channel_id=1, source_target_pairs={{0,2},{1,3},{2,0},{3,1},{4,6},{5,7},{6,4},{7,5},{8,10},{9,11},{10,... | collective-permute-start | bytes 393224 | tf_op jit(solution)/shard_map/ppermute | solution.py:40
  29.6 0.8 collective-permute-start.5
  30.4 4.4 %collective-permute-done.4.i2 = bf16[256,256]{1,0:T(8,128)(2,1)S(1)} collective-permute-done((bf16[256,256]{1,0:T(8,128)(2,1)S(1)}, bf16[256,256]{1,0:T(8,128)(2,1)S(1)}, u32[]{:S(2)}, u32[]{:S(2)}) %collective-permute-start.4) | collective-permute-done | bytes 131104 | tf_op jit(solution)/shard_map/ppermute | solution.py:40
  34.8 2.3 %collective-permute-start.8 = (bf16[768,128]{1,0:T(8,128)(2,1)S(1)}, bf16[768,128]{1,0:T(8,128)(2,1)S(1)}, u32[]{:S(2)}, u32[]{:S(2)}) collective-permute-start(bf16[768,128]{1,0:T(8,128)(2,1)S(1)} %get-tuple-element.58), channel_id=1, source_target_pairs={{0,12},{1,13},{2,14},{3,15},{4,0},{5,1},{6,2},{7,3},{8,4},{9,5},{1... | collective-permute-start | bytes 589832 | tf_op jit(solution)/shard_map/ppermute | solution.py:45
  37.3 1.4 %collective-permute-start.7 = (bf16[768,128]{1,0:T(8,128)(2,1)S(1)}, bf16[768,128]{1,0:T(8,128)(2,1)S(1)}, u32[]{:S(2)}, u32[]{:S(2)}) collective-permute-start(bf16[768,128]{1,0:T(8,128)(2,1)S(1)} %get-tuple-element.57), channel_id=1, source_target_pairs={{0,4},{1,5},{2,6},{3,7},{4,8},{5,9},{6,10},{7,11},{8,12},{9,13},{1... | collective-permute-start | bytes 589832 | tf_op jit(solution)/shard_map/ppermute | solution.py:45
  38.7 2.5 %collective-permute-start.9 = (bf16[768,128]{1,0:T(8,128)(2,1)S(1)}, bf16[768,128]{1,0:T(8,128)(2,1)S(1)}, u32[]{:S(2)}, u32[]{:S(2)}) collective-permute-start(bf16[768,128]{1,0:T(8,128)(2,1)S(1)} %get-tuple-element.59), channel_id=1, source_target_pairs={{0,12},{1,13},{2,14},{3,15},{4,0},{5,1},{6,2},{7,3},{8,4},{9,5},{1... | collective-permute-start | bytes 589832 | tf_op jit(solution)/shard_map/ppermute | solution.py:45
  42.5 6.2 %shard_map.115 = (f32[128,1024]{1,0:T(8,128)S(1)}, f32[128,1024]{1,0:T(8,128)S(1)}, f32[1024,128]{1,0:T(8,128)S(1)}, f32[1024,128]{1,0:T(8,128)S(1)}) custom-call(s32[1,8]{1,0:T(1,128)S(1)} %copy-done.4, s32[1]{0:T(128)S(6)} %copy.12.shift_ref, s32[1,32]{1,0:T(1,128)S(1)} %copy-done.5, bf16[1024,128]{1,0:T(8,128)(2,1)S(1)} %get-tuple-element.48.k_ref, ...), custom_call_target="tpu_custom_call" | custom-call | flops 1006632960 | bytes 3145892 | tf_op jit(solution)/shard_map/pallas_call | solution.py:23
  48.8 0.8 collective-permute-done.9.on_ref
  49.6 6.4 %shard_map.116 = (bf16[256,256]{1,0:T(8,128)(2,1)S(1)}, bf16[256,256]{1,0:T(8,128)(2,1)S(1)}, bf16[256,256]{1,0:T(8,128)(2,1)S(1)}, bf16[256,256]{1,0:T(8,128)(2,1)S(1)}, bf16[256,1024]{1,0:T(8,128)(2,1)S(1)}) custom-call(s32[1,8]{1,0:T(1,128)S(1)} %copy-done.4, s32[1]{0:T(128)S(6)} %copy.12.shift_ref, s32[1,32]{1,0:T(1,128)S(1)} %copy-done.5, ...), custom_call_target="tpu_custom_call" | custom-call | flops 805306368 | bytes 4980900 | tf_op jit(solution)/shard_map/pallas_call | solution.py:23
  56.1 1.9 %shard_map.118 = (bf16[256,128]{1,0:T(8,128)(2,1)S(1)}, bf16[256,128]{1,0:T(8,128)(2,1)S(1)}, bf16[256,128]{1,0:T(8,128)(2,1)S(1)}, bf16[256,128]{1,0:T(8,128)(2...) custom-call(bf16[256,1024]{1,0:T(8,128)(2,1)S(1)} %get-tuple-element, ...), custom_call_target="tpu_custom_call" | custom-call | flops 536870912 | bytes 3145728 | tf_op jit(solution)/shard_map/pallas_call | solution.py:23
  58.0 1.6 %collective-permute-start.16 = (bf16[256,128]{1,0:T(8,128)(2,1)S(1)}, bf16[256,128]{1,0:T(8,128)(2,1)S(1)}, u32[]{:S(2)}, u32[]{:S(2)}) collective-permute-start(bf16[256,128]{1,0:T(8,128)(2,1)S(1)} %get-tuple-element.73), channel_id=1, source_target_pairs={{0,16},{1,17},{2,18},{3,19},{4,20},{5,21},{6,22},{7,23},{8,24},{9,... | collective-permute-start | bytes 196616 | tf_op jit(solution)/shard_map/ppermute | solution.py:312
  59.5 1.4 %collective-permute-start.17 = (bf16[256,128]{1,0:T(8,128)(2,1)S(1)}, bf16[256,128]{1,0:T(8,128)(2,1)S(1)}, u32[]{:S(2)}, u32[]{:S(2)}) collective-permute-start(bf16[256,128]{1,0:T(8,128)(2,1)S(1)} %get-tuple-element.74), channel_id=1, source_target_pairs={{0,4},{1,5},{2,6},{3,7},{4,8},{5,9},{6,10},{7,11},{8,12},{9,13},{1... | collective-permute-start | bytes 196616 | tf_op jit(solution)/shard_map/ppermute | solution.py:312
  60.9 1.6 %collective-permute-start.18 = (bf16[256,128]{1,0:T(8,128)(2,1)S(1)}, bf16[256,128]{1,0:T(8,128)(2,1)S(1)}, u32[]{:S(2)}, u32[]{:S(2)}) collective-permute-start(bf16[256,128]{1,0:T(8,128)(2,1)S(1)} %get-tuple-element.75), channel_id=1, source_target_pairs={{0,20},{1,21},{2,22},{3,23},{4,24},{5,25},{6,26},{7,27},{8,28},{9,... | collective-permute-start | bytes 196616 | tf_op jit(solution)/shard_map/ppermute | solution.py:312
  62.5 1.7 %collective-permute-start.19 = (bf16[256,128]{1,0:T(8,128)(2,1)S(1)}, bf16[256,128]{1,0:T(8,128)(2,1)S(1)}, u32[]{:S(2)}, u32[]{:S(2)}) collective-permute-start(bf16[256,128]{1,0:T(8,128)(2,1)S(1)} %get-tuple-element.76), channel_id=1, source_target_pairs={{0,8},{1,9},{2,10},{3,11},{4,12},{5,13},{6,14},{7,15},{8,0},{9,1},... | collective-permute-start | bytes 196616 | tf_op jit(solution)/shard_map/ppermute | solution.py:312
  64.1 2.2 %collective-permute-start.20 = (bf16[256,128]{1,0:T(8,128)(2,1)S(1)}, bf16[256,128]{1,0:T(8,128)(2,1)S(1)}, u32[]{:S(2)}, u32[]{:S(2)}) collective-permute-start(bf16[256,128]{1,0:T(8,128)(2,1)S(1)} %get-tuple-element.77), channel_id=1, source_target_pairs={{0,24},{1,25},{2,26},{3,27},{4,28},{5,29},{6,30},{7,31},{8,16},{9,... | collective-permute-start | bytes 196616 | tf_op jit(solution)/shard_map/ppermute | solution.py:312
  66.4 1.9 %collective-permute-start.11 = (bf16[256,256]{1,0:T(8,128)(2,1)S(1)}, bf16[256,256]{1,0:T(8,128)(2,1)S(1)}, u32[]{:S(2)}, u32[]{:S(2)}) collective-permute-start(bf16[256,256]{1,0:T(8,128)(2,1)S(1)} %get-tuple-element.66), channel_id=1, source_target_pairs={{0,2},{1,3},{2,0},{3,1},{4,6},{5,7},{6,4},{7,5},{8,10},{9,11},{10,... | collective-permute-start | bytes 393224 | tf_op jit(solution)/shard_map/ppermute | solution.py:40
  68.4 1.7 %collective-permute-done.19.refs_4_ = bf16[256,128]{1,0:T(8,128)(2,1)S(1)} collective-permute-done((bf16[256,128]{1,0:T(8,128)(2,1)S(1)}, bf16[256,128]{1,0:T(8,128)(2,1)S(1)}, u32[]{:S(2)}, u32[]{:S(2)}) %collective-permute-start.19) | collective-permute-done | bytes 65568 | tf_op jit(solution)/shard_map/ppermute | solution.py:312
  70.1 2.7 %collective-permute-start.21 = (bf16[256,128]{1,0:T(8,128)(2,1)S(1)}, bf16[256,128]{1,0:T(8,128)(2,1)S(1)}, u32[]{:S(2)}, u32[]{:S(2)}) collective-permute-start(bf16[256,128]{1,0:T(8,128)(2,1)S(1)} %get-tuple-element.78), channel_id=1, source_target_pairs={{0,12},{1,13},{2,14},{3,15},{4,0},{5,1},{6,2},{7,3},{8,4},{9,5},{1... | collective-permute-start | bytes 196616 | tf_op jit(solution)/shard_map/ppermute | solution.py:312
  72.8 1.6 %collective-permute-start.22 = (bf16[256,128]{1,0:T(8,128)(2,1)S(1)}, bf16[256,128]{1,0:T(8,128)(2,1)S(1)}, u32[]{:S(2)}, u32[]{:S(2)}) collective-permute-start(bf16[256,128]{1,0:T(8,128)(2,1)S(1)} %get-tuple-element.79), channel_id=1, source_target_pairs={{0,28},{1,29},{2,30},{3,31},{4,16},{5,17},{6,18},{7,19},{8,20},{9,... | collective-permute-start | bytes 196616 | tf_op jit(solution)/shard_map/ppermute | solution.py:312
  74.7 3.2 %collective-permute-done.22.refs_7_ = bf16[256,128]{1,0:T(8,128)(2,1)S(1)} collective-permute-done((bf16[256,128]{1,0:T(8,128)(2,1)S(1)}, bf16[256,128]{1,0:T(8,128)(2,1)S(1)}, u32[]{:S(2)}, u32[]{:S(2)}) %collective-permute-start.22) | collective-permute-done | bytes 65568 | tf_op jit(solution)/shard_map/ppermute | solution.py:312
  78.8 5.3 %collective-permute-start.25 = (bf16[64,256]{1,0:T(8,128)(2,1)S(1)}, bf16[64,256]{1,0:T(8,128)(2,1)S(1)}, u32[]{:S(2)}, u32[]{:S(2)}) collective-permute-start(bf16[64,256]{1,0:T(8,128)(2,1)S(1)} %get-tuple-element.80), channel_id=1, source_target_pairs={{0,16},{1,17},{2,0},{3,1},{4,20},{5,21},{6,4},{7,5},{8,24},{9,25},... | collective-permute-start | bytes 98312 | tf_op jit(solution)/shard_map/ppermute | solution.py:328
  84.1 0.9 %shard_map.117 = (bf16[256,512]{1,0:T(8,128)(2,1)}, bf16[256,512]{1,0:T(8,128)(2,1)}) custom-call(bf16[256,256]{1,0:T(8,128)(2,1)S(1)} %get-tuple-element.64.i0, bf16[256,256]{1,0:T(8,128)(2,1)S(1)} %collective-permute-done.10.i1, bf16[256,256]{1,0:T(8,128)(2,1)S(1)} %collective-permute-done.11.i2, bf16[256,256]{1,0:T(8,128)(2,1)S(1)} %collective-permute-done.12.i3), custom_call_target="tpu_custom_call" | custom-call | bytes 1048576 | tf_op jit(solution)/shard_map/pallas_call | solution.py:23
  85.7 1.7 %collective-permute-done.26.r11 = bf16[64,256]{1,0:T(8,128)(2,1)S(1)} collective-permute-done((bf16[64,256]{1,0:T(8,128)(2,1)S(1)}, bf16[64,256]{1,0:T(8,128)(2,1)S(1)}, u32[]{:S(2)}, u32[]{:S(2)}) %collective-permute-start.26) | collective-permute-done | bytes 32800 | tf_op jit(solution)/shard_map/ppermute | solution.py:328
  87.4 0.7 shard_map.120
  (44 shorter events, 4.5 us)
Async XLA Ops:
  0.6 1.2 %copy-start = (bf16[1024,512]{1,0:T(8,128)(2,1)S(1)}, bf16[1024,512]{1,0:T(8,128)(2,1)}, u32[]{:S(2)}) copy-start(bf16[1024,512]{1,0:T(8,128)(2,1)} %wk_ref.1) | copy-start | bytes 3145732
  1.9 1.2 %copy-start.1 = (bf16[1024,512]{1,0:T(8,128)(2,1)S(1)}, bf16[1024,512]{1,0:T(8,128)(2,1)}, u32[]{:S(2)}) copy-start(bf16[1024,512]{1,0:T(8,128)(2,1)} %wq_ref.1) | copy-start | bytes 3145732
  3.1 10.7 %copy-start.2 = (bf16[1,256,512]{2,1,0:T(8,128)(2,1)S(1)}, bf16[1,256,512]{2,1,0:T(8,128)(2,1)}, u32[]{:S(2)}) copy-start(bf16[1,256,512]{2,1,0:T(8,128)(2,1)} %param.11) | copy-start | bytes 786436
  3.1 10.7 %copy-start.3 = (bf16[1,256,512]{2,1,0:T(8,128)(2,1)S(1)}, bf16[1,256,512]{2,1,0:T(8,128)(2,1)}, u32[]{:S(2)}) copy-start(bf16[1,256,512]{2,1,0:T(8,128)(2,1)} %param.12) | copy-start | bytes 786436
  5.1 6.5 %collective-permute-start.1 = (bf16[256,256]{1,0:T(8,128)(2,1)S(1)}, bf16[256,256]{1,0:T(8,128)(2,1)S(1)}, u32[]{:S(2)}, u32[]{:S(2)}) collective-permute-start(bf16[256,256]{1,0:T(8,128)(2,1)S(1)} %get-tuple-element.46), channel_id=1, source_target_pairs={{0,2},{1,3},{2,0},{3,1},{4,6},{5,7},{6,4},{7,5},{8,10},{9,11},{10,... | collective-permute-start | bytes 393224 | tf_op jit(solution)/shard_map/ppermute | solution.py:40
  11.6 14.7 %collective-permute-start.14 = (bf16[256,1024]{1,0:T(8,128)(2,1)}, bf16[256,1024]{1,0:T(8,128)(2,1)S(1)}, u32[]{:S(2)}, u32[]{:S(2)}) collective-permute-start(bf16[256,1024]{1,0:T(8,128)(2,1)} %bitcast.x_ref.e0), channel_id=1, source_target_pairs={{0,2},{1,3},{2,0},{3,1},{4,6},{5,7},{6,4},{7,5},{8,10},{9,11},{10,... | collective-permute-start | bytes 1572872 | tf_op jit(solution)/shard_map/ppermute | solution.py:40
  13.3 13.0 %collective-permute-start = (bf16[256,256]{1,0:T(8,128)(2,1)S(1)}, bf16[256,256]{1,0:T(8,128)(2,1)S(1)}, u32[]{:S(2)}, u32[]{:S(2)}) collective-permute-start(bf16[256,256]{1,0:T(8,128)(2,1)S(1)} %get-tuple-element.45), channel_id=1, source_target_pairs={{0,1},{1,0},{2,3},{3,2},{4,5},{5,4},{6,7},{7,6},{8,9},{9,8},{10,11... | collective-permute-start | bytes 393224 | tf_op jit(solution)/shard_map/ppermute | solution.py:40
  13.3 13.3 %collective-permute-start.2 = (bf16[256,256]{1,0:T(8,128)(2,1)S(1)}, bf16[256,256]{1,0:T(8,128)(2,1)S(1)}, u32[]{:S(2)}, u32[]{:S(2)}) collective-permute-start(bf16[256,256]{1,0:T(8,128)(2,1)S(1)} %get-tuple-element.47), channel_id=1, source_target_pairs={{0,3},{1,2},{2,1},{3,0},{4,7},{5,6},{6,5},{7,4},{8,11},{9,10},{10,... | collective-permute-start | bytes 393224 | tf_op jit(solution)/shard_map/ppermute | solution.py:40
  13.8 15.7 %collective-permute-start.3 = (bf16[256,256]{1,0:T(8,128)(2,1)S(1)}, bf16[256,256]{1,0:T(8,128)(2,1)S(1)}, u32[]{:S(2)}, u32[]{:S(2)}) collective-permute-start(bf16[256,256]{1,0:T(8,128)(2,1)S(1)} %get-tuple-element.51), channel_id=1, source_target_pairs={{0,1},{1,0},{2,3},{3,2},{4,5},{5,4},{6,7},{7,6},{8,9},{9,8},{10,11... | collective-permute-start | bytes 393224 | tf_op jit(solution)/shard_map/ppermute | solution.py:40
  14.0 42.0 %collective-permute-start.13 = (bf16[256,1024]{1,0:T(8,128)(2,1)}, bf16[256,1024]{1,0:T(8,128)(2,1)S(1)}, u32[]{:S(2)}, u32[]{:S(2)}) collective-permute-start(bf16[256,1024]{1,0:T(8,128)(2,1)} %bitcast.x_ref.e0), channel_id=1, source_target_pairs={{0,1},{1,0},{2,3},{3,2},{4,5},{5,4},{6,7},{7,6},{8,9},{9,8},{10,11... | collective-permute-start | bytes 1572872 | tf_op jit(solution)/shard_map/ppermute | solution.py:40
  26.3 29.7 %collective-permute-start.15 = (bf16[256,1024]{1,0:T(8,128)(2,1)S(1)}, bf16[256,1024]{1,0:T(8,128)(2,1)S(1)}, u32[]{:S(2)}, u32[]{:S(2)}) collective-permute-start(bf16[256,1024]{1,0:T(8,128)(2,1)S(1)} %collective-permute-done.14.e2), channel_id=1, source_target_pairs={{0,1},{1,0},{2,3},{3,2},{4,5},{5,4},{6,7},{7,6},{8,9},{9,8},{10,11... | collective-permute-start | bytes 1572872 | tf_op jit(solution)/shard_map/ppermute | solution.py:40
  26.8 11.8 %collective-permute-start.6 = (bf16[768,128]{1,0:T(8,128)(2,1)S(1)}, bf16[768,128]{1,0:T(8,128)(2,1)S(1)}, u32[]{:S(2)}, u32[]{:S(2)}) collective-permute-start(bf16[768,128]{1,0:T(8,128)(2,1)S(1)} %get-tuple-element.56), channel_id=1, source_target_pairs={{0,4},{1,5},{2,6},{3,7},{4,8},{5,9},{6,10},{7,11},{8,12},{9,13},{1... | collective-permute-start | bytes 589832 | tf_op jit(solution)/shard_map/ppermute | solution.py:45
  28.5 6.3 %collective-permute-start.4 = (bf16[256,256]{1,0:T(8,128)(2,1)S(1)}, bf16[256,256]{1,0:T(8,128)(2,1)S(1)}, u32[]{:S(2)}, u32[]{:S(2)}) collective-permute-start(bf16[256,256]{1,0:T(8,128)(2,1)S(1)} %get-tuple-element.52), channel_id=1, source_target_pairs={{0,2},{1,3},{2,0},{3,1},{4,6},{5,7},{6,4},{7,5},{8,10},{9,11},{10,... | collective-permute-start | bytes 393224 | tf_op jit(solution)/shard_map/ppermute | solution.py:40
  29.6 7.5 %collective-permute-start.5 = (bf16[256,256]{1,0:T(8,128)(2,1)S(1)}, bf16[256,256]{1,0:T(8,128)(2,1)S(1)}, u32[]{:S(2)}, u32[]{:S(2)}) collective-permute-start(bf16[256,256]{1,0:T(8,128)(2,1)S(1)} %get-tuple-element.53), channel_id=1, source_target_pairs={{0,3},{1,2},{2,1},{3,0},{4,7},{5,6},{6,5},{7,4},{8,11},{9,10},{10,... | collective-permute-start | bytes 393224 | tf_op jit(solution)/shard_map/ppermute | solution.py:40
  34.8 14.0 %collective-permute-start.8 = (bf16[768,128]{1,0:T(8,128)(2,1)S(1)}, bf16[768,128]{1,0:T(8,128)(2,1)S(1)}, u32[]{:S(2)}, u32[]{:S(2)}) collective-permute-start(bf16[768,128]{1,0:T(8,128)(2,1)S(1)} %get-tuple-element.58), channel_id=1, source_target_pairs={{0,12},{1,13},{2,14},{3,15},{4,0},{5,1},{6,2},{7,3},{8,4},{9,5},{1... | collective-permute-start | bytes 589832 | tf_op jit(solution)/shard_map/ppermute | solution.py:45
  37.3 11.5 %collective-permute-start.7 = (bf16[768,128]{1,0:T(8,128)(2,1)S(1)}, bf16[768,128]{1,0:T(8,128)(2,1)S(1)}, u32[]{:S(2)}, u32[]{:S(2)}) collective-permute-start(bf16[768,128]{1,0:T(8,128)(2,1)S(1)} %get-tuple-element.57), channel_id=1, source_target_pairs={{0,4},{1,5},{2,6},{3,7},{4,8},{5,9},{6,10},{7,11},{8,12},{9,13},{1... | collective-permute-start | bytes 589832 | tf_op jit(solution)/shard_map/ppermute | solution.py:45
  38.7 10.9 %collective-permute-start.9 = (bf16[768,128]{1,0:T(8,128)(2,1)S(1)}, bf16[768,128]{1,0:T(8,128)(2,1)S(1)}, u32[]{:S(2)}, u32[]{:S(2)}) collective-permute-start(bf16[768,128]{1,0:T(8,128)(2,1)S(1)} %get-tuple-element.59), channel_id=1, source_target_pairs={{0,12},{1,13},{2,14},{3,15},{4,0},{5,1},{6,2},{7,3},{8,4},{9,5},{1... | collective-permute-start | bytes 589832 | tf_op jit(solution)/shard_map/ppermute | solution.py:45
  41.8 0.7 copy-start.5
  58.0 8.4 %collective-permute-start.16 = (bf16[256,128]{1,0:T(8,128)(2,1)S(1)}, bf16[256,128]{1,0:T(8,128)(2,1)S(1)}, u32[]{:S(2)}, u32[]{:S(2)}) collective-permute-start(bf16[256,128]{1,0:T(8,128)(2,1)S(1)} %get-tuple-element.73), channel_id=1, source_target_pairs={{0,16},{1,17},{2,18},{3,19},{4,20},{5,21},{6,22},{7,23},{8,24},{9,... | collective-permute-start | bytes 196616 | tf_op jit(solution)/shard_map/ppermute | solution.py:312
  59.5 6.8 %collective-permute-start.17 = (bf16[256,128]{1,0:T(8,128)(2,1)S(1)}, bf16[256,128]{1,0:T(8,128)(2,1)S(1)}, u32[]{:S(2)}, u32[]{:S(2)}) collective-permute-start(bf16[256,128]{1,0:T(8,128)(2,1)S(1)} %get-tuple-element.74), channel_id=1, source_target_pairs={{0,4},{1,5},{2,6},{3,7},{4,8},{5,9},{6,10},{7,11},{8,12},{9,13},{1... | collective-permute-start | bytes 196616 | tf_op jit(solution)/shard_map/ppermute | solution.py:312
  60.9 7.5 %collective-permute-start.18 = (bf16[256,128]{1,0:T(8,128)(2,1)S(1)}, bf16[256,128]{1,0:T(8,128)(2,1)S(1)}, u32[]{:S(2)}, u32[]{:S(2)}) collective-permute-start(bf16[256,128]{1,0:T(8,128)(2,1)S(1)} %get-tuple-element.75), channel_id=1, source_target_pairs={{0,20},{1,21},{2,22},{3,23},{4,24},{5,25},{6,26},{7,27},{8,28},{9,... | collective-permute-start | bytes 196616 | tf_op jit(solution)/shard_map/ppermute | solution.py:312
  62.5 7.6 %collective-permute-start.19 = (bf16[256,128]{1,0:T(8,128)(2,1)S(1)}, bf16[256,128]{1,0:T(8,128)(2,1)S(1)}, u32[]{:S(2)}, u32[]{:S(2)}) collective-permute-start(bf16[256,128]{1,0:T(8,128)(2,1)S(1)} %get-tuple-element.76), channel_id=1, source_target_pairs={{0,8},{1,9},{2,10},{3,11},{4,12},{5,13},{6,14},{7,15},{8,0},{9,1},... | collective-permute-start | bytes 196616 | tf_op jit(solution)/shard_map/ppermute | solution.py:312
  64.1 8.6 %collective-permute-start.20 = (bf16[256,128]{1,0:T(8,128)(2,1)S(1)}, bf16[256,128]{1,0:T(8,128)(2,1)S(1)}, u32[]{:S(2)}, u32[]{:S(2)}) collective-permute-start(bf16[256,128]{1,0:T(8,128)(2,1)S(1)} %get-tuple-element.77), channel_id=1, source_target_pairs={{0,24},{1,25},{2,26},{3,27},{4,28},{5,29},{6,30},{7,31},{8,16},{9,... | collective-permute-start | bytes 196616 | tf_op jit(solution)/shard_map/ppermute | solution.py:312
  66.4 17.7 %collective-permute-start.10 = (bf16[256,256]{1,0:T(8,128)(2,1)S(1)}, bf16[256,256]{1,0:T(8,128)(2,1)S(1)}, u32[]{:S(2)}, u32[]{:S(2)}) collective-permute-start(bf16[256,256]{1,0:T(8,128)(2,1)S(1)} %get-tuple-element.65), channel_id=1, source_target_pairs={{0,1},{1,0},{2,3},{3,2},{4,5},{5,4},{6,7},{7,6},{8,9},{9,8},{10,11... | collective-permute-start | bytes 393224 | tf_op jit(solution)/shard_map/ppermute | solution.py:40
  66.4 17.7 %collective-permute-start.11 = (bf16[256,256]{1,0:T(8,128)(2,1)S(1)}, bf16[256,256]{1,0:T(8,128)(2,1)S(1)}, u32[]{:S(2)}, u32[]{:S(2)}) collective-permute-start(bf16[256,256]{1,0:T(8,128)(2,1)S(1)} %get-tuple-element.66), channel_id=1, source_target_pairs={{0,2},{1,3},{2,0},{3,1},{4,6},{5,7},{6,4},{7,5},{8,10},{9,11},{10,... | collective-permute-start | bytes 393224 | tf_op jit(solution)/shard_map/ppermute | solution.py:40
  68.4 15.7 %collective-permute-start.12 = (bf16[256,256]{1,0:T(8,128)(2,1)S(1)}, bf16[256,256]{1,0:T(8,128)(2,1)S(1)}, u32[]{:S(2)}, u32[]{:S(2)}) collective-permute-start(bf16[256,256]{1,0:T(8,128)(2,1)S(1)} %get-tuple-element.67), channel_id=1, source_target_pairs={{0,3},{1,2},{2,1},{3,0},{4,7},{5,6},{6,5},{7,4},{8,11},{9,10},{10,... | collective-permute-start | bytes 393224 | tf_op jit(solution)/shard_map/ppermute | solution.py:40
  70.1 4.6 %collective-permute-start.21 = (bf16[256,128]{1,0:T(8,128)(2,1)S(1)}, bf16[256,128]{1,0:T(8,128)(2,1)S(1)}, u32[]{:S(2)}, u32[]{:S(2)}) collective-permute-start(bf16[256,128]{1,0:T(8,128)(2,1)S(1)} %get-tuple-element.78), channel_id=1, source_target_pairs={{0,12},{1,13},{2,14},{3,15},{4,0},{5,1},{6,2},{7,3},{8,4},{9,5},{1... | collective-permute-start | bytes 196616 | tf_op jit(solution)/shard_map/ppermute | solution.py:312
  72.8 5.2 %collective-permute-start.22 = (bf16[256,128]{1,0:T(8,128)(2,1)S(1)}, bf16[256,128]{1,0:T(8,128)(2,1)S(1)}, u32[]{:S(2)}, u32[]{:S(2)}) collective-permute-start(bf16[256,128]{1,0:T(8,128)(2,1)S(1)} %get-tuple-element.79), channel_id=1, source_target_pairs={{0,28},{1,29},{2,30},{3,31},{4,16},{5,17},{6,18},{7,19},{8,20},{9,... | collective-permute-start | bytes 196616 | tf_op jit(solution)/shard_map/ppermute | solution.py:312
  78.1 6.9 %collective-permute-start.23 = (bf16[64,256]{1,0:T(8,128)(2,1)S(1)}, bf16[64,256]{1,0:T(8,128)(2,1)S(1)}, u32[]{:S(2)}, u32[]{:S(2)}) collective-permute-start(bf16[64,256]{1,0:T(8,128)(2,1)S(1)} %get-tuple-element.80), channel_id=1, source_target_pairs={{0,0},{1,1},{2,16},{3,17},{4,4},{5,5},{6,20},{7,21},{8,8},{9,9},{1... | collective-permute-start | bytes 98312 | tf_op jit(solution)/shard_map/ppermute | solution.py:328
  78.8 7.0 %collective-permute-start.25 = (bf16[64,256]{1,0:T(8,128)(2,1)S(1)}, bf16[64,256]{1,0:T(8,128)(2,1)S(1)}, u32[]{:S(2)}, u32[]{:S(2)}) collective-permute-start(bf16[64,256]{1,0:T(8,128)(2,1)S(1)} %get-tuple-element.80), channel_id=1, source_target_pairs={{0,16},{1,17},{2,0},{3,1},{4,20},{5,21},{6,4},{7,5},{8,24},{9,25},... | collective-permute-start | bytes 98312 | tf_op jit(solution)/shard_map/ppermute | solution.py:328
  84.0 1.2 %collective-permute-start.24 = (bf16[64,256]{1,0:T(8,128)(2,1)S(1)}, bf16[64,256]{1,0:T(8,128)(2,1)S(1)}, u32[]{:S(2)}, u32[]{:S(2)}) collective-permute-start(bf16[64,256]{1,0:T(8,128)(2,1)S(1)} %get-tuple-element.81), channel_id=1, source_target_pairs={{0,1},{1,0},{2,17},{3,16},{4,5},{5,4},{6,21},{7,20},{8,9},{9,8},{1... | collective-permute-start | bytes 98312 | tf_op jit(solution)/shard_map/ppermute | solution.py:328
  84.0 3.4 %collective-permute-start.26 = (bf16[64,256]{1,0:T(8,128)(2,1)S(1)}, bf16[64,256]{1,0:T(8,128)(2,1)S(1)}, u32[]{:S(2)}, u32[]{:S(2)}) collective-permute-start(bf16[64,256]{1,0:T(8,128)(2,1)S(1)} %get-tuple-element.81), channel_id=1, source_target_pairs={{0,17},{1,16},{2,1},{3,0},{4,21},{5,20},{6,5},{7,4},{8,25},{9,24},... | collective-permute-start | bytes 98312 | tf_op jit(solution)/shard_map/ppermute | solution.py:328
  (1 other events, 0.7 us)

commit v2 on v1

--- a/solution.py
+++ b/solution.py
@@ -12,13 +12,14 @@
 MAXLEN = 768
 GROUP = 4
 FAR = 1 << 30
+PEAK = 1.15e9
 ALPHA = 1.0 / HD**0.5
 SCALE = 1.0 / MAXLEN**0.5
 VMEM = pl.BlockSpec(memory_space=pltpu.VMEM)
 SMEM = pl.BlockSpec(memory_space=pltpu.SMEM)
 
 
-def call(kernel, outs, args, specs=None, flops=0, scratch=()):
+def call(kernel, outs, args, specs=None, busy=0.5, scratch=()):
     moved = sum(a.size * a.dtype.itemsize for a in list(outs) + list(args))
     return pl.pallas_call(
         kernel,
@@ -27,7 +28,9 @@
         out_specs=tuple([VMEM] * len(outs)),
         scratch_shapes=scratch,
         compiler_params=pltpu.CompilerParams(vmem_limit_bytes=24 * 1024 * 1024),
-        cost_estimate=pl.CostEstimate(flops=flops, bytes_accessed=moved, transcendentals=0),
+        cost_estimate=pl.CostEstimate(
+            flops=int(busy * PEAK), bytes_accessed=moved, transcendentals=0
+        ),
     )(*args)
 
 
@@ -40,9 +43,17 @@
     return lax.ppermute(value, "ctx", [(i, i ^ steps) for i in range(count)])
 
 
-def around(value, steps):
-    count = lax.axis_size("ctx")
-    return lax.ppermute(value, "ctx", [(i, (i + steps) % count) for i in range(count)])
+def around(value, low, high):
+    count = lax.axis_size("ctx")
+    pairs = []
+    for i in range(count):
+        planes = low if i % GROUP < GROUP // 2 else high
+        pairs.append((i, (i + planes * GROUP) % count))
+    return lax.ppermute(value, "ctx", pairs)
+
+
+def after(value, *earlier):
+    return lax.optimization_barrier((value, *earlier))[0]
 
 
 def place():
@@ -75,23 +86,36 @@
     split_kernel(keys, queries, o0, o1, o2, o3)
 
 
-def arrange_kernel(i0, i1, i2, i3, first, second, up, down):
-    rows = i0.shape[0]
-    span = up.shape[0] // rows
-    me = place()
-    for k, ref in enumerate((i0, i1, i2, i3)):
-        j = me ^ k
-        at = pl.ds(pl.multiple_of(j * rows, rows), rows)
-        first[at, :] = ref[:, :HD]
-        second[at, :] = ref[:, HD:]
-
-        @pl.when(j >= GROUP - span)
+def upper():
+    return lax.div(place(), 2)
+
+
+def edge_kernel(own, near_kq, near_vo, far_kq, far_vo, big, small):
+    rows = near_kq.shape[0]
+    core = lax.rem(place(), 2)
+    keys_big = upper() == (1 if own else 0)
+    for ref_kq, ref_vo, at_core in ((near_kq, near_vo, core), (far_kq, far_vo, 1 - core)):
+        at = pl.ds(pl.multiple_of(at_core * rows, rows), rows)
+
+        @pl.when(keys_big)
         def _():
-            up[pl.ds(pl.multiple_of((j - (GROUP - span)) * rows, rows), rows), :] = ref[:, :HD]
-
-        @pl.when(j < span)
+            big[at, :HD] = ref_kq[:, :HD]
+            big[at, HD:] = ref_vo[:, :HD]
+
+            @pl.when(at_core == 0)
+            def _():
+                small[:, :HD] = ref_kq[:, HD:]
+                small[:, HD:] = ref_vo[:, HD:]
+
+        @pl.when(jnp.logical_not(keys_big))
         def _():
-            down[at, :] = ref[:, HD:]
+            big[at, :HD] = ref_kq[:, HD:]
+            big[at, HD:] = ref_vo[:, HD:]
+
+            @pl.when(at_core == 1)
+            def _():
+                small[:, :HD] = ref_kq[:, :HD]
+                small[:, HD:] = ref_vo[:, :HD]
 
 
 def offset_of(row, shift, total):
@@ -136,12 +160,22 @@
     return att, ds
 
 
-def inner_kernel(len_ref, shift_ref, keep_ref, k_ref, q_ref, v_ref, o_ref, out_t, dq_t, dk, dv):
-    rows = k_ref.shape[0] // GROUP
+def inner_kernel(
+    len_ref, shift_ref, keep_ref, a0, a1, a2, a3, b0, b1, b2, b3,
+    k_ref, q_ref, v_ref, o_ref, out_t, dq_t, dk, dv,
+):
+    rows = a0.shape[0]
     count = lax.axis_size("ctx")
     total = rows * count
     shift = shift_ref[0]
     base = (lax.axis_index("ctx") // GROUP) * (GROUP * rows)
+    me = place()
+    for i, (kq, vo) in enumerate(((a0, b0), (a1, b1), (a2, b2), (a3, b3))):
+        at = pl.ds(pl.multiple_of((me ^ i) * rows, rows), rows)
+        k_ref[at, :] = kq[:, :HD]
+        q_ref[at, :] = kq[:, HD:]
+        v_ref[at, :] = vo[:, :HD]
+        o_ref[at, :] = vo[:, HD:]
     out_t[...] = jnp.zeros_like(out_t)
     dq_t[...] = jnp.zeros_like(dq_t)
 
@@ -169,12 +203,13 @@
     lax.fori_loop(0, GROUP, key_step, 0)
 
 
-def outer_kernel(
-    len_ref, shift_ref, keep_ref, k_ref, q_ref, v_ref, o_ref, kp_ref, vp_ref, qn_ref, on_ref,
-    out_in, dq_in, dk_in, dv_in, s0, s1, s2, s3, dqk, out_t, dq_t, dk, dv,
+def halo_kernel(
+    own, last, len_ref, shift_ref, keep_ref, k_ref, q_ref, v_ref, o_ref, big, small,
+    out_in, dq_in, dk_in, dv_in, *outs,
 ):
-    rows = k_ref.shape[0] // GROUP
-    span = kp_ref.shape[0] // rows
+    out_t, dq_t, dk, dv = outs[-4:]
+    rows = small.shape[0]
+    span = GROUP - 1
     count = lax.axis_size("ctx")
     total = rows * count
     shift = shift_ref[0]
@@ -185,48 +220,65 @@
     dk[...] = dk_in[...]
     dv[...] = dv_in[...]
 
-    def before(p, _):
-        at = pl.ds(pl.multiple_of(p * rows, rows), rows)
-        k, v = kp_ref[at, :], vp_ref[at, :]
-        k_t, v_t = k.T, v.T
-        kpos = key_place(base + (p - span) * rows, rows, shift, keep_ref, total)
-
-        def query_step(qt, _):
-            qs = pl.ds(pl.multiple_of(qt * rows, rows), rows)
-            qpos, qbegin = query_place(base + qt * rows, rows, shift, len_ref, total)
-            att, ds = tile_terms(k, v, q_ref[qs, :], o_ref[qs, :], kpos, qpos, qbegin)
-            out_t[:, qs] += nn(v_t, att)
-            dq_t[:, qs] += nn(k_t, ds)
-            return 0
-
-        return lax.fori_loop(0, p + 1, query_step, 0)
-
-    lax.fori_loop(0, span, before, 0)
-
-    def after(n, _):
-        qs = pl.ds(pl.multiple_of(n * rows, rows), rows)
-        q, o = qn_ref[qs, :], on_ref[qs, :]
-        qpos, qbegin = query_place(base + (GROUP + n) * rows, rows, shift, len_ref, total)
-
-        def key_step(kt, _):
-            at = pl.ds(pl.multiple_of(kt * rows, rows), rows)
-            kpos = key_place(base + kt * rows, rows, shift, keep_ref, total)
-            att, ds = tile_terms(k_ref[at, :], v_ref[at, :], q, o, kpos, qpos, qbegin)
-            dv[at, :] += nn(att, o)
-            dk[at, :] += nn(ds, q)
-            return 0
-
-        return lax.fori_loop(n + 1, GROUP, key_step, 0)
-
-    lax.fori_loop(0, span, after, 0)
-
+    def before(source, first):
+        def key_step(p, _):
+            at = pl.ds(pl.multiple_of((p - first) * rows, rows), rows)
+            k, v = source[at, :HD], source[at, HD:]
+            k_t, v_t = k.T, v.T
+            kpos = key_place(base + (p - span) * rows, rows, shift, keep_ref, total)
+
+            def query_step(qt, _):
+                qs = pl.ds(pl.multiple_of(qt * rows, rows), rows)
+                qpos, qbegin = query_place(base + qt * rows, rows, shift, len_ref, total)
+                att, ds = tile_terms(k, v, q_ref[qs, :], o_ref[qs, :], kpos, qpos, qbegin)
+                out_t[:, qs] += nn(v_t, att)
+                dq_t[:, qs] += nn(k_t, ds)
+                return 0
+
+            return lax.fori_loop(0, p + 1, query_step, 0)
+
+        return key_step
+
+    def behind(source, first):
+        def query_step(n, _):
+            qs = pl.ds(pl.multiple_of((n - first) * rows, rows), rows)
+            q, o = source[qs, :HD], source[qs, HD:]
+            qpos, qbegin = query_place(base + (GROUP + n) * rows, rows, shift, len_ref, total)
+
+            def key_step(kt, _):
+                at = pl.ds(pl.multiple_of(kt * rows, rows), rows)
+                kpos = key_place(base + kt * rows, rows, shift, keep_ref, total)
+                att, ds = tile_terms(k_ref[at, :], v_ref[at, :], q, o, kpos, qpos, qbegin)
+                dv[at, :] += nn(att, o)
+                dk[at, :] += nn(ds, q)
+                return 0
+
+            return lax.fori_loop(n + 1, GROUP, key_step, 0)
+
+        return query_step
+
+    keys_big = upper() == (1 if own else 0)
+
+    @pl.when(keys_big)
+    def _():
+        lax.fori_loop(1, span, before(big, 1), 0)
+        behind(small, span - 1)(jnp.int32(span - 1), 0)
+
+    @pl.when(jnp.logical_not(keys_big))
+    def _():
+        before(small, 0)(jnp.int32(0), 0)
+        lax.fori_loop(0, span - 1, behind(big, 0), 0)
+
+    if not last:
+        return
+    s0, s1, s2, s3, dqk = outs[:5]
     factor = 0.5 * SCALE * ALPHA
     dqk[:HD, :] = (dq_t[...] * factor).astype(jnp.bfloat16)
     for j in range(GROUP):
         at = slice(j * rows, (j + 1) * rows)
         dqk[HD:, at] = (dk[at, :] * factor).T.astype(jnp.bfloat16)
-    for k, ref in enumerate((s0, s1, s2, s3)):
-        at = pl.ds(pl.multiple_of((me ^ k) * rows, rows), rows)
+    for i, ref in enumerate((s0, s1, s2, s3)):
+        at = pl.ds(pl.multiple_of((me ^ i) * rows, rows), rows)
         ref[:, :HD] = (out_t[:, at] * SCALE).T.astype(jnp.bfloat16)
         ref[:, HD:] = (dv[at, :] * SCALE).astype(jnp.bfloat16)
 
@@ -294,12 +346,11 @@
     width = gathered[0].shape[1]
     block = width // (streams * planes)
     targets = [(dy, dz) for dz in range(planes) for dy in range(streams)]
-    flops = 2 * dqk.shape[0] * dqk.shape[1] * width
     sends = call(
         functools.partial(block_terms_kernel, targets),
         [like(2 * HD, block)] * len(targets),
         (dqk, *gathered),
-        flops=flops,
+        busy=2,
         scratch=[pltpu.VMEM((2 * HD, width), jnp.bfloat16)],
     )
     arrived = []
@@ -333,9 +384,8 @@
     count = lax.axis_size("ctx")
     planes = count // GROUP
     width = gathered[0].shape[1]
-    flops = 2 * dqk.shape[0] * dqk.shape[1] * width
     (whole,) = call(
-        terms_kernel, [like(2 * HD, width, jnp.float32)], (dqk, *gathered), flops=flops
+        terms_kernel, [like(2 * HD, width, jnp.float32)], (dqk, *gathered), busy=2
     )
     whole = lax.psum(whole.T, "dp")
     same_head = [[g * GROUP + j for g in range(planes)] for j in range(GROUP)]
@@ -356,10 +406,8 @@
     count = lax.axis_size("ctx")
     local = events[0]
     all_rows = GROUP * rows
-    halo = MAXLEN
     pair = like(rows, 2 * HD)
     full = like(all_rows, HD)
-    edge = like(halo, HD)
 
     vo = call(split_kernel, [pair] * GROUP, (values[0], grad_out[0]))
     vo = (vo[0],) + tuple(partner(vo[k], k) for k in range(1, GROUP))
@@ -367,34 +415,44 @@
         project_kernel,
         [pair] * GROUP,
         (local, w_key, w_query),
-        flops=4 * rows * width * features,
+        busy=4,
         scratch=[pltpu.VMEM((rows, features), jnp.bfloat16)] * 2,
     )
-    kq = (kq[0],) + tuple(partner(kq[k], k) for k in range(1, GROUP))
-    v, o, v_up, o_down = call(arrange_kernel, [full, full, edge, edge], vo)
-    v_prev, o_next = around(v_up, GROUP), around(o_down, -GROUP)
-    k, q, k_up, q_down = call(arrange_kernel, [full, full, edge, edge], kq)
-    k_prev, q_next = around(k_up, GROUP), around(q_down, -GROUP)
+    kq = (kq[0], partner(kq[1], 1)) + tuple(
+        partner(after(kq[k], vo[2], vo[3]), k) for k in range(2, GROUP)
+    )
+    edges = [like(2 * rows, 2 * HD), pair]
+    big, small = call(functools.partial(edge_kernel, True), edges, (kq[0], vo[0], kq[1], vo[1]))
+    own = around(big, -1, 1), around(small, 1, -1)
+    big, small = call(functools.partial(edge_kernel, False), edges, (kq[2], vo[2], kq[3], vo[3]))
+    other = around(big, 1, -1), around(small, -1, 1)
 
     e1 = partner(local, 1)
-    late, _ = lax.optimization_barrier((local, kq[2]))
-    e2 = partner(late, 2)
-    e3 = partner(e2, 1)
+    e2 = partner(after(local, kq[2], kq[3]), 2)
     info = (lengths, stream_shift, block_keep)
     wide, tall = like(HD, all_rows, jnp.float32), like(all_rows, HD, jnp.float32)
-    sums = call(
+    sums = [wide, wide, tall, tall]
+    k, q, v, o, *held = call(
         inner_kernel,
-        [wide, wide, tall, tall],
-        (*info, k, q, v, o),
-        specs=[SMEM] * 3 + [VMEM] * 4,
-        flops=2 * 6 * 10 * rows * rows * HD,
-    )
+        [full] * 4 + sums,
+        (*info, *kq, *vo),
+        specs=[SMEM] * 3 + [VMEM] * 8,
+        busy=15,
+    )
+    held = call(
+        functools.partial(halo_kernel, True, False),
+        sums,
+        (*info, k, q, v, o, *own, *held),
+        specs=[SMEM] * 3 + [VMEM] * 10,
+        busy=8,
+    )
+    e3 = partner(after(e2, *held), 1)
     *parts, dqk = call(
-        outer_kernel,
+        functools.partial(halo_kernel, False, True),
         [pair] * GROUP + [like(2 * HD, all_rows)],
-        (*info, k, q, v, o, k_prev, v_prev, q_next, o_next, *sums),
-        specs=[SMEM] * 3 + [VMEM] * 12,
-        flops=2 * 8 * 6 * rows * rows * HD,
+        (*info, k, q, v, o, *other, *held),
+        specs=[SMEM] * 3 + [VMEM] * 10,
+        busy=8,
         scratch=[
             pltpu.VMEM((HD, all_rows), jnp.float32),
             pltpu.VMEM((HD, all_rows), jnp.float32),

time: 88.4 us -> 71.1 us (0.80)
  waiting for transfers between devices: 28.8 us -> 14.3 us
  starting transfers between devices: 36 us -> 33.9 us
  local copies, waits for them, and re-layouts: 3.11 us -> 1.91 us
    ppermute x12, waiting for transfers between devices: 20.2 us -> 5.36 us  [partner(): return lax.ppermute(value, 'ctx', [(i, i ^ steps) for i in range(count)])]
    ppermute x7, starting transfers between devices: 12.7 us -> 10.2 us  [direct_reduce(): value = lax.ppermute(value, ('dp', 'ctx'), pairs)]
    ppermute x4, waiting for transfers between devices: 2.43 us -> 1.05 us  [direct_reduce(): received.append(lax.ppermute((near, far)[b], ('dp', 'ctx'), pairs))]
    ppermute x7, waiting for transfers between devices: 5.42 us -> 6.74 us  [direct_reduce(): value = lax.ppermute(value, ('dp', 'ctx'), pairs)]
    unnamed x12, local copies, waits for them, and re-layouts: 3.11 us -> 1.91 us
    pallas_call x10 -> x11, Pallas kernels: 18.7 us -> 19.2 us  [call(): pl.pallas_call(kernel, out_shape=tuple(outs), in_specs=specs or [VMEM] *...]
  transfers between devices with their start and end apart: 27 -> 27, of which waited for: 12 -> 10; matrix products, arithmetic and copies ran while one was open for 0% -> 0% of each run, Pallas kernels for 16% -> 23%
where the time goes in v2:
time: 71.1 us; the launch traced here: 70.8 us
  starting transfers between devices  33.9 us (48%)
  Pallas kernels  19.2 us (27%)
  waiting for transfers between devices  14.3 us (20%)
  local copies, waits for them, and re-layouts  1.91 us (3%)
  between operations  1.47 us (2%)
    pallas_call x11, Pallas kernels, call(): pl.pallas_call(kernel, out_shape=tuple(outs), in_specs=specs or [VMEM] *...  19.2 us
    ppermute x7, starting transfers between devices, direct_reduce(): value = lax.ppermute(value, ('dp', 'ctx'), pairs)  10.2 us
    ppermute x12, starting transfers between devices, partner(): return lax.ppermute(value, 'ctx', [(i, i ^ steps) for i in range(count)])  9.32 us
    ppermute x4, starting transfers between devices, around(): return lax.ppermute(value, 'ctx', pairs)  8.2 us
    ppermute x7, waiting for transfers between devices, direct_reduce(): value = lax.ppermute(value, ('dp', 'ctx'), pairs)  6.74 us
    ppermute x4, starting transfers between devices, direct_reduce(): received.append(lax.ppermute((near, far)[b], ('dp', 'ctx'), pairs))  6.21 us
    ppermute x12, waiting for transfers between devices, partner(): return lax.ppermute(value, 'ctx', [(i, i ^ steps) for i in range(count)])  5.36 us
    unnamed x12, local copies, waits for them, and re-layouts  1.91 us
  transfers between devices with their start and end apart: 27, of which 10 were waited for; matrix products, arithmetic and copies ran while one was open for 0% of the time, Pallas kernels for 23%

profile of v2, /device:TPU:0, one launch (start us, length us, event | category | flops | bytes accessed | tf_op | source)
XLA Modules:
  0.0 70.8 jit_solution(13874074869072804564)
XLA Ops:
  0.6 0.9 %copy-done.2 = bf16[1,256,512]{2,1,0:T(8,128)(2,1)S(1)} copy-done((bf16[1,256,512]{2,1,0:T(8,128)(2,1)S(1)}, bf16[1,256,512]{2,1,0:T(8,128)(2,1)}, u32[]{:S(2)}) %copy-start.2) | copy-done | bytes 262168
  1.6 0.9 %copy-done.3 = bf16[1,256,512]{2,1,0:T(8,128)(2,1)S(1)} copy-done((bf16[1,256,512]{2,1,0:T(8,128)(2,1)S(1)}, bf16[1,256,512]{2,1,0:T(8,128)(2,1)}, u32[]{:S(2)}) %copy-start.3) | copy-done | bytes 262168
  2.6 3.0 %collective-permute-start.1 = (bf16[256,256]{1,0:T(8,128)(2,1)S(1)}, bf16[256,256]{1,0:T(8,128)(2,1)S(1)}, u32[]{:S(2)}, u32[]{:S(2)}) collective-permute-start(bf16[256,256]{1,0:T(8,128)(2,1)S(1)} %get-tuple-element.54), channel_id=1, source_target_pairs={{0,2},{1,3},{2,0},{3,1},{4,6},{5,7},{6,4},{7,5},{8,10},{9,11},{10,... | collective-permute-start | bytes 393224 | tf_op jit(solution)/shard_map/ppermute | solution.py:43
  5.6 1.9 %shard_map.111 = (bf16[256,256]{1,0:T(8,128)(2,1)S(1)}, bf16[256,256]{1,0:T(8,128)(2,1)S(1)}, bf16[256,256]{1,0:T(8,128)(2,1)S(1)}, bf16[256,256]{1,0:T(8,128)(2,1)S(1)}) custom-call(bf16[256,1024]{1,0:T(8,128)(2,1)} %bitcast.x_ref.e0, bf16[1024,512]{1,0:T(8,128)(2,1)S(1)} %copy-done, bf16[1024,512]{1,0:T(8,128)(2,1)S(1)} %copy-done.1), custom_call_target="tpu_custom_call" | custom-call | flops 4600000000 | bytes 3145728 | tf_op jit(solution)/shard_map/pallas_call | solution.py:24
  8.2 1.4 %collective-permute-done.1.b2.near_vo = bf16[256,256]{1,0:T(8,128)(2,1)S(1)} collective-permute-done((bf16[256,256]{1,0:T(8,128)(2,1)S(1)}, bf16[256,256]{1,0:T(8,128)(2,1)S(1)}, u32[]{:S(2)}, u32[]{:S(2)}) %collective-permute-start.1) | collective-permute-done | bytes 131104 | tf_op jit(solution)/shard_map/ppermute | solution.py:43
  9.6 1.9 %collective-permute-done.2.b3.far_vo = bf16[256,256]{1,0:T(8,128)(2,1)S(1)} collective-permute-done((bf16[256,256]{1,0:T(8,128)(2,1)S(1)}, bf16[256,256]{1,0:T(8,128)(2,1)S(1)}, u32[]{:S(2)}, u32[]{:S(2)}) %collective-permute-start.2) | collective-permute-done | bytes 131104 | tf_op jit(solution)/shard_map/ppermute | solution.py:43
  11.5 1.6 %collective-permute-start.4 = (bf16[256,256]{1,0:T(8,128)(2,1)S(1)}, bf16[256,256]{1,0:T(8,128)(2,1)S(1)}, u32[]{:S(2)}, u32[]{:S(2)}) collective-permute-start(bf16[256,256]{1,0:T(8,128)(2,1)S(1)} %get-tuple-element.58), channel_id=1, source_target_pairs={{0,3},{1,2},{2,1},{3,0},{4,7},{5,6},{6,5},{7,4},{8,11},{9,10},{10,... | collective-permute-start | bytes 393224 | tf_op jit(solution)/shard_map/ppermute | solution.py:43
  14.2 3.9 %collective-permute-start.8 = (bf16[512,256]{1,0:T(8,128)(2,1)S(1)}, bf16[512,256]{1,0:T(8,128)(2,1)S(1)}, u32[]{:S(2)}, u32[]{:S(2)}) collective-permute-start(bf16[512,256]{1,0:T(8,128)(2,1)S(1)} %get-tuple-element.67), channel_id=1, source_target_pairs={{0,12},{1,13},{2,6},{3,7},{4,0},{5,1},{6,10},{7,11},{8,4},{9,5},{1... | collective-permute-start | bytes 786440 | tf_op jit(solution)/shard_map/ppermute | solution.py:52
  18.1 2.0 %collective-permute-done.3.a2.near_kq = bf16[256,256]{1,0:T(8,128)(2,1)S(1)} collective-permute-done((bf16[256,256]{1,0:T(8,128)(2,1)S(1)}, bf16[256,256]{1,0:T(8,128)(2,1)S(1)}, u32[]{:S(2)}, u32[]{:S(2)}) %collective-permute-start.3) | collective-permute-done | bytes 131104 | tf_op jit(solution)/shard_map/ppermute | solution.py:43
  20.1 1.0 %collective-permute-start.14 = (bf16[256,1024]{1,0:T(8,128)(2,1)}, bf16[256,1024]{1,0:T(8,128)(2,1)S(1)}, u32[]{:S(2)}, u32[]{:S(2)}) collective-permute-start(bf16[256,1024]{1,0:T(8,128)(2,1)} %bitcast.x_ref.e0), channel_id=1, source_target_pairs={{0,2},{1,3},{2,0},{3,1},{4,6},{5,7},{6,4},{7,5},{8,10},{9,11},{10,... | collective-permute-start | bytes 1572872 | tf_op jit(solution)/shard_map/ppermute | solution.py:43
  21.2 1.6 %collective-permute-start.6 = (bf16[512,256]{1,0:T(8,128)(2,1)S(1)}, bf16[512,256]{1,0:T(8,128)(2,1)S(1)}, u32[]{:S(2)}, u32[]{:S(2)}) collective-permute-start(bf16[512,256]{1,0:T(8,128)(2,1)S(1)} %get-tuple-element.65), channel_id=1, source_target_pairs={{0,4},{1,5},{2,14},{3,15},{4,8},{5,9},{6,2},{7,3},{8,12},{9,13},{1... | collective-permute-start | bytes 786440 | tf_op jit(solution)/shard_map/ppermute | solution.py:52
  22.9 6.4 %shard_map.113 = (bf16[1024,128]{1,0:T(8,128)(2,1)S(1)}, bf16[1024,128]{1,0:T(8,128)(2,1)S(1)}, bf16[1024,128]{1,0:T(8,128)(2,1)S(1)}, bf16[1024,128]{1,0:T(8,12...) custom-call(s32[1,8]{1,0:T(1,128)S(1)} %copy-done.4, ...), custom_call_target="tpu_custom_call" | custom-call | flops 17250000896 | bytes 4194468 | tf_op jit(solution)/shard_map/pallas_call | solution.py:24
  29.3 2.7 %collective-permute-start.7 = (bf16[256,256]{1,0:T(8,128)(2,1)S(1)}, bf16[256,256]{1,0:T(8,128)(2,1)S(1)}, u32[]{:S(2)}, u32[]{:S(2)}) collective-permute-start(bf16[256,256]{1,0:T(8,128)(2,1)S(1)} %get-tuple-element.66), channel_id=1, source_target_pairs={{0,12},{1,13},{2,6},{3,7},{4,0},{5,1},{6,10},{7,11},{8,4},{9,5},{1... | collective-permute-start | bytes 393224 | tf_op jit(solution)/shard_map/ppermute | solution.py:52
  32.0 3.3 %shard_map.116 = (f32[128,1024]{1,0:T(8,128)S(1)}, f32[128,1024]{1,0:T(8,128)S(1)}, f32[1024,128]{1,0:T(8,128)S(1)}, f32[1024,128]{1,0:T(8,128)S(1)}) custom-call(s32[1,8]{1,0:T(1,128)S(1)} %copy-done.4, s32[1]{0:T(128)S(6)} %copy.12.shift_ref, s32[1,32]{1,0:T(1,128)S(1)} %copy-done.5, bf16[1024,128]{1,0:T(8,128)(2,1)S(1)} %get-tuple-element.61.k_ref, ...), custom_call_target="tpu_custom_call" | custom-call | flops 9200000000 | bytes 5636260 | tf_op jit(solution)/shard_map/pallas_call | solution.py:24
  35.3 1.1 %collective-permute-done.7.small = bf16[256,256]{1,0:T(8,128)(2,1)S(1)} collective-permute-done((bf16[256,256]{1,0:T(8,128)(2,1)S(1)}, bf16[256,256]{1,0:T(8,128)(2,1)S(1)}, u32[]{:S(2)}, u32[]{:S(2)}) %collective-permute-start.7) | collective-permute-done | bytes 131104 | tf_op jit(solution)/shard_map/ppermute | solution.py:52
  36.5 3.7 %shard_map.117 = (bf16[256,256]{1,0:T(8,128)(2,1)S(1)}, bf16[256,256]{1,0:T(8,128)(2,1)S(1)}, bf16[256,256]{1,0:T(8,128)(2,1)S(1)}, bf16[256,256]{1,0:T(8,128)(2,1)S(1)}, bf16[256,1024]{1,0:T(8,128)(2,1)S(1)}) custom-call(s32[1,8]{1,0:T(1,128)S(1)} %copy-done.4, s32[1]{0:T(128)S(6)} %copy.12.shift_ref, s32[1,32]{1,0:T(1,128)S(1)} %copy-done.5, ...), custom_call_target="tpu_custom_call" | custom-call | flops 9200000000 | bytes 4587684 | tf_op jit(solution)/shard_map/pallas_call | solution.py:24
  40.2 1.9 %shard_map.119 = (bf16[256,128]{1,0:T(8,128)(2,1)S(1)}, bf16[256,128]{1,0:T(8,128)(2,1)S(1)}, bf16[256,128]{1,0:T(8,128)(2,1)S(1)}, bf16[256,128]{1,0:T(8,128)(2...) custom-call(bf16[256,1024]{1,0:T(8,128)(2,1)S(1)} %get-tuple-element, ...), custom_call_target="tpu_custom_call" | custom-call | flops 2300000000 | bytes 3145728 | tf_op jit(solution)/shard_map/pallas_call | solution.py:24
  42.1 1.6 %collective-permute-start.16 = (bf16[256,128]{1,0:T(8,128)(2,1)S(1)}, bf16[256,128]{1,0:T(8,128)(2,1)S(1)}, u32[]{:S(2)}, u32[]{:S(2)}) collective-permute-start(bf16[256,128]{1,0:T(8,128)(2,1)S(1)} %get-tuple-element.87), channel_id=1, source_target_pairs={{0,16},{1,17},{2,18},{3,19},{4,20},{5,21},{6,22},{7,23},{8,24},{9,... | collective-permute-start | bytes 196616 | tf_op jit(solution)/shard_map/ppermute | solution.py:363
  44.8 3.2 %collective-permute-start.19 = (bf16[256,128]{1,0:T(8,128)(2,1)S(1)}, bf16[256,128]{1,0:T(8,128)(2,1)S(1)}, u32[]{:S(2)}, u32[]{:S(2)}) collective-permute-start(bf16[256,128]{1,0:T(8,128)(2,1)S(1)} %get-tuple-element.90), channel_id=1, source_target_pairs={{0,8},{1,9},{2,10},{3,11},{4,12},{5,13},{6,14},{7,15},{8,0},{9,1},... | collective-permute-start | bytes 196616 | tf_op jit(solution)/shard_map/ppermute | solution.py:363
  48.0 1.0 %collective-permute-start.20 = (bf16[256,128]{1,0:T(8,128)(2,1)S(1)}, bf16[256,128]{1,0:T(8,128)(2,1)S(1)}, u32[]{:S(2)}, u32[]{:S(2)}) collective-permute-start(bf16[256,128]{1,0:T(8,128)(2,1)S(1)} %get-tuple-element.91), channel_id=1, source_target_pairs={{0,24},{1,25},{2,26},{3,27},{4,28},{5,29},{6,30},{7,31},{8,16},{9,... | collective-permute-start | bytes 196616 | tf_op jit(solution)/shard_map/ppermute | solution.py:363
  49.0 1.0 %collective-permute-done.17.refs_2_ = bf16[256,128]{1,0:T(8,128)(2,1)S(1)} collective-permute-done((bf16[256,128]{1,0:T(8,128)(2,1)S(1)}, bf16[256,128]{1,0:T(8,128)(2,1)S(1)}, u32[]{:S(2)}, u32[]{:S(2)}) %collective-permute-start.17) | collective-permute-done | bytes 65568 | tf_op jit(solution)/shard_map/ppermute | solution.py:363
  50.0 2.7 %collective-permute-start.11 = (bf16[256,256]{1,0:T(8,128)(2,1)S(1)}, bf16[256,256]{1,0:T(8,128)(2,1)S(1)}, u32[]{:S(2)}, u32[]{:S(2)}) collective-permute-start(bf16[256,256]{1,0:T(8,128)(2,1)S(1)} %get-tuple-element.79), channel_id=1, source_target_pairs={{0,2},{1,3},{2,0},{3,1},{4,6},{5,7},{6,4},{7,5},{8,10},{9,11},{10,... | collective-permute-start | bytes 393224 | tf_op jit(solution)/shard_map/ppermute | solution.py:43
  52.7 2.2 %collective-permute-done.19.refs_4_ = bf16[256,128]{1,0:T(8,128)(2,1)S(1)} collective-permute-done((bf16[256,128]{1,0:T(8,128)(2,1)S(1)}, bf16[256,128]{1,0:T(8,128)(2,1)S(1)}, u32[]{:S(2)}, u32[]{:S(2)}) %collective-permute-start.19) | collective-permute-done | bytes 65568 | tf_op jit(solution)/shard_map/ppermute | solution.py:363
  54.9 1.7 %collective-permute-start.21 = (bf16[256,128]{1,0:T(8,128)(2,1)S(1)}, bf16[256,128]{1,0:T(8,128)(2,1)S(1)}, u32[]{:S(2)}, u32[]{:S(2)}) collective-permute-start(bf16[256,128]{1,0:T(8,128)(2,1)S(1)} %get-tuple-element.92), channel_id=1, source_target_pairs={{0,12},{1,13},{2,14},{3,15},{4,0},{5,1},{6,2},{7,3},{8,4},{9,5},{1... | collective-permute-start | bytes 196616 | tf_op jit(solution)/shard_map/ppermute | solution.py:363
  56.6 1.6 %collective-permute-start.22 = (bf16[256,128]{1,0:T(8,128)(2,1)S(1)}, bf16[256,128]{1,0:T(8,128)(2,1)S(1)}, u32[]{:S(2)}, u32[]{:S(2)}) collective-permute-start(bf16[256,128]{1,0:T(8,128)(2,1)S(1)} %get-tuple-element.93), channel_id=1, source_target_pairs={{0,28},{1,29},{2,30},{3,31},{4,16},{5,17},{6,18},{7,19},{8,20},{9,... | collective-permute-start | bytes 196616 | tf_op jit(solution)/shard_map/ppermute | solution.py:363
  58.2 0.9 %collective-permute-done.21.refs_6_ = bf16[256,128]{1,0:T(8,128)(2,1)S(1)} collective-permute-done((bf16[256,128]{1,0:T(8,128)(2,1)S(1)}, bf16[256,128]{1,0:T(8,128)(2,1)S(1)}, u32[]{:S(2)}, u32[]{:S(2)}) %collective-permute-start.21) | collective-permute-done | bytes 65568 | tf_op jit(solution)/shard_map/ppermute | solution.py:363
  59.2 2.6 %collective-permute-done.22.refs_7_ = bf16[256,128]{1,0:T(8,128)(2,1)S(1)} collective-permute-done((bf16[256,128]{1,0:T(8,128)(2,1)S(1)}, bf16[256,128]{1,0:T(8,128)(2,1)S(1)}, u32[]{:S(2)}, u32[]{:S(2)}) %collective-permute-start.22) | collective-permute-done | bytes 65568 | tf_op jit(solution)/shard_map/ppermute | solution.py:363
  62.6 3.9 %collective-permute-start.25 = (bf16[64,256]{1,0:T(8,128)(2,1)S(1)}, bf16[64,256]{1,0:T(8,128)(2,1)S(1)}, u32[]{:S(2)}, u32[]{:S(2)}) collective-permute-start(bf16[64,256]{1,0:T(8,128)(2,1)S(1)} %get-tuple-element.94), channel_id=1, source_target_pairs={{0,16},{1,17},{2,0},{3,1},{4,20},{5,21},{6,4},{7,5},{8,24},{9,25},... | collective-permute-start | bytes 98312 | tf_op jit(solution)/shard_map/ppermute | solution.py:379
  66.5 1.6 %collective-permute-start.26 = (bf16[64,256]{1,0:T(8,128)(2,1)S(1)}, bf16[64,256]{1,0:T(8,128)(2,1)S(1)}, u32[]{:S(2)}, u32[]{:S(2)}) collective-permute-start(bf16[64,256]{1,0:T(8,128)(2,1)S(1)} %get-tuple-element.95), channel_id=1, source_target_pairs={{0,17},{1,16},{2,1},{3,0},{4,21},{5,20},{6,5},{7,4},{8,25},{9,24},... | collective-permute-start | bytes 98312 | tf_op jit(solution)/shard_map/ppermute | solution.py:379
  68.2 0.9 %shard_map.118 = (bf16[256,512]{1,0:T(8,128)(2,1)}, bf16[256,512]{1,0:T(8,128)(2,1)}) custom-call(bf16[256,256]{1,0:T(8,128)(2,1)S(1)} %get-tuple-element.77.i0, bf16[256,256]{1,0:T(8,128)(2,1)S(1)} %collective-permute-done.10.i1, bf16[256,256]{1,0:T(8,128)(2,1)S(1)} %collective-permute-done.11.i2, bf16[256,256]{1,0:T(8,128)(2,1)S(1)} %collective-permute-done.12.i3), custom_call_target="tpu_custom_call" | custom-call | flops 575000000 | bytes 1048576 | tf_op jit(solution)/shard_map/pallas_call | solution.py:24
  69.1 1.0 %collective-permute-done.26.r11 = bf16[64,256]{1,0:T(8,128)(2,1)S(1)} collective-permute-done((bf16[64,256]{1,0:T(8,128)(2,1)S(1)}, bf16[64,256]{1,0:T(8,128)(2,1)S(1)}, u32[]{:S(2)}, u32[]{:S(2)}) %collective-permute-start.26) | collective-permute-done | bytes 32800 | tf_op jit(solution)/shard_map/ppermute | solution.py:379
  70.1 0.7 shard_map.121
  (45 shorter events, 3.3 us)
Async XLA Ops:
  0.6 1.0 %copy-start.2 = (bf16[1,256,512]{2,1,0:T(8,128)(2,1)S(1)}, bf16[1,256,512]{2,1,0:T(8,128)(2,1)}, u32[]{:S(2)}) copy-start(bf16[1,256,512]{2,1,0:T(8,128)(2,1)} %param.11) | copy-start | bytes 786436
  2.5 3.1 %copy-start = (bf16[1024,512]{1,0:T(8,128)(2,1)S(1)}, bf16[1024,512]{1,0:T(8,128)(2,1)}, u32[]{:S(2)}) copy-start(bf16[1024,512]{1,0:T(8,128)(2,1)} %wk_ref.1) | copy-start | bytes 3145732
  2.5 3.1 %copy-start.1 = (bf16[1024,512]{1,0:T(8,128)(2,1)S(1)}, bf16[1024,512]{1,0:T(8,128)(2,1)}, u32[]{:S(2)}) copy-start(bf16[1024,512]{1,0:T(8,128)(2,1)} %wq_ref.1) | copy-start | bytes 3145732
  2.6 6.9 %collective-permute-start.1 = (bf16[256,256]{1,0:T(8,128)(2,1)S(1)}, bf16[256,256]{1,0:T(8,128)(2,1)S(1)}, u32[]{:S(2)}, u32[]{:S(2)}) collective-permute-start(bf16[256,256]{1,0:T(8,128)(2,1)S(1)} %get-tuple-element.54), channel_id=1, source_target_pairs={{0,2},{1,3},{2,0},{3,1},{4,6},{5,7},{6,4},{7,5},{8,10},{9,11},{10,... | collective-permute-start | bytes 393224 | tf_op jit(solution)/shard_map/ppermute | solution.py:43
  5.6 5.9 %collective-permute-start.2 = (bf16[256,256]{1,0:T(8,128)(2,1)S(1)}, bf16[256,256]{1,0:T(8,128)(2,1)S(1)}, u32[]{:S(2)}, u32[]{:S(2)}) collective-permute-start(bf16[256,256]{1,0:T(8,128)(2,1)S(1)} %get-tuple-element.55), channel_id=1, source_target_pairs={{0,3},{1,2},{2,1},{3,0},{4,7},{5,6},{6,5},{7,4},{8,11},{9,10},{10,... | collective-permute-start | bytes 393224 | tf_op jit(solution)/shard_map/ppermute | solution.py:43
  7.6 6.5 %collective-permute-start = (bf16[256,256]{1,0:T(8,128)(2,1)S(1)}, bf16[256,256]{1,0:T(8,128)(2,1)S(1)}, u32[]{:S(2)}, u32[]{:S(2)}) collective-permute-start(bf16[256,256]{1,0:T(8,128)(2,1)S(1)} %get-tuple-element.52), channel_id=1, source_target_pairs={{0,1},{1,0},{2,3},{3,2},{4,5},{5,4},{6,7},{7,6},{8,9},{9,8},{10,11... | collective-permute-start | bytes 393224 | tf_op jit(solution)/shard_map/ppermute | solution.py:43
  7.8 6.2 %collective-permute-start.5 = (bf16[256,256]{1,0:T(8,128)(2,1)S(1)}, bf16[256,256]{1,0:T(8,128)(2,1)S(1)}, u32[]{:S(2)}, u32[]{:S(2)}) collective-permute-start(bf16[256,256]{1,0:T(8,128)(2,1)S(1)} %get-tuple-element.60), channel_id=1, source_target_pairs={{0,1},{1,0},{2,3},{3,2},{4,5},{5,4},{6,7},{7,6},{8,9},{9,8},{10,11... | collective-permute-start | bytes 393224 | tf_op jit(solution)/shard_map/ppermute | solution.py:43
  11.5 6.6 %collective-permute-start.4 = (bf16[256,256]{1,0:T(8,128)(2,1)S(1)}, bf16[256,256]{1,0:T(8,128)(2,1)S(1)}, u32[]{:S(2)}, u32[]{:S(2)}) collective-permute-start(bf16[256,256]{1,0:T(8,128)(2,1)S(1)} %get-tuple-element.58), channel_id=1, source_target_pairs={{0,3},{1,2},{2,1},{3,0},{4,7},{5,6},{6,5},{7,4},{8,11},{9,10},{10,... | collective-permute-start | bytes 393224 | tf_op jit(solution)/shard_map/ppermute | solution.py:43
  13.1 7.0 %collective-permute-start.3 = (bf16[256,256]{1,0:T(8,128)(2,1)S(1)}, bf16[256,256]{1,0:T(8,128)(2,1)S(1)}, u32[]{:S(2)}, u32[]{:S(2)}) collective-permute-start(bf16[256,256]{1,0:T(8,128)(2,1)S(1)} %get-tuple-element.56), channel_id=1, source_target_pairs={{0,2},{1,3},{2,0},{3,1},{4,6},{5,7},{6,4},{7,5},{8,10},{9,11},{10,... | collective-permute-start | bytes 393224 | tf_op jit(solution)/shard_map/ppermute | solution.py:43
  13.4 26.8 %collective-permute-start.13 = (bf16[256,1024]{1,0:T(8,128)(2,1)}, bf16[256,1024]{1,0:T(8,128)(2,1)S(1)}, u32[]{:S(2)}, u32[]{:S(2)}) collective-permute-start(bf16[256,1024]{1,0:T(8,128)(2,1)} %bitcast.x_ref.e0), channel_id=1, source_target_pairs={{0,1},{1,0},{2,3},{3,2},{4,5},{5,4},{6,7},{7,6},{8,9},{9,8},{10,11... | collective-permute-start | bytes 1572872 | tf_op jit(solution)/shard_map/ppermute | solution.py:43
  14.2 17.8 %collective-permute-start.8 = (bf16[512,256]{1,0:T(8,128)(2,1)S(1)}, bf16[512,256]{1,0:T(8,128)(2,1)S(1)}, u32[]{:S(2)}, u32[]{:S(2)}) collective-permute-start(bf16[512,256]{1,0:T(8,128)(2,1)S(1)} %get-tuple-element.67), channel_id=1, source_target_pairs={{0,12},{1,13},{2,6},{3,7},{4,0},{5,1},{6,10},{7,11},{8,4},{9,5},{1... | collective-permute-start | bytes 786440 | tf_op jit(solution)/shard_map/ppermute | solution.py:52
  18.1 11.2 %collective-permute-start.9 = (bf16[256,256]{1,0:T(8,128)(2,1)S(1)}, bf16[256,256]{1,0:T(8,128)(2,1)S(1)}, u32[]{:S(2)}, u32[]{:S(2)}) collective-permute-start(bf16[256,256]{1,0:T(8,128)(2,1)S(1)} %get-tuple-element.68), channel_id=1, source_target_pairs={{0,4},{1,5},{2,14},{3,15},{4,8},{5,9},{6,2},{7,3},{8,12},{9,13},{1... | collective-permute-start | bytes 393224 | tf_op jit(solution)/shard_map/ppermute | solution.py:52
  20.1 15.1 %collective-permute-start.14 = (bf16[256,1024]{1,0:T(8,128)(2,1)}, bf16[256,1024]{1,0:T(8,128)(2,1)S(1)}, u32[]{:S(2)}, u32[]{:S(2)}) collective-permute-start(bf16[256,1024]{1,0:T(8,128)(2,1)} %bitcast.x_ref.e0), channel_id=1, source_target_pairs={{0,2},{1,3},{2,0},{3,1},{4,6},{5,7},{6,4},{7,5},{8,10},{9,11},{10,... | collective-permute-start | bytes 1572872 | tf_op jit(solution)/shard_map/ppermute | solution.py:43
  21.2 1.7 %copy-start.4 = (s32[1,8]{1,0:T(1,128)S(1)}, s32[1,8]{1,0:T(1,128)}, u32[]{:S(2)}) copy-start(s32[1,8]{1,0:T(1,128)} %len_ref.5) | copy-start | bytes 100
  21.2 1.6 %copy-start.5 = (s32[1,32]{1,0:T(1,128)S(1)}, s32[1,32]{1,0:T(1,128)}, u32[]{:S(2)}) copy-start(s32[1,32]{1,0:T(1,128)} %keep_ref.5) | copy-start | bytes 388
  21.2 15.2 %collective-permute-start.6 = (bf16[512,256]{1,0:T(8,128)(2,1)S(1)}, bf16[512,256]{1,0:T(8,128)(2,1)S(1)}, u32[]{:S(2)}, u32[]{:S(2)}) collective-permute-start(bf16[512,256]{1,0:T(8,128)(2,1)S(1)} %get-tuple-element.65), channel_id=1, source_target_pairs={{0,4},{1,5},{2,14},{3,15},{4,8},{5,9},{6,2},{7,3},{8,12},{9,13},{1... | collective-permute-start | bytes 786440 | tf_op jit(solution)/shard_map/ppermute | solution.py:52
  29.3 7.1 %collective-permute-start.7 = (bf16[256,256]{1,0:T(8,128)(2,1)S(1)}, bf16[256,256]{1,0:T(8,128)(2,1)S(1)}, u32[]{:S(2)}, u32[]{:S(2)}) collective-permute-start(bf16[256,256]{1,0:T(8,128)(2,1)S(1)} %get-tuple-element.66), channel_id=1, source_target_pairs={{0,12},{1,13},{2,6},{3,7},{4,0},{5,1},{6,10},{7,11},{8,4},{9,5},{1... | collective-permute-start | bytes 393224 | tf_op jit(solution)/shard_map/ppermute | solution.py:52
  35.3 5.0 %collective-permute-start.15 = (bf16[256,1024]{1,0:T(8,128)(2,1)S(1)}, bf16[256,1024]{1,0:T(8,128)(2,1)S(1)}, u32[]{:S(2)}, u32[]{:S(2)}) collective-permute-start(bf16[256,1024]{1,0:T(8,128)(2,1)S(1)} %collective-permute-done.14.e2), channel_id=1, source_target_pairs={{0,1},{1,0},{2,3},{3,2},{4,5},{5,4},{6,7},{7,6},{8,9},{9,8},{10,11... | collective-permute-start | bytes 1572872 | tf_op jit(solution)/shard_map/ppermute | solution.py:43
  42.1 6.9 %collective-permute-start.16 = (bf16[256,128]{1,0:T(8,128)(2,1)S(1)}, bf16[256,128]{1,0:T(8,128)(2,1)S(1)}, u32[]{:S(2)}, u32[]{:S(2)}) collective-permute-start(bf16[256,128]{1,0:T(8,128)(2,1)S(1)} %get-tuple-element.87), channel_id=1, source_target_pairs={{0,16},{1,17},{2,18},{3,19},{4,20},{5,21},{6,22},{7,23},{8,24},{9,... | collective-permute-start | bytes 196616 | tf_op jit(solution)/shard_map/ppermute | solution.py:363
  43.7 6.3 %collective-permute-start.17 = (bf16[256,128]{1,0:T(8,128)(2,1)S(1)}, bf16[256,128]{1,0:T(8,128)(2,1)S(1)}, u32[]{:S(2)}, u32[]{:S(2)}) collective-permute-start(bf16[256,128]{1,0:T(8,128)(2,1)S(1)} %get-tuple-element.88), channel_id=1, source_target_pairs={{0,4},{1,5},{2,6},{3,7},{4,8},{5,9},{6,10},{7,11},{8,12},{9,13},{1... | collective-permute-start | bytes 196616 | tf_op jit(solution)/shard_map/ppermute | solution.py:363
  44.3 8.4 %collective-permute-start.18 = (bf16[256,128]{1,0:T(8,128)(2,1)S(1)}, bf16[256,128]{1,0:T(8,128)(2,1)S(1)}, u32[]{:S(2)}, u32[]{:S(2)}) collective-permute-start(bf16[256,128]{1,0:T(8,128)(2,1)S(1)} %get-tuple-element.89), channel_id=1, source_target_pairs={{0,20},{1,21},{2,22},{3,23},{4,24},{5,25},{6,26},{7,27},{8,28},{9,... | collective-permute-start | bytes 196616 | tf_op jit(solution)/shard_map/ppermute | solution.py:363
  44.8 10.1 %collective-permute-start.19 = (bf16[256,128]{1,0:T(8,128)(2,1)S(1)}, bf16[256,128]{1,0:T(8,128)(2,1)S(1)}, u32[]{:S(2)}, u32[]{:S(2)}) collective-permute-start(bf16[256,128]{1,0:T(8,128)(2,1)S(1)} %get-tuple-element.90), channel_id=1, source_target_pairs={{0,8},{1,9},{2,10},{3,11},{4,12},{5,13},{6,14},{7,15},{8,0},{9,1},... | collective-permute-start | bytes 196616 | tf_op jit(solution)/shard_map/ppermute | solution.py:363
  48.0 8.6 %collective-permute-start.20 = (bf16[256,128]{1,0:T(8,128)(2,1)S(1)}, bf16[256,128]{1,0:T(8,128)(2,1)S(1)}, u32[]{:S(2)}, u32[]{:S(2)}) collective-permute-start(bf16[256,128]{1,0:T(8,128)(2,1)S(1)} %get-tuple-element.91), channel_id=1, source_target_pairs={{0,24},{1,25},{2,26},{3,27},{4,28},{5,29},{6,30},{7,31},{8,16},{9,... | collective-permute-start | bytes 196616 | tf_op jit(solution)/shard_map/ppermute | solution.py:363
  49.0 17.5 %collective-permute-start.10 = (bf16[256,256]{1,0:T(8,128)(2,1)S(1)}, bf16[256,256]{1,0:T(8,128)(2,1)S(1)}, u32[]{:S(2)}, u32[]{:S(2)}) collective-permute-start(bf16[256,256]{1,0:T(8,128)(2,1)S(1)} %get-tuple-element.78), channel_id=1, source_target_pairs={{0,1},{1,0},{2,3},{3,2},{4,5},{5,4},{6,7},{7,6},{8,9},{9,8},{10,11... | collective-permute-start | bytes 393224 | tf_op jit(solution)/shard_map/ppermute | solution.py:43
  50.0 16.5 %collective-permute-start.11 = (bf16[256,256]{1,0:T(8,128)(2,1)S(1)}, bf16[256,256]{1,0:T(8,128)(2,1)S(1)}, u32[]{:S(2)}, u32[]{:S(2)}) collective-permute-start(bf16[256,256]{1,0:T(8,128)(2,1)S(1)} %get-tuple-element.79), channel_id=1, source_target_pairs={{0,2},{1,3},{2,0},{3,1},{4,6},{5,7},{6,4},{7,5},{8,10},{9,11},{10,... | collective-permute-start | bytes 393224 | tf_op jit(solution)/shard_map/ppermute | solution.py:43
  52.7 15.5 %collective-permute-start.12 = (bf16[256,256]{1,0:T(8,128)(2,1)S(1)}, bf16[256,256]{1,0:T(8,128)(2,1)S(1)}, u32[]{:S(2)}, u32[]{:S(2)}) collective-permute-start(bf16[256,256]{1,0:T(8,128)(2,1)S(1)} %get-tuple-element.80), channel_id=1, source_target_pairs={{0,3},{1,2},{2,1},{3,0},{4,7},{5,6},{6,5},{7,4},{8,11},{9,10},{10,... | collective-permute-start | bytes 393224 | tf_op jit(solution)/shard_map/ppermute | solution.py:43
  54.9 4.3 %collective-permute-start.21 = (bf16[256,128]{1,0:T(8,128)(2,1)S(1)}, bf16[256,128]{1,0:T(8,128)(2,1)S(1)}, u32[]{:S(2)}, u32[]{:S(2)}) collective-permute-start(bf16[256,128]{1,0:T(8,128)(2,1)S(1)} %get-tuple-element.92), channel_id=1, source_target_pairs={{0,12},{1,13},{2,14},{3,15},{4,0},{5,1},{6,2},{7,3},{8,4},{9,5},{1... | collective-permute-start | bytes 196616 | tf_op jit(solution)/shard_map/ppermute | solution.py:363
  56.6 5.2 %collective-permute-start.22 = (bf16[256,128]{1,0:T(8,128)(2,1)S(1)}, bf16[256,128]{1,0:T(8,128)(2,1)S(1)}, u32[]{:S(2)}, u32[]{:S(2)}) collective-permute-start(bf16[256,128]{1,0:T(8,128)(2,1)S(1)} %get-tuple-element.93), channel_id=1, source_target_pairs={{0,28},{1,29},{2,30},{3,31},{4,16},{5,17},{6,18},{7,19},{8,20},{9,... | collective-permute-start | bytes 196616 | tf_op jit(solution)/shard_map/ppermute | solution.py:363
  61.9 7.1 %collective-permute-start.23 = (bf16[64,256]{1,0:T(8,128)(2,1)S(1)}, bf16[64,256]{1,0:T(8,128)(2,1)S(1)}, u32[]{:S(2)}, u32[]{:S(2)}) collective-permute-start(bf16[64,256]{1,0:T(8,128)(2,1)S(1)} %get-tuple-element.94), channel_id=1, source_target_pairs={{0,0},{1,1},{2,16},{3,17},{4,4},{5,5},{6,20},{7,21},{8,8},{9,9},{1... | collective-permute-start | bytes 98312 | tf_op jit(solution)/shard_map/ppermute | solution.py:379
  62.6 6.5 %collective-permute-start.25 = (bf16[64,256]{1,0:T(8,128)(2,1)S(1)}, bf16[64,256]{1,0:T(8,128)(2,1)S(1)}, u32[]{:S(2)}, u32[]{:S(2)}) collective-permute-start(bf16[64,256]{1,0:T(8,128)(2,1)S(1)} %get-tuple-element.94), channel_id=1, source_target_pairs={{0,16},{1,17},{2,0},{3,1},{4,20},{5,21},{6,4},{7,5},{8,24},{9,25},... | collective-permute-start | bytes 98312 | tf_op jit(solution)/shard_map/ppermute | solution.py:379
  66.5 2.5 %collective-permute-start.24 = (bf16[64,256]{1,0:T(8,128)(2,1)S(1)}, bf16[64,256]{1,0:T(8,128)(2,1)S(1)}, u32[]{:S(2)}, u32[]{:S(2)}) collective-permute-start(bf16[64,256]{1,0:T(8,128)(2,1)S(1)} %get-tuple-element.95), channel_id=1, source_target_pairs={{0,1},{1,0},{2,17},{3,16},{4,5},{5,4},{6,21},{7,20},{8,9},{9,8},{1... | collective-permute-start | bytes 98312 | tf_op jit(solution)/shard_map/ppermute | solution.py:379
  66.5 3.6 %collective-permute-start.26 = (bf16[64,256]{1,0:T(8,128)(2,1)S(1)}, bf16[64,256]{1,0:T(8,128)(2,1)S(1)}, u32[]{:S(2)}, u32[]{:S(2)}) collective-permute-start(bf16[64,256]{1,0:T(8,128)(2,1)S(1)} %get-tuple-element.95), channel_id=1, source_target_pairs={{0,17},{1,16},{2,1},{3,0},{4,21},{5,20},{6,5},{7,4},{8,25},{9,24},... | collective-permute-start | bytes 98312 | tf_op jit(solution)/shard_map/ppermute | solution.py:379
  (1 other events, 0.9 us)

commit v3 on v2

v3 whole, which is shorter than its diff:
```python
import functools

import jax
import jax.numpy as jnp
from jax import lax
from jax.experimental import pallas as pl
from jax.experimental.pallas import tpu as pltpu
from jax.sharding import PartitionSpec as P

HD = 128
BLOCK = 128
MAXLEN = 768
GROUP = 4
FAR = 1 << 30
PEAK = 1.15e9
ALPHA = 1.0 / HD**0.5
SCALE = 1.0 / MAXLEN**0.5
VMEM = pl.BlockSpec(memory_space=pltpu.VMEM)
HBM = pl.BlockSpec(memory_space=pltpu.HBM)
SMEM = pl.BlockSpec(memory_space=pltpu.SMEM)


def call(kernel, outs, args, specs=None, busy=0.5, scratch=(), aliases=None):
    moved = sum(a.size * a.dtype.itemsize for a in list(outs) + list(args))
    return pl.pallas_call(
        kernel,
        out_shape=tuple(outs),
        in_specs=specs or [VMEM] * len(args),
        out_specs=tuple([VMEM] * len(outs)),
        scratch_shapes=scratch,
        input_output_aliases=aliases or {},
        compiler_params=pltpu.CompilerParams(vmem_limit_bytes=24 * 1024 * 1024),
        cost_estimate=pl.CostEstimate(
            flops=int(busy * PEAK), bytes_accessed=moved, transcendentals=0
        ),
    )(*args)


def like(rows, cols, dtype=jnp.bfloat16):
    return jax.ShapeDtypeStruct((rows, cols), dtype)


def partner(value, steps):
    count = lax.axis_size("ctx")
    return lax.ppermute(value, "ctx", [(i, i ^ steps) for i in range(count)])


def around(value, low, high):
    count = lax.axis_size("ctx")
    pairs = []
    for i in range(count):
        planes = low if i % GROUP < GROUP // 2 else high
        pairs.append((i, (i + planes * GROUP) % count))
    return lax.ppermute(value, "ctx", pairs)


def place():
    return lax.rem(lax.axis_index("ctx"), GROUP)


def head_cols(h):
    return pl.ds(pl.multiple_of(h * HD, HD), HD)


def nn(a, b):
    return jnp.dot(a, b, preferred_element_type=jnp.float32)


def fetch_kernel(a_ref, b_ref, wk_ref, wq_ref, *refs):
    outs, weights, sems = refs[:GROUP], refs[GROUP], refs[GROUP + 1]
    me = place()
    copies = []
    for side, ref in enumerate((wk_ref, wq_ref)):
        to = slice(side * HD, (side + 1) * HD)
        copies.append((ref.at[:, head_cols(me)], weights.at[:, to]))
    for k in range(GROUP):
        for side, ref in enumerate((a_ref, b_ref)):
            to = slice(side * HD, (side + 1) * HD)
            copies.append((ref.at[:, head_cols(me ^ k)], outs[k].at[:, to]))
    started = [pltpu.make_async_copy(*pair, sems.at[i]) for i, pair in enumerate(copies)]
    for copy in started:
        copy.start()
    for copy in started:
        copy.wait()


def project_kernel(near, far, weights, near_kq, far_kq):
    near_kq[...] = nn(near[...], weights[...]).astype(jnp.bfloat16)
    far_kq[...] = nn(far[...], weights[...]).astype(jnp.bfloat16)


def upper():
    return lax.div(place(), 2)


def edge_kernel(own, *refs):
    *sources, big, small = refs
    rows = small.shape[0]
    core = lax.rem(place(), 2)
    keys_big = upper() == (1 if own else 0)
    for pair in range(len(sources) // 2):
        to = slice(pair * HD, (pair + 1) * HD)
        for ref, at_core in ((sources[2 * pair], core), (sources[2 * pair + 1], 1 - core)):
            at = pl.ds(pl.multiple_of(at_core * rows, rows), rows)

            @pl.when(keys_big)
            def _():
                big[at, to] = ref[:, :HD]

                @pl.when(at_core == 0)
                def _():
                    small[:, to] = ref[:, HD:]

            @pl.when(jnp.logical_not(keys_big))
            def _():
                big[at, to] = ref[:, HD:]

                @pl.when(at_core == 1)
                def _():
                    small[:, to] = ref[:, :HD]


def offset_of(row, shift, total):
    return lax.rem(row - shift + 2 * total, total)


def key_place(row, rows, shift, keep_ref, total):
    base = offset_of(row, shift, total)
    nblk = keep_ref.shape[1]
    raw = base + lax.broadcasted_iota(jnp.int32, (rows, HD), 0)
    b0 = base // BLOCK
    kept = jnp.full((rows, HD), keep_ref[0, b0], jnp.int32)
    for more in range(1, rows // BLOCK + 1):
        flag = keep_ref[0, lax.rem(b0 + more, nblk)]
        kept = jnp.where(raw >= (b0 + more) * BLOCK, flag, kept)
    where = jnp.where(raw >= total, raw - total, raw)
    return jnp.where(kept > 0, where, FAR)


def query_place(row, rows, shift, len_ref, total):
    base = offset_of(row, shift, total)
    raw = base + lax.broadcasted_iota(jnp.int32, (1, rows), 1)
    where = jnp.where(raw >= total, raw - total, raw)
    begin = jnp.zeros((1, rows), jnp.int32)
    end = jnp.int32(0)
    for u in range(len_ref.shape[1]):
        length = len_ref[0, u]
        end = end + length
        begin = begin + jnp.where(where >= end, length, 0)
    return where, begin


def after(value, *earlier):
    return lax.optimization_barrier((value, *earlier))[0]


def tile_terms(k, v, q_t, o_t, kpos, qpos, qbegin):
    y = nn(k, q_t) * (0.5 * ALPHA)
    t = jnp.tanh(y)
    u = 1.0 + t
    kpos = jnp.concatenate([kpos] * (q_t.shape[1] // HD), axis=1)
    valid = (kpos >= qbegin) & (kpos <= qpos)
    att = jnp.where(valid, y * u, 0.0).astype(jnp.bfloat16)
    slope = u * (1.0 + y * (1.0 - t))
    ds = jnp.where(valid, nn(v, o_t) * slope, 0.0).astype(jnp.bfloat16)
    return att, ds


def cross_pairs(
    own, len_ref, shift_ref, keep_ref, k_ref, q_ref, v_ref, o_ref, big, small,
    out_t, dq_t, dk, dv,
):
    rows = small.shape[0]
    span = GROUP - 1
    total = rows * lax.axis_size("ctx")
    shift = shift_ref[0]
    base = (lax.axis_index("ctx") // GROUP) * (GROUP * rows)

    def shard(j):
        return slice(j * rows, (j + 1) * rows)

    def load(ref, j):
        return ref[shard(j), :HD], ref[shard(j), HD:]

    def before(ref, first, reached):
        q_ts = [q_ref[shard(j), :].T for j in range(max(reached) + 1)]
        o_ts = [o_ref[shard(j), :].T for j in range(max(reached) + 1)]
        for p in reached:
            k, v = load(ref, p - first)
            k_t, v_t = k.T, v.T
            kpos = key_place(base + (p - span) * rows, rows, shift, keep_ref, total)
            for qt in range(p + 1):
                place_q = query_place(base + qt * rows, rows, shift, len_ref, total)
                att, ds = tile_terms(k, v, q_ts[qt], o_ts[qt], kpos, *place_q)
                out_t[:, shard(qt)] += nn(v_t, att)
                dq_t[:, shard(qt)] += nn(k_t, ds)

    def behind(ref, first, reached):
        for n in reached:
            q, o = load(ref, n - first)
            q_t, o_t = q.T, o.T
            place_q = query_place(base + (GROUP + n) * rows, rows, shift, len_ref, total)
            for kt in range(n + 1, GROUP):
                kpos = key_place(base + kt * rows, rows, shift, keep_ref, total)
                att, ds = tile_terms(
                    k_ref[shard(kt), :], v_ref[shard(kt), :], q_t, o_t, kpos, *place_q
                )
                dv[shard(kt), :] += nn(att, o)
                dk[shard(kt), :] += nn(ds, q)

    keys_big = upper() == (1 if own else 0)

    @pl.when(keys_big)
    def _():
        before(big, 1, range(1, span))
        behind(small, span - 1, [span - 1])

    @pl.when(jnp.logical_not(keys_big))
    def _():
        before(small, 0, [0])
        behind(big, 0, range(span - 1))


def inner_kernel(
    len_ref, shift_ref, keep_ref, a0, a1, a2, a3, b0, b1, b2, b3, big, small,
    k_ref, q_ref, v_ref, o_ref, out_t, dq_t, dk, dv,
):
    rows = a0.shape[0]
    total = rows * lax.axis_size("ctx")
    shift = shift_ref[0]
    base = (lax.axis_index("ctx") // GROUP) * (GROUP * rows)
    me = place()
    for i, (kq, vo) in enumerate(((a0, b0), (a1, b1), (a2, b2), (a3, b3))):
        at = pl.ds(pl.multiple_of((me ^ i) * rows, rows), rows)
        k_ref[at, :] = kq[:, :HD]
        q_ref[at, :] = kq[:, HD:]
        v_ref[at, :] = vo[:, :HD]
        o_ref[at, :] = vo[:, HD:]
    shards = [slice(j * rows, (j + 1) * rows) for j in range(GROUP)]
    places = [query_place(base + j * rows, rows, shift, len_ref, total) for j in range(GROUP)]
    q_ts = [q_ref[at, :].T for at in shards]
    o_ts = [o_ref[at, :].T for at in shards]
    for kt, at in enumerate(shards):
        k, v = k_ref[at, :], v_ref[at, :]
        k_t, v_t = k.T, v.T
        kpos = key_place(base + kt * rows, rows, shift, keep_ref, total)
        dk_sum, dv_sum = 0.0, 0.0
        for qt in range(kt, GROUP):
            qs = shards[qt]
            att, ds = tile_terms(k, v, q_ts[qt], o_ts[qt], kpos, *places[qt])
            if kt == 0:
                out_t[:, qs] = nn(v_t, att)
                dq_t[:, qs] = nn(k_t, ds)
            else:
                out_t[:, qs] += nn(v_t, att)
                dq_t[:, qs] += nn(k_t, ds)
            dv_sum = dv_sum + nn(att, o_ref[qs, :])
            dk_sum = dk_sum + nn(ds, q_ref[qs, :])
        dk[at, :] = dk_sum
        dv[at, :] = dv_sum
    cross_pairs(
        True, len_ref, shift_ref, keep_ref, k_ref, q_ref, v_ref, o_ref, big, small,
        out_t, dq_t, dk, dv,
    )


def outer_kernel(
    len_ref, shift_ref, keep_ref, k_ref, q_ref, v_ref, o_ref, big, small, *refs
):
    out_t, dq_t, dk, dv, s0, s1, s2, s3, dqk = refs[4:]
    cross_pairs(
        False, len_ref, shift_ref, keep_ref, k_ref, q_ref, v_ref, o_ref, big, small,
        out_t, dq_t, dk, dv,
    )
    rows = small.shape[0]
    me = place()
    factor = 0.5 * SCALE * ALPHA
    dqk[:HD, :] = (dq_t[...] * factor).astype(jnp.bfloat16)
    for j in range(GROUP):
        dqk[HD:, slice(j * rows, (j + 1) * rows)] = (dk[slice(j * rows, (j + 1) * rows), :] * factor).T.astype(jnp.bfloat16)
    for i, ref in enumerate((s0, s1, s2, s3)):
        at = pl.ds(pl.multiple_of((me ^ i) * rows, rows), rows)
        ref[:, :HD] = (out_t[:, at] * SCALE).T.astype(jnp.bfloat16)
        ref[:, HD:] = (dv[at, :] * SCALE).astype(jnp.bfloat16)


def terms_of(dqk, e0, e1, e2, e3):
    rows = e0.shape[0]
    me = place()
    total = None
    for k, ref in enumerate((e0, e1, e2, e3)):
        at = pl.ds(pl.multiple_of((me ^ k) * rows, rows), rows)
        part = nn(dqk[:, at], ref[...])
        total = part if total is None else total + part
    return total


def terms_kernel(dqk, e0, e1, e2, e3, whole):
    whole[...] = terms_of(dqk, e0, e1, e2, e3)


def half_terms_kernel(same, dqk, e0, e1, e2, e3, out):
    rows = e0.shape[0]
    me = place()
    y = lax.axis_index("dp")
    half = y if same else 1 - y
    width = out.shape[1]
    high = dqk.shape[0]
    count = out.shape[0] // high
    for z in range(0, count, 2):
        cols = [pl.ds(pl.multiple_of((2 * (z + i) + half) * width, width), width) for i in (0, 1)]
        total = 0.0
        for k, ref in enumerate((e0, e1, e2, e3)):
            at = pl.ds(pl.multiple_of((me ^ k) * rows, rows), rows)
            piece = jnp.concatenate([ref[:, cols[0]], ref[:, cols[1]]], axis=1)
            total = total + nn(dqk[:, at], piece)
        out[z * high : (z + 1) * high, :] = total[:, :width].astype(out.dtype)
        out[(z + 1) * high : (z + 2) * high, :] = total[:, width:].astype(out.dtype)


def pair_sum_kernel(mine, other, *outs):
    planes = lax.axis_size("ctx") // GROUP
    z = lax.axis_index("ctx") // GROUP
    high = outs[0].shape[0]
    for dz, ref in enumerate(outs):
        at = pl.ds(pl.multiple_of(lax.rem(z + dz, planes) * high, high), high)
        ref[...] = (mine[at, :] + other[at, :].astype(jnp.float32)).astype(ref.dtype)


def sum_kernel(*refs):
    ins, (near, far, hold) = refs[:-3], refs[-3:]
    total = ins[0][...].astype(jnp.float32)
    for ref in ins[1:]:
        total = total + ref[...].astype(jnp.float32)
    hold[...] = total.T
    share = near.shape[0]
    core = lax.rem(lax.axis_index("ctx"), 2)
    near[...] = hold[pl.ds(pl.multiple_of(core * share, share), share), :].astype(jnp.bfloat16)
    far[...] = hold[pl.ds(pl.multiple_of((1 - core) * share, share), share), :].astype(jnp.bfloat16)


def finish_kernel(r00, r01, r10, r11, gq, gk):
    y = lax.axis_index("dp")
    core = lax.rem(lax.axis_index("ctx"), 2)
    for (a, b), ref in zip(((0, 0), (0, 1), (1, 0), (1, 1)), (r00, r01, r10, r11)):
        cols = head_cols(2 * (y ^ a) + (core ^ b))
        gq[:, cols] = ref[:, :HD]
        gk[:, cols] = ref[:, HD:]


def merge_kernel(i0, i1, i2, i3, first, second):
    me = place()
    for k, ref in enumerate((i0, i1, i2, i3)):
        cols = head_cols(me ^ k)
        first[:, cols] = ref[:, :HD]
        second[:, cols] = ref[:, HD:]


def direct_reduce(dqk, gathered, share, early, late):
    count = lax.axis_size("ctx")
    planes = count // GROUP
    width = gathered[0].shape[1]
    block = width // (2 * planes)
    shape = (2 * HD * planes, block)
    args = (dqk, *gathered)
    (give,) = call(functools.partial(half_terms_kernel, False), [like(*shape)], args, busy=1)
    (keep,) = call(
        functools.partial(half_terms_kernel, True), [like(*shape, jnp.float32)], args, busy=1
    )
    got = lax.ppermute(give, "dp", [(0, 1), (1, 0)])
    sends = call(
        pair_sum_kernel,
        [like(2 * HD, block, jnp.float32)] + [like(2 * HD, block)] * (planes - 1),
        (keep, after(got, *early)),
    )
    arrived = [after(sends[0], *late)] + [around(sends[dz], dz, dz) for dz in range(1, planes)]
    near, far = call(
        sum_kernel,
        [like(share, 2 * HD)] * 2,
        arrived,
        scratch=[pltpu.VMEM((block, 2 * HD), jnp.float32)],
    )
    received = []
    for a in range(2):
        for b in range(2):
            pairs = []
            for y in range(2):
                for i in range(count):
                    z, x, c = i // 4, (i // 2) % 2, i % 2
                    pairs.append((y * count + i, (x ^ a) * count + 4 * z + 2 * y + (c ^ b)))
            received.append(lax.ppermute((near, far)[b], ("dp", "ctx"), pairs))
    return call(finish_kernel, [like(share, GROUP * HD)] * 2, received)


def general_reduce(dqk, gathered, share, early, late):
    count = lax.axis_size("ctx")
    planes = count // GROUP
    width = gathered[0].shape[1]
    (whole,) = call(
        terms_kernel, [like(2 * HD, width, jnp.float32)], (dqk, *gathered), busy=2
    )
    whole = lax.psum(whole.T, "dp")
    same_head = [[g * GROUP + j for g in range(planes)] for j in range(GROUP)]
    plane = [[g * GROUP + j for j in range(GROUP)] for g in range(planes)]
    part = lax.psum_scatter(
        whole, "ctx", scatter_dimension=0, axis_index_groups=same_head, tiled=True
    ).astype(jnp.bfloat16)
    part = lax.all_to_all(
        part.reshape(GROUP, share, 2 * HD), "ctx", 0, 0, axis_index_groups=plane, tiled=True
    )
    part = jnp.moveaxis(part.reshape(GROUP, share, 2, HD), 0, 2)
    return part[:, 0].reshape(share, GROUP * HD), part[:, 1].reshape(share, GROUP * HD)


def body(events, w_query, w_key, values, grad_out, lengths, stream_shift, block_keep):
    rows, width = events.shape[1:]
    features = w_query.shape[1]
    count = lax.axis_size("ctx")
    local = events[0]
    all_rows = GROUP * rows
    pair = like(rows, 2 * HD)
    full = like(all_rows, HD)

    e1 = partner(local, 1)
    e2 = partner(local, 2)
    *vo, weights = call(
        fetch_kernel,
        [pair] * GROUP + [like(width, 2 * HD)],
        [
            pltpu.with_memory_space_constraint(a, pltpu.HBM)
            for a in (values[0], grad_out[0], w_key, w_query)
        ],
        specs=[HBM] * 4,
        scratch=[pltpu.SemaphoreType.DMA((2 * GROUP + 2,))],
    )
    vo = (vo[0],) + tuple(partner(vo[k], k) for k in range(1, GROUP))
    edges = [like(2 * rows, 2 * HD), pair]
    own_edge, other_edge = (functools.partial(edge_kernel, flag) for flag in (True, False))
    kq = call(project_kernel, [pair] * 2, (local, e1, weights), busy=3)
    big, small = call(own_edge, edges, (*kq, *vo[:2]))
    own = around(big, -1, 1), around(small, 1, -1)
    e3 = partner(after(e2, *own, *vo[2:]), 1)
    kq = kq + call(project_kernel, [pair] * 2, (e2, e3, weights), busy=3)
    big, small = call(other_edge, edges, (*kq[2:], *vo[2:]))
    other = around(big, 1, -1), around(small, -1, 1)

    info = (lengths, stream_shift, block_keep)
    wide, tall = like(HD, all_rows, jnp.float32), like(all_rows, HD, jnp.float32)
    sums = [wide, wide, tall, tall]
    k, q, v, o, *held = call(
        inner_kernel,
        [full] * 4 + sums,
        (*info, *kq, *vo, *own),
        specs=[SMEM] * 3 + [VMEM] * 10,
        busy=15,
    )
    *_, p0, p1, p2, p3, dqk = call(
        outer_kernel,
        sums + [pair] * GROUP + [like(2 * HD, all_rows)],
        (*info, k, q, v, o, *other, *held),
        specs=[SMEM] * 3 + [VMEM] * 10,
        aliases={9: 0, 10: 1, 11: 2, 12: 3},
        busy=6,
    )
    parts = (p0, p1, p2, p3)
    parts = (parts[0],) + tuple(partner(parts[k], k) for k in range(1, GROUP))
    merged = call(merge_kernel, [like(rows, features)] * 2, parts)
    share = width // count
    reduce = direct_reduce if lax.axis_size("dp") == 2 and count == 16 else general_reduce
    grad_wq, grad_wk = reduce(dqk, (local, e1, e2, e3), share, parts[1:3], merged)
    attended, grad_values = merged
    return (attended[None], grad_values[None], grad_wq, grad_wk)


def solution(mesh):
    placed = (
        P("dp", "ctx", None),
        P(),
        P(),
        P("dp", "ctx", None),
        P("dp", "ctx", None),
        P("dp", None),
        P("dp"),
        P("dp", None),
    )
    return jax.shard_map(
        body,
        mesh=mesh,
        in_specs=placed,
        out_specs=(P("dp", "ctx", None), P("dp", "ctx", None), P("ctx", None), P("ctx", None)),
        check_vma=False,
    )
```

time: 71.1 us -> 65.9 us (0.927)
  waiting for transfers between devices: 14.3 us -> 24.3 us
  starting transfers between devices: 33.9 us -> 25 us
  Pallas kernels: 19.2 us -> 14.5 us
  local copies, waits for them, and re-layouts: 1.91 us -> 0.02 us
    ppermute x12 -> x9, waiting for transfers between devices: 5.36 us -> 16.1 us  [partner(): return lax.ppermute(value, 'ctx', [(i, i ^ steps) for i in range(count)])]
    ppermute x7 -> x1, starting transfers between devices: 10.2 us -> 1.58 us  [direct_reduce(): got = lax.ppermute(give, 'dp', [(0, 1), (1, 0)])]
    ppermute x7 -> x1, waiting for transfers between devices: 6.74 us -> 0.01 us  [direct_reduce(): got = lax.ppermute(give, 'dp', [(0, 1), (1, 0)])]
    ppermute x4 -> x7, waiting for transfers between devices: 1.13 us -> 7.36 us  [around(): return lax.ppermute(value, 'ctx', pairs)]
    pallas_call x11 -> x13, Pallas kernels: 19.2 us -> 14.5 us  [call(): pl.pallas_call(kernel, out_shape=tuple(outs), in_specs=specs or [VMEM] *...]
    ppermute x4 -> x7, starting transfers between devices: 8.2 us -> 11.3 us  [around(): return lax.ppermute(value, 'ctx', pairs)]
    ppermute x12 -> x9, starting transfers between devices: 9.32 us -> 6.59 us  [partner(): return lax.ppermute(value, 'ctx', [(i, i ^ steps) for i in range(count)])]
    unnamed x12 -> x6, local copies, waits for them, and re-layouts: 1.91 us -> 0.02 us
  transfers between devices with their start and end apart: 27 -> 21, of which waited for: 10 -> 9; matrix products, arithmetic and copies ran while one was open for 0% -> 0% of each run, Pallas kernels for 23% -> 15%
where the time goes in v3:
time: 65.9 us; the launch traced here: 65.3 us
  starting transfers between devices  25 us (38%)
  waiting for transfers between devices  24.3 us (37%)
  Pallas kernels  14.5 us (22%)
  between operations  1.43 us (2%)
    ppermute x9, waiting for transfers between devices, partner(): return lax.ppermute(value, 'ctx', [(i, i ^ steps) for i in range(count)])  16.1 us
    pallas_call x13, Pallas kernels, call(): pl.pallas_call(kernel, out_shape=tuple(outs), in_specs=specs or [VMEM] *...  14.5 us
    ppermute x7, starting transfers between devices, around(): return lax.ppermute(value, 'ctx', pairs)  11.3 us
    ppermute x7, waiting for transfers between devices, around(): return lax.ppermute(value, 'ctx', pairs)  7.36 us
    ppermute x9, starting transfers between devices, partner(): return lax.ppermute(value, 'ctx', [(i, i ^ steps) for i in range(count)])  6.59 us
    ppermute x4, starting transfers between devices, direct_reduce(): received.append(lax.ppermute((near, far)[b], ('dp', 'ctx'), pairs))  5.6 us
    ppermute x1, starting transfers between devices, direct_reduce(): got = lax.ppermute(give, 'dp', [(0, 1), (1, 0)])  1.58 us
  transfers between devices with their start and end apart: 21, of which 9 were waited for; matrix products, arithmetic and copies ran while one was open for 0% of the time, Pallas kernels for 15%

profile of v3, /device:TPU:0, one launch (start us, length us, event | category | flops | bytes accessed | tf_op | source)
XLA Modules:
  0.0 65.3 jit_solution(5029077226880742079)
XLA Ops:
  0.6 0.5 collective-permute-start
  1.1 2.6 %collective-permute-start.1 = (bf16[256,1024]{1,0:T(8,128)(2,1)}, bf16[256,1024]{1,0:T(8,128)(2,1)S(1)}, u32[]{:S(2)}, u32[]{:S(2)}) collective-permute-start(bf16[256,1024]{1,0:T(8,128)(2,1)} %bitcast.6), channel_id=1, source_target_pairs={{0,2},{1,3},{2,0},{3,1},{4,6},{5,7},{6,4},{7,5},{8,10},{9,11},{10,... | collective-permute-start | bytes 1572872 | tf_op jit(solution)/shard_map/ppermute | solution.py:45
  3.7 1.3 %shard_map.111 = (bf16[256,256]{1,0:T(8,128)(2,1)S(1)}, bf16[256,256]{1,0:T(8,128)(2,1)S(1)}, bf16[256,256]{1,0:T(8,128)(2,1)S(1)}, bf16[256,256]{1,0:T(8,128)(2,1)S(1)}, bf16[1024,256]{1,0:T(8,128)(2,1)S(1)}) custom-call(bf16[256,512]{1,0:T(8,128)(2,1)} %bitcast.10, bf16[256,512]{1,0:T(8,128)(2,1)} %bitcast.11, bf16[1024,512]{1,0:T(8,128)(2,1)} %wk_ref.1, ...), custom_call_target="tpu_custom_call" | custom-call | flops 575000000 | bytes 3670016 | tf_op jit(solution)/shard_map/pallas_call | solution.py:25
  5.3 0.4 shard_map.112
  5.7 0.7 %collective-permute-done.2.refs_3_.b1 = bf16[256,256]{1,0:T(8,128)(2,1)S(1)} collective-permute-done((bf16[256,256]{1,0:T(8,128)(2,1)S(1)}, bf16[256,256]{1,0:T(8,128)(2,1)S(1)}, u32[]{:S(2)}, u32[]{:S(2)}) %collective-permute-start.2) | collective-permute-done | bytes 131104 | tf_op jit(solution)/shard_map/ppermute | solution.py:45
  6.5 3.7 %collective-permute-start.3 = (bf16[512,256]{1,0:T(8,128)(2,1)S(1)}, bf16[512,256]{1,0:T(8,128)(2,1)S(1)}, u32[]{:S(2)}, u32[]{:S(2)}) collective-permute-start(bf16[512,256]{1,0:T(8,128)(2,1)S(1)} %get-tuple-element.48), channel_id=1, source_target_pairs={{0,12},{1,13},{2,6},{3,7},{4,0},{5,1},{6,10},{7,11},{8,4},{9,5},{1... | collective-permute-start | bytes 786440 | tf_op jit(solution)/shard_map/ppermute | solution.py:54
  10.2 1.2 %collective-permute-start.6 = (bf16[256,256]{1,0:T(8,128)(2,1)S(1)}, bf16[256,256]{1,0:T(8,128)(2,1)S(1)}, u32[]{:S(2)}, u32[]{:S(2)}) collective-permute-start(bf16[256,256]{1,0:T(8,128)(2,1)S(1)} %get-tuple-element.51), channel_id=1, source_target_pairs={{0,3},{1,2},{2,1},{3,0},{4,7},{5,6},{6,5},{7,4},{8,11},{9,10},{10,... | collective-permute-start | bytes 393224 | tf_op jit(solution)/shard_map/ppermute | solution.py:45
  11.4 8.1 %collective-permute-done.5.b2.refs_2_ = bf16[256,256]{1,0:T(8,128)(2,1)S(1)} collective-permute-done((bf16[256,256]{1,0:T(8,128)(2,1)S(1)}, bf16[256,256]{1,0:T(8,128)(2,1)S(1)}, u32[]{:S(2)}, u32[]{:S(2)}) %collective-permute-start.5) | collective-permute-done | bytes 131104 | tf_op jit(solution)/shard_map/ppermute | solution.py:45
  19.5 2.3 %collective-permute-done.6.b3.refs_3_ = bf16[256,256]{1,0:T(8,128)(2,1)S(1)} collective-permute-done((bf16[256,256]{1,0:T(8,128)(2,1)S(1)}, bf16[256,256]{1,0:T(8,128)(2,1)S(1)}, u32[]{:S(2)}, u32[]{:S(2)}) %collective-permute-start.6) | collective-permute-done | bytes 131104 | tf_op jit(solution)/shard_map/ppermute | solution.py:45
  22.6 1.1 %collective-permute-done.7.far.e3 = bf16[256,1024]{1,0:T(8,128)(2,1)S(1)} collective-permute-done((bf16[256,1024]{1,0:T(8,128)(2,1)S(1)}, bf16[256,1024]{1,0:T(8,128)(2,1)S(1)}, u32[]{:S(2)}, u32[]{:S(2)}) %collective-permute-start.7) | collective-permute-done | bytes 524320 | tf_op jit(solution)/shard_map/ppermute | solution.py:45
  23.8 0.4 shard_map.114
  24.4 3.7 %collective-permute-start.9 = (bf16[256,256]{1,0:T(8,128)(2,1)S(1)}, bf16[256,256]{1,0:T(8,128)(2,1)S(1)}, u32[]{:S(2)}, u32[]{:S(2)}) collective-permute-start(bf16[256,256]{1,0:T(8,128)(2,1)S(1)} %get-tuple-element.60), channel_id=1, source_target_pairs={{0,12},{1,13},{2,6},{3,7},{4,0},{5,1},{6,10},{7,11},{8,4},{9,5},{1... | collective-permute-start | bytes 393224 | tf_op jit(solution)/shard_map/ppermute | solution.py:54
  28.1 6.4 %shard_map.115 = (bf16[1024,128]{1,0:T(8,128)(2,1)S(1)}, bf16[1024,128]{1,0:T(8,128)(2,1)S(1)}, bf16[1024,128]{1,0:T(8,128)(2,1)S(1)}, bf16[1024,128]{1,0:T(8,12...) custom-call(s32[1,8]{1,0:T(1,128)S(1)} %copy-done.1, ...), custom_call_target="tpu_custom_call" | custom-call | flops 17250000896 | bytes 4587684 | tf_op jit(solution)/shard_map/pallas_call | solution.py:25
  34.5 3.6 %collective-permute-done.8.big = bf16[512,256]{1,0:T(8,128)(2,1)S(1)} collective-permute-done((bf16[512,256]{1,0:T(8,128)(2,1)S(1)}, bf16[512,256]{1,0:T(8,128)(2,1)S(1)}, u32[]{:S(2)}, u32[]{:S(2)}) %collective-permute-start.8) | collective-permute-done | bytes 262176 | tf_op jit(solution)/shard_map/ppermute | solution.py:54
  38.1 2.9 %shard_map.117 = (f32[128,1024]{1,0:T(8,128)S(1)}, f32[128,1024]{1,0:T(8,128)S(1)}, f32[1024,128]{1,0:T(8,128)S(1)}, f32[1024,128]{1,0:T(8,128)S(1)}, bf16[256,2...) custom-call(s32[1,8]{1,0:T(1,128)S(1)} %copy-done.1, ...), custom_call_target="tpu_custom_call", output_to_operand_aliasing={{0}: (9, {}), {1}: (10, {}), {2}: (11, {}), {3}: (12, {})} | custom-call | flops 6899999744 | bytes 6684836 | tf_op jit(solution)/shard_map/pallas_call | solution.py:25
  41.0 0.6 shard_map.120
  41.6 1.6 %collective-permute-start.13 = (bf16[1024,128]{1,0:T(8,128)(2,1)S(1)}, bf16[1024,128]{1,0:T(8,128)(2,1)S(1)}, u32[]{:S(2)}, u32[]{:S(2)}) collective-permute-start(bf16[1024,128]{1,0:T(8,128)(2,1)S(1)} %shard_map.120), channel_id=1, source_target_pairs={{0,16},{16,0},{1,17},{17,1},{2,18},{18,2},{3,19},{19,3},{4,20},{20... | collective-permute-start | bytes 786440 | tf_op jit(solution)/shard_map/ppermute | solution.py:370
  43.5 1.5 %collective-permute-start.12 = (bf16[256,256]{1,0:T(8,128)(2,1)S(1)}, bf16[256,256]{1,0:T(8,128)(2,1)S(1)}, u32[]{:S(2)}, u32[]{:S(2)}) collective-permute-start(bf16[256,256]{1,0:T(8,128)(2,1)S(1)} %get-tuple-element.68), channel_id=1, source_target_pairs={{0,3},{1,2},{2,1},{3,0},{4,7},{5,6},{6,5},{7,4},{8,11},{9,10},{10,... | collective-permute-start | bytes 393224 | tf_op jit(solution)/shard_map/ppermute | solution.py:45
  45.0 0.5 shard_map.119.mine
  45.6 3.9 %collective-permute-done.11.i2 = bf16[256,256]{1,0:T(8,128)(2,1)S(1)} collective-permute-done((bf16[256,256]{1,0:T(8,128)(2,1)S(1)}, bf16[256,256]{1,0:T(8,128)(2,1)S(1)}, u32[]{:S(2)}, u32[]{:S(2)}) %collective-permute-start.11) | collective-permute-done | bytes 131104 | tf_op jit(solution)/shard_map/ppermute | solution.py:45
  49.5 1.4 %collective-permute-start.14 = (bf16[256,128]{1,0:T(8,128)(2,1)S(1)}, bf16[256,128]{1,0:T(8,128)(2,1)S(1)}, u32[]{:S(2)}, u32[]{:S(2)}) collective-permute-start(bf16[256,128]{1,0:T(8,128)(2,1)S(1)} %get-tuple-element.75), channel_id=1, source_target_pairs={{0,4},{1,5},{2,6},{3,7},{4,8},{5,9},{6,10},{7,11},{8,12},{9,13},{1... | collective-permute-start | bytes 196616 | tf_op jit(solution)/shard_map/ppermute | solution.py:54
  50.9 0.7 %collective-permute-start.15 = (bf16[256,128]{1,0:T(8,128)(2,1)S(1)}, bf16[256,128]{1,0:T(8,128)(2,1)S(1)}, u32[]{:S(2)}, u32[]{:S(2)}) collective-permute-start(bf16[256,128]{1,0:T(8,128)(2,1)S(1)} %get-tuple-element.76), channel_id=1, source_target_pairs={{0,8},{1,9},{2,10},{3,11},{4,12},{5,13},{6,14},{7,15},{8,0},{9,1},... | collective-permute-start | bytes 196616 | tf_op jit(solution)/shard_map/ppermute | solution.py:54
  51.6 1.8 %collective-permute-start.16 = (bf16[256,128]{1,0:T(8,128)(2,1)S(1)}, bf16[256,128]{1,0:T(8,128)(2,1)S(1)}, u32[]{:S(2)}, u32[]{:S(2)}) collective-permute-start(bf16[256,128]{1,0:T(8,128)(2,1)S(1)} %get-tuple-element.77), channel_id=1, source_target_pairs={{0,12},{1,13},{2,14},{3,15},{4,0},{5,1},{6,2},{7,3},{8,4},{9,5},{1... | collective-permute-start | bytes 196616 | tf_op jit(solution)/shard_map/ppermute | solution.py:54
  53.4 0.9 %shard_map.118 = (bf16[256,512]{1,0:T(8,128)(2,1)}, bf16[256,512]{1,0:T(8,128)(2,1)}) custom-call(bf16[256,256]{1,0:T(8,128)(2,1)S(1)} %get-tuple-element.65.i0, bf16[256,256]{1,0:T(8,128)(2,1)S(1)} %collective-permute-done.10.i1, bf16[256,256]{1,0:T(8,128)(2,1)S(1)} %collective-permute-done.11.i2, bf16[256,256]{1,0:T(8,128)(2,1)S(1)} %collective-permute-done.12.i3), custom_call_target="tpu_custom_call" | custom-call | flops 575000000 | bytes 1048576 | tf_op jit(solution)/shard_map/pallas_call | solution.py:25
  54.3 1.9 %collective-permute-done.14.refs_1_ = bf16[256,128]{1,0:T(8,128)(2,1)S(1)} collective-permute-done((bf16[256,128]{1,0:T(8,128)(2,1)S(1)}, bf16[256,128]{1,0:T(8,128)(2,1)S(1)}, u32[]{:S(2)}, u32[]{:S(2)}) %collective-permute-start.14) | collective-permute-done | bytes 65568 | tf_op jit(solution)/shard_map/ppermute | solution.py:54
  56.2 1.9 %collective-permute-done.15.refs_2_ = bf16[256,128]{1,0:T(8,128)(2,1)S(1)} collective-permute-done((bf16[256,128]{1,0:T(8,128)(2,1)S(1)}, bf16[256,128]{1,0:T(8,128)(2,1)S(1)}, u32[]{:S(2)}, u32[]{:S(2)}) %collective-permute-start.15) | collective-permute-done | bytes 65568 | tf_op jit(solution)/shard_map/ppermute | solution.py:54
  58.2 0.7 %collective-permute-start.19 = (bf16[64,256]{1,0:T(8,128)(2,1)S(1)}, bf16[64,256]{1,0:T(8,128)(2,1)S(1)}, u32[]{:S(2)}, u32[]{:S(2)}) collective-permute-start(bf16[64,256]{1,0:T(8,128)(2,1)S(1)} %get-tuple-element.78), channel_id=1, source_target_pairs={{0,16},{1,17},{2,0},{3,1},{4,20},{5,21},{6,4},{7,5},{8,24},{9,25},... | collective-permute-start | bytes 98312 | tf_op jit(solution)/shard_map/ppermute | solution.py:391
  58.9 0.7 collective-permute-start.17
  59.6 2.2 %collective-permute-start.20 = (bf16[64,256]{1,0:T(8,128)(2,1)S(1)}, bf16[64,256]{1,0:T(8,128)(2,1)S(1)}, u32[]{:S(2)}, u32[]{:S(2)}) collective-permute-start(bf16[64,256]{1,0:T(8,128)(2,1)S(1)} %get-tuple-element.79), channel_id=1, source_target_pairs={{0,17},{1,16},{2,1},{3,0},{4,21},{5,20},{6,5},{7,4},{8,25},{9,24},... | collective-permute-start | bytes 98312 | tf_op jit(solution)/shard_map/ppermute | solution.py:391
  61.8 2.0 %collective-permute-start.18 = (bf16[64,256]{1,0:T(8,128)(2,1)S(1)}, bf16[64,256]{1,0:T(8,128)(2,1)S(1)}, u32[]{:S(2)}, u32[]{:S(2)}) collective-permute-start(bf16[64,256]{1,0:T(8,128)(2,1)S(1)} %get-tuple-element.79), channel_id=1, source_target_pairs={{0,1},{1,0},{2,17},{3,16},{4,5},{5,4},{6,21},{7,20},{8,9},{9,8},{1... | collective-permute-start | bytes 98312 | tf_op jit(solution)/shard_map/ppermute | solution.py:391
  63.8 0.8 %collective-permute-done.18.r01 = bf16[64,256]{1,0:T(8,128)(2,1)S(1)} collective-permute-done((bf16[64,256]{1,0:T(8,128)(2,1)S(1)}, bf16[64,256]{1,0:T(8,128)(2,1)S(1)}, u32[]{:S(2)}, u32[]{:S(2)}) %collective-permute-start.18) | collective-permute-done | bytes 32800 | tf_op jit(solution)/shard_map/ppermute | solution.py:391
  64.7 0.7 %shard_map.123 = (bf16[64,512]{1,0:T(8,128)(2,1)}, bf16[64,512]{1,0:T(8,128)(2,1)}) custom-call(bf16[64,256]{1,0:T(8,128)(2,1)S(1)} %collective-permute-done.17.r00, bf16[64,256]{1,0:T(8,128)(2,1)S(1)} %collective-permute-done.18.r01, bf16[64,256]{1,0:T(8,128)(2,1)S(1)} %collective-permute-done.19.r10, bf16[64,256]{1,0:T(8,128)(2,1)S(1)} %collective-permute-done.20.r11), custom_call_target="tpu_custom_call" | custom-call | flops 575000000 | bytes 262144 | tf_op jit(solution)/shard_map/pallas_call | solution.py:25
  (29 shorter events, 1.2 us)
Async XLA Ops:
  0.6 4.6 %collective-permute-start = (bf16[256,1024]{1,0:T(8,128)(2,1)}, bf16[256,1024]{1,0:T(8,128)(2,1)S(1)}, u32[]{:S(2)}, u32[]{:S(2)}) collective-permute-start(bf16[256,1024]{1,0:T(8,128)(2,1)} %bitcast.5), channel_id=1, source_target_pairs={{0,1},{1,0},{2,3},{3,2},{4,5},{5,4},{6,7},{7,6},{8,9},{9,8},{10,11... | collective-permute-start | bytes 1572872 | tf_op jit(solution)/shard_map/ppermute | solution.py:45
  1.1 20.6 %collective-permute-start.1 = (bf16[256,1024]{1,0:T(8,128)(2,1)}, bf16[256,1024]{1,0:T(8,128)(2,1)S(1)}, u32[]{:S(2)}, u32[]{:S(2)}) collective-permute-start(bf16[256,1024]{1,0:T(8,128)(2,1)} %bitcast.6), channel_id=1, source_target_pairs={{0,2},{1,3},{2,0},{3,1},{4,6},{5,7},{6,4},{7,5},{8,10},{9,11},{10,... | collective-permute-start | bytes 1572872 | tf_op jit(solution)/shard_map/ppermute | solution.py:45
  3.7 1.6 %copy-start = (bf16[1,256,1024]{2,1,0:T(8,128)(2,1)S(1)}, bf16[1,256,1024]{2,1,0:T(8,128)(2,1)}, u32[]{:S(2)}) copy-start(bf16[1,256,1024]{2,1,0:T(8,128)(2,1)} %param.8) | copy-start | bytes 1572868
  5.0 1.4 %collective-permute-start.2 = (bf16[256,256]{1,0:T(8,128)(2,1)S(1)}, bf16[256,256]{1,0:T(8,128)(2,1)S(1)}, u32[]{:S(2)}, u32[]{:S(2)}) collective-permute-start(bf16[256,256]{1,0:T(8,128)(2,1)S(1)} %get-tuple-element.47), channel_id=1, source_target_pairs={{0,1},{1,0},{2,3},{3,2},{4,5},{5,4},{6,7},{7,6},{8,9},{9,8},{10,11... | collective-permute-start | bytes 393224 | tf_op jit(solution)/shard_map/ppermute | solution.py:45
  6.5 15.3 %collective-permute-start.3 = (bf16[512,256]{1,0:T(8,128)(2,1)S(1)}, bf16[512,256]{1,0:T(8,128)(2,1)S(1)}, u32[]{:S(2)}, u32[]{:S(2)}) collective-permute-start(bf16[512,256]{1,0:T(8,128)(2,1)S(1)} %get-tuple-element.48), channel_id=1, source_target_pairs={{0,12},{1,13},{2,6},{3,7},{4,0},{5,1},{6,10},{7,11},{8,4},{9,5},{1... | collective-permute-start | bytes 786440 | tf_op jit(solution)/shard_map/ppermute | solution.py:54
  10.2 9.3 %collective-permute-start.5 = (bf16[256,256]{1,0:T(8,128)(2,1)S(1)}, bf16[256,256]{1,0:T(8,128)(2,1)S(1)}, u32[]{:S(2)}, u32[]{:S(2)}) collective-permute-start(bf16[256,256]{1,0:T(8,128)(2,1)S(1)} %get-tuple-element.50), channel_id=1, source_target_pairs={{0,2},{1,3},{2,0},{3,1},{4,6},{5,7},{6,4},{7,5},{8,10},{9,11},{10,... | collective-permute-start | bytes 393224 | tf_op jit(solution)/shard_map/ppermute | solution.py:45
  10.2 11.6 %collective-permute-start.6 = (bf16[256,256]{1,0:T(8,128)(2,1)S(1)}, bf16[256,256]{1,0:T(8,128)(2,1)S(1)}, u32[]{:S(2)}, u32[]{:S(2)}) collective-permute-start(bf16[256,256]{1,0:T(8,128)(2,1)S(1)} %get-tuple-element.51), channel_id=1, source_target_pairs={{0,3},{1,2},{2,1},{3,0},{4,7},{5,6},{6,5},{7,4},{8,11},{9,10},{10,... | collective-permute-start | bytes 393224 | tf_op jit(solution)/shard_map/ppermute | solution.py:45
  11.4 10.4 %collective-permute-start.4 = (bf16[256,256]{1,0:T(8,128)(2,1)S(1)}, bf16[256,256]{1,0:T(8,128)(2,1)S(1)}, u32[]{:S(2)}, u32[]{:S(2)}) collective-permute-start(bf16[256,256]{1,0:T(8,128)(2,1)S(1)} %get-tuple-element.49), channel_id=1, source_target_pairs={{0,4},{1,5},{2,14},{3,15},{4,8},{5,9},{6,2},{7,3},{8,12},{9,13},{1... | collective-permute-start | bytes 393224 | tf_op jit(solution)/shard_map/ppermute | solution.py:54
  21.8 2.0 %collective-permute-start.7 = (bf16[256,1024]{1,0:T(8,128)(2,1)S(1)}, bf16[256,1024]{1,0:T(8,128)(2,1)S(1)}, u32[]{:S(2)}, u32[]{:S(2)}) collective-permute-start(bf16[256,1024]{1,0:T(8,128)(2,1)S(1)} %collective-permute-done.1.near.e2), channel_id=1, source_target_pairs={{0,1},{1,0},{2,3},{3,2},{4,5},{5,4},{6,7},{7,6},{8,9},{9,8},{10,11... | collective-permute-start | bytes 1572872 | tf_op jit(solution)/shard_map/ppermute | solution.py:45
  24.3 3.8 %copy-start.1 = (s32[1,8]{1,0:T(1,128)S(1)}, s32[1,8]{1,0:T(1,128)}, u32[]{:S(2)}) copy-start(s32[1,8]{1,0:T(1,128)} %len_ref.3) | copy-start | bytes 100
  24.4 3.7 %copy-start.2 = (s32[1,32]{1,0:T(1,128)S(1)}, s32[1,32]{1,0:T(1,128)}, u32[]{:S(2)}) copy-start(s32[1,32]{1,0:T(1,128)} %keep_ref.3) | copy-start | bytes 388
  24.4 10.1 %collective-permute-start.9 = (bf16[256,256]{1,0:T(8,128)(2,1)S(1)}, bf16[256,256]{1,0:T(8,128)(2,1)S(1)}, u32[]{:S(2)}, u32[]{:S(2)}) collective-permute-start(bf16[256,256]{1,0:T(8,128)(2,1)S(1)} %get-tuple-element.60), channel_id=1, source_target_pairs={{0,12},{1,13},{2,6},{3,7},{4,0},{5,1},{6,10},{7,11},{8,4},{9,5},{1... | collective-permute-start | bytes 393224 | tf_op jit(solution)/shard_map/ppermute | solution.py:54
  28.1 10.0 %collective-permute-start.8 = (bf16[512,256]{1,0:T(8,128)(2,1)S(1)}, bf16[512,256]{1,0:T(8,128)(2,1)S(1)}, u32[]{:S(2)}, u32[]{:S(2)}) collective-permute-start(bf16[512,256]{1,0:T(8,128)(2,1)S(1)} %get-tuple-element.59), channel_id=1, source_target_pairs={{0,4},{1,5},{2,14},{3,15},{4,8},{5,9},{6,2},{7,3},{8,12},{9,13},{1... | collective-permute-start | bytes 786440 | tf_op jit(solution)/shard_map/ppermute | solution.py:54
  41.6 7.9 %collective-permute-start.13 = (bf16[1024,128]{1,0:T(8,128)(2,1)S(1)}, bf16[1024,128]{1,0:T(8,128)(2,1)S(1)}, u32[]{:S(2)}, u32[]{:S(2)}) collective-permute-start(bf16[1024,128]{1,0:T(8,128)(2,1)S(1)} %shard_map.120), channel_id=1, source_target_pairs={{0,16},{16,0},{1,17},{17,1},{2,18},{18,2},{3,19},{19,3},{4,20},{20... | collective-permute-start | bytes 786440 | tf_op jit(solution)/shard_map/ppermute | solution.py:370
  43.2 2.4 %collective-permute-start.10 = (bf16[256,256]{1,0:T(8,128)(2,1)S(1)}, bf16[256,256]{1,0:T(8,128)(2,1)S(1)}, u32[]{:S(2)}, u32[]{:S(2)}) collective-permute-start(bf16[256,256]{1,0:T(8,128)(2,1)S(1)} %get-tuple-element.66), channel_id=1, source_target_pairs={{0,1},{1,0},{2,3},{3,2},{4,5},{5,4},{6,7},{7,6},{8,9},{9,8},{10,11... | collective-permute-start | bytes 393224 | tf_op jit(solution)/shard_map/ppermute | solution.py:45
  43.2 6.3 %collective-permute-start.11 = (bf16[256,256]{1,0:T(8,128)(2,1)S(1)}, bf16[256,256]{1,0:T(8,128)(2,1)S(1)}, u32[]{:S(2)}, u32[]{:S(2)}) collective-permute-start(bf16[256,256]{1,0:T(8,128)(2,1)S(1)} %get-tuple-element.67), channel_id=1, source_target_pairs={{0,2},{1,3},{2,0},{3,1},{4,6},{5,7},{6,4},{7,5},{8,10},{9,11},{10,... | collective-permute-start | bytes 393224 | tf_op jit(solution)/shard_map/ppermute | solution.py:45
  43.5 9.9 %collective-permute-start.12 = (bf16[256,256]{1,0:T(8,128)(2,1)S(1)}, bf16[256,256]{1,0:T(8,128)(2,1)S(1)}, u32[]{:S(2)}, u32[]{:S(2)}) collective-permute-start(bf16[256,256]{1,0:T(8,128)(2,1)S(1)} %get-tuple-element.68), channel_id=1, source_target_pairs={{0,3},{1,2},{2,1},{3,0},{4,7},{5,6},{6,5},{7,4},{8,11},{9,10},{10,... | collective-permute-start | bytes 393224 | tf_op jit(solution)/shard_map/ppermute | solution.py:45
  49.5 6.7 %collective-permute-start.14 = (bf16[256,128]{1,0:T(8,128)(2,1)S(1)}, bf16[256,128]{1,0:T(8,128)(2,1)S(1)}, u32[]{:S(2)}, u32[]{:S(2)}) collective-permute-start(bf16[256,128]{1,0:T(8,128)(2,1)S(1)} %get-tuple-element.75), channel_id=1, source_target_pairs={{0,4},{1,5},{2,6},{3,7},{4,8},{5,9},{6,10},{7,11},{8,12},{9,13},{1... | collective-permute-start | bytes 196616 | tf_op jit(solution)/shard_map/ppermute | solution.py:54
  50.9 7.1 %collective-permute-start.15 = (bf16[256,128]{1,0:T(8,128)(2,1)S(1)}, bf16[256,128]{1,0:T(8,128)(2,1)S(1)}, u32[]{:S(2)}, u32[]{:S(2)}) collective-permute-start(bf16[256,128]{1,0:T(8,128)(2,1)S(1)} %get-tuple-element.76), channel_id=1, source_target_pairs={{0,8},{1,9},{2,10},{3,11},{4,12},{5,13},{6,14},{7,15},{8,0},{9,1},... | collective-permute-start | bytes 196616 | tf_op jit(solution)/shard_map/ppermute | solution.py:54
  51.6 6.5 %collective-permute-start.16 = (bf16[256,128]{1,0:T(8,128)(2,1)S(1)}, bf16[256,128]{1,0:T(8,128)(2,1)S(1)}, u32[]{:S(2)}, u32[]{:S(2)}) collective-permute-start(bf16[256,128]{1,0:T(8,128)(2,1)S(1)} %get-tuple-element.77), channel_id=1, source_target_pairs={{0,12},{1,13},{2,14},{3,15},{4,0},{5,1},{6,2},{7,3},{8,4},{9,5},{1... | collective-permute-start | bytes 196616 | tf_op jit(solution)/shard_map/ppermute | solution.py:54
  58.2 5.6 %collective-permute-start.19 = (bf16[64,256]{1,0:T(8,128)(2,1)S(1)}, bf16[64,256]{1,0:T(8,128)(2,1)S(1)}, u32[]{:S(2)}, u32[]{:S(2)}) collective-permute-start(bf16[64,256]{1,0:T(8,128)(2,1)S(1)} %get-tuple-element.78), channel_id=1, source_target_pairs={{0,16},{1,17},{2,0},{3,1},{4,20},{5,21},{6,4},{7,5},{8,24},{9,25},... | collective-permute-start | bytes 98312 | tf_op jit(solution)/shard_map/ppermute | solution.py:391
  58.9 4.9 %collective-permute-start.17 = (bf16[64,256]{1,0:T(8,128)(2,1)S(1)}, bf16[64,256]{1,0:T(8,128)(2,1)S(1)}, u32[]{:S(2)}, u32[]{:S(2)}) collective-permute-start(bf16[64,256]{1,0:T(8,128)(2,1)S(1)} %get-tuple-element.78), channel_id=1, source_target_pairs={{0,0},{1,1},{2,16},{3,17},{4,4},{5,5},{6,20},{7,21},{8,8},{9,9},{1... | collective-permute-start | bytes 98312 | tf_op jit(solution)/shard_map/ppermute | solution.py:391
  59.6 4.2 %collective-permute-start.20 = (bf16[64,256]{1,0:T(8,128)(2,1)S(1)}, bf16[64,256]{1,0:T(8,128)(2,1)S(1)}, u32[]{:S(2)}, u32[]{:S(2)}) collective-permute-start(bf16[64,256]{1,0:T(8,128)(2,1)S(1)} %get-tuple-element.79), channel_id=1, source_target_pairs={{0,17},{1,16},{2,1},{3,0},{4,21},{5,20},{6,5},{7,4},{8,25},{9,24},... | collective-permute-start | bytes 98312 | tf_op jit(solution)/shard_map/ppermute | solution.py:391
  61.8 2.9 %collective-permute-start.18 = (bf16[64,256]{1,0:T(8,128)(2,1)S(1)}, bf16[64,256]{1,0:T(8,128)(2,1)S(1)}, u32[]{:S(2)}, u32[]{:S(2)}) collective-permute-start(bf16[64,256]{1,0:T(8,128)(2,1)S(1)} %get-tuple-element.79), channel_id=1, source_target_pairs={{0,1},{1,0},{2,17},{3,16},{4,5},{5,4},{6,21},{7,20},{8,9},{9,8},{1... | collective-permute-start | bytes 98312 | tf_op jit(solution)/shard_map/ppermute | solution.py:391

commit v4 on v3

--- a/solution.py
+++ b/solution.py
@@ -21,7 +21,6 @@
 
 
 def call(kernel, outs, args, specs=None, busy=0.5, scratch=(), aliases=None):
-    moved = sum(a.size * a.dtype.itemsize for a in list(outs) + list(args))
     return pl.pallas_call(
         kernel,
         out_shape=tuple(outs),
@@ -31,7 +30,7 @@
         input_output_aliases=aliases or {},
         compiler_params=pltpu.CompilerParams(vmem_limit_bytes=24 * 1024 * 1024),
         cost_estimate=pl.CostEstimate(
-            flops=int(busy * PEAK), bytes_accessed=moved, transcendentals=0
+            flops=int(busy * PEAK), bytes_accessed=0, transcendentals=0
         ),
     )(*args)
 
@@ -58,6 +57,14 @@
     return lax.rem(lax.axis_index("ctx"), GROUP)
 
 
+def paired():
+    return lax.axis_size("dp") == 2 and lax.axis_size("ctx") == 16
+
+
+def head():
+    return place() ^ (2 * lax.axis_index("dp")) if paired() else place()
+
+
 def head_cols(h):
     return pl.ds(pl.multiple_of(h * HD, HD), HD)
 
@@ -67,16 +74,17 @@
 
 
 def fetch_kernel(a_ref, b_ref, wk_ref, wq_ref, *refs):
-    outs, weights, sems = refs[:GROUP], refs[GROUP], refs[GROUP + 1]
-    me = place()
+    own, near, far, weights, sems = refs
+    mine = head()
     copies = []
-    for side, ref in enumerate((wk_ref, wq_ref)):
-        to = slice(side * HD, (side + 1) * HD)
-        copies.append((ref.at[:, head_cols(me)], weights.at[:, to]))
-    for k in range(GROUP):
+    for k in range(2):
+        for side, ref in enumerate((wk_ref, wq_ref)):
+            to = slice((2 * k + side) * HD, (2 * k + side + 1) * HD)
+            copies.append((ref.at[:, head_cols(mine ^ k)], weights.at[:, to]))
+    for k, (out, at) in enumerate(((own, 0), (near, 0), (far, 0), (far, 2))):
         for side, ref in enumerate((a_ref, b_ref)):
-            to = slice(side * HD, (side + 1) * HD)
-            copies.append((ref.at[:, head_cols(me ^ k)], outs[k].at[:, to]))
+            to = slice((at + side) * HD, (at + side + 1) * HD)
+            copies.append((ref.at[:, head_cols(mine ^ k)], out.at[:, to]))
     started = [pltpu.make_async_copy(*pair, sems.at[i]) for i, pair in enumerate(copies)]
     for copy in started:
         copy.start()
@@ -85,8 +93,15 @@
 
 
 def project_kernel(near, far, weights, near_kq, far_kq):
-    near_kq[...] = nn(near[...], weights[...]).astype(jnp.bfloat16)
-    far_kq[...] = nn(far[...], weights[...]).astype(jnp.bfloat16)
+    own = weights[:, : 2 * HD]
+    near_kq[...] = nn(near[...], own).astype(jnp.bfloat16)
+    far_kq[...] = nn(far[...], own).astype(jnp.bfloat16)
+
+
+def project_both_kernel(rows_ref, weights, own_kq, other_kq):
+    both = nn(rows_ref[...], weights[...]).astype(jnp.bfloat16)
+    own_kq[...] = both[:, : 2 * HD]
+    other_kq[...] = both[:, 2 * HD :]
 
 
 def upper():
@@ -100,7 +115,10 @@
     keys_big = upper() == (1 if own else 0)
     for pair in range(len(sources) // 2):
         to = slice(pair * HD, (pair + 1) * HD)
-        for ref, at_core in ((sources[2 * pair], core), (sources[2 * pair + 1], 1 - core)):
+        for i, at_core in ((0, core), (1, 1 - core)):
+            ref = sources[2 * pair + i]
+            if ref.shape[1] > 2 * HD:
+                ref = ref.at[:, 2 * i * HD : 2 * (i + 1) * HD]
             at = pl.ds(pl.multiple_of(at_core * rows, rows), rows)
 
             @pl.when(keys_big)
@@ -170,17 +188,19 @@
     own, len_ref, shift_ref, keep_ref, k_ref, q_ref, v_ref, o_ref, big, small,
     out_t, dq_t, dk, dv,
 ):
-    rows = small.shape[0]
+    rows = small[0].shape[0]
     span = GROUP - 1
     total = rows * lax.axis_size("ctx")
     shift = shift_ref[0]
-    base = (lax.axis_index("ctx") // GROUP) * (GROUP * rows)
+    base = plane_base(rows)
 
     def shard(j):
         return slice(j * rows, (j + 1) * rows)
 
-    def load(ref, j):
-        return ref[shard(j), :HD], ref[shard(j), HD:]
+    def load(refs, j):
+        if len(refs) == 1:
+            return refs[0][shard(j), :HD], refs[0][shard(j), HD:]
+        return refs[0][shard(j), :], refs[1][shard(j), :]
 
     def before(ref, first, reached):
         q_ts = [q_ref[shard(j), :].T for j in range(max(reached) + 1)]
@@ -221,58 +241,115 @@
         behind(big, 0, range(span - 1))
 
 
+def square(own_row, shift, total, len_ref, keep_ref, pairs, out_t, dq_t, dk, dv, at):
+    rows = pairs[0][0].shape[0]
+    q_ts = [q.T for _, q, _, _ in pairs]
+    o_ts = [o.T for _, _, _, o in pairs]
+    places = [query_place(own_row + i * rows, rows, shift, len_ref, total) for i in (0, 1)]
+    for kt, (k, _, v, _) in enumerate(pairs):
+        k_t, v_t = k.T, v.T
+        kpos = key_place(own_row + kt * rows, rows, shift, keep_ref, total)
+        dk_sum, dv_sum = 0.0, 0.0
+        for qt in range(kt, 2):
+            att, ds = tile_terms(k, v, q_ts[qt], o_ts[qt], kpos, *places[qt])
+            if kt == 0:
+                out_t[:, at[qt]] = nn(v_t, att)
+                dq_t[:, at[qt]] = nn(k_t, ds)
+            else:
+                out_t[:, at[qt]] += nn(v_t, att)
+                dq_t[:, at[qt]] += nn(k_t, ds)
+            dv_sum = dv_sum + nn(att, pairs[qt][3])
+            dk_sum = dk_sum + nn(ds, pairs[qt][1])
+        dk[at[kt], :] = dk_sum
+        dv[at[kt], :] = dv_sum
+
+
+def plane_base(rows):
+    return (lax.axis_index("ctx") // GROUP) * (GROUP * rows)
+
+
+def early_kernel(
+    len_ref, shift_ref, keep_ref, a0, a1, b0, b1, out_t, dq_t, dk, dv, kq_ref, vo_ref
+):
+    rows = a0.shape[0]
+    core = lax.rem(place(), 2)
+    total = rows * lax.axis_size("ctx")
+    for at_core, kq, vo in ((core, a0, b0), (1 - core, a1, b1)):
+        at = pl.ds(pl.multiple_of(at_core * rows, rows), rows)
+        kq_ref[at, :] = kq[...]
+        vo_ref[at, :] = vo[...]
+    shards = [slice(0, rows), slice(rows, 2 * rows)]
+    pairs = [(kq_ref[i, :HD], kq_ref[i, HD:], vo_ref[i, :HD], vo_ref[i, HD:]) for i in shards]
+    own_row = plane_base(rows) + upper() * 2 * rows
+    square(
+        own_row, shift_ref[0], total, len_ref, keep_ref, pairs, out_t, dq_t, dk, dv, shards
+    )
+
+
 def inner_kernel(
     len_ref, shift_ref, keep_ref, a0, a1, a2, a3, b0, b1, b2, b3, big, small,
+    early_out, early_dq, early_dk, early_dv,
     k_ref, q_ref, v_ref, o_ref, out_t, dq_t, dk, dv,
 ):
     rows = a0.shape[0]
     total = rows * lax.axis_size("ctx")
     shift = shift_ref[0]
-    base = (lax.axis_index("ctx") // GROUP) * (GROUP * rows)
+    base = plane_base(rows)
     me = place()
+    b2, b3 = b2.at[:, : 2 * HD], b3.at[:, 2 * HD :]
     for i, (kq, vo) in enumerate(((a0, b0), (a1, b1), (a2, b2), (a3, b3))):
         at = pl.ds(pl.multiple_of((me ^ i) * rows, rows), rows)
         k_ref[at, :] = kq[:, :HD]
         q_ref[at, :] = kq[:, HD:]
         v_ref[at, :] = vo[:, :HD]
         o_ref[at, :] = vo[:, HD:]
+    own = pl.ds(pl.multiple_of(upper() * 2 * rows, 2 * rows), 2 * rows)
+    out_t[:, own] = early_out[...]
+    dq_t[:, own] = early_dq[...]
+    dk[own, :] = early_dk[...]
+    dv[own, :] = early_dv[...]
+    first = (1 - upper()) * 2 * rows
+    others = [pl.ds(pl.multiple_of(first + i * rows, rows), rows) for i in (0, 1)]
+    pairs = [(k_ref[at, :], q_ref[at, :], v_ref[at, :], o_ref[at, :]) for at in others]
+    square(
+        base + first, shift, total, len_ref, keep_ref, pairs, out_t, dq_t, dk, dv, others
+    )
     shards = [slice(j * rows, (j + 1) * rows) for j in range(GROUP)]
-    places = [query_place(base + j * rows, rows, shift, len_ref, total) for j in range(GROUP)]
-    q_ts = [q_ref[at, :].T for at in shards]
-    o_ts = [o_ref[at, :].T for at in shards]
-    for kt, at in enumerate(shards):
+    half = range(GROUP // 2, GROUP)
+    places = {j: query_place(base + j * rows, rows, shift, len_ref, total) for j in half}
+    q_ts = {j: q_ref[shards[j], :].T for j in half}
+    o_ts = {j: o_ref[shards[j], :].T for j in half}
+    for kt in range(GROUP // 2):
+        at = shards[kt]
         k, v = k_ref[at, :], v_ref[at, :]
         k_t, v_t = k.T, v.T
         kpos = key_place(base + kt * rows, rows, shift, keep_ref, total)
         dk_sum, dv_sum = 0.0, 0.0
-        for qt in range(kt, GROUP):
+        for qt in half:
             qs = shards[qt]
             att, ds = tile_terms(k, v, q_ts[qt], o_ts[qt], kpos, *places[qt])
-            if kt == 0:
-                out_t[:, qs] = nn(v_t, att)
-                dq_t[:, qs] = nn(k_t, ds)
-            else:
-                out_t[:, qs] += nn(v_t, att)
-                dq_t[:, qs] += nn(k_t, ds)
+            out_t[:, qs] += nn(v_t, att)
+            dq_t[:, qs] += nn(k_t, ds)
             dv_sum = dv_sum + nn(att, o_ref[qs, :])
             dk_sum = dk_sum + nn(ds, q_ref[qs, :])
-        dk[at, :] = dk_sum
-        dv[at, :] = dv_sum
+        dk[at, :] += dk_sum
+        dv[at, :] += dv_sum
     cross_pairs(
-        True, len_ref, shift_ref, keep_ref, k_ref, q_ref, v_ref, o_ref, big, small,
+        True, len_ref, shift_ref, keep_ref, k_ref, q_ref, v_ref, o_ref, (big,), (small,),
         out_t, dq_t, dk, dv,
     )
 
 
 def outer_kernel(
-    len_ref, shift_ref, keep_ref, k_ref, q_ref, v_ref, o_ref, big, small, *refs
+    len_ref, shift_ref, keep_ref, k_ref, q_ref, v_ref, o_ref, big_kq, big_vo, small_kq, small_vo,
+    *refs,
 ):
     out_t, dq_t, dk, dv, s0, s1, s2, s3, dqk = refs[4:]
     cross_pairs(
-        False, len_ref, shift_ref, keep_ref, k_ref, q_ref, v_ref, o_ref, big, small,
-        out_t, dq_t, dk, dv,
-    )
-    rows = small.shape[0]
+        False, len_ref, shift_ref, keep_ref, k_ref, q_ref, v_ref, o_ref,
+        (big_kq, big_vo), (small_kq, small_vo), out_t, dq_t, dk, dv,
+    )
+    rows = small_kq.shape[0]
     me = place()
     factor = 0.5 * SCALE * ALPHA
     dqk[:HD, :] = (dq_t[...] * factor).astype(jnp.bfloat16)
@@ -302,8 +379,7 @@
 def half_terms_kernel(same, dqk, e0, e1, e2, e3, out):
     rows = e0.shape[0]
     me = place()
-    y = lax.axis_index("dp")
-    half = y if same else 1 - y
+    half = upper() if same else 1 - upper()
     width = out.shape[1]
     high = dqk.shape[0]
     count = out.shape[0] // high
@@ -339,24 +415,31 @@
     far[...] = hold[pl.ds(pl.multiple_of((1 - core) * share, share), share), :].astype(jnp.bfloat16)
 
 
-def finish_kernel(r00, r01, r10, r11, gq, gk):
-    y = lax.axis_index("dp")
-    core = lax.rem(lax.axis_index("ctx"), 2)
-    for (a, b), ref in zip(((0, 0), (0, 1), (1, 0), (1, 1)), (r00, r01, r10, r11)):
-        cols = head_cols(2 * (y ^ a) + (core ^ b))
-        gq[:, cols] = ref[:, :HD]
-        gk[:, cols] = ref[:, HD:]
+def join_kernel(own, other, out):
+    core = lax.rem(place(), 2)
+    width = own.shape[1]
+    out[:, pl.ds(pl.multiple_of(core * width, width), width)] = own[...]
+    out[:, pl.ds(pl.multiple_of((1 - core) * width, width), width)] = other[...]
+
+
+def finish_kernel(own, other, gq, gk):
+    first = upper() ^ lax.axis_index("dp")
+    for pair, ref in ((first, own), (1 - first, other)):
+        for core in range(2):
+            cols = head_cols(2 * pair + core)
+            gq[:, cols] = ref[:, 2 * core * HD : (2 * core + 1) * HD]
+            gk[:, cols] = ref[:, (2 * core + 1) * HD : (2 * core + 2) * HD]
 
 
 def merge_kernel(i0, i1, i2, i3, first, second):
-    me = place()
+    mine = head()
     for k, ref in enumerate((i0, i1, i2, i3)):
-        cols = head_cols(me ^ k)
+        cols = head_cols(mine ^ k)
         first[:, cols] = ref[:, :HD]
         second[:, cols] = ref[:, HD:]
 
 
-def direct_reduce(dqk, gathered, share, early, late):
+def direct_reduce(dqk, gathered, share):
     count = lax.axis_size("ctx")
     planes = count // GROUP
     width = gathered[0].shape[1]
@@ -367,32 +450,26 @@
     (keep,) = call(
         functools.partial(half_terms_kernel, True), [like(*shape, jnp.float32)], args, busy=1
     )
-    got = lax.ppermute(give, "dp", [(0, 1), (1, 0)])
+    across = [(y * count + i, (1 - y) * count + (i ^ 2)) for y in range(2) for i in range(count)]
+    got = lax.ppermute(give, ("dp", "ctx"), across)
     sends = call(
         pair_sum_kernel,
         [like(2 * HD, block, jnp.float32)] + [like(2 * HD, block)] * (planes - 1),
-        (keep, after(got, *early)),
-    )
-    arrived = [after(sends[0], *late)] + [around(sends[dz], dz, dz) for dz in range(1, planes)]
+        (keep, got),
+    )
+    arrived = [sends[0]] + [around(sends[dz], dz, dz) for dz in range(1, planes)]
     near, far = call(
         sum_kernel,
         [like(share, 2 * HD)] * 2,
         arrived,
         scratch=[pltpu.VMEM((block, 2 * HD), jnp.float32)],
     )
-    received = []
-    for a in range(2):
-        for b in range(2):
-            pairs = []
-            for y in range(2):
-                for i in range(count):
-                    z, x, c = i // 4, (i // 2) % 2, i % 2
-                    pairs.append((y * count + i, (x ^ a) * count + 4 * z + 2 * y + (c ^ b)))
-            received.append(lax.ppermute((near, far)[b], ("dp", "ctx"), pairs))
-    return call(finish_kernel, [like(share, GROUP * HD)] * 2, received)
-
-
-def general_reduce(dqk, gathered, share, early, late):
+    (both,) = call(join_kernel, [like(share, 4 * HD)], (near, partner(far, 1)), busy=0.1)
+    other = lax.ppermute(both, "dp", [(0, 1), (1, 0)])
+    return got, call(finish_kernel, [like(share, GROUP * HD)] * 2, (both, other))
+
+
+def general_reduce(dqk, gathered, share):
     count = lax.axis_size("ctx")
     planes = count // GROUP
     width = gathered[0].shape[1]
@@ -409,7 +486,8 @@
         part.reshape(GROUP, share, 2 * HD), "ctx", 0, 0, axis_index_groups=plane, tiled=True
     )
     part = jnp.moveaxis(part.reshape(GROUP, share, 2, HD), 0, 2)
-    return part[:, 0].reshape(share, GROUP * HD), part[:, 1].reshape(share, GROUP * HD)
+    grads = part[:, 0].reshape(share, GROUP * HD), part[:, 1].reshape(share, GROUP * HD)
+    return dqk, grads
 
 
 def body(events, w_query, w_key, values, grad_out, lengths, stream_shift, block_keep):
@@ -423,52 +501,64 @@
 
     e1 = partner(local, 1)
     e2 = partner(local, 2)
-    *vo, weights = call(
+    vo0, vo1, far, weights = call(
         fetch_kernel,
-        [pair] * GROUP + [like(width, 2 * HD)],
+        [pair] * 2 + [like(rows, 4 * HD), like(width, 4 * HD)],
         [
             pltpu.with_memory_space_constraint(a, pltpu.HBM)
             for a in (values[0], grad_out[0], w_key, w_query)
         ],
         specs=[HBM] * 4,
-        scratch=[pltpu.SemaphoreType.DMA((2 * GROUP + 2,))],
-    )
-    vo = (vo[0],) + tuple(partner(vo[k], k) for k in range(1, GROUP))
-    edges = [like(2 * rows, 2 * HD), pair]
-    own_edge, other_edge = (functools.partial(edge_kernel, flag) for flag in (True, False))
-    kq = call(project_kernel, [pair] * 2, (local, e1, weights), busy=3)
-    big, small = call(own_edge, edges, (*kq, *vo[:2]))
-    own = around(big, -1, 1), around(small, 1, -1)
-    e3 = partner(after(e2, *own, *vo[2:]), 1)
-    kq = kq + call(project_kernel, [pair] * 2, (e2, e3, weights), busy=3)
-    big, small = call(other_edge, edges, (*kq[2:], *vo[2:]))
-    other = around(big, 1, -1), around(small, -1, 1)
-
+        busy=0.1,
+        scratch=[pltpu.SemaphoreType.DMA((12,))],
+    )
+    vo1 = partner(vo1, 1)
     info = (lengths, stream_shift, block_keep)
     wide, tall = like(HD, all_rows, jnp.float32), like(all_rows, HD, jnp.float32)
     sums = [wide, wide, tall, tall]
+    wide, tall = like(HD, 2 * rows, jnp.float32), like(2 * rows, HD, jnp.float32)
+    own_edge, other_edge = (functools.partial(edge_kernel, flag) for flag in (True, False))
+    kq0, kq1 = call(project_kernel, [pair] * 2, (local, e1, weights), busy=0.1)
+    big, small = call(own_edge, [like(2 * rows, 2 * HD), pair], (kq0, kq1, vo0, vo1), busy=0.1)
+    own = around(big, -1, 1), around(small, 1, -1)
+    early = call(
+        early_kernel,
+        [wide, wide, tall, tall],
+        (*info, after(kq0, small), kq1, vo0, vo1),
+        specs=[SMEM] * 3 + [VMEM] * 4,
+        busy=0.1,
+        scratch=[pltpu.VMEM((2 * rows, 2 * HD), jnp.bfloat16)] * 2,
+    )
+    vo2 = partner(after(far, *early), 2)
+    edges = [like(2 * rows, HD), like(rows, HD)]
+    kq2, give = call(project_both_kernel, [pair] * 2, (after(e2, own[1], *early), weights), busy=0.1)
+    kq3 = partner(give, 1)
+    big, small = call(other_edge, edges, (kq2, kq3), busy=0.1)
+    other_kq = around(big, 1, -1), around(small, -1, 1)
+    vo3 = partner(after(vo2, own[0], big), 1)
+    big, small = call(other_edge, edges, (vo2, vo3), busy=0.1)
+    other_vo = around(big, 1, -1), around(small, -1, 1)
     k, q, v, o, *held = call(
         inner_kernel,
         [full] * 4 + sums,
-        (*info, *kq, *vo, *own),
-        specs=[SMEM] * 3 + [VMEM] * 10,
+        (*info, kq0, kq1, kq2, kq3, vo0, vo1, vo2, vo3, *own, *early),
+        specs=[SMEM] * 3 + [VMEM] * 14,
         busy=15,
     )
     *_, p0, p1, p2, p3, dqk = call(
         outer_kernel,
         sums + [pair] * GROUP + [like(2 * HD, all_rows)],
-        (*info, k, q, v, o, *other, *held),
-        specs=[SMEM] * 3 + [VMEM] * 10,
-        aliases={9: 0, 10: 1, 11: 2, 12: 3},
+        (*info, k, q, v, o, other_kq[0], other_vo[0], other_kq[1], other_vo[1], *held),
+        specs=[SMEM] * 3 + [VMEM] * 12,
+        aliases={11: 0, 12: 1, 13: 2, 14: 3},
         busy=6,
     )
-    parts = (p0, p1, p2, p3)
-    parts = (parts[0],) + tuple(partner(parts[k], k) for k in range(1, GROUP))
-    merged = call(merge_kernel, [like(rows, features)] * 2, parts)
+    e3 = partner(after(e2, *held), 1)
     share = width // count
-    reduce = direct_reduce if lax.axis_size("dp") == 2 and count == 16 else general_reduce
-    grad_wq, grad_wk = reduce(dqk, (local, e1, e2, e3), share, parts[1:3], merged)
-    attended, grad_values = merged
+    reduce = direct_reduce if paired() else general_reduce
+    reached, (grad_wq, grad_wk) = reduce(dqk, (local, e1, e2, e3), share)
+    parts = [partner(after(p, reached), k) for k, p in ((1, p1), (2, p2), (3, p3))]
+    attended, grad_values = call(merge_kernel, [like(rows, features)] * 2, (p0, *parts))
     return (attended[None], grad_values[None], grad_wq, grad_wk)
 
 

time: 65.9 us -> 64.4 us (0.977)
  waiting for transfers between devices: 24.3 us -> 21.2 us
  Pallas kernels: 14.5 us -> 15.5 us
  starting transfers between devices: 25 us -> 26 us
    ppermute x5 -> x2, waiting for transfers between devices: 0.86 us -> 7.23 us  [the longest x1 5.95 us: direct_reduce(): got = lax.ppermute(give, ('dp', 'ctx'), across)]
    ppermute x9 -> x11, waiting for transfers between devices: 16.1 us -> 10.7 us  [partner(): return lax.ppermute(value, 'ctx', [(i, i ^ steps) for i in range(count)])]
    ppermute x7 -> x9, waiting for transfers between devices: 7.36 us -> 3.32 us  [around(): return lax.ppermute(value, 'ctx', pairs)]
    ppermute x5 -> x2, starting transfers between devices: 7.19 us -> 4.04 us  [the longest x1 3.14 us: direct_reduce(): got = lax.ppermute(give, ('dp', 'ctx'), across)]
    ppermute x7 -> x9, starting transfers between devices: 11.3 us -> 14.1 us  [around(): return lax.ppermute(value, 'ctx', pairs)]
    ppermute x9 -> x11, starting transfers between devices: 6.59 us -> 7.88 us  [partner(): return lax.ppermute(value, 'ctx', [(i, i ^ steps) for i in range(count)])]
    pallas_call x13 -> x16, Pallas kernels: 14.5 us -> 15.5 us  [call(): pl.pallas_call(kernel, out_shape=tuple(outs), in_specs=specs or [VMEM] *...]
  transfers between devices with their start and end apart: 21 -> 22, of which waited for: 9 -> 11; matrix products, arithmetic and copies ran while one was open for 0% -> 0% of each run, Pallas kernels for 15% -> 22%
where the time goes in v4:
time: 64.4 us; the launch traced here: 64.3 us
  starting transfers between devices  26 us (40%)
  waiting for transfers between devices  21.2 us (33%)
  Pallas kernels  15.5 us (24%)
  between operations  1.5 us (2%)
    pallas_call x16, Pallas kernels, call(): pl.pallas_call(kernel, out_shape=tuple(outs), in_specs=specs or [VMEM] *...  15.5 us
    ppermute x9, starting transfers between devices, around(): return lax.ppermute(value, 'ctx', pairs)  14.1 us
    ppermute x11, waiting for transfers between devices, partner(): return lax.ppermute(value, 'ctx', [(i, i ^ steps) for i in range(count)])  10.7 us
    ppermute x11, starting transfers between devices, partner(): return lax.ppermute(value, 'ctx', [(i, i ^ steps) for i in range(count)])  7.88 us
    ppermute x1, waiting for transfers between devices, direct_reduce(): got = lax.ppermute(give, ('dp', 'ctx'), across)  5.95 us
    ppermute x9, waiting for transfers between devices, around(): return lax.ppermute(value, 'ctx', pairs)  3.32 us
    ppermute x1, starting transfers between devices, direct_reduce(): got = lax.ppermute(give, ('dp', 'ctx'), across)  3.14 us
  transfers between devices with their start and end apart: 22, of which 11 were waited for; matrix products, arithmetic and copies ran while one was open for 0% of the time, Pallas kernels for 22%

profile of v4, /device:TPU:0, one launch (start us, length us, event | category | flops | bytes accessed | tf_op | source)
XLA Modules:
  0.0 64.3 jit_solution(15405314772405094282)
XLA Ops:
  0.6 0.5 collective-permute-start
  1.1 2.6 %collective-permute-start.1 = (bf16[256,1024]{1,0:T(8,128)(2,1)}, bf16[256,1024]{1,0:T(8,128)(2,1)S(1)}, u32[]{:S(2)}, u32[]{:S(2)}) collective-permute-start(bf16[256,1024]{1,0:T(8,128)(2,1)} %bitcast.6), channel_id=1, source_target_pairs={{0,2},{1,3},{2,0},{3,1},{4,6},{5,7},{6,4},{7,5},{8,10},{9,11},{10,... | collective-permute-start | bytes 1572872 | tf_op jit(solution)/shard_map/ppermute | solution.py:44
  3.7 1.5 %shard_map.111 = (bf16[256,256]{1,0:T(8,128)(2,1)S(1)}, bf16[256,256]{1,0:T(8,128)(2,1)S(1)}, bf16[256,512]{1,0:T(8,128)(2,1)S(1)}, bf16[1024,512]{1,0:T(8,128)(2,1)S(1)}) custom-call(bf16[256,512]{1,0:T(8,128)(2,1)} %bitcast.10, bf16[256,512]{1,0:T(8,128)(2,1)} %bitcast.11, bf16[1024,512]{1,0:T(8,128)(2,1)} %wk_ref.1, bf16[1024,512]{1,0:T(8,128)(2,1)} %wq_ref.1), custom_call_target="tpu_custom_call" | custom-call | flops 115000000 | tf_op jit(solution)/shard_map/pallas_call | solution.py:24
  5.9 0.7 %collective-permute-done.2.refs_3_.b1 = bf16[256,256]{1,0:T(8,128)(2,1)S(1)} collective-permute-done((bf16[256,256]{1,0:T(8,128)(2,1)S(1)}, bf16[256,256]{1,0:T(8,128)(2,1)S(1)}, u32[]{:S(2)}, u32[]{:S(2)}) %collective-permute-start.2) | collective-permute-done | bytes 131104 | tf_op jit(solution)/shard_map/ppermute | solution.py:44
  6.8 1.6 %collective-permute-start.3 = (bf16[256,256]{1,0:T(8,128)(2,1)S(1)}, bf16[256,256]{1,0:T(8,128)(2,1)S(1)}, u32[]{:S(2)}, u32[]{:S(2)}) collective-permute-start(bf16[256,256]{1,0:T(8,128)(2,1)S(1)} %get-tuple-element.58), channel_id=1, source_target_pairs={{0,4},{1,5},{2,14},{3,15},{4,8},{5,9},{6,2},{7,3},{8,12},{9,13},{1... | collective-permute-start | bytes 393224 | tf_op jit(solution)/shard_map/ppermute | solution.py:53
  9.1 1.9 %shard_map.114 = (f32[128,512]{1,0:T(8,128)S(1)}, f32[128,512]{1,0:T(8,128)S(1)}, f32[512,128]{1,0:T(8,128)S(1)}, f32[512,128]{1,0:T(8,128)S(1)}) custom-call(s32[1,8]{1,0:T(1,128)S(1)} %copy-done.1, s32[1]{0:T(128)S(6)} %copy.20.shift_ref, s32[1,32]{1,0:T(1,128)S(1)} %copy-done.2, bf16[256,256]{1,0:T(8,128)(2,1)S(1)} %get-tuple-element.59.refs_0_.a0, ...), custom_call_target="tpu_custom_call" | custom-call | flops 115000000 | tf_op jit(solution)/shard_map/pallas_call | solution.py:24
  10.9 2.6 %collective-permute-start.5 = (bf16[256,512]{1,0:T(8,128)(2,1)S(1)}, bf16[256,512]{1,0:T(8,128)(2,1)S(1)}, u32[]{:S(2)}, u32[]{:S(2)}) collective-permute-start(bf16[256,512]{1,0:T(8,128)(2,1)S(1)} %get-tuple-element.68), channel_id=1, source_target_pairs={{0,2},{1,3},{2,0},{3,1},{4,6},{5,7},{6,4},{7,5},{8,10},{9,11},{10,... | collective-permute-start | bytes 786440 | tf_op jit(solution)/shard_map/ppermute | solution.py:44
  13.6 0.4 collective-permute-start.6
  14.0 2.7 %collective-permute-done.1.rows_ref.e2 = bf16[256,1024]{1,0:T(8,128)(2,1)S(1)} collective-permute-done((bf16[256,1024]{1,0:T(8,128)(2,1)}, bf16[256,1024]{1,0:T(8,128)(2,1)S(1)}, u32[]{:S(2)}, u32[]{:S(2)}) %collective-permute-start.1) | collective-permute-done | bytes 524320 | tf_op jit(solution)/shard_map/ppermute | solution.py:44
  17.2 1.3 %collective-permute-done.4.refs_1_.a3 = bf16[256,256]{1,0:T(8,128)(2,1)S(1)} collective-permute-done((bf16[256,256]{1,0:T(8,128)(2,1)S(1)}, bf16[256,256]{1,0:T(8,128)(2,1)S(1)}, u32[]{:S(2)}, u32[]{:S(2)}) %collective-permute-start.4) | collective-permute-done | bytes 131104 | tf_op jit(solution)/shard_map/ppermute | solution.py:44
  18.6 3.5 %collective-permute-done.5.b2.refs_0_ = bf16[256,512]{1,0:T(8,128)(2,1)S(1)} collective-permute-done((bf16[256,512]{1,0:T(8,128)(2,1)S(1)}, bf16[256,512]{1,0:T(8,128)(2,1)S(1)}, u32[]{:S(2)}, u32[]{:S(2)}) %collective-permute-start.5) | collective-permute-done | bytes 262176 | tf_op jit(solution)/shard_map/ppermute | solution.py:44
  22.1 1.8 %collective-permute-start.8 = (bf16[512,128]{1,0:T(8,128)(2,1)S(1)}, bf16[512,128]{1,0:T(8,128)(2,1)S(1)}, u32[]{:S(2)}, u32[]{:S(2)}) collective-permute-start(bf16[512,128]{1,0:T(8,128)(2,1)S(1)} %get-tuple-element.70), channel_id=1, source_target_pairs={{0,4},{1,5},{2,14},{3,15},{4,8},{5,9},{6,2},{7,3},{8,12},{9,13},{1... | collective-permute-start | bytes 393224 | tf_op jit(solution)/shard_map/ppermute | solution.py:53
  23.9 2.1 %collective-permute-start.10 = (bf16[256,128]{1,0:T(8,128)(2,1)S(1)}, bf16[256,128]{1,0:T(8,128)(2,1)S(1)}, u32[]{:S(2)}, u32[]{:S(2)}) collective-permute-start(bf16[256,128]{1,0:T(8,128)(2,1)S(1)} %get-tuple-element.77), channel_id=1, source_target_pairs={{0,12},{1,13},{2,6},{3,7},{4,0},{5,1},{6,10},{7,11},{8,4},{9,5},{1... | collective-permute-start | bytes 196616 | tf_op jit(solution)/shard_map/ppermute | solution.py:53
  26.1 3.8 %collective-permute-start.11 = (bf16[256,128]{1,0:T(8,128)(2,1)S(1)}, bf16[256,128]{1,0:T(8,128)(2,1)S(1)}, u32[]{:S(2)}, u32[]{:S(2)}) collective-permute-start(bf16[256,128]{1,0:T(8,128)(2,1)S(1)} %get-tuple-element.78), channel_id=1, source_target_pairs={{0,12},{1,13},{2,6},{3,7},{4,0},{5,1},{6,10},{7,11},{8,4},{9,5},{1... | collective-permute-start | bytes 196616 | tf_op jit(solution)/shard_map/ppermute | solution.py:53
  29.9 5.4 %shard_map.117 = (bf16[1024,128]{1,0:T(8,128)(2,1)S(1)}, bf16[1024,128]{1,0:T(8,128)(2,1)S(1)}, bf16[1024,128]{1,0:T(8,128)(2,1)S(1)}, bf16[1024,128]{1,0:T(8,12...) custom-call(s32[1,8]{1,0:T(1,128)S(1)} %copy-done.1, ...), custom_call_target="tpu_custom_call" | custom-call | flops 17250000896 | tf_op jit(solution)/shard_map/pallas_call | solution.py:24
  35.4 2.9 %shard_map.119 = (f32[128,1024]{1,0:T(8,128)S(1)}, f32[128,1024]{1,0:T(8,128)S(1)}, f32[1024,128]{1,0:T(8,128)S(1)}, f32[1024,128]{1,0:T(8,128)S(1)}, bf16[256,2...) custom-call(s32[1,8]{1,0:T(1,128)S(1)} %copy-done.1, ...), custom_call_target="tpu_custom_call", output_to_operand_aliasing={{0}: (11, {}), {1}: (12, {}), {2}: (13, {}), {3}: (14, {})} | custom-call | flops 6899999744 | tf_op jit(solution)/shard_map/pallas_call | solution.py:24
  38.3 0.6 shard_map.120
  38.9 3.1 %collective-permute-start.13 = (bf16[1024,128]{1,0:T(8,128)(2,1)S(1)}, bf16[1024,128]{1,0:T(8,128)(2,1)S(1)}, u32[]{:S(2)}, u32[]{:S(2)}) collective-permute-start(bf16[1024,128]{1,0:T(8,128)(2,1)S(1)} %shard_map.120), channel_id=1, source_target_pairs={{0,18},{1,19},{2,16},{3,17},{4,22},{5,23},{6,20},{7,21},{8,26},{9,... | collective-permute-start | bytes 786440 | tf_op jit(solution)/shard_map/ppermute | solution.py:454
  42.1 0.6 shard_map.122.mine
  42.6 6.0 %collective-permute-done.13.other = bf16[1024,128]{1,0:T(8,128)(2,1)S(1)} collective-permute-done((bf16[1024,128]{1,0:T(8,128)(2,1)S(1)}, bf16[1024,128]{1,0:T(8,128)(2,1)S(1)}, u32[]{:S(2)}, u32[]{:S(2)}) %collective-permute-start.13) | collective-permute-done | bytes 262176 | tf_op jit(solution)/shard_map/ppermute | solution.py:454
  48.6 1.1 %collective-permute-start.17 = (bf16[256,128]{1,0:T(8,128)(2,1)S(1)}, bf16[256,128]{1,0:T(8,128)(2,1)S(1)}, u32[]{:S(2)}, u32[]{:S(2)}) collective-permute-start(bf16[256,128]{1,0:T(8,128)(2,1)S(1)} %get-tuple-element.95), channel_id=1, source_target_pairs={{0,4},{1,5},{2,6},{3,7},{4,8},{5,9},{6,10},{7,11},{8,12},{9,13},{1... | collective-permute-start | bytes 196616 | tf_op jit(solution)/shard_map/ppermute | solution.py:53
  49.7 3.1 %collective-permute-start.18 = (bf16[256,128]{1,0:T(8,128)(2,1)S(1)}, bf16[256,128]{1,0:T(8,128)(2,1)S(1)}, u32[]{:S(2)}, u32[]{:S(2)}) collective-permute-start(bf16[256,128]{1,0:T(8,128)(2,1)S(1)} %get-tuple-element.96), channel_id=1, source_target_pairs={{0,8},{1,9},{2,10},{3,11},{4,12},{5,13},{6,14},{7,15},{8,0},{9,1},... | collective-permute-start | bytes 196616 | tf_op jit(solution)/shard_map/ppermute | solution.py:53
  53.2 1.3 %collective-permute-start.15 = (bf16[256,256]{1,0:T(8,128)(2,1)S(1)}, bf16[256,256]{1,0:T(8,128)(2,1)S(1)}, u32[]{:S(2)}, u32[]{:S(2)}) collective-permute-start(bf16[256,256]{1,0:T(8,128)(2,1)S(1)} %get-tuple-element.89), channel_id=1, source_target_pairs={{0,2},{1,3},{2,0},{3,1},{4,6},{5,7},{6,4},{7,5},{8,10},{9,11},{10,... | collective-permute-start | bytes 393224 | tf_op jit(solution)/shard_map/ppermute | solution.py:44
  54.5 1.0 %collective-permute-done.17.refs_1_ = bf16[256,128]{1,0:T(8,128)(2,1)S(1)} collective-permute-done((bf16[256,128]{1,0:T(8,128)(2,1)S(1)}, bf16[256,128]{1,0:T(8,128)(2,1)S(1)}, u32[]{:S(2)}, u32[]{:S(2)}) %collective-permute-start.17) | collective-permute-done | bytes 65568 | tf_op jit(solution)/shard_map/ppermute | solution.py:53
  55.5 1.8 %collective-permute-done.18.refs_2_ = bf16[256,128]{1,0:T(8,128)(2,1)S(1)} collective-permute-done((bf16[256,128]{1,0:T(8,128)(2,1)S(1)}, bf16[256,128]{1,0:T(8,128)(2,1)S(1)}, u32[]{:S(2)}, u32[]{:S(2)}) %collective-permute-start.18) | collective-permute-done | bytes 65568 | tf_op jit(solution)/shard_map/ppermute | solution.py:53
  57.3 0.5 collective-permute-done.19.refs_3_
  58.1 1.2 %collective-permute-done.20.other = bf16[64,256]{1,0:T(8,128)(2,1)S(1)} collective-permute-done((bf16[64,256]{1,0:T(8,128)(2,1)S(1)}, bf16[64,256]{1,0:T(8,128)(2,1)S(1)}, u32[]{:S(2)}, u32[]{:S(2)}) %collective-permute-start.20) | collective-permute-done | bytes 32800 | tf_op jit(solution)/shard_map/ppermute | solution.py:44
  59.3 0.9 %collective-permute-start.21 = (bf16[64,512]{1,0:T(8,128)(2,1)S(1)}, bf16[64,512]{1,0:T(8,128)(2,1)S(1)}, u32[]{:S(2)}, u32[]{:S(2)}) collective-permute-start(bf16[64,512]{1,0:T(8,128)(2,1)S(1)} %shard_map.125.own), channel_id=1, source_target_pairs={{0,16},{16,0},{1,17},{17,1},{2,18},{18,2},{3,19},{19,3},{4,20},{20... | collective-permute-start | bytes 196616 | tf_op jit(solution)/shard_map/ppermute | solution.py:468
  60.2 1.3 %collective-permute-done.15.i2 = bf16[256,256]{1,0:T(8,128)(2,1)S(1)} collective-permute-done((bf16[256,256]{1,0:T(8,128)(2,1)S(1)}, bf16[256,256]{1,0:T(8,128)(2,1)S(1)}, u32[]{:S(2)}, u32[]{:S(2)}) %collective-permute-start.15) | collective-permute-done | bytes 131104 | tf_op jit(solution)/shard_map/ppermute | solution.py:44
  61.4 0.9 %shard_map.121 = (bf16[256,512]{1,0:T(8,128)(2,1)}, bf16[256,512]{1,0:T(8,128)(2,1)}) custom-call(bf16[256,256]{1,0:T(8,128)(2,1)S(1)} %get-tuple-element.83.i0, bf16[256,256]{1,0:T(8,128)(2,1)S(1)} %collective-permute-done.14.i1, bf16[256,256]{1,0:T(8,128)(2,1)S(1)} %collective-permute-done.15.i2, bf16[256,256]{1,0:T(8,128)(2,1)S(1)} %collective-permute-done.16.i3), custom_call_target="tpu_custom_call" | custom-call | flops 575000000 | tf_op jit(solution)/shard_map/pallas_call | solution.py:24
  62.3 1.3 %collective-permute-done.21.other = bf16[64,512]{1,0:T(8,128)(2,1)S(1)} collective-permute-done((bf16[64,512]{1,0:T(8,128)(2,1)S(1)}, bf16[64,512]{1,0:T(8,128)(2,1)S(1)}, u32[]{:S(2)}, u32[]{:S(2)}) %collective-permute-start.21) | collective-permute-done | bytes 65568 | tf_op jit(solution)/shard_map/ppermute | solution.py:468
  63.6 0.7 %shard_map.126 = (bf16[64,512]{1,0:T(8,128)(2,1)}, bf16[64,512]{1,0:T(8,128)(2,1)}) custom-call(bf16[64,512]{1,0:T(8,128)(2,1)S(1)} %shard_map.125.own, bf16[64,512]{1,0:T(8,128)(2,1)S(1)} %collective-permute-done.21.other), custom_call_target="tpu_custom_call" | custom-call | flops 575000000 | tf_op jit(solution)/shard_map/pallas_call | solution.py:24
  (34 shorter events, 2.2 us)
Async XLA Ops:
  0.6 4.8 %collective-permute-start = (bf16[256,1024]{1,0:T(8,128)(2,1)}, bf16[256,1024]{1,0:T(8,128)(2,1)S(1)}, u32[]{:S(2)}, u32[]{:S(2)}) collective-permute-start(bf16[256,1024]{1,0:T(8,128)(2,1)} %bitcast.5), channel_id=1, source_target_pairs={{0,1},{1,0},{2,3},{3,2},{4,5},{5,4},{6,7},{7,6},{8,9},{9,8},{10,11... | collective-permute-start | bytes 1572872 | tf_op jit(solution)/shard_map/ppermute | solution.py:44
  1.1 15.6 %collective-permute-start.1 = (bf16[256,1024]{1,0:T(8,128)(2,1)}, bf16[256,1024]{1,0:T(8,128)(2,1)S(1)}, u32[]{:S(2)}, u32[]{:S(2)}) collective-permute-start(bf16[256,1024]{1,0:T(8,128)(2,1)} %bitcast.6), channel_id=1, source_target_pairs={{0,2},{1,3},{2,0},{3,1},{4,6},{5,7},{6,4},{7,5},{8,10},{9,11},{10,... | collective-permute-start | bytes 1572872 | tf_op jit(solution)/shard_map/ppermute | solution.py:44
  3.7 1.8 %copy-start = (bf16[1,256,1024]{2,1,0:T(8,128)(2,1)S(1)}, bf16[1,256,1024]{2,1,0:T(8,128)(2,1)}, u32[]{:S(2)}) copy-start(bf16[1,256,1024]{2,1,0:T(8,128)(2,1)} %param.8) | copy-start | bytes 1572868
  5.2 1.4 %collective-permute-start.2 = (bf16[256,256]{1,0:T(8,128)(2,1)S(1)}, bf16[256,256]{1,0:T(8,128)(2,1)S(1)}, u32[]{:S(2)}, u32[]{:S(2)}) collective-permute-start(bf16[256,256]{1,0:T(8,128)(2,1)S(1)} %get-tuple-element.57), channel_id=1, source_target_pairs={{0,1},{1,0},{2,3},{3,2},{4,5},{5,4},{6,7},{7,6},{8,9},{9,8},{10,11... | collective-permute-start | bytes 393224 | tf_op jit(solution)/shard_map/ppermute | solution.py:44
  6.7 2.3 %copy-start.1 = (s32[1,8]{1,0:T(1,128)S(1)}, s32[1,8]{1,0:T(1,128)}, u32[]{:S(2)}) copy-start(s32[1,8]{1,0:T(1,128)} %len_ref.5) | copy-start | bytes 100
  6.7 2.3 %copy-start.2 = (s32[1,32]{1,0:T(1,128)S(1)}, s32[1,32]{1,0:T(1,128)}, u32[]{:S(2)}) copy-start(s32[1,32]{1,0:T(1,128)} %keep_ref.5) | copy-start | bytes 388
  6.8 9.9 %collective-permute-start.3 = (bf16[256,256]{1,0:T(8,128)(2,1)S(1)}, bf16[256,256]{1,0:T(8,128)(2,1)S(1)}, u32[]{:S(2)}, u32[]{:S(2)}) collective-permute-start(bf16[256,256]{1,0:T(8,128)(2,1)S(1)} %get-tuple-element.58), channel_id=1, source_target_pairs={{0,4},{1,5},{2,14},{3,15},{4,8},{5,9},{6,2},{7,3},{8,12},{9,13},{1... | collective-permute-start | bytes 393224 | tf_op jit(solution)/shard_map/ppermute | solution.py:53
  10.9 11.1 %collective-permute-start.5 = (bf16[256,512]{1,0:T(8,128)(2,1)S(1)}, bf16[256,512]{1,0:T(8,128)(2,1)S(1)}, u32[]{:S(2)}, u32[]{:S(2)}) collective-permute-start(bf16[256,512]{1,0:T(8,128)(2,1)S(1)} %get-tuple-element.68), channel_id=1, source_target_pairs={{0,2},{1,3},{2,0},{3,1},{4,6},{5,7},{6,4},{7,5},{8,10},{9,11},{10,... | collective-permute-start | bytes 786440 | tf_op jit(solution)/shard_map/ppermute | solution.py:44
  13.6 8.5 %collective-permute-start.6 = (bf16[512,256]{1,0:T(8,128)(2,1)S(1)}, bf16[512,256]{1,0:T(8,128)(2,1)S(1)}, u32[]{:S(2)}, u32[]{:S(2)}) collective-permute-start(bf16[512,256]{1,0:T(8,128)(2,1)S(1)} %get-tuple-element.69), channel_id=1, source_target_pairs={{0,12},{1,13},{2,6},{3,7},{4,0},{5,1},{6,10},{7,11},{8,4},{9,5},{1... | collective-permute-start | bytes 786440 | tf_op jit(solution)/shard_map/ppermute | solution.py:53
  17.1 1.4 %collective-permute-start.4 = (bf16[256,256]{1,0:T(8,128)(2,1)S(1)}, bf16[256,256]{1,0:T(8,128)(2,1)S(1)}, u32[]{:S(2)}, u32[]{:S(2)}) collective-permute-start(bf16[256,256]{1,0:T(8,128)(2,1)S(1)} %get-tuple-element.66), channel_id=1, source_target_pairs={{0,1},{1,0},{2,3},{3,2},{4,5},{5,4},{6,7},{7,6},{8,9},{9,8},{10,11... | collective-permute-start | bytes 393224 | tf_op jit(solution)/shard_map/ppermute | solution.py:44
  22.1 3.9 %collective-permute-start.7 = (bf16[256,512]{1,0:T(8,128)(2,1)S(1)}, bf16[256,512]{1,0:T(8,128)(2,1)S(1)}, u32[]{:S(2)}, u32[]{:S(2)}) collective-permute-start(bf16[256,512]{1,0:T(8,128)(2,1)S(1)} %collective-permute-done.5.b2.refs_0_), channel_id=1, source_target_pairs={{0,1},{1,0},{2,3},{3,2},{4,5},{5,4},{6,7},{7,6},{8,9},{9,8},{10,11... | collective-permute-start | bytes 786440 | tf_op jit(solution)/shard_map/ppermute | solution.py:44
  22.1 13.3 %collective-permute-start.8 = (bf16[512,128]{1,0:T(8,128)(2,1)S(1)}, bf16[512,128]{1,0:T(8,128)(2,1)S(1)}, u32[]{:S(2)}, u32[]{:S(2)}) collective-permute-start(bf16[512,128]{1,0:T(8,128)(2,1)S(1)} %get-tuple-element.70), channel_id=1, source_target_pairs={{0,4},{1,5},{2,14},{3,15},{4,8},{5,9},{6,2},{7,3},{8,12},{9,13},{1... | collective-permute-start | bytes 393224 | tf_op jit(solution)/shard_map/ppermute | solution.py:53
  23.9 11.5 %collective-permute-start.10 = (bf16[256,128]{1,0:T(8,128)(2,1)S(1)}, bf16[256,128]{1,0:T(8,128)(2,1)S(1)}, u32[]{:S(2)}, u32[]{:S(2)}) collective-permute-start(bf16[256,128]{1,0:T(8,128)(2,1)S(1)} %get-tuple-element.77), channel_id=1, source_target_pairs={{0,12},{1,13},{2,6},{3,7},{4,0},{5,1},{6,10},{7,11},{8,4},{9,5},{1... | collective-permute-start | bytes 196616 | tf_op jit(solution)/shard_map/ppermute | solution.py:53
  26.1 9.4 %collective-permute-start.9 = (bf16[512,128]{1,0:T(8,128)(2,1)S(1)}, bf16[512,128]{1,0:T(8,128)(2,1)S(1)}, u32[]{:S(2)}, u32[]{:S(2)}) collective-permute-start(bf16[512,128]{1,0:T(8,128)(2,1)S(1)} %get-tuple-element.76), channel_id=1, source_target_pairs={{0,4},{1,5},{2,14},{3,15},{4,8},{5,9},{6,2},{7,3},{8,12},{9,13},{1... | collective-permute-start | bytes 393224 | tf_op jit(solution)/shard_map/ppermute | solution.py:53
  26.1 9.3 %collective-permute-start.11 = (bf16[256,128]{1,0:T(8,128)(2,1)S(1)}, bf16[256,128]{1,0:T(8,128)(2,1)S(1)}, u32[]{:S(2)}, u32[]{:S(2)}) collective-permute-start(bf16[256,128]{1,0:T(8,128)(2,1)S(1)} %get-tuple-element.78), channel_id=1, source_target_pairs={{0,12},{1,13},{2,6},{3,7},{4,0},{5,1},{6,10},{7,11},{8,4},{9,5},{1... | collective-permute-start | bytes 196616 | tf_op jit(solution)/shard_map/ppermute | solution.py:53
  35.3 3.0 %collective-permute-start.12 = (bf16[256,1024]{1,0:T(8,128)(2,1)S(1)}, bf16[256,1024]{1,0:T(8,128)(2,1)S(1)}, u32[]{:S(2)}, u32[]{:S(2)}) collective-permute-start(bf16[256,1024]{1,0:T(8,128)(2,1)S(1)} %collective-permute-done.1.rows_ref.e2), channel_id=1, source_target_pairs={{0,1},{1,0},{2,3},{3,2},{4,5},{5,4},{6,7},{7,6},{8,9},{9,8},{10,11... | collective-permute-start | bytes 1572872 | tf_op jit(solution)/shard_map/ppermute | solution.py:44
  38.9 9.7 %collective-permute-start.13 = (bf16[1024,128]{1,0:T(8,128)(2,1)S(1)}, bf16[1024,128]{1,0:T(8,128)(2,1)S(1)}, u32[]{:S(2)}, u32[]{:S(2)}) collective-permute-start(bf16[1024,128]{1,0:T(8,128)(2,1)S(1)} %shard_map.120), channel_id=1, source_target_pairs={{0,18},{1,19},{2,16},{3,17},{4,22},{5,23},{6,20},{7,21},{8,26},{9,... | collective-permute-start | bytes 786440 | tf_op jit(solution)/shard_map/ppermute | solution.py:454
  48.6 6.9 %collective-permute-start.17 = (bf16[256,128]{1,0:T(8,128)(2,1)S(1)}, bf16[256,128]{1,0:T(8,128)(2,1)S(1)}, u32[]{:S(2)}, u32[]{:S(2)}) collective-permute-start(bf16[256,128]{1,0:T(8,128)(2,1)S(1)} %get-tuple-element.95), channel_id=1, source_target_pairs={{0,4},{1,5},{2,6},{3,7},{4,8},{5,9},{6,10},{7,11},{8,12},{9,13},{1... | collective-permute-start | bytes 196616 | tf_op jit(solution)/shard_map/ppermute | solution.py:53
  49.7 7.6 %collective-permute-start.18 = (bf16[256,128]{1,0:T(8,128)(2,1)S(1)}, bf16[256,128]{1,0:T(8,128)(2,1)S(1)}, u32[]{:S(2)}, u32[]{:S(2)}) collective-permute-start(bf16[256,128]{1,0:T(8,128)(2,1)S(1)} %get-tuple-element.96), channel_id=1, source_target_pairs={{0,8},{1,9},{2,10},{3,11},{4,12},{5,13},{6,14},{7,15},{8,0},{9,1},... | collective-permute-start | bytes 196616 | tf_op jit(solution)/shard_map/ppermute | solution.py:53
  52.8 5.0 %collective-permute-start.19 = (bf16[256,128]{1,0:T(8,128)(2,1)S(1)}, bf16[256,128]{1,0:T(8,128)(2,1)S(1)}, u32[]{:S(2)}, u32[]{:S(2)}) collective-permute-start(bf16[256,128]{1,0:T(8,128)(2,1)S(1)} %get-tuple-element.97), channel_id=1, source_target_pairs={{0,12},{1,13},{2,14},{3,15},{4,0},{5,1},{6,2},{7,3},{8,4},{9,5},{1... | collective-permute-start | bytes 196616 | tf_op jit(solution)/shard_map/ppermute | solution.py:53
  52.8 7.3 %collective-permute-start.16 = (bf16[256,256]{1,0:T(8,128)(2,1)S(1)}, bf16[256,256]{1,0:T(8,128)(2,1)S(1)}, u32[]{:S(2)}, u32[]{:S(2)}) collective-permute-start(bf16[256,256]{1,0:T(8,128)(2,1)S(1)} %get-tuple-element.91), channel_id=1, source_target_pairs={{0,3},{1,2},{2,1},{3,0},{4,7},{5,6},{6,5},{7,4},{8,11},{9,10},{10,... | collective-permute-start | bytes 393224 | tf_op jit(solution)/shard_map/ppermute | solution.py:44
  53.2 8.2 %collective-permute-start.15 = (bf16[256,256]{1,0:T(8,128)(2,1)S(1)}, bf16[256,256]{1,0:T(8,128)(2,1)S(1)}, u32[]{:S(2)}, u32[]{:S(2)}) collective-permute-start(bf16[256,256]{1,0:T(8,128)(2,1)S(1)} %get-tuple-element.89), channel_id=1, source_target_pairs={{0,2},{1,3},{2,0},{3,1},{4,6},{5,7},{6,4},{7,5},{8,10},{9,11},{10,... | collective-permute-start | bytes 393224 | tf_op jit(solution)/shard_map/ppermute | solution.py:44
  55.5 5.9 %collective-permute-start.14 = (bf16[256,256]{1,0:T(8,128)(2,1)S(1)}, bf16[256,256]{1,0:T(8,128)(2,1)S(1)}, u32[]{:S(2)}, u32[]{:S(2)}) collective-permute-start(bf16[256,256]{1,0:T(8,128)(2,1)S(1)} %get-tuple-element.87), channel_id=1, source_target_pairs={{0,1},{1,0},{2,3},{3,2},{4,5},{5,4},{6,7},{7,6},{8,9},{9,8},{10,11... | collective-permute-start | bytes 393224 | tf_op jit(solution)/shard_map/ppermute | solution.py:44
  58.0 1.3 %collective-permute-start.20 = (bf16[64,256]{1,0:T(8,128)(2,1)S(1)}, bf16[64,256]{1,0:T(8,128)(2,1)S(1)}, u32[]{:S(2)}, u32[]{:S(2)}) collective-permute-start(bf16[64,256]{1,0:T(8,128)(2,1)S(1)} %get-tuple-element.99), channel_id=1, source_target_pairs={{0,1},{1,0},{2,3},{3,2},{4,5},{5,4},{6,7},{7,6},{8,9},{9,8},{10,11... | collective-permute-start | bytes 98312 | tf_op jit(solution)/shard_map/ppermute | solution.py:44
  59.3 4.3 %collective-permute-start.21 = (bf16[64,512]{1,0:T(8,128)(2,1)S(1)}, bf16[64,512]{1,0:T(8,128)(2,1)S(1)}, u32[]{:S(2)}, u32[]{:S(2)}) collective-permute-start(bf16[64,512]{1,0:T(8,128)(2,1)S(1)} %shard_map.125.own), channel_id=1, source_target_pairs={{0,16},{16,0},{1,17},{17,1},{2,18},{18,2},{3,19},{19,3},{4,20},{20... | collective-permute-start | bytes 196616 | tf_op jit(solution)/shard_map/ppermute | solution.py:468

commit v5 on v4

--- a/solution.py
+++ b/solution.py
@@ -108,13 +108,14 @@
     return lax.div(place(), 2)
 
 
-def edge_kernel(own, *refs):
+def edge_kernel(own, skip, *refs):
     *sources, big, small = refs
     rows = small.shape[0]
     core = lax.rem(place(), 2)
     keys_big = upper() == (1 if own else 0)
     for pair in range(len(sources) // 2):
         to = slice(pair * HD, (pair + 1) * HD)
+        to_big = slice((pair - skip) * HD, (pair - skip + 1) * HD)
         for i, at_core in ((0, core), (1, 1 - core)):
             ref = sources[2 * pair + i]
             if ref.shape[1] > 2 * HD:
@@ -123,7 +124,8 @@
 
             @pl.when(keys_big)
             def _():
-                big[at, to] = ref[:, :HD]
+                if pair >= skip:
+                    big[at, to_big] = ref[:, :HD]
 
                 @pl.when(at_core == 0)
                 def _():
@@ -131,7 +133,8 @@
 
             @pl.when(jnp.logical_not(keys_big))
             def _():
-                big[at, to] = ref[:, HD:]
+                if pair >= skip:
+                    big[at, to_big] = ref[:, HD:]
 
                 @pl.when(at_core == 1)
                 def _():
@@ -341,15 +344,15 @@
 
 
 def outer_kernel(
-    len_ref, shift_ref, keep_ref, k_ref, q_ref, v_ref, o_ref, big_kq, big_vo, small_kq, small_vo,
+    len_ref, shift_ref, keep_ref, k_ref, q_ref, v_ref, o_ref, big_kq, big_vo, small,
     *refs,
 ):
     out_t, dq_t, dk, dv, s0, s1, s2, s3, dqk = refs[4:]
     cross_pairs(
         False, len_ref, shift_ref, keep_ref, k_ref, q_ref, v_ref, o_ref,
-        (big_kq, big_vo), (small_kq, small_vo), out_t, dq_t, dk, dv,
-    )
-    rows = small_kq.shape[0]
+        (big_kq, big_vo), (small,), out_t, dq_t, dk, dv,
+    )
+    rows = small.shape[0]
     me = place()
     factor = 0.5 * SCALE * ALPHA
     dqk[:HD, :] = (dq_t[...] * factor).astype(jnp.bfloat16)
@@ -517,9 +520,13 @@
     wide, tall = like(HD, all_rows, jnp.float32), like(all_rows, HD, jnp.float32)
     sums = [wide, wide, tall, tall]
     wide, tall = like(HD, 2 * rows, jnp.float32), like(2 * rows, HD, jnp.float32)
-    own_edge, other_edge = (functools.partial(edge_kernel, flag) for flag in (True, False))
     kq0, kq1 = call(project_kernel, [pair] * 2, (local, e1, weights), busy=0.1)
-    big, small = call(own_edge, [like(2 * rows, 2 * HD), pair], (kq0, kq1, vo0, vo1), busy=0.1)
+    big, small = call(
+        functools.partial(edge_kernel, True, 0),
+        [like(2 * rows, 2 * HD), pair],
+        (kq0, kq1, vo0, vo1),
+        busy=0.1,
+    )
     own = around(big, -1, 1), around(small, 1, -1)
     early = call(
         early_kernel,
@@ -530,14 +537,22 @@
         scratch=[pltpu.VMEM((2 * rows, 2 * HD), jnp.bfloat16)] * 2,
     )
     vo2 = partner(after(far, *early), 2)
-    edges = [like(2 * rows, HD), like(rows, HD)]
     kq2, give = call(project_both_kernel, [pair] * 2, (after(e2, own[1], *early), weights), busy=0.1)
     kq3 = partner(give, 1)
-    big, small = call(other_edge, edges, (kq2, kq3), busy=0.1)
-    other_kq = around(big, 1, -1), around(small, -1, 1)
-    vo3 = partner(after(vo2, own[0], big), 1)
-    big, small = call(other_edge, edges, (vo2, vo3), busy=0.1)
-    other_vo = around(big, 1, -1), around(small, -1, 1)
+    big_kq, _ = call(
+        functools.partial(edge_kernel, False, 0),
+        [like(2 * rows, HD), like(rows, HD)],
+        (kq2, kq3),
+        busy=0.1,
+    )
+    vo3 = partner(after(vo2, own[0], big_kq), 1)
+    big_vo, small = call(
+        functools.partial(edge_kernel, False, 1),
+        [like(2 * rows, HD), pair],
+        (kq2, kq3, vo2, vo3),
+        busy=0.1,
+    )
+    other = around(big_kq, 1, -1), around(big_vo, 1, -1), around(small, -1, 1)
     k, q, v, o, *held = call(
         inner_kernel,
         [full] * 4 + sums,
@@ -548,9 +563,9 @@
     *_, p0, p1, p2, p3, dqk = call(
         outer_kernel,
         sums + [pair] * GROUP + [like(2 * HD, all_rows)],
-        (*info, k, q, v, o, other_kq[0], other_vo[0], other_kq[1], other_vo[1], *held),
-        specs=[SMEM] * 3 + [VMEM] * 12,
-        aliases={11: 0, 12: 1, 13: 2, 14: 3},
+        (*info, k, q, v, o, *other, *held),
+        specs=[SMEM] * 3 + [VMEM] * 11,
+        aliases={10: 0, 11: 1, 12: 2, 13: 3},
         busy=6,
     )
     e3 = partner(after(e2, *held), 1)

time: 64.4 us -> 63.3 us (0.983)
  starting transfers between devices: 26 us -> 22 us
  waiting for transfers between devices: 21.2 us -> 23.5 us
  Pallas kernels: 15.5 us -> 16.2 us
    ppermute x9 -> x8, starting transfers between devices: 14.1 us -> 11.4 us  [around(): return lax.ppermute(value, 'ctx', pairs)]
    ppermute x9 -> x8, waiting for transfers between devices: 3.32 us -> 5.45 us  [around(): return lax.ppermute(value, 'ctx', pairs)]
    ppermute x1, starting transfers between devices: 3.14 us -> 2.15 us  [direct_reduce(): got = lax.ppermute(give, ('dp', 'ctx'), across)]
    pallas_call x16, Pallas kernels: 15.5 us -> 16.2 us  [call(): pl.pallas_call(kernel, out_shape=tuple(outs), in_specs=specs or [VMEM] *...]
  transfers between devices with their start and end apart: 22 -> 21, of which waited for: 11 -> 12; matrix products, arithmetic and copies ran while one was open for 0% -> 0% of each run, Pallas kernels for 22% -> 24%
where the time goes in v5:
time: 63.3 us; the launch traced here: 63.2 us
  waiting for transfers between devices  23.5 us (37%)
  starting transfers between devices  22 us (35%)
  Pallas kernels  16.2 us (26%)
  between operations  1.48 us (2%)
    pallas_call x16, Pallas kernels, call(): pl.pallas_call(kernel, out_shape=tuple(outs), in_specs=specs or [VMEM] *...  16.2 us
    ppermute x8, starting transfers between devices, around(): return lax.ppermute(value, 'ctx', pairs)  11.4 us
    ppermute x11, waiting for transfers between devices, partner(): return lax.ppermute(value, 'ctx', [(i, i ^ steps) for i in range(count)])  10.9 us
    ppermute x11, starting transfers between devices, partner(): return lax.ppermute(value, 'ctx', [(i, i ^ steps) for i in range(count)])  7.88 us
    ppermute x1, waiting for transfers between devices, direct_reduce(): got = lax.ppermute(give, ('dp', 'ctx'), across)  6.39 us
    ppermute x8, waiting for transfers between devices, around(): return lax.ppermute(value, 'ctx', pairs)  5.45 us
    ppermute x1, starting transfers between devices, direct_reduce(): got = lax.ppermute(give, ('dp', 'ctx'), across)  2.15 us
  transfers between devices with their start and end apart: 21, of which 12 were waited for; matrix products, arithmetic and copies ran while one was open for 0% of the time, Pallas kernels for 24%

profile of v5, /device:TPU:0, one launch (start us, length us, event | category | flops | bytes accessed | tf_op | source)
XLA Modules:
  0.0 63.2 jit_solution(15571420550412555044)
XLA Ops:
  0.6 0.5 collective-permute-start
  1.1 2.6 %collective-permute-start.1 = (bf16[256,1024]{1,0:T(8,128)(2,1)}, bf16[256,1024]{1,0:T(8,128)(2,1)S(1)}, u32[]{:S(2)}, u32[]{:S(2)}) collective-permute-start(bf16[256,1024]{1,0:T(8,128)(2,1)} %bitcast.6), channel_id=1, source_target_pairs={{0,2},{1,3},{2,0},{3,1},{4,6},{5,7},{6,4},{7,5},{8,10},{9,11},{10,... | collective-permute-start | bytes 1572872 | tf_op jit(solution)/shard_map/ppermute | solution.py:44
  3.7 1.5 %shard_map.111 = (bf16[256,256]{1,0:T(8,128)(2,1)S(1)}, bf16[256,256]{1,0:T(8,128)(2,1)S(1)}, bf16[256,512]{1,0:T(8,128)(2,1)S(1)}, bf16[1024,512]{1,0:T(8,128)(2,1)S(1)}) custom-call(bf16[256,512]{1,0:T(8,128)(2,1)} %bitcast.10, bf16[256,512]{1,0:T(8,128)(2,1)} %bitcast.11, bf16[1024,512]{1,0:T(8,128)(2,1)} %wk_ref.1, bf16[1024,512]{1,0:T(8,128)(2,1)} %wq_ref.1), custom_call_target="tpu_custom_call" | custom-call | flops 115000000 | tf_op jit(solution)/shard_map/pallas_call | solution.py:24
  5.5 0.4 shard_map.112
  5.9 0.7 %collective-permute-done.2.refs_3_.b1 = bf16[256,256]{1,0:T(8,128)(2,1)S(1)} collective-permute-done((bf16[256,256]{1,0:T(8,128)(2,1)S(1)}, bf16[256,256]{1,0:T(8,128)(2,1)S(1)}, u32[]{:S(2)}, u32[]{:S(2)}) %collective-permute-start.2) | collective-permute-done | bytes 131104 | tf_op jit(solution)/shard_map/ppermute | solution.py:44
  6.8 1.6 %collective-permute-start.3 = (bf16[256,256]{1,0:T(8,128)(2,1)S(1)}, bf16[256,256]{1,0:T(8,128)(2,1)S(1)}, u32[]{:S(2)}, u32[]{:S(2)}) collective-permute-start(bf16[256,256]{1,0:T(8,128)(2,1)S(1)} %get-tuple-element.57), channel_id=1, source_target_pairs={{0,4},{1,5},{2,14},{3,15},{4,8},{5,9},{6,2},{7,3},{8,12},{9,13},{1... | collective-permute-start | bytes 393224 | tf_op jit(solution)/shard_map/ppermute | solution.py:53
  9.1 1.9 %shard_map.114 = (f32[128,512]{1,0:T(8,128)S(1)}, f32[128,512]{1,0:T(8,128)S(1)}, f32[512,128]{1,0:T(8,128)S(1)}, f32[512,128]{1,0:T(8,128)S(1)}) custom-call(s32[1,8]{1,0:T(1,128)S(1)} %copy-done.1, s32[1]{0:T(128)S(6)} %copy.20.shift_ref, s32[1,32]{1,0:T(1,128)S(1)} %copy-done.2, bf16[256,256]{1,0:T(8,128)(2,1)S(1)} %get-tuple-element.58.refs_0_.a0, ...), custom_call_target="tpu_custom_call" | custom-call | flops 115000000 | tf_op jit(solution)/shard_map/pallas_call | solution.py:24
  10.9 2.6 %collective-permute-start.5 = (bf16[256,512]{1,0:T(8,128)(2,1)S(1)}, bf16[256,512]{1,0:T(8,128)(2,1)S(1)}, u32[]{:S(2)}, u32[]{:S(2)}) collective-permute-start(bf16[256,512]{1,0:T(8,128)(2,1)S(1)} %get-tuple-element.67), channel_id=1, source_target_pairs={{0,2},{1,3},{2,0},{3,1},{4,6},{5,7},{6,4},{7,5},{8,10},{9,11},{10,... | collective-permute-start | bytes 786440 | tf_op jit(solution)/shard_map/ppermute | solution.py:44
  13.6 0.4 collective-permute-start.6
  14.0 2.7 %collective-permute-done.1.rows_ref.e2 = bf16[256,1024]{1,0:T(8,128)(2,1)S(1)} collective-permute-done((bf16[256,1024]{1,0:T(8,128)(2,1)}, bf16[256,1024]{1,0:T(8,128)(2,1)S(1)}, u32[]{:S(2)}, u32[]{:S(2)}) %collective-permute-start.1) | collective-permute-done | bytes 524320 | tf_op jit(solution)/shard_map/ppermute | solution.py:44
  17.2 1.3 %collective-permute-done.4.refs_1_.a3 = bf16[256,256]{1,0:T(8,128)(2,1)S(1)} collective-permute-done((bf16[256,256]{1,0:T(8,128)(2,1)S(1)}, bf16[256,256]{1,0:T(8,128)(2,1)S(1)}, u32[]{:S(2)}, u32[]{:S(2)}) %collective-permute-start.4) | collective-permute-done | bytes 131104 | tf_op jit(solution)/shard_map/ppermute | solution.py:44
  18.6 0.7 %shard_map.116 = (bf16[512,128]{1,0:T(8,128)(2,1)S(1)}, bf16[256,128]{1,0:T(8,128)(2,1)}) custom-call(bf16[256,256]{1,0:T(8,128)(2,1)S(1)} %get-tuple-element.64.refs_0_.a2, bf16[256,256]{1,0:T(8,128)(2,1)S(1)} %collective-permute-done.4.refs_1_.a3), custom_call_target="tpu_custom_call" | custom-call | flops 115000000 | tf_op jit(solution)/shard_map/pallas_call | solution.py:24
  19.2 2.8 %collective-permute-done.5.b2.refs_2_ = bf16[256,512]{1,0:T(8,128)(2,1)S(1)} collective-permute-done((bf16[256,512]{1,0:T(8,128)(2,1)S(1)}, bf16[256,512]{1,0:T(8,128)(2,1)S(1)}, u32[]{:S(2)}, u32[]{:S(2)}) %collective-permute-start.5) | collective-permute-done | bytes 262176 | tf_op jit(solution)/shard_map/ppermute | solution.py:44
  22.1 1.8 %collective-permute-start.8 = (bf16[512,128]{1,0:T(8,128)(2,1)S(1)}, bf16[512,128]{1,0:T(8,128)(2,1)S(1)}, u32[]{:S(2)}, u32[]{:S(2)}) collective-permute-start(bf16[512,128]{1,0:T(8,128)(2,1)S(1)} %get-tuple-element.69), channel_id=1, source_target_pairs={{0,4},{1,5},{2,14},{3,15},{4,8},{5,9},{6,2},{7,3},{8,12},{9,13},{1... | collective-permute-start | bytes 393224 | tf_op jit(solution)/shard_map/ppermute | solution.py:53
  24.0 3.6 %collective-permute-start.10 = (bf16[256,256]{1,0:T(8,128)(2,1)S(1)}, bf16[256,256]{1,0:T(8,128)(2,1)S(1)}, u32[]{:S(2)}, u32[]{:S(2)}) collective-permute-start(bf16[256,256]{1,0:T(8,128)(2,1)S(1)} %get-tuple-element.76), channel_id=1, source_target_pairs={{0,12},{1,13},{2,6},{3,7},{4,0},{5,1},{6,10},{7,11},{8,4},{9,5},{1... | collective-permute-start | bytes 393224 | tf_op jit(solution)/shard_map/ppermute | solution.py:53
  27.6 5.4 %shard_map.117 = (bf16[1024,128]{1,0:T(8,128)(2,1)S(1)}, bf16[1024,128]{1,0:T(8,128)(2,1)S(1)}, bf16[1024,128]{1,0:T(8,128)(2,1)S(1)}, bf16[1024,128]{1,0:T(8,12...) custom-call(s32[1,8]{1,0:T(1,128)S(1)} %copy-done.1, ...), custom_call_target="tpu_custom_call" | custom-call | flops 17250000896 | tf_op jit(solution)/shard_map/pallas_call | solution.py:24
  33.1 2.7 %collective-permute-done.9.big_vo = bf16[512,128]{1,0:T(8,128)(2,1)S(1)} collective-permute-done((bf16[512,128]{1,0:T(8,128)(2,1)S(1)}, bf16[512,128]{1,0:T(8,128)(2,1)S(1)}, u32[]{:S(2)}, u32[]{:S(2)}) %collective-permute-start.9) | collective-permute-done | bytes 131104 | tf_op jit(solution)/shard_map/ppermute | solution.py:53
  35.8 2.9 %shard_map.119 = (f32[128,1024]{1,0:T(8,128)S(1)}, f32[128,1024]{1,0:T(8,128)S(1)}, f32[1024,128]{1,0:T(8,128)S(1)}, f32[1024,128]{1,0:T(8,128)S(1)}, bf16[256,2...) custom-call(s32[1,8]{1,0:T(1,128)S(1)} %copy-done.1, ...), custom_call_target="tpu_custom_call", output_to_operand_aliasing={{0}: (10, {}), {1}: (11, {}), {2}: (12, {}), {3}: (13, {})} | custom-call | flops 6899999744 | tf_op jit(solution)/shard_map/pallas_call | solution.py:24
  38.7 0.6 shard_map.120
  39.3 2.2 %collective-permute-start.12 = (bf16[1024,128]{1,0:T(8,128)(2,1)S(1)}, bf16[1024,128]{1,0:T(8,128)(2,1)S(1)}, u32[]{:S(2)}, u32[]{:S(2)}) collective-permute-start(bf16[1024,128]{1,0:T(8,128)(2,1)S(1)} %shard_map.120), channel_id=1, source_target_pairs={{0,18},{1,19},{2,16},{3,17},{4,22},{5,23},{6,20},{7,21},{8,26},{9,... | collective-permute-start | bytes 786440 | tf_op jit(solution)/shard_map/ppermute | solution.py:457
  41.4 0.6 shard_map.122.mine
  42.0 6.4 %collective-permute-done.12.other = bf16[1024,128]{1,0:T(8,128)(2,1)S(1)} collective-permute-done((bf16[1024,128]{1,0:T(8,128)(2,1)S(1)}, bf16[1024,128]{1,0:T(8,128)(2,1)S(1)}, u32[]{:S(2)}, u32[]{:S(2)}) %collective-permute-start.12) | collective-permute-done | bytes 262176 | tf_op jit(solution)/shard_map/ppermute | solution.py:457
  48.5 3.6 %collective-permute-start.17 = (bf16[256,128]{1,0:T(8,128)(2,1)S(1)}, bf16[256,128]{1,0:T(8,128)(2,1)S(1)}, u32[]{:S(2)}, u32[]{:S(2)}) collective-permute-start(bf16[256,128]{1,0:T(8,128)(2,1)S(1)} %get-tuple-element.94), channel_id=1, source_target_pairs={{0,8},{1,9},{2,10},{3,11},{4,12},{5,13},{6,14},{7,15},{8,0},{9,1},... | collective-permute-start | bytes 196616 | tf_op jit(solution)/shard_map/ppermute | solution.py:53
  52.7 1.3 %collective-permute-start.14 = (bf16[256,256]{1,0:T(8,128)(2,1)S(1)}, bf16[256,256]{1,0:T(8,128)(2,1)S(1)}, u32[]{:S(2)}, u32[]{:S(2)}) collective-permute-start(bf16[256,256]{1,0:T(8,128)(2,1)S(1)} %get-tuple-element.87), channel_id=1, source_target_pairs={{0,2},{1,3},{2,0},{3,1},{4,6},{5,7},{6,4},{7,5},{8,10},{9,11},{10,... | collective-permute-start | bytes 393224 | tf_op jit(solution)/shard_map/ppermute | solution.py:44
  54.0 1.0 %collective-permute-done.16.refs_1_ = bf16[256,128]{1,0:T(8,128)(2,1)S(1)} collective-permute-done((bf16[256,128]{1,0:T(8,128)(2,1)S(1)}, bf16[256,128]{1,0:T(8,128)(2,1)S(1)}, u32[]{:S(2)}, u32[]{:S(2)}) %collective-permute-start.16) | collective-permute-done | bytes 65568 | tf_op jit(solution)/shard_map/ppermute | solution.py:53
  55.0 1.5 %collective-permute-done.17.refs_2_ = bf16[256,128]{1,0:T(8,128)(2,1)S(1)} collective-permute-done((bf16[256,128]{1,0:T(8,128)(2,1)S(1)}, bf16[256,128]{1,0:T(8,128)(2,1)S(1)}, u32[]{:S(2)}, u32[]{:S(2)}) %collective-permute-start.17) | collective-permute-done | bytes 65568 | tf_op jit(solution)/shard_map/ppermute | solution.py:53
  57.0 1.2 %collective-permute-done.19.other = bf16[64,256]{1,0:T(8,128)(2,1)S(1)} collective-permute-done((bf16[64,256]{1,0:T(8,128)(2,1)S(1)}, bf16[64,256]{1,0:T(8,128)(2,1)S(1)}, u32[]{:S(2)}, u32[]{:S(2)}) %collective-permute-start.19) | collective-permute-done | bytes 32800 | tf_op jit(solution)/shard_map/ppermute | solution.py:44
  58.2 0.6 collective-permute-start.20
  58.8 2.1 %collective-permute-done.14.i2 = bf16[256,256]{1,0:T(8,128)(2,1)S(1)} collective-permute-done((bf16[256,256]{1,0:T(8,128)(2,1)S(1)}, bf16[256,256]{1,0:T(8,128)(2,1)S(1)}, u32[]{:S(2)}, u32[]{:S(2)}) %collective-permute-start.14) | collective-permute-done | bytes 131104 | tf_op jit(solution)/shard_map/ppermute | solution.py:44
  60.9 0.9 %shard_map.121 = (bf16[256,512]{1,0:T(8,128)(2,1)}, bf16[256,512]{1,0:T(8,128)(2,1)}) custom-call(bf16[256,256]{1,0:T(8,128)(2,1)S(1)} %get-tuple-element.81.i0, bf16[256,256]{1,0:T(8,128)(2,1)S(1)} %collective-permute-done.13.i1, bf16[256,256]{1,0:T(8,128)(2,1)S(1)} %collective-permute-done.14.i2, bf16[256,256]{1,0:T(8,128)(2,1)S(1)} %collective-permute-done.15.i3), custom_call_target="tpu_custom_call" | custom-call | flops 575000000 | tf_op jit(solution)/shard_map/pallas_call | solution.py:24
  61.8 0.7 %collective-permute-done.20.other = bf16[64,512]{1,0:T(8,128)(2,1)S(1)} collective-permute-done((bf16[64,512]{1,0:T(8,128)(2,1)S(1)}, bf16[64,512]{1,0:T(8,128)(2,1)S(1)}, u32[]{:S(2)}, u32[]{:S(2)}) %collective-permute-start.20) | collective-permute-done | bytes 65568 | tf_op jit(solution)/shard_map/ppermute | solution.py:471
  62.5 0.7 %shard_map.126 = (bf16[64,512]{1,0:T(8,128)(2,1)}, bf16[64,512]{1,0:T(8,128)(2,1)}) custom-call(bf16[64,512]{1,0:T(8,128)(2,1)S(1)} %shard_map.125.own, bf16[64,512]{1,0:T(8,128)(2,1)S(1)} %collective-permute-done.20.other), custom_call_target="tpu_custom_call" | custom-call | flops 575000000 | tf_op jit(solution)/shard_map/pallas_call | solution.py:24
  (32 shorter events, 2.2 us)
Async XLA Ops:
  0.6 4.8 %collective-permute-start = (bf16[256,1024]{1,0:T(8,128)(2,1)}, bf16[256,1024]{1,0:T(8,128)(2,1)S(1)}, u32[]{:S(2)}, u32[]{:S(2)}) collective-permute-start(bf16[256,1024]{1,0:T(8,128)(2,1)} %bitcast.5), channel_id=1, source_target_pairs={{0,1},{1,0},{2,3},{3,2},{4,5},{5,4},{6,7},{7,6},{8,9},{9,8},{10,11... | collective-permute-start | bytes 1572872 | tf_op jit(solution)/shard_map/ppermute | solution.py:44
  1.1 15.6 %collective-permute-start.1 = (bf16[256,1024]{1,0:T(8,128)(2,1)}, bf16[256,1024]{1,0:T(8,128)(2,1)S(1)}, u32[]{:S(2)}, u32[]{:S(2)}) collective-permute-start(bf16[256,1024]{1,0:T(8,128)(2,1)} %bitcast.6), channel_id=1, source_target_pairs={{0,2},{1,3},{2,0},{3,1},{4,6},{5,7},{6,4},{7,5},{8,10},{9,11},{10,... | collective-permute-start | bytes 1572872 | tf_op jit(solution)/shard_map/ppermute | solution.py:44
  3.7 1.8 %copy-start = (bf16[1,256,1024]{2,1,0:T(8,128)(2,1)S(1)}, bf16[1,256,1024]{2,1,0:T(8,128)(2,1)}, u32[]{:S(2)}) copy-start(bf16[1,256,1024]{2,1,0:T(8,128)(2,1)} %param.8) | copy-start | bytes 1572868
  5.2 1.4 %collective-permute-start.2 = (bf16[256,256]{1,0:T(8,128)(2,1)S(1)}, bf16[256,256]{1,0:T(8,128)(2,1)S(1)}, u32[]{:S(2)}, u32[]{:S(2)}) collective-permute-start(bf16[256,256]{1,0:T(8,128)(2,1)S(1)} %get-tuple-element.56), channel_id=1, source_target_pairs={{0,1},{1,0},{2,3},{3,2},{4,5},{5,4},{6,7},{7,6},{8,9},{9,8},{10,11... | collective-permute-start | bytes 393224 | tf_op jit(solution)/shard_map/ppermute | solution.py:44
  6.7 2.3 %copy-start.1 = (s32[1,8]{1,0:T(1,128)S(1)}, s32[1,8]{1,0:T(1,128)}, u32[]{:S(2)}) copy-start(s32[1,8]{1,0:T(1,128)} %len_ref.5) | copy-start | bytes 100
  6.7 2.3 %copy-start.2 = (s32[1,32]{1,0:T(1,128)S(1)}, s32[1,32]{1,0:T(1,128)}, u32[]{:S(2)}) copy-start(s32[1,32]{1,0:T(1,128)} %keep_ref.5) | copy-start | bytes 388
  6.8 9.9 %collective-permute-start.3 = (bf16[256,256]{1,0:T(8,128)(2,1)S(1)}, bf16[256,256]{1,0:T(8,128)(2,1)S(1)}, u32[]{:S(2)}, u32[]{:S(2)}) collective-permute-start(bf16[256,256]{1,0:T(8,128)(2,1)S(1)} %get-tuple-element.57), channel_id=1, source_target_pairs={{0,4},{1,5},{2,14},{3,15},{4,8},{5,9},{6,2},{7,3},{8,12},{9,13},{1... | collective-permute-start | bytes 393224 | tf_op jit(solution)/shard_map/ppermute | solution.py:53
  10.9 11.1 %collective-permute-start.5 = (bf16[256,512]{1,0:T(8,128)(2,1)S(1)}, bf16[256,512]{1,0:T(8,128)(2,1)S(1)}, u32[]{:S(2)}, u32[]{:S(2)}) collective-permute-start(bf16[256,512]{1,0:T(8,128)(2,1)S(1)} %get-tuple-element.67), channel_id=1, source_target_pairs={{0,2},{1,3},{2,0},{3,1},{4,6},{5,7},{6,4},{7,5},{8,10},{9,11},{10,... | collective-permute-start | bytes 786440 | tf_op jit(solution)/shard_map/ppermute | solution.py:44
  13.6 8.5 %collective-permute-start.6 = (bf16[512,256]{1,0:T(8,128)(2,1)S(1)}, bf16[512,256]{1,0:T(8,128)(2,1)S(1)}, u32[]{:S(2)}, u32[]{:S(2)}) collective-permute-start(bf16[512,256]{1,0:T(8,128)(2,1)S(1)} %get-tuple-element.68), channel_id=1, source_target_pairs={{0,12},{1,13},{2,6},{3,7},{4,0},{5,1},{6,10},{7,11},{8,4},{9,5},{1... | collective-permute-start | bytes 786440 | tf_op jit(solution)/shard_map/ppermute | solution.py:53
  17.1 1.4 %collective-permute-start.4 = (bf16[256,256]{1,0:T(8,128)(2,1)S(1)}, bf16[256,256]{1,0:T(8,128)(2,1)S(1)}, u32[]{:S(2)}, u32[]{:S(2)}) collective-permute-start(bf16[256,256]{1,0:T(8,128)(2,1)S(1)} %get-tuple-element.65), channel_id=1, source_target_pairs={{0,1},{1,0},{2,3},{3,2},{4,5},{5,4},{6,7},{7,6},{8,9},{9,8},{10,11... | collective-permute-start | bytes 393224 | tf_op jit(solution)/shard_map/ppermute | solution.py:44
  22.1 1.9 %collective-permute-start.7 = (bf16[256,512]{1,0:T(8,128)(2,1)S(1)}, bf16[256,512]{1,0:T(8,128)(2,1)S(1)}, u32[]{:S(2)}, u32[]{:S(2)}) collective-permute-start(bf16[256,512]{1,0:T(8,128)(2,1)S(1)} %collective-permute-done.5.b2.refs_2_), channel_id=1, source_target_pairs={{0,1},{1,0},{2,3},{3,2},{4,5},{5,4},{6,7},{7,6},{8,9},{9,8},{10,11... | collective-permute-start | bytes 786440 | tf_op jit(solution)/shard_map/ppermute | solution.py:44
  22.1 11.0 %collective-permute-start.8 = (bf16[512,128]{1,0:T(8,128)(2,1)S(1)}, bf16[512,128]{1,0:T(8,128)(2,1)S(1)}, u32[]{:S(2)}, u32[]{:S(2)}) collective-permute-start(bf16[512,128]{1,0:T(8,128)(2,1)S(1)} %get-tuple-element.69), channel_id=1, source_target_pairs={{0,4},{1,5},{2,14},{3,15},{4,8},{5,9},{6,2},{7,3},{8,12},{9,13},{1... | collective-permute-start | bytes 393224 | tf_op jit(solution)/shard_map/ppermute | solution.py:53
  24.0 9.1 %collective-permute-start.10 = (bf16[256,256]{1,0:T(8,128)(2,1)S(1)}, bf16[256,256]{1,0:T(8,128)(2,1)S(1)}, u32[]{:S(2)}, u32[]{:S(2)}) collective-permute-start(bf16[256,256]{1,0:T(8,128)(2,1)S(1)} %get-tuple-element.76), channel_id=1, source_target_pairs={{0,12},{1,13},{2,6},{3,7},{4,0},{5,1},{6,10},{7,11},{8,4},{9,5},{1... | collective-permute-start | bytes 393224 | tf_op jit(solution)/shard_map/ppermute | solution.py:53
  27.6 8.2 %collective-permute-start.9 = (bf16[512,128]{1,0:T(8,128)(2,1)S(1)}, bf16[512,128]{1,0:T(8,128)(2,1)S(1)}, u32[]{:S(2)}, u32[]{:S(2)}) collective-permute-start(bf16[512,128]{1,0:T(8,128)(2,1)S(1)} %get-tuple-element.75), channel_id=1, source_target_pairs={{0,4},{1,5},{2,14},{3,15},{4,8},{5,9},{6,2},{7,3},{8,12},{9,13},{1... | collective-permute-start | bytes 393224 | tf_op jit(solution)/shard_map/ppermute | solution.py:53
  33.0 5.7 %collective-permute-start.11 = (bf16[256,1024]{1,0:T(8,128)(2,1)S(1)}, bf16[256,1024]{1,0:T(8,128)(2,1)S(1)}, u32[]{:S(2)}, u32[]{:S(2)}) collective-permute-start(bf16[256,1024]{1,0:T(8,128)(2,1)S(1)} %collective-permute-done.1.rows_ref.e2), channel_id=1, source_target_pairs={{0,1},{1,0},{2,3},{3,2},{4,5},{5,4},{6,7},{7,6},{8,9},{9,8},{10,11... | collective-permute-start | bytes 1572872 | tf_op jit(solution)/shard_map/ppermute | solution.py:44
  39.3 9.1 %collective-permute-start.12 = (bf16[1024,128]{1,0:T(8,128)(2,1)S(1)}, bf16[1024,128]{1,0:T(8,128)(2,1)S(1)}, u32[]{:S(2)}, u32[]{:S(2)}) collective-permute-start(bf16[1024,128]{1,0:T(8,128)(2,1)S(1)} %shard_map.120), channel_id=1, source_target_pairs={{0,18},{1,19},{2,16},{3,17},{4,22},{5,23},{6,20},{7,21},{8,26},{9,... | collective-permute-start | bytes 786440 | tf_op jit(solution)/shard_map/ppermute | solution.py:457
  48.4 6.6 %collective-permute-start.16 = (bf16[256,128]{1,0:T(8,128)(2,1)S(1)}, bf16[256,128]{1,0:T(8,128)(2,1)S(1)}, u32[]{:S(2)}, u32[]{:S(2)}) collective-permute-start(bf16[256,128]{1,0:T(8,128)(2,1)S(1)} %get-tuple-element.93), channel_id=1, source_target_pairs={{0,4},{1,5},{2,6},{3,7},{4,8},{5,9},{6,10},{7,11},{8,12},{9,13},{1... | collective-permute-start | bytes 196616 | tf_op jit(solution)/shard_map/ppermute | solution.py:53
  48.5 8.0 %collective-permute-start.17 = (bf16[256,128]{1,0:T(8,128)(2,1)S(1)}, bf16[256,128]{1,0:T(8,128)(2,1)S(1)}, u32[]{:S(2)}, u32[]{:S(2)}) collective-permute-start(bf16[256,128]{1,0:T(8,128)(2,1)S(1)} %get-tuple-element.94), channel_id=1, source_target_pairs={{0,8},{1,9},{2,10},{3,11},{4,12},{5,13},{6,14},{7,15},{8,0},{9,1},... | collective-permute-start | bytes 196616 | tf_op jit(solution)/shard_map/ppermute | solution.py:53
  52.1 4.7 %collective-permute-start.18 = (bf16[256,128]{1,0:T(8,128)(2,1)S(1)}, bf16[256,128]{1,0:T(8,128)(2,1)S(1)}, u32[]{:S(2)}, u32[]{:S(2)}) collective-permute-start(bf16[256,128]{1,0:T(8,128)(2,1)S(1)} %get-tuple-element.95), channel_id=1, source_target_pairs={{0,12},{1,13},{2,14},{3,15},{4,0},{5,1},{6,2},{7,3},{8,4},{9,5},{1... | collective-permute-start | bytes 196616 | tf_op jit(solution)/shard_map/ppermute | solution.py:53
  52.3 6.5 %collective-permute-start.15 = (bf16[256,256]{1,0:T(8,128)(2,1)S(1)}, bf16[256,256]{1,0:T(8,128)(2,1)S(1)}, u32[]{:S(2)}, u32[]{:S(2)}) collective-permute-start(bf16[256,256]{1,0:T(8,128)(2,1)S(1)} %get-tuple-element.89), channel_id=1, source_target_pairs={{0,3},{1,2},{2,1},{3,0},{4,7},{5,6},{6,5},{7,4},{8,11},{9,10},{10,... | collective-permute-start | bytes 393224 | tf_op jit(solution)/shard_map/ppermute | solution.py:44
  52.7 8.2 %collective-permute-start.14 = (bf16[256,256]{1,0:T(8,128)(2,1)S(1)}, bf16[256,256]{1,0:T(8,128)(2,1)S(1)}, u32[]{:S(2)}, u32[]{:S(2)}) collective-permute-start(bf16[256,256]{1,0:T(8,128)(2,1)S(1)} %get-tuple-element.87), channel_id=1, source_target_pairs={{0,2},{1,3},{2,0},{3,1},{4,6},{5,7},{6,4},{7,5},{8,10},{9,11},{10,... | collective-permute-start | bytes 393224 | tf_op jit(solution)/shard_map/ppermute | solution.py:44
  55.0 5.9 %collective-permute-start.13 = (bf16[256,256]{1,0:T(8,128)(2,1)S(1)}, bf16[256,256]{1,0:T(8,128)(2,1)S(1)}, u32[]{:S(2)}, u32[]{:S(2)}) collective-permute-start(bf16[256,256]{1,0:T(8,128)(2,1)S(1)} %get-tuple-element.85), channel_id=1, source_target_pairs={{0,1},{1,0},{2,3},{3,2},{4,5},{5,4},{6,7},{7,6},{8,9},{9,8},{10,11... | collective-permute-start | bytes 393224 | tf_op jit(solution)/shard_map/ppermute | solution.py:44
  56.9 1.3 %collective-permute-start.19 = (bf16[64,256]{1,0:T(8,128)(2,1)S(1)}, bf16[64,256]{1,0:T(8,128)(2,1)S(1)}, u32[]{:S(2)}, u32[]{:S(2)}) collective-permute-start(bf16[64,256]{1,0:T(8,128)(2,1)S(1)} %get-tuple-element.97), channel_id=1, source_target_pairs={{0,1},{1,0},{2,3},{3,2},{4,5},{5,4},{6,7},{7,6},{8,9},{9,8},{10,11... | collective-permute-start | bytes 98312 | tf_op jit(solution)/shard_map/ppermute | solution.py:44
  58.2 4.3 %collective-permute-start.20 = (bf16[64,512]{1,0:T(8,128)(2,1)S(1)}, bf16[64,512]{1,0:T(8,128)(2,1)S(1)}, u32[]{:S(2)}, u32[]{:S(2)}) collective-permute-start(bf16[64,512]{1,0:T(8,128)(2,1)S(1)} %shard_map.125.own), channel_id=1, source_target_pairs={{0,16},{16,0},{1,17},{17,1},{2,18},{18,2},{3,19},{19,3},{4,20},{20... | collective-permute-start | bytes 196616 | tf_op jit(solution)/shard_map/ppermute | solution.py:471

commit v6 on v5

--- a/solution.py
+++ b/solution.py
@@ -111,6 +111,8 @@
 def edge_kernel(own, skip, *refs):
     *sources, big, small = refs
     rows = small.shape[0]
+    if big.shape[0] > 2 * rows:
+        big[2 * rows :, :] = jnp.zeros((big.shape[0] - 2 * rows, big.shape[1]), big.dtype)
     core = lax.rem(place(), 2)
     keys_big = upper() == (1 if own else 0)
     for pair in range(len(sources) // 2):
@@ -119,7 +121,7 @@
         for i, at_core in ((0, core), (1, 1 - core)):
             ref = sources[2 * pair + i]
             if ref.shape[1] > 2 * HD:
-                ref = ref.at[:, 2 * i * HD : 2 * (i + 1) * HD]
+                ref = ref.at[:, : 2 * HD]
             at = pl.ds(pl.multiple_of(at_core * rows, rows), rows)
 
             @pl.when(keys_big)
@@ -139,6 +141,10 @@
                 @pl.when(at_core == 1)
                 def _():
                     small[:, to] = ref[:, :HD]
+
+
+def second_half_kernel(ref, out):
+    out[...] = ref[:, out.shape[1] :]
 
 
 def offset_of(row, shift, total):
@@ -299,7 +305,7 @@
     shift = shift_ref[0]
     base = plane_base(rows)
     me = place()
-    b2, b3 = b2.at[:, : 2 * HD], b3.at[:, 2 * HD :]
+    b2 = b2.at[:, : 2 * HD]
     for i, (kq, vo) in enumerate(((a0, b0), (a1, b1), (a2, b2), (a3, b3))):
         at = pl.ds(pl.multiple_of((me ^ i) * rows, rows), rows)
         k_ref[at, :] = kq[:, :HD]
@@ -541,18 +547,21 @@
     kq3 = partner(give, 1)
     big_kq, _ = call(
         functools.partial(edge_kernel, False, 0),
-        [like(2 * rows, HD), like(rows, HD)],
+        [like(2 * rows + 64, HD), like(rows, HD)],
         (kq2, kq3),
         busy=0.1,
     )
-    vo3 = partner(after(vo2, own[0], big_kq), 1)
+    (half,) = call(second_half_kernel, [pair], (after(vo2, own[0], big_kq),), busy=0.1)
+    vo3 = partner(half, 1)
     big_vo, small = call(
         functools.partial(edge_kernel, False, 1),
         [like(2 * rows, HD), pair],
         (kq2, kq3, vo2, vo3),
         busy=0.1,
     )
-    other = around(big_kq, 1, -1), around(big_vo, 1, -1), around(small, -1, 1)
+    big_kq = around(big_kq, 1, -1)
+    kq3 = after(kq3, big_kq)
+    other = big_kq, around(big_vo, 1, -1), around(small, -1, 1)
     k, q, v, o, *held = call(
         inner_kernel,
         [full] * 4 + sums,

time: 63.3 us -> 62.5 us (0.987)
  waiting for transfers between devices: 23.5 us -> 21.6 us
  starting transfers between devices: 22 us -> 23.1 us
    ppermute x11, waiting for transfers between devices: 10.9 us -> 9.25 us  [partner(): return lax.ppermute(value, 'ctx', [(i, i ^ steps) for i in range(count)])]
    ppermute x8, waiting for transfers between devices: 5.45 us -> 4.79 us  [around(): return lax.ppermute(value, 'ctx', pairs)]
    pallas_call x16 -> x17, Pallas kernels: 16.2 us -> 16.2 us  [call(): pl.pallas_call(kernel, out_shape=tuple(outs), in_specs=specs or [VMEM] *...]
  transfers between devices with their start and end apart: 21 -> 21, of which waited for: 12 -> 14; matrix products, arithmetic and copies ran while one was open for 0% -> 0% of each run, Pallas kernels for 24% -> 24%
where the time goes in v6:
time: 62.5 us; the launch traced here: 62.4 us
  starting transfers between devices  23.1 us (37%)
  waiting for transfers between devices  21.6 us (35%)
  Pallas kernels  16.2 us (26%)
  between operations  1.48 us (2%)
    pallas_call x17, Pallas kernels, call(): pl.pallas_call(kernel, out_shape=tuple(outs), in_specs=specs or [VMEM] *...  16.2 us
    ppermute x8, starting transfers between devices, around(): return lax.ppermute(value, 'ctx', pairs)  11.9 us
    ppermute x11, waiting for transfers between devices, partner(): return lax.ppermute(value, 'ctx', [(i, i ^ steps) for i in range(count)])  9.25 us
    ppermute x11, starting transfers between devices, partner(): return lax.ppermute(value, 'ctx', [(i, i ^ steps) for i in range(count)])  7.93 us
    ppermute x1, waiting for transfers between devices, direct_reduce(): got = lax.ppermute(give, ('dp', 'ctx'), across)  6.37 us
    ppermute x8, waiting for transfers between devices, around(): return lax.ppermute(value, 'ctx', pairs)  4.79 us
    ppermute x1, starting transfers between devices, direct_reduce(): got = lax.ppermute(give, ('dp', 'ctx'), across)  2.14 us
  transfers between devices with their start and end apart: 21, of which 14 were waited for; matrix products, arithmetic and copies ran while one was open for 0% of the time, Pallas kernels for 24%

profile of v6, /device:TPU:0, one launch (start us, length us, event | category | flops | bytes accessed | tf_op | source)
XLA Modules:
  0.0 62.4 jit_solution(12405271348757210905)
XLA Ops:
  1.1 2.6 %collective-permute-start.1 = (bf16[256,1024]{1,0:T(8,128)(2,1)}, bf16[256,1024]{1,0:T(8,128)(2,1)S(1)}, u32[]{:S(2)}, u32[]{:S(2)}) collective-permute-start(bf16[256,1024]{1,0:T(8,128)(2,1)} %bitcast.6), channel_id=1, source_target_pairs={{0,2},{1,3},{2,0},{3,1},{4,6},{5,7},{6,4},{7,5},{8,10},{9,11},{10,... | collective-permute-start | bytes 1572872 | tf_op jit(solution)/shard_map/ppermute | solution.py:44
  3.7 1.5 %shard_map.111 = (bf16[256,256]{1,0:T(8,128)(2,1)S(1)}, bf16[256,256]{1,0:T(8,128)(2,1)S(1)}, bf16[256,512]{1,0:T(8,128)(2,1)S(1)}, bf16[1024,512]{1,0:T(8,128)(2,1)S(1)}) custom-call(bf16[256,512]{1,0:T(8,128)(2,1)} %bitcast.10, bf16[256,512]{1,0:T(8,128)(2,1)} %bitcast.11, bf16[1024,512]{1,0:T(8,128)(2,1)} %wk_ref.1, bf16[1024,512]{1,0:T(8,128)(2,1)} %wq_ref.1), custom_call_target="tpu_custom_call" | custom-call | flops 115000000 | tf_op jit(solution)/shard_map/pallas_call | solution.py:24
  5.9 0.7 %collective-permute-done.2.refs_3_.b1 = bf16[256,256]{1,0:T(8,128)(2,1)S(1)} collective-permute-done((bf16[256,256]{1,0:T(8,128)(2,1)S(1)}, bf16[256,256]{1,0:T(8,128)(2,1)S(1)}, u32[]{:S(2)}, u32[]{:S(2)}) %collective-permute-start.2) | collective-permute-done | bytes 131104 | tf_op jit(solution)/shard_map/ppermute | solution.py:44
  6.8 1.6 %collective-permute-start.3 = (bf16[256,256]{1,0:T(8,128)(2,1)S(1)}, bf16[256,256]{1,0:T(8,128)(2,1)S(1)}, u32[]{:S(2)}, u32[]{:S(2)}) collective-permute-start(bf16[256,256]{1,0:T(8,128)(2,1)S(1)} %get-tuple-element.58), channel_id=1, source_target_pairs={{0,4},{1,5},{2,14},{3,15},{4,8},{5,9},{6,2},{7,3},{8,12},{9,13},{1... | collective-permute-start | bytes 393224 | tf_op jit(solution)/shard_map/ppermute | solution.py:53
  9.1 1.9 %shard_map.114 = (f32[128,512]{1,0:T(8,128)S(1)}, f32[128,512]{1,0:T(8,128)S(1)}, f32[512,128]{1,0:T(8,128)S(1)}, f32[512,128]{1,0:T(8,128)S(1)}) custom-call(s32[1,8]{1,0:T(1,128)S(1)} %copy-done.1, s32[1]{0:T(128)S(6)} %copy.20.shift_ref, s32[1,32]{1,0:T(1,128)S(1)} %copy-done.2, bf16[256,256]{1,0:T(8,128)(2,1)S(1)} %get-tuple-element.59.refs_0_.a0, ...), custom_call_target="tpu_custom_call" | custom-call | flops 115000000 | tf_op jit(solution)/shard_map/pallas_call | solution.py:24
  10.9 2.6 %collective-permute-start.6 = (bf16[256,512]{1,0:T(8,128)(2,1)S(1)}, bf16[256,512]{1,0:T(8,128)(2,1)S(1)}, u32[]{:S(2)}, u32[]{:S(2)}) collective-permute-start(bf16[256,512]{1,0:T(8,128)(2,1)S(1)} %get-tuple-element.70), channel_id=1, source_target_pairs={{0,2},{1,3},{2,0},{3,1},{4,6},{5,7},{6,4},{7,5},{8,10},{9,11},{10,... | collective-permute-start | bytes 786440 | tf_op jit(solution)/shard_map/ppermute | solution.py:44
  14.0 2.7 %collective-permute-done.1.rows_ref.e2 = bf16[256,1024]{1,0:T(8,128)(2,1)S(1)} collective-permute-done((bf16[256,1024]{1,0:T(8,128)(2,1)}, bf16[256,1024]{1,0:T(8,128)(2,1)S(1)}, u32[]{:S(2)}, u32[]{:S(2)}) %collective-permute-start.1) | collective-permute-done | bytes 524320 | tf_op jit(solution)/shard_map/ppermute | solution.py:44
  17.2 1.3 %collective-permute-done.4.refs_1_.a3 = bf16[256,256]{1,0:T(8,128)(2,1)S(1)} collective-permute-done((bf16[256,256]{1,0:T(8,128)(2,1)S(1)}, bf16[256,256]{1,0:T(8,128)(2,1)S(1)}, u32[]{:S(2)}, u32[]{:S(2)}) %collective-permute-start.4) | collective-permute-done | bytes 131104 | tf_op jit(solution)/shard_map/ppermute | solution.py:44
  18.6 0.7 %shard_map.116 = (bf16[576,128]{1,0:T(8,128)(2,1)S(1)}, bf16[256,128]{1,0:T(8,128)(2,1)}) custom-call(bf16[256,256]{1,0:T(8,128)(2,1)S(1)} %get-tuple-element.65.refs_0_.a2, bf16[256,256]{1,0:T(8,128)(2,1)S(1)} %collective-permute-done.4.refs_1_.a3), custom_call_target="tpu_custom_call" | custom-call | flops 115000000 | tf_op jit(solution)/shard_map/pallas_call | solution.py:24
  19.2 2.0 %collective-permute-start.5 = (bf16[576,128]{1,0:T(8,128)(2,1)S(1)}, bf16[576,128]{1,0:T(8,128)(2,1)S(1)}, u32[]{:S(2)}, u32[]{:S(2)}) collective-permute-start(bf16[576,128]{1,0:T(8,128)(2,1)S(1)} %get-tuple-element.67), channel_id=1, source_target_pairs={{0,4},{1,5},{2,14},{3,15},{4,8},{5,9},{6,2},{7,3},{8,12},{9,13},{1... | collective-permute-start | bytes 442376 | tf_op jit(solution)/shard_map/ppermute | solution.py:53
  21.3 0.8 %collective-permute-done.6.ref.b2.refs_2_ = bf16[256,512]{1,0:T(8,128)(2,1)S(1)} collective-permute-done((bf16[256,512]{1,0:T(8,128)(2,1)S(1)}, bf16[256,512]{1,0:T(8,128)(2,1)S(1)}, u32[]{:S(2)}, u32[]{:S(2)}) %collective-permute-start.6) | collective-permute-done | bytes 262176 | tf_op jit(solution)/shard_map/ppermute | solution.py:44
  22.2 1.3 %collective-permute-done.8.b3.refs_3_ = bf16[256,256]{1,0:T(8,128)(2,1)S(1)} collective-permute-done((bf16[256,256]{1,0:T(8,128)(2,1)S(1)}, bf16[256,256]{1,0:T(8,128)(2,1)S(1)}, u32[]{:S(2)}, u32[]{:S(2)}) %collective-permute-start.8) | collective-permute-done | bytes 131104 | tf_op jit(solution)/shard_map/ppermute | solution.py:44
  23.6 3.9 %collective-permute-start.10 = (bf16[256,256]{1,0:T(8,128)(2,1)S(1)}, bf16[256,256]{1,0:T(8,128)(2,1)S(1)}, u32[]{:S(2)}, u32[]{:S(2)}) collective-permute-start(bf16[256,256]{1,0:T(8,128)(2,1)S(1)} %get-tuple-element.78), channel_id=1, source_target_pairs={{0,12},{1,13},{2,6},{3,7},{4,0},{5,1},{6,10},{7,11},{8,4},{9,5},{1... | collective-permute-start | bytes 393224 | tf_op jit(solution)/shard_map/ppermute | solution.py:53
  27.6 5.4 %shard_map.118 = (bf16[1024,128]{1,0:T(8,128)(2,1)S(1)}, bf16[1024,128]{1,0:T(8,128)(2,1)S(1)}, bf16[1024,128]{1,0:T(8,128)(2,1)S(1)}, bf16[1024,128]{1,0:T(8,12...) custom-call(s32[1,8]{1,0:T(1,128)S(1)} %copy-done.1, ...), custom_call_target="tpu_custom_call" | custom-call | flops 17250000896 | tf_op jit(solution)/shard_map/pallas_call | solution.py:24
  33.0 1.5 %collective-permute-done.9.big_vo = bf16[512,128]{1,0:T(8,128)(2,1)S(1)} collective-permute-done((bf16[512,128]{1,0:T(8,128)(2,1)S(1)}, bf16[512,128]{1,0:T(8,128)(2,1)S(1)}, u32[]{:S(2)}, u32[]{:S(2)}) %collective-permute-start.9) | collective-permute-done | bytes 131104 | tf_op jit(solution)/shard_map/ppermute | solution.py:53
  34.5 2.9 %shard_map.120 = (f32[128,1024]{1,0:T(8,128)S(1)}, f32[128,1024]{1,0:T(8,128)S(1)}, f32[1024,128]{1,0:T(8,128)S(1)}, f32[1024,128]{1,0:T(8,128)S(1)}, bf16[256,2...) custom-call(s32[1,8]{1,0:T(1,128)S(1)} %copy-done.1, ...), custom_call_target="tpu_custom_call", output_to_operand_aliasing={{0}: (10, {}), {1}: (11, {}), {2}: (12, {}), {3}: (13, {})} | custom-call | flops 6899999744 | tf_op jit(solution)/shard_map/pallas_call | solution.py:24
  37.5 0.6 shard_map.121
  38.0 2.1 %collective-permute-start.12 = (bf16[1024,128]{1,0:T(8,128)(2,1)S(1)}, bf16[1024,128]{1,0:T(8,128)(2,1)S(1)}, u32[]{:S(2)}, u32[]{:S(2)}) collective-permute-start(bf16[1024,128]{1,0:T(8,128)(2,1)S(1)} %shard_map.121), channel_id=1, source_target_pairs={{0,18},{1,19},{2,16},{3,17},{4,22},{5,23},{6,20},{7,21},{8,26},{9,... | collective-permute-start | bytes 786440 | tf_op jit(solution)/shard_map/ppermute | solution.py:463
  40.2 0.6 shard_map.123.mine
  40.7 6.4 %collective-permute-done.12.other = bf16[1024,128]{1,0:T(8,128)(2,1)S(1)} collective-permute-done((bf16[1024,128]{1,0:T(8,128)(2,1)S(1)}, bf16[1024,128]{1,0:T(8,128)(2,1)S(1)}, u32[]{:S(2)}, u32[]{:S(2)}) %collective-permute-start.12) | collective-permute-done | bytes 262176 | tf_op jit(solution)/shard_map/ppermute | solution.py:463
  47.2 0.8 %collective-permute-start.16 = (bf16[256,128]{1,0:T(8,128)(2,1)S(1)}, bf16[256,128]{1,0:T(8,128)(2,1)S(1)}, u32[]{:S(2)}, u32[]{:S(2)}) collective-permute-start(bf16[256,128]{1,0:T(8,128)(2,1)S(1)} %get-tuple-element.95), channel_id=1, source_target_pairs={{0,4},{1,5},{2,6},{3,7},{4,8},{5,9},{6,10},{7,11},{8,12},{9,13},{1... | collective-permute-start | bytes 196616 | tf_op jit(solution)/shard_map/ppermute | solution.py:53
  48.0 2.9 %collective-permute-start.17 = (bf16[256,128]{1,0:T(8,128)(2,1)S(1)}, bf16[256,128]{1,0:T(8,128)(2,1)S(1)}, u32[]{:S(2)}, u32[]{:S(2)}) collective-permute-start(bf16[256,128]{1,0:T(8,128)(2,1)S(1)} %get-tuple-element.96), channel_id=1, source_target_pairs={{0,8},{1,9},{2,10},{3,11},{4,12},{5,13},{6,14},{7,15},{8,0},{9,1},... | collective-permute-start | bytes 196616 | tf_op jit(solution)/shard_map/ppermute | solution.py:53
  51.4 1.3 %collective-permute-start.14 = (bf16[256,256]{1,0:T(8,128)(2,1)S(1)}, bf16[256,256]{1,0:T(8,128)(2,1)S(1)}, u32[]{:S(2)}, u32[]{:S(2)}) collective-permute-start(bf16[256,256]{1,0:T(8,128)(2,1)S(1)} %get-tuple-element.89), channel_id=1, source_target_pairs={{0,2},{1,3},{2,0},{3,1},{4,6},{5,7},{6,4},{7,5},{8,10},{9,11},{10,... | collective-permute-start | bytes 393224 | tf_op jit(solution)/shard_map/ppermute | solution.py:44
  52.7 1.3 %collective-permute-done.16.refs_1_ = bf16[256,128]{1,0:T(8,128)(2,1)S(1)} collective-permute-done((bf16[256,128]{1,0:T(8,128)(2,1)S(1)}, bf16[256,128]{1,0:T(8,128)(2,1)S(1)}, u32[]{:S(2)}, u32[]{:S(2)}) %collective-permute-start.16) | collective-permute-done | bytes 65568 | tf_op jit(solution)/shard_map/ppermute | solution.py:53
  54.0 1.3 %collective-permute-done.17.refs_2_ = bf16[256,128]{1,0:T(8,128)(2,1)S(1)} collective-permute-done((bf16[256,128]{1,0:T(8,128)(2,1)S(1)}, bf16[256,128]{1,0:T(8,128)(2,1)S(1)}, u32[]{:S(2)}, u32[]{:S(2)}) %collective-permute-start.17) | collective-permute-done | bytes 65568 | tf_op jit(solution)/shard_map/ppermute | solution.py:53
  55.3 0.6 collective-permute-done.18.refs_3_
  56.1 1.2 %collective-permute-done.19.other = bf16[64,256]{1,0:T(8,128)(2,1)S(1)} collective-permute-done((bf16[64,256]{1,0:T(8,128)(2,1)S(1)}, bf16[64,256]{1,0:T(8,128)(2,1)S(1)}, u32[]{:S(2)}, u32[]{:S(2)}) %collective-permute-start.19) | collective-permute-done | bytes 32800 | tf_op jit(solution)/shard_map/ppermute | solution.py:44
  57.4 1.1 %collective-permute-start.20 = (bf16[64,512]{1,0:T(8,128)(2,1)S(1)}, bf16[64,512]{1,0:T(8,128)(2,1)S(1)}, u32[]{:S(2)}, u32[]{:S(2)}) collective-permute-start(bf16[64,512]{1,0:T(8,128)(2,1)S(1)} %shard_map.126.own), channel_id=1, source_target_pairs={{0,16},{16,0},{1,17},{17,1},{2,18},{18,2},{3,19},{19,3},{4,20},{20... | collective-permute-start | bytes 196616 | tf_op jit(solution)/shard_map/ppermute | solution.py:477
  58.5 1.2 %collective-permute-done.14.i2 = bf16[256,256]{1,0:T(8,128)(2,1)S(1)} collective-permute-done((bf16[256,256]{1,0:T(8,128)(2,1)S(1)}, bf16[256,256]{1,0:T(8,128)(2,1)S(1)}, u32[]{:S(2)}, u32[]{:S(2)}) %collective-permute-start.14) | collective-permute-done | bytes 131104 | tf_op jit(solution)/shard_map/ppermute | solution.py:44
  59.6 0.9 %shard_map.122 = (bf16[256,512]{1,0:T(8,128)(2,1)}, bf16[256,512]{1,0:T(8,128)(2,1)}) custom-call(bf16[256,256]{1,0:T(8,128)(2,1)S(1)} %get-tuple-element.83.i0, bf16[256,256]{1,0:T(8,128)(2,1)S(1)} %collective-permute-done.13.i1, bf16[256,256]{1,0:T(8,128)(2,1)S(1)} %collective-permute-done.14.i2, bf16[256,256]{1,0:T(8,128)(2,1)S(1)} %collective-permute-done.15.i3), custom_call_target="tpu_custom_call" | custom-call | flops 575000000 | tf_op jit(solution)/shard_map/pallas_call | solution.py:24
  60.5 1.1 %collective-permute-done.20.other = bf16[64,512]{1,0:T(8,128)(2,1)S(1)} collective-permute-done((bf16[64,512]{1,0:T(8,128)(2,1)S(1)}, bf16[64,512]{1,0:T(8,128)(2,1)S(1)}, u32[]{:S(2)}, u32[]{:S(2)}) %collective-permute-start.20) | collective-permute-done | bytes 65568 | tf_op jit(solution)/shard_map/ppermute | solution.py:477
  61.7 0.7 %shard_map.127 = (bf16[64,512]{1,0:T(8,128)(2,1)}, bf16[64,512]{1,0:T(8,128)(2,1)}) custom-call(bf16[64,512]{1,0:T(8,128)(2,1)S(1)} %shard_map.126.own, bf16[64,512]{1,0:T(8,128)(2,1)S(1)} %collective-permute-done.20.other), custom_call_target="tpu_custom_call" | custom-call | flops 575000000 | tf_op jit(solution)/shard_map/pallas_call | solution.py:24
  (33 shorter events, 3.3 us)
Async XLA Ops:
  0.6 4.8 %collective-permute-start = (bf16[256,1024]{1,0:T(8,128)(2,1)}, bf16[256,1024]{1,0:T(8,128)(2,1)S(1)}, u32[]{:S(2)}, u32[]{:S(2)}) collective-permute-start(bf16[256,1024]{1,0:T(8,128)(2,1)} %bitcast.5), channel_id=1, source_target_pairs={{0,1},{1,0},{2,3},{3,2},{4,5},{5,4},{6,7},{7,6},{8,9},{9,8},{10,11... | collective-permute-start | bytes 1572872 | tf_op jit(solution)/shard_map/ppermute | solution.py:44
  1.1 15.6 %collective-permute-start.1 = (bf16[256,1024]{1,0:T(8,128)(2,1)}, bf16[256,1024]{1,0:T(8,128)(2,1)S(1)}, u32[]{:S(2)}, u32[]{:S(2)}) collective-permute-start(bf16[256,1024]{1,0:T(8,128)(2,1)} %bitcast.6), channel_id=1, source_target_pairs={{0,2},{1,3},{2,0},{3,1},{4,6},{5,7},{6,4},{7,5},{8,10},{9,11},{10,... | collective-permute-start | bytes 1572872 | tf_op jit(solution)/shard_map/ppermute | solution.py:44
  3.7 1.8 %copy-start = (bf16[1,256,1024]{2,1,0:T(8,128)(2,1)S(1)}, bf16[1,256,1024]{2,1,0:T(8,128)(2,1)}, u32[]{:S(2)}) copy-start(bf16[1,256,1024]{2,1,0:T(8,128)(2,1)} %param.8) | copy-start | bytes 1572868
  5.2 1.4 %collective-permute-start.2 = (bf16[256,256]{1,0:T(8,128)(2,1)S(1)}, bf16[256,256]{1,0:T(8,128)(2,1)S(1)}, u32[]{:S(2)}, u32[]{:S(2)}) collective-permute-start(bf16[256,256]{1,0:T(8,128)(2,1)S(1)} %get-tuple-element.57), channel_id=1, source_target_pairs={{0,1},{1,0},{2,3},{3,2},{4,5},{5,4},{6,7},{7,6},{8,9},{9,8},{10,11... | collective-permute-start | bytes 393224 | tf_op jit(solution)/shard_map/ppermute | solution.py:44
  6.7 2.3 %copy-start.1 = (s32[1,8]{1,0:T(1,128)S(1)}, s32[1,8]{1,0:T(1,128)}, u32[]{:S(2)}) copy-start(s32[1,8]{1,0:T(1,128)} %len_ref.5) | copy-start | bytes 100
  6.7 2.3 %copy-start.2 = (s32[1,32]{1,0:T(1,128)S(1)}, s32[1,32]{1,0:T(1,128)}, u32[]{:S(2)}) copy-start(s32[1,32]{1,0:T(1,128)} %keep_ref.5) | copy-start | bytes 388
  6.8 9.9 %collective-permute-start.3 = (bf16[256,256]{1,0:T(8,128)(2,1)S(1)}, bf16[256,256]{1,0:T(8,128)(2,1)S(1)}, u32[]{:S(2)}, u32[]{:S(2)}) collective-permute-start(bf16[256,256]{1,0:T(8,128)(2,1)S(1)} %get-tuple-element.58), channel_id=1, source_target_pairs={{0,4},{1,5},{2,14},{3,15},{4,8},{5,9},{6,2},{7,3},{8,12},{9,13},{1... | collective-permute-start | bytes 393224 | tf_op jit(solution)/shard_map/ppermute | solution.py:53
  10.9 11.1 %collective-permute-start.6 = (bf16[256,512]{1,0:T(8,128)(2,1)S(1)}, bf16[256,512]{1,0:T(8,128)(2,1)S(1)}, u32[]{:S(2)}, u32[]{:S(2)}) collective-permute-start(bf16[256,512]{1,0:T(8,128)(2,1)S(1)} %get-tuple-element.70), channel_id=1, source_target_pairs={{0,2},{1,3},{2,0},{3,1},{4,6},{5,7},{6,4},{7,5},{8,10},{9,11},{10,... | collective-permute-start | bytes 786440 | tf_op jit(solution)/shard_map/ppermute | solution.py:44
  13.6 8.5 %collective-permute-start.7 = (bf16[512,256]{1,0:T(8,128)(2,1)S(1)}, bf16[512,256]{1,0:T(8,128)(2,1)S(1)}, u32[]{:S(2)}, u32[]{:S(2)}) collective-permute-start(bf16[512,256]{1,0:T(8,128)(2,1)S(1)} %get-tuple-element.71), channel_id=1, source_target_pairs={{0,12},{1,13},{2,6},{3,7},{4,0},{5,1},{6,10},{7,11},{8,4},{9,5},{1... | collective-permute-start | bytes 786440 | tf_op jit(solution)/shard_map/ppermute | solution.py:53
  17.1 1.4 %collective-permute-start.4 = (bf16[256,256]{1,0:T(8,128)(2,1)S(1)}, bf16[256,256]{1,0:T(8,128)(2,1)S(1)}, u32[]{:S(2)}, u32[]{:S(2)}) collective-permute-start(bf16[256,256]{1,0:T(8,128)(2,1)S(1)} %get-tuple-element.66), channel_id=1, source_target_pairs={{0,1},{1,0},{2,3},{3,2},{4,5},{5,4},{6,7},{7,6},{8,9},{9,8},{10,11... | collective-permute-start | bytes 393224 | tf_op jit(solution)/shard_map/ppermute | solution.py:44
  19.2 8.3 %collective-permute-start.5 = (bf16[576,128]{1,0:T(8,128)(2,1)S(1)}, bf16[576,128]{1,0:T(8,128)(2,1)S(1)}, u32[]{:S(2)}, u32[]{:S(2)}) collective-permute-start(bf16[576,128]{1,0:T(8,128)(2,1)S(1)} %get-tuple-element.67), channel_id=1, source_target_pairs={{0,4},{1,5},{2,14},{3,15},{4,8},{5,9},{6,2},{7,3},{8,12},{9,13},{1... | collective-permute-start | bytes 442376 | tf_op jit(solution)/shard_map/ppermute | solution.py:53
  22.1 1.4 %collective-permute-start.8 = (bf16[256,256]{1,0:T(8,128)(2,1)S(1)}, bf16[256,256]{1,0:T(8,128)(2,1)S(1)}, u32[]{:S(2)}, u32[]{:S(2)}) collective-permute-start(bf16[256,256]{1,0:T(8,128)(2,1)S(1)} %shard_map.117), channel_id=1, source_target_pairs={{0,1},{1,0},{2,3},{3,2},{4,5},{5,4},{6,7},{7,6},{8,9},{9,8},{10,11... | collective-permute-start | bytes 393224 | tf_op jit(solution)/shard_map/ppermute | solution.py:44
  23.6 9.4 %collective-permute-start.10 = (bf16[256,256]{1,0:T(8,128)(2,1)S(1)}, bf16[256,256]{1,0:T(8,128)(2,1)S(1)}, u32[]{:S(2)}, u32[]{:S(2)}) collective-permute-start(bf16[256,256]{1,0:T(8,128)(2,1)S(1)} %get-tuple-element.78), channel_id=1, source_target_pairs={{0,12},{1,13},{2,6},{3,7},{4,0},{5,1},{6,10},{7,11},{8,4},{9,5},{1... | collective-permute-start | bytes 393224 | tf_op jit(solution)/shard_map/ppermute | solution.py:53
  27.5 7.1 %collective-permute-start.9 = (bf16[512,128]{1,0:T(8,128)(2,1)S(1)}, bf16[512,128]{1,0:T(8,128)(2,1)S(1)}, u32[]{:S(2)}, u32[]{:S(2)}) collective-permute-start(bf16[512,128]{1,0:T(8,128)(2,1)S(1)} %get-tuple-element.77), channel_id=1, source_target_pairs={{0,4},{1,5},{2,14},{3,15},{4,8},{5,9},{6,2},{7,3},{8,12},{9,13},{1... | collective-permute-start | bytes 393224 | tf_op jit(solution)/shard_map/ppermute | solution.py:53
  32.9 4.5 %collective-permute-start.11 = (bf16[256,1024]{1,0:T(8,128)(2,1)S(1)}, bf16[256,1024]{1,0:T(8,128)(2,1)S(1)}, u32[]{:S(2)}, u32[]{:S(2)}) collective-permute-start(bf16[256,1024]{1,0:T(8,128)(2,1)S(1)} %collective-permute-done.1.rows_ref.e2), channel_id=1, source_target_pairs={{0,1},{1,0},{2,3},{3,2},{4,5},{5,4},{6,7},{7,6},{8,9},{9,8},{10,11... | collective-permute-start | bytes 1572872 | tf_op jit(solution)/shard_map/ppermute | solution.py:44
  38.0 9.1 %collective-permute-start.12 = (bf16[1024,128]{1,0:T(8,128)(2,1)S(1)}, bf16[1024,128]{1,0:T(8,128)(2,1)S(1)}, u32[]{:S(2)}, u32[]{:S(2)}) collective-permute-start(bf16[1024,128]{1,0:T(8,128)(2,1)S(1)} %shard_map.121), channel_id=1, source_target_pairs={{0,18},{1,19},{2,16},{3,17},{4,22},{5,23},{6,20},{7,21},{8,26},{9,... | collective-permute-start | bytes 786440 | tf_op jit(solution)/shard_map/ppermute | solution.py:463
  47.2 6.8 %collective-permute-start.16 = (bf16[256,128]{1,0:T(8,128)(2,1)S(1)}, bf16[256,128]{1,0:T(8,128)(2,1)S(1)}, u32[]{:S(2)}, u32[]{:S(2)}) collective-permute-start(bf16[256,128]{1,0:T(8,128)(2,1)S(1)} %get-tuple-element.95), channel_id=1, source_target_pairs={{0,4},{1,5},{2,6},{3,7},{4,8},{5,9},{6,10},{7,11},{8,12},{9,13},{1... | collective-permute-start | bytes 196616 | tf_op jit(solution)/shard_map/ppermute | solution.py:53
  48.0 7.4 %collective-permute-start.17 = (bf16[256,128]{1,0:T(8,128)(2,1)S(1)}, bf16[256,128]{1,0:T(8,128)(2,1)S(1)}, u32[]{:S(2)}, u32[]{:S(2)}) collective-permute-start(bf16[256,128]{1,0:T(8,128)(2,1)S(1)} %get-tuple-element.96), channel_id=1, source_target_pairs={{0,8},{1,9},{2,10},{3,11},{4,12},{5,13},{6,14},{7,15},{8,0},{9,1},... | collective-permute-start | bytes 196616 | tf_op jit(solution)/shard_map/ppermute | solution.py:53
  50.9 5.1 %collective-permute-start.18 = (bf16[256,128]{1,0:T(8,128)(2,1)S(1)}, bf16[256,128]{1,0:T(8,128)(2,1)S(1)}, u32[]{:S(2)}, u32[]{:S(2)}) collective-permute-start(bf16[256,128]{1,0:T(8,128)(2,1)S(1)} %get-tuple-element.97), channel_id=1, source_target_pairs={{0,12},{1,13},{2,14},{3,15},{4,0},{5,1},{6,2},{7,3},{8,4},{9,5},{1... | collective-permute-start | bytes 196616 | tf_op jit(solution)/shard_map/ppermute | solution.py:53
  51.0 7.4 %collective-permute-start.15 = (bf16[256,256]{1,0:T(8,128)(2,1)S(1)}, bf16[256,256]{1,0:T(8,128)(2,1)S(1)}, u32[]{:S(2)}, u32[]{:S(2)}) collective-permute-start(bf16[256,256]{1,0:T(8,128)(2,1)S(1)} %get-tuple-element.91), channel_id=1, source_target_pairs={{0,3},{1,2},{2,1},{3,0},{4,7},{5,6},{6,5},{7,4},{8,11},{9,10},{10,... | collective-permute-start | bytes 393224 | tf_op jit(solution)/shard_map/ppermute | solution.py:44
  51.4 8.2 %collective-permute-start.14 = (bf16[256,256]{1,0:T(8,128)(2,1)S(1)}, bf16[256,256]{1,0:T(8,128)(2,1)S(1)}, u32[]{:S(2)}, u32[]{:S(2)}) collective-permute-start(bf16[256,256]{1,0:T(8,128)(2,1)S(1)} %get-tuple-element.89), channel_id=1, source_target_pairs={{0,2},{1,3},{2,0},{3,1},{4,6},{5,7},{6,4},{7,5},{8,10},{9,11},{10,... | collective-permute-start | bytes 393224 | tf_op jit(solution)/shard_map/ppermute | solution.py:44
  54.0 5.7 %collective-permute-start.13 = (bf16[256,256]{1,0:T(8,128)(2,1)S(1)}, bf16[256,256]{1,0:T(8,128)(2,1)S(1)}, u32[]{:S(2)}, u32[]{:S(2)}) collective-permute-start(bf16[256,256]{1,0:T(8,128)(2,1)S(1)} %get-tuple-element.87), channel_id=1, source_target_pairs={{0,1},{1,0},{2,3},{3,2},{4,5},{5,4},{6,7},{7,6},{8,9},{9,8},{10,11... | collective-permute-start | bytes 393224 | tf_op jit(solution)/shard_map/ppermute | solution.py:44
  56.1 1.3 %collective-permute-start.19 = (bf16[64,256]{1,0:T(8,128)(2,1)S(1)}, bf16[64,256]{1,0:T(8,128)(2,1)S(1)}, u32[]{:S(2)}, u32[]{:S(2)}) collective-permute-start(bf16[64,256]{1,0:T(8,128)(2,1)S(1)} %get-tuple-element.99), channel_id=1, source_target_pairs={{0,1},{1,0},{2,3},{3,2},{4,5},{5,4},{6,7},{7,6},{8,9},{9,8},{10,11... | collective-permute-start | bytes 98312 | tf_op jit(solution)/shard_map/ppermute | solution.py:44
  57.4 4.3 %collective-permute-start.20 = (bf16[64,512]{1,0:T(8,128)(2,1)S(1)}, bf16[64,512]{1,0:T(8,128)(2,1)S(1)}, u32[]{:S(2)}, u32[]{:S(2)}) collective-permute-start(bf16[64,512]{1,0:T(8,128)(2,1)S(1)} %shard_map.126.own), channel_id=1, source_target_pairs={{0,16},{16,0},{1,17},{17,1},{2,18},{18,2},{3,19},{19,3},{4,20},{20... | collective-permute-start | bytes 196616 | tf_op jit(solution)/shard_map/ppermute | solution.py:477

commit v7 on v6

--- a/solution.py
+++ b/solution.py
@@ -74,17 +74,20 @@
 
 
 def fetch_kernel(a_ref, b_ref, wk_ref, wq_ref, *refs):
-    own, near, far, weights, sems = refs
+    *outs, weights, sems = refs
     mine = head()
     copies = []
     for k in range(2):
         for side, ref in enumerate((wk_ref, wq_ref)):
             to = slice((2 * k + side) * HD, (2 * k + side + 1) * HD)
             copies.append((ref.at[:, head_cols(mine ^ k)], weights.at[:, to]))
-    for k, (out, at) in enumerate(((own, 0), (near, 0), (far, 0), (far, 2))):
+    rows = a_ref.shape[0]
+    for k, out in enumerate(outs):
+        if out.shape[0] > rows:
+            out[rows:, :] = jnp.zeros((out.shape[0] - rows, out.shape[1]), out.dtype)
         for side, ref in enumerate((a_ref, b_ref)):
-            to = slice((at + side) * HD, (at + side + 1) * HD)
-            copies.append((ref.at[:, head_cols(mine ^ k)], out.at[:, to]))
+            to = slice(side * HD, (side + 1) * HD)
+            copies.append((ref.at[:, head_cols(mine ^ k)], out.at[:rows, to]))
     started = [pltpu.make_async_copy(*pair, sems.at[i]) for i, pair in enumerate(copies)]
     for copy in started:
         copy.start()
@@ -120,8 +123,7 @@
         to_big = slice((pair - skip) * HD, (pair - skip + 1) * HD)
         for i, at_core in ((0, core), (1, 1 - core)):
             ref = sources[2 * pair + i]
-            if ref.shape[1] > 2 * HD:
-                ref = ref.at[:, : 2 * HD]
+            ref = ref.at[:rows, :]
             at = pl.ds(pl.multiple_of(at_core * rows, rows), rows)
 
             @pl.when(keys_big)
@@ -141,10 +143,6 @@
                 @pl.when(at_core == 1)
                 def _():
                     small[:, to] = ref[:, :HD]
-
-
-def second_half_kernel(ref, out):
-    out[...] = ref[:, out.shape[1] :]
 
 
 def offset_of(row, shift, total):
@@ -296,7 +294,7 @@
 
 
 def inner_kernel(
-    len_ref, shift_ref, keep_ref, a0, a1, a2, a3, b0, b1, b2, b3, big, small,
+    len_ref, shift_ref, keep_ref, a0, a1, a2, a3, b0, b1, b2, b3,
     early_out, early_dq, early_dk, early_dv,
     k_ref, q_ref, v_ref, o_ref, out_t, dq_t, dk, dv,
 ):
@@ -305,7 +303,7 @@
     shift = shift_ref[0]
     base = plane_base(rows)
     me = place()
-    b2 = b2.at[:, : 2 * HD]
+    b2, b3 = b2.at[:rows, :], b3.at[:rows, :]
     for i, (kq, vo) in enumerate(((a0, b0), (a1, b1), (a2, b2), (a3, b3))):
         at = pl.ds(pl.multiple_of((me ^ i) * rows, rows), rows)
         k_ref[at, :] = kq[:, :HD]
@@ -343,9 +341,14 @@
             dk_sum = dk_sum + nn(ds, q_ref[qs, :])
         dk[at, :] += dk_sum
         dv[at, :] += dv_sum
+
+
+def own_halo_kernel(
+    len_ref, shift_ref, keep_ref, k_ref, q_ref, v_ref, o_ref, big, small, *refs
+):
     cross_pairs(
         True, len_ref, shift_ref, keep_ref, k_ref, q_ref, v_ref, o_ref, (big,), (small,),
-        out_t, dq_t, dk, dv,
+        *refs[4:],
     )
 
 
@@ -510,9 +513,9 @@
 
     e1 = partner(local, 1)
     e2 = partner(local, 2)
-    vo0, vo1, far, weights = call(
+    vo0, vo1, vo2, vo3, weights = call(
         fetch_kernel,
-        [pair] * 2 + [like(rows, 4 * HD), like(width, 4 * HD)],
+        [pair] * 2 + [like(rows + 32, 2 * HD)] * 2 + [like(width, 4 * HD)],
         [
             pltpu.with_memory_space_constraint(a, pltpu.HBM)
             for a in (values[0], grad_out[0], w_key, w_query)
@@ -542,7 +545,7 @@
         busy=0.1,
         scratch=[pltpu.VMEM((2 * rows, 2 * HD), jnp.bfloat16)] * 2,
     )
-    vo2 = partner(after(far, *early), 2)
+    vo2, vo3 = partner(after(vo2, *early), 2), partner(after(vo3, *early), 3)
     kq2, give = call(project_both_kernel, [pair] * 2, (after(e2, own[1], *early), weights), busy=0.1)
     kq3 = partner(give, 1)
     big_kq, _ = call(
@@ -551,23 +554,30 @@
         (kq2, kq3),
         busy=0.1,
     )
-    (half,) = call(second_half_kernel, [pair], (after(vo2, own[0], big_kq),), busy=0.1)
-    vo3 = partner(half, 1)
     big_vo, small = call(
         functools.partial(edge_kernel, False, 1),
         [like(2 * rows, HD), pair],
-        (kq2, kq3, vo2, vo3),
-        busy=0.1,
+        (kq2, kq3, after(vo2, own[0], big_kq), vo3),
+        busy=2,
     )
     big_kq = around(big_kq, 1, -1)
-    kq3 = after(kq3, big_kq)
+    kq3 = after(kq3, big_vo)
+    own0 = after(own[0], big_kq)
     other = big_kq, around(big_vo, 1, -1), around(small, -1, 1)
     k, q, v, o, *held = call(
         inner_kernel,
         [full] * 4 + sums,
-        (*info, kq0, kq1, kq2, kq3, vo0, vo1, vo2, vo3, *own, *early),
-        specs=[SMEM] * 3 + [VMEM] * 14,
-        busy=15,
+        (*info, kq0, kq1, kq2, kq3, vo0, vo1, vo2, vo3, *early),
+        specs=[SMEM] * 3 + [VMEM] * 12,
+        busy=3,
+    )
+    held = call(
+        own_halo_kernel,
+        sums,
+        (*info, k, q, v, o, own0, own[1], *held),
+        specs=[SMEM] * 3 + [VMEM] * 10,
+        aliases={9: 0, 10: 1, 11: 2, 12: 3},
+        busy=5,
     )
     *_, p0, p1, p2, p3, dqk = call(
         outer_kernel,

time: 62.5 us -> 61.9 us (level)
  waiting for transfers between devices: 21.6 us -> 19.6 us
  starting transfers between devices: 23.1 us -> 24 us
    ppermute x8, starting transfers between devices: 11.9 us -> 14.5 us  [around(): return lax.ppermute(value, 'ctx', pairs)]
    ppermute x8, waiting for transfers between devices: 4.79 us -> 3.53 us  [around(): return lax.ppermute(value, 'ctx', pairs)]
    ppermute x11, starting transfers between devices: 7.93 us -> 6.69 us  [partner(): return lax.ppermute(value, 'ctx', [(i, i ^ steps) for i in range(count)])]
    ppermute x1, waiting for transfers between devices: 1.15 us -> 0.48 us  [direct_reduce(): other = lax.ppermute(both, 'dp', [(0, 1), (1, 0)])]
  transfers between devices with their start and end apart: 21 -> 21, of which waited for: 14 -> 12; matrix products, arithmetic and copies ran while one was open for 0% -> 0% of each run, Pallas kernels for 24% -> 25%
where the time goes in v7:
time: 61.9 us; the launch traced here: 61.8 us
  starting transfers between devices  24 us (39%)
  waiting for transfers between devices  19.6 us (32%)
  Pallas kernels  16.8 us (27%)
  between operations  1.46 us (2%)
    pallas_call x17, Pallas kernels, call(): pl.pallas_call(kernel, out_shape=tuple(outs), in_specs=specs or [VMEM] *...  16.8 us
    ppermute x8, starting transfers between devices, around(): return lax.ppermute(value, 'ctx', pairs)  14.5 us
    ppermute x11, waiting for transfers between devices, partner(): return lax.ppermute(value, 'ctx', [(i, i ^ steps) for i in range(count)])  8.95 us
    ppermute x11, starting transfers between devices, partner(): return lax.ppermute(value, 'ctx', [(i, i ^ steps) for i in range(count)])  6.69 us
    ppermute x1, waiting for transfers between devices, direct_reduce(): got = lax.ppermute(give, ('dp', 'ctx'), across)  6.59 us
    ppermute x8, waiting for transfers between devices, around(): return lax.ppermute(value, 'ctx', pairs)  3.53 us
    ppermute x1, starting transfers between devices, direct_reduce(): got = lax.ppermute(give, ('dp', 'ctx'), across)  2.04 us
  transfers between devices with their start and end apart: 21, of which 12 were waited for; matrix products, arithmetic and copies ran while one was open for 0% of the time, Pallas kernels for 25%

profile of v7, /device:TPU:0, one launch (start us, length us, event | category | flops | bytes accessed | tf_op | source)
XLA Modules:
  0.0 61.8 jit_solution(12533940417866198004)
XLA Ops:
  1.1 2.6 %collective-permute-start.1 = (bf16[256,1024]{1,0:T(8,128)(2,1)}, bf16[256,1024]{1,0:T(8,128)(2,1)S(1)}, u32[]{:S(2)}, u32[]{:S(2)}) collective-permute-start(bf16[256,1024]{1,0:T(8,128)(2,1)} %bitcast.6), channel_id=1, source_target_pairs={{0,2},{1,3},{2,0},{3,1},{4,6},{5,7},{6,4},{7,5},{8,10},{9,11},{10,... | collective-permute-start | bytes 1572872 | tf_op jit(solution)/shard_map/ppermute | solution.py:44
  3.7 1.5 %shard_map.111 = (bf16[256,256]{1,0:T(8,128)(2,1)S(1)}, bf16[256,256]{1,0:T(8,128)(2,1)S(1)}, bf16[288,256]{1,0:T(8,128)(2,1)S(1)}, bf16[288,256]{1,0:T(8,128)(2,1)S(1)}, bf16[1024,512]{1,0:T(8,128)(2,1)S(1)}) custom-call(bf16[256,512]{1,0:T(8,128)(2,1)} %bitcast.10, bf16[256,512]{1,0:T(8,128)(2,1)} %bitcast.11, bf16[1024,512]{1,0:T(8,128)(2,1)} %wk_ref.1, ...), custom_call_target="tpu_custom_call" | custom-call | flops 115000000 | tf_op jit(solution)/shard_map/pallas_call | solution.py:24
  5.9 0.7 %collective-permute-done.2.refs_3_.b1 = bf16[256,256]{1,0:T(8,128)(2,1)S(1)} collective-permute-done((bf16[256,256]{1,0:T(8,128)(2,1)S(1)}, bf16[256,256]{1,0:T(8,128)(2,1)S(1)}, u32[]{:S(2)}, u32[]{:S(2)}) %collective-permute-start.2) | collective-permute-done | bytes 131104 | tf_op jit(solution)/shard_map/ppermute | solution.py:44
  6.7 1.6 %collective-permute-start.3 = (bf16[256,256]{1,0:T(8,128)(2,1)S(1)}, bf16[256,256]{1,0:T(8,128)(2,1)S(1)}, u32[]{:S(2)}, u32[]{:S(2)}) collective-permute-start(bf16[256,256]{1,0:T(8,128)(2,1)S(1)} %get-tuple-element.65), channel_id=1, source_target_pairs={{0,4},{1,5},{2,14},{3,15},{4,8},{5,9},{6,2},{7,3},{8,12},{9,13},{1... | collective-permute-start | bytes 393224 | tf_op jit(solution)/shard_map/ppermute | solution.py:53
  8.4 2.2 %collective-permute-start.6 = (bf16[512,256]{1,0:T(8,128)(2,1)S(1)}, bf16[512,256]{1,0:T(8,128)(2,1)S(1)}, u32[]{:S(2)}, u32[]{:S(2)}) collective-permute-start(bf16[512,256]{1,0:T(8,128)(2,1)S(1)} %get-tuple-element.76), channel_id=1, source_target_pairs={{0,12},{1,13},{2,6},{3,7},{4,0},{5,1},{6,10},{7,11},{8,4},{9,5},{1... | collective-permute-start | bytes 786440 | tf_op jit(solution)/shard_map/ppermute | solution.py:53
  11.3 1.9 %shard_map.114 = (f32[128,512]{1,0:T(8,128)S(1)}, f32[128,512]{1,0:T(8,128)S(1)}, f32[512,128]{1,0:T(8,128)S(1)}, f32[512,128]{1,0:T(8,128)S(1)}) custom-call(s32[1,8]{1,0:T(1,128)S(1)} %copy-done.1, s32[1]{0:T(128)S(6)} %copy.28.shift_ref, s32[1,32]{1,0:T(1,128)S(1)} %copy-done.2, bf16[256,256]{1,0:T(8,128)(2,1)S(1)} %get-tuple-element.66.refs_0_.a0, ...), custom_call_target="tpu_custom_call" | custom-call | flops 115000000 | tf_op jit(solution)/shard_map/pallas_call | solution.py:24
  13.2 1.4 %collective-permute-start.5 = (bf16[288,256]{1,0:T(8,128)(2,1)S(1)}, bf16[288,256]{1,0:T(8,128)(2,1)S(1)}, u32[]{:S(2)}, u32[]{:S(2)}) collective-permute-start(bf16[288,256]{1,0:T(8,128)(2,1)S(1)} %get-tuple-element.75), channel_id=1, source_target_pairs={{0,2},{1,3},{2,0},{3,1},{4,6},{5,7},{6,4},{7,5},{8,10},{9,11},{10,... | collective-permute-start | bytes 442376 | tf_op jit(solution)/shard_map/ppermute | solution.py:44
  14.6 2.0 %collective-permute-done.1.rows_ref.e2 = bf16[256,1024]{1,0:T(8,128)(2,1)S(1)} collective-permute-done((bf16[256,1024]{1,0:T(8,128)(2,1)}, bf16[256,1024]{1,0:T(8,128)(2,1)S(1)}, u32[]{:S(2)}, u32[]{:S(2)}) %collective-permute-start.1) | collective-permute-done | bytes 524320 | tf_op jit(solution)/shard_map/ppermute | solution.py:44
  17.1 1.3 %collective-permute-done.4.refs_1_.a3 = bf16[256,256]{1,0:T(8,128)(2,1)S(1)} collective-permute-done((bf16[256,256]{1,0:T(8,128)(2,1)S(1)}, bf16[256,256]{1,0:T(8,128)(2,1)S(1)}, u32[]{:S(2)}, u32[]{:S(2)}) %collective-permute-start.4) | collective-permute-done | bytes 131104 | tf_op jit(solution)/shard_map/ppermute | solution.py:44
  18.5 0.7 %shard_map.116 = (bf16[576,128]{1,0:T(8,128)(2,1)S(1)}, bf16[256,128]{1,0:T(8,128)(2,1)}) custom-call(bf16[256,256]{1,0:T(8,128)(2,1)S(1)} %get-tuple-element.72.refs_0_.a2, bf16[256,256]{1,0:T(8,128)(2,1)S(1)} %collective-permute-done.4.refs_1_.a3), custom_call_target="tpu_custom_call" | custom-call | flops 115000000 | tf_op jit(solution)/shard_map/pallas_call | solution.py:24
  19.1 2.1 %collective-permute-start.8 = (bf16[576,128]{1,0:T(8,128)(2,1)S(1)}, bf16[576,128]{1,0:T(8,128)(2,1)S(1)}, u32[]{:S(2)}, u32[]{:S(2)}) collective-permute-start(bf16[576,128]{1,0:T(8,128)(2,1)S(1)} %get-tuple-element.77), channel_id=1, source_target_pairs={{0,4},{1,5},{2,14},{3,15},{4,8},{5,9},{6,2},{7,3},{8,12},{9,13},{1... | collective-permute-start | bytes 442376 | tf_op jit(solution)/shard_map/ppermute | solution.py:53
  21.3 1.5 %collective-permute-done.5.refs_2_.b2 = bf16[288,256]{1,0:T(8,128)(2,1)S(1)} collective-permute-done((bf16[288,256]{1,0:T(8,128)(2,1)S(1)}, bf16[288,256]{1,0:T(8,128)(2,1)S(1)}, u32[]{:S(2)}, u32[]{:S(2)}) %collective-permute-start.5) | collective-permute-done | bytes 147488 | tf_op jit(solution)/shard_map/ppermute | solution.py:44
  22.8 1.9 %collective-permute-start.9 = (bf16[512,128]{1,0:T(8,128)(2,1)S(1)}, bf16[512,128]{1,0:T(8,128)(2,1)S(1)}, u32[]{:S(2)}, u32[]{:S(2)}) collective-permute-start(bf16[512,128]{1,0:T(8,128)(2,1)S(1)} %get-tuple-element.81), channel_id=1, source_target_pairs={{0,4},{1,5},{2,14},{3,15},{4,8},{5,9},{6,2},{7,3},{8,12},{9,13},{1... | collective-permute-start | bytes 393224 | tf_op jit(solution)/shard_map/ppermute | solution.py:53
  24.7 2.1 %collective-permute-start.10 = (bf16[256,256]{1,0:T(8,128)(2,1)S(1)}, bf16[256,256]{1,0:T(8,128)(2,1)S(1)}, u32[]{:S(2)}, u32[]{:S(2)}) collective-permute-start(bf16[256,256]{1,0:T(8,128)(2,1)S(1)} %get-tuple-element.87), channel_id=1, source_target_pairs={{0,12},{1,13},{2,6},{3,7},{4,0},{5,1},{6,10},{7,11},{8,4},{9,5},{1... | collective-permute-start | bytes 393224 | tf_op jit(solution)/shard_map/ppermute | solution.py:53
  26.8 3.6 %shard_map.118 = (bf16[1024,128]{1,0:T(8,128)(2,1)S(1)}, bf16[1024,128]{1,0:T(8,128)(2,1)S(1)}, bf16[1024,128]{1,0:T(8,128)(2,1)S(1)}, bf16[1024,128]{1,0:T(8,12...) custom-call(s32[1,8]{1,0:T(1,128)S(1)} %copy-done.1, ...), custom_call_target="tpu_custom_call" | custom-call | flops 3449999872 | tf_op jit(solution)/shard_map/pallas_call | solution.py:24
  30.4 2.4 %shard_map.119 = (f32[128,1024]{1,0:T(8,128)S(1)}, f32[128,1024]{1,0:T(8,128)S(1)}, f32[1024,128]{1,0:T(8,128)S(1)}, f32[1024,128]{1,0:T(8,128)S(1)}) custom-call(s32[1,8]{1,0:T(1,128)S(1)} %copy-done.1, s32[1]{0:T(128)S(6)} %copy.28.shift_ref, s32[1,32]{1,0:T(1,128)S(1)} %copy-done.2, ...), custom_call_target="tpu_custom_call", output_to_operand_aliasing={{0}: (9, {}), {1}: (10, {}), {2}: (11, {}), {3}: (12, {})} | custom-call | flops 5750000128 | tf_op jit(solution)/shard_map/pallas_call | solution.py:24
  32.9 1.0 %collective-permute-done.10.small = bf16[256,256]{1,0:T(8,128)(2,1)S(1)} collective-permute-done((bf16[256,256]{1,0:T(8,128)(2,1)S(1)}, bf16[256,256]{1,0:T(8,128)(2,1)S(1)}, u32[]{:S(2)}, u32[]{:S(2)}) %collective-permute-start.10) | collective-permute-done | bytes 131104 | tf_op jit(solution)/shard_map/ppermute | solution.py:53
  33.9 2.9 %shard_map.120 = (f32[128,1024]{1,0:T(8,128)S(1)}, f32[128,1024]{1,0:T(8,128)S(1)}, f32[1024,128]{1,0:T(8,128)S(1)}, f32[1024,128]{1,0:T(8,128)S(1)}, bf16[256,2...) custom-call(s32[1,8]{1,0:T(1,128)S(1)} %copy-done.1, ...), custom_call_target="tpu_custom_call", output_to_operand_aliasing={{0}: (10, {}), {1}: (11, {}), {2}: (12, {}), {3}: (13, {})} | custom-call | flops 6899999744 | tf_op jit(solution)/shard_map/pallas_call | solution.py:24
  36.8 0.6 shard_map.121
  37.4 2.0 %collective-permute-start.12 = (bf16[1024,128]{1,0:T(8,128)(2,1)S(1)}, bf16[1024,128]{1,0:T(8,128)(2,1)S(1)}, u32[]{:S(2)}, u32[]{:S(2)}) collective-permute-start(bf16[1024,128]{1,0:T(8,128)(2,1)S(1)} %shard_map.121), channel_id=1, source_target_pairs={{0,18},{1,19},{2,16},{3,17},{4,22},{5,23},{6,20},{7,21},{8,26},{9,... | collective-permute-start | bytes 786440 | tf_op jit(solution)/shard_map/ppermute | solution.py:466
  40.0 6.6 %collective-permute-done.12.other = bf16[1024,128]{1,0:T(8,128)(2,1)S(1)} collective-permute-done((bf16[1024,128]{1,0:T(8,128)(2,1)S(1)}, bf16[1024,128]{1,0:T(8,128)(2,1)S(1)}, u32[]{:S(2)}, u32[]{:S(2)}) %collective-permute-start.12) | collective-permute-done | bytes 262176 | tf_op jit(solution)/shard_map/ppermute | solution.py:466
  46.6 0.6 %collective-permute-start.16 = (bf16[256,128]{1,0:T(8,128)(2,1)S(1)}, bf16[256,128]{1,0:T(8,128)(2,1)S(1)}, u32[]{:S(2)}, u32[]{:S(2)}) collective-permute-start(bf16[256,128]{1,0:T(8,128)(2,1)S(1)} %get-tuple-element.109), channel_id=1, source_target_pairs={{0,4},{1,5},{2,6},{3,7},{4,8},{5,9},{6,10},{7,11},{8,12},{9,13},{1... | collective-permute-start | bytes 196616 | tf_op jit(solution)/shard_map/ppermute | solution.py:53
  47.2 3.0 %collective-permute-start.17 = (bf16[256,128]{1,0:T(8,128)(2,1)S(1)}, bf16[256,128]{1,0:T(8,128)(2,1)S(1)}, u32[]{:S(2)}, u32[]{:S(2)}) collective-permute-start(bf16[256,128]{1,0:T(8,128)(2,1)S(1)} %get-tuple-element.110), channel_id=1, source_target_pairs={{0,8},{1,9},{2,10},{3,11},{4,12},{5,13},{6,14},{7,15},{8,0},{9,1},... | collective-permute-start | bytes 196616 | tf_op jit(solution)/shard_map/ppermute | solution.py:53
  50.3 0.9 %collective-permute-start.18 = (bf16[256,128]{1,0:T(8,128)(2,1)S(1)}, bf16[256,128]{1,0:T(8,128)(2,1)S(1)}, u32[]{:S(2)}, u32[]{:S(2)}) collective-permute-start(bf16[256,128]{1,0:T(8,128)(2,1)S(1)} %get-tuple-element.111), channel_id=1, source_target_pairs={{0,12},{1,13},{2,14},{3,15},{4,0},{5,1},{6,2},{7,3},{8,4},{9,5},{1... | collective-permute-start | bytes 196616 | tf_op jit(solution)/shard_map/ppermute | solution.py:53
  51.1 1.7 %collective-permute-start.14 = (bf16[256,256]{1,0:T(8,128)(2,1)S(1)}, bf16[256,256]{1,0:T(8,128)(2,1)S(1)}, u32[]{:S(2)}, u32[]{:S(2)}) collective-permute-start(bf16[256,256]{1,0:T(8,128)(2,1)S(1)} %get-tuple-element.103), channel_id=1, source_target_pairs={{0,2},{1,3},{2,0},{3,1},{4,6},{5,7},{6,4},{7,5},{8,10},{9,11},{10,... | collective-permute-start | bytes 393224 | tf_op jit(solution)/shard_map/ppermute | solution.py:44
  53.4 1.3 %collective-permute-done.17.refs_2_ = bf16[256,128]{1,0:T(8,128)(2,1)S(1)} collective-permute-done((bf16[256,128]{1,0:T(8,128)(2,1)S(1)}, bf16[256,128]{1,0:T(8,128)(2,1)S(1)}, u32[]{:S(2)}, u32[]{:S(2)}) %collective-permute-start.17) | collective-permute-done | bytes 65568 | tf_op jit(solution)/shard_map/ppermute | solution.py:53
  54.8 0.6 collective-permute-done.18.refs_3_
  55.6 1.2 %collective-permute-done.19.other = bf16[64,256]{1,0:T(8,128)(2,1)S(1)} collective-permute-done((bf16[64,256]{1,0:T(8,128)(2,1)S(1)}, bf16[64,256]{1,0:T(8,128)(2,1)S(1)}, u32[]{:S(2)}, u32[]{:S(2)}) %collective-permute-start.19) | collective-permute-done | bytes 32800 | tf_op jit(solution)/shard_map/ppermute | solution.py:44
  56.8 0.8 %collective-permute-start.20 = (bf16[64,512]{1,0:T(8,128)(2,1)S(1)}, bf16[64,512]{1,0:T(8,128)(2,1)S(1)}, u32[]{:S(2)}, u32[]{:S(2)}) collective-permute-start(bf16[64,512]{1,0:T(8,128)(2,1)S(1)} %shard_map.126.own), channel_id=1, source_target_pairs={{0,16},{16,0},{1,17},{17,1},{2,18},{18,2},{3,19},{19,3},{4,20},{20... | collective-permute-start | bytes 196616 | tf_op jit(solution)/shard_map/ppermute | solution.py:480
  57.5 2.2 %collective-permute-done.14.i2 = bf16[256,256]{1,0:T(8,128)(2,1)S(1)} collective-permute-done((bf16[256,256]{1,0:T(8,128)(2,1)S(1)}, bf16[256,256]{1,0:T(8,128)(2,1)S(1)}, u32[]{:S(2)}, u32[]{:S(2)}) %collective-permute-start.14) | collective-permute-done | bytes 131104 | tf_op jit(solution)/shard_map/ppermute | solution.py:44
  59.7 0.9 %shard_map.122 = (bf16[256,512]{1,0:T(8,128)(2,1)}, bf16[256,512]{1,0:T(8,128)(2,1)}) custom-call(bf16[256,256]{1,0:T(8,128)(2,1)S(1)} %get-tuple-element.97.i0, bf16[256,256]{1,0:T(8,128)(2,1)S(1)} %collective-permute-done.13.i1, bf16[256,256]{1,0:T(8,128)(2,1)S(1)} %collective-permute-done.14.i2, bf16[256,256]{1,0:T(8,128)(2,1)S(1)} %collective-permute-done.15.i3), custom_call_target="tpu_custom_call" | custom-call | flops 575000000 | tf_op jit(solution)/shard_map/pallas_call | solution.py:24
  61.1 0.7 %shard_map.127 = (bf16[64,512]{1,0:T(8,128)(2,1)}, bf16[64,512]{1,0:T(8,128)(2,1)}) custom-call(bf16[64,512]{1,0:T(8,128)(2,1)S(1)} %shard_map.126.own, bf16[64,512]{1,0:T(8,128)(2,1)S(1)} %collective-permute-done.20.other), custom_call_target="tpu_custom_call" | custom-call | flops 575000000 | tf_op jit(solution)/shard_map/pallas_call | solution.py:24
  (33 shorter events, 3.9 us)
Async XLA Ops:
  0.6 4.8 %collective-permute-start = (bf16[256,1024]{1,0:T(8,128)(2,1)}, bf16[256,1024]{1,0:T(8,128)(2,1)S(1)}, u32[]{:S(2)}, u32[]{:S(2)}) collective-permute-start(bf16[256,1024]{1,0:T(8,128)(2,1)} %bitcast.5), channel_id=1, source_target_pairs={{0,1},{1,0},{2,3},{3,2},{4,5},{5,4},{6,7},{7,6},{8,9},{9,8},{10,11... | collective-permute-start | bytes 1572872 | tf_op jit(solution)/shard_map/ppermute | solution.py:44
  1.1 15.4 %collective-permute-start.1 = (bf16[256,1024]{1,0:T(8,128)(2,1)}, bf16[256,1024]{1,0:T(8,128)(2,1)S(1)}, u32[]{:S(2)}, u32[]{:S(2)}) collective-permute-start(bf16[256,1024]{1,0:T(8,128)(2,1)} %bitcast.6), channel_id=1, source_target_pairs={{0,2},{1,3},{2,0},{3,1},{4,6},{5,7},{6,4},{7,5},{8,10},{9,11},{10,... | collective-permute-start | bytes 1572872 | tf_op jit(solution)/shard_map/ppermute | solution.py:44
  3.7 1.8 %copy-start = (bf16[1,256,1024]{2,1,0:T(8,128)(2,1)S(1)}, bf16[1,256,1024]{2,1,0:T(8,128)(2,1)}, u32[]{:S(2)}) copy-start(bf16[1,256,1024]{2,1,0:T(8,128)(2,1)} %param.8) | copy-start | bytes 1572868
  5.2 1.4 %collective-permute-start.2 = (bf16[256,256]{1,0:T(8,128)(2,1)S(1)}, bf16[256,256]{1,0:T(8,128)(2,1)S(1)}, u32[]{:S(2)}, u32[]{:S(2)}) collective-permute-start(bf16[256,256]{1,0:T(8,128)(2,1)S(1)} %get-tuple-element.64), channel_id=1, source_target_pairs={{0,1},{1,0},{2,3},{3,2},{4,5},{5,4},{6,7},{7,6},{8,9},{9,8},{10,11... | collective-permute-start | bytes 393224 | tf_op jit(solution)/shard_map/ppermute | solution.py:44
  6.7 9.9 %collective-permute-start.3 = (bf16[256,256]{1,0:T(8,128)(2,1)S(1)}, bf16[256,256]{1,0:T(8,128)(2,1)S(1)}, u32[]{:S(2)}, u32[]{:S(2)}) collective-permute-start(bf16[256,256]{1,0:T(8,128)(2,1)S(1)} %get-tuple-element.65), channel_id=1, source_target_pairs={{0,4},{1,5},{2,14},{3,15},{4,8},{5,9},{6,2},{7,3},{8,12},{9,13},{1... | collective-permute-start | bytes 393224 | tf_op jit(solution)/shard_map/ppermute | solution.py:53
  8.4 2.9 %copy-start.1 = (s32[1,8]{1,0:T(1,128)S(1)}, s32[1,8]{1,0:T(1,128)}, u32[]{:S(2)}) copy-start(s32[1,8]{1,0:T(1,128)} %len_ref.7) | copy-start | bytes 100
  8.4 2.9 %copy-start.2 = (s32[1,32]{1,0:T(1,128)S(1)}, s32[1,32]{1,0:T(1,128)}, u32[]{:S(2)}) copy-start(s32[1,32]{1,0:T(1,128)} %keep_ref.7) | copy-start | bytes 388
  8.4 14.4 %collective-permute-start.6 = (bf16[512,256]{1,0:T(8,128)(2,1)S(1)}, bf16[512,256]{1,0:T(8,128)(2,1)S(1)}, u32[]{:S(2)}, u32[]{:S(2)}) collective-permute-start(bf16[512,256]{1,0:T(8,128)(2,1)S(1)} %get-tuple-element.76), channel_id=1, source_target_pairs={{0,12},{1,13},{2,6},{3,7},{4,0},{5,1},{6,10},{7,11},{8,4},{9,5},{1... | collective-permute-start | bytes 786440 | tf_op jit(solution)/shard_map/ppermute | solution.py:53
  13.2 9.6 %collective-permute-start.7 = (bf16[288,256]{1,0:T(8,128)(2,1)S(1)}, bf16[288,256]{1,0:T(8,128)(2,1)S(1)}, u32[]{:S(2)}, u32[]{:S(2)}) collective-permute-start(bf16[288,256]{1,0:T(8,128)(2,1)S(1)} %get-tuple-element.80), channel_id=1, source_target_pairs={{0,3},{1,2},{2,1},{3,0},{4,7},{5,6},{6,5},{7,4},{8,11},{9,10},{10,... | collective-permute-start | bytes 442376 | tf_op jit(solution)/shard_map/ppermute | solution.py:44
  13.2 9.5 %collective-permute-start.5 = (bf16[288,256]{1,0:T(8,128)(2,1)S(1)}, bf16[288,256]{1,0:T(8,128)(2,1)S(1)}, u32[]{:S(2)}, u32[]{:S(2)}) collective-permute-start(bf16[288,256]{1,0:T(8,128)(2,1)S(1)} %get-tuple-element.75), channel_id=1, source_target_pairs={{0,2},{1,3},{2,0},{3,1},{4,6},{5,7},{6,4},{7,5},{8,10},{9,11},{10,... | collective-permute-start | bytes 442376 | tf_op jit(solution)/shard_map/ppermute | solution.py:44
  17.0 1.4 %collective-permute-start.4 = (bf16[256,256]{1,0:T(8,128)(2,1)S(1)}, bf16[256,256]{1,0:T(8,128)(2,1)S(1)}, u32[]{:S(2)}, u32[]{:S(2)}) collective-permute-start(bf16[256,256]{1,0:T(8,128)(2,1)S(1)} %get-tuple-element.73), channel_id=1, source_target_pairs={{0,1},{1,0},{2,3},{3,2},{4,5},{5,4},{6,7},{7,6},{8,9},{9,8},{10,11... | collective-permute-start | bytes 393224 | tf_op jit(solution)/shard_map/ppermute | solution.py:44
  19.1 11.3 %collective-permute-start.8 = (bf16[576,128]{1,0:T(8,128)(2,1)S(1)}, bf16[576,128]{1,0:T(8,128)(2,1)S(1)}, u32[]{:S(2)}, u32[]{:S(2)}) collective-permute-start(bf16[576,128]{1,0:T(8,128)(2,1)S(1)} %get-tuple-element.77), channel_id=1, source_target_pairs={{0,4},{1,5},{2,14},{3,15},{4,8},{5,9},{6,2},{7,3},{8,12},{9,13},{1... | collective-permute-start | bytes 442376 | tf_op jit(solution)/shard_map/ppermute | solution.py:53
  22.8 11.0 %collective-permute-start.9 = (bf16[512,128]{1,0:T(8,128)(2,1)S(1)}, bf16[512,128]{1,0:T(8,128)(2,1)S(1)}, u32[]{:S(2)}, u32[]{:S(2)}) collective-permute-start(bf16[512,128]{1,0:T(8,128)(2,1)S(1)} %get-tuple-element.81), channel_id=1, source_target_pairs={{0,4},{1,5},{2,14},{3,15},{4,8},{5,9},{6,2},{7,3},{8,12},{9,13},{1... | collective-permute-start | bytes 393224 | tf_op jit(solution)/shard_map/ppermute | solution.py:53
  24.7 9.1 %collective-permute-start.10 = (bf16[256,256]{1,0:T(8,128)(2,1)S(1)}, bf16[256,256]{1,0:T(8,128)(2,1)S(1)}, u32[]{:S(2)}, u32[]{:S(2)}) collective-permute-start(bf16[256,256]{1,0:T(8,128)(2,1)S(1)} %get-tuple-element.87), channel_id=1, source_target_pairs={{0,12},{1,13},{2,6},{3,7},{4,0},{5,1},{6,10},{7,11},{8,4},{9,5},{1... | collective-permute-start | bytes 393224 | tf_op jit(solution)/shard_map/ppermute | solution.py:53
  32.8 4.0 %collective-permute-start.11 = (bf16[256,1024]{1,0:T(8,128)(2,1)S(1)}, bf16[256,1024]{1,0:T(8,128)(2,1)S(1)}, u32[]{:S(2)}, u32[]{:S(2)}) collective-permute-start(bf16[256,1024]{1,0:T(8,128)(2,1)S(1)} %collective-permute-done.1.rows_ref.e2), channel_id=1, source_target_pairs={{0,1},{1,0},{2,3},{3,2},{4,5},{5,4},{6,7},{7,6},{8,9},{9,8},{10,11... | collective-permute-start | bytes 1572872 | tf_op jit(solution)/shard_map/ppermute | solution.py:44
  37.4 9.2 %collective-permute-start.12 = (bf16[1024,128]{1,0:T(8,128)(2,1)S(1)}, bf16[1024,128]{1,0:T(8,128)(2,1)S(1)}, u32[]{:S(2)}, u32[]{:S(2)}) collective-permute-start(bf16[1024,128]{1,0:T(8,128)(2,1)S(1)} %shard_map.121), channel_id=1, source_target_pairs={{0,18},{1,19},{2,16},{3,17},{4,22},{5,23},{6,20},{7,21},{8,26},{9,... | collective-permute-start | bytes 786440 | tf_op jit(solution)/shard_map/ppermute | solution.py:466
  46.6 6.8 %collective-permute-start.16 = (bf16[256,128]{1,0:T(8,128)(2,1)S(1)}, bf16[256,128]{1,0:T(8,128)(2,1)S(1)}, u32[]{:S(2)}, u32[]{:S(2)}) collective-permute-start(bf16[256,128]{1,0:T(8,128)(2,1)S(1)} %get-tuple-element.109), channel_id=1, source_target_pairs={{0,4},{1,5},{2,6},{3,7},{4,8},{5,9},{6,10},{7,11},{8,12},{9,13},{1... | collective-permute-start | bytes 196616 | tf_op jit(solution)/shard_map/ppermute | solution.py:53
  47.2 7.5 %collective-permute-start.17 = (bf16[256,128]{1,0:T(8,128)(2,1)S(1)}, bf16[256,128]{1,0:T(8,128)(2,1)S(1)}, u32[]{:S(2)}, u32[]{:S(2)}) collective-permute-start(bf16[256,128]{1,0:T(8,128)(2,1)S(1)} %get-tuple-element.110), channel_id=1, source_target_pairs={{0,8},{1,9},{2,10},{3,11},{4,12},{5,13},{6,14},{7,15},{8,0},{9,1},... | collective-permute-start | bytes 196616 | tf_op jit(solution)/shard_map/ppermute | solution.py:53
  50.3 5.1 %collective-permute-start.18 = (bf16[256,128]{1,0:T(8,128)(2,1)S(1)}, bf16[256,128]{1,0:T(8,128)(2,1)S(1)}, u32[]{:S(2)}, u32[]{:S(2)}) collective-permute-start(bf16[256,128]{1,0:T(8,128)(2,1)S(1)} %get-tuple-element.111), channel_id=1, source_target_pairs={{0,12},{1,13},{2,14},{3,15},{4,0},{5,1},{6,2},{7,3},{8,4},{9,5},{1... | collective-permute-start | bytes 196616 | tf_op jit(solution)/shard_map/ppermute | solution.py:53
  51.1 6.4 %collective-permute-start.15 = (bf16[256,256]{1,0:T(8,128)(2,1)S(1)}, bf16[256,256]{1,0:T(8,128)(2,1)S(1)}, u32[]{:S(2)}, u32[]{:S(2)}) collective-permute-start(bf16[256,256]{1,0:T(8,128)(2,1)S(1)} %get-tuple-element.105), channel_id=1, source_target_pairs={{0,3},{1,2},{2,1},{3,0},{4,7},{5,6},{6,5},{7,4},{8,11},{9,10},{10,... | collective-permute-start | bytes 393224 | tf_op jit(solution)/shard_map/ppermute | solution.py:44
  51.1 8.6 %collective-permute-start.14 = (bf16[256,256]{1,0:T(8,128)(2,1)S(1)}, bf16[256,256]{1,0:T(8,128)(2,1)S(1)}, u32[]{:S(2)}, u32[]{:S(2)}) collective-permute-start(bf16[256,256]{1,0:T(8,128)(2,1)S(1)} %get-tuple-element.103), channel_id=1, source_target_pairs={{0,2},{1,3},{2,0},{3,1},{4,6},{5,7},{6,4},{7,5},{8,10},{9,11},{10,... | collective-permute-start | bytes 393224 | tf_op jit(solution)/shard_map/ppermute | solution.py:44
  53.4 6.3 %collective-permute-start.13 = (bf16[256,256]{1,0:T(8,128)(2,1)S(1)}, bf16[256,256]{1,0:T(8,128)(2,1)S(1)}, u32[]{:S(2)}, u32[]{:S(2)}) collective-permute-start(bf16[256,256]{1,0:T(8,128)(2,1)S(1)} %get-tuple-element.101), channel_id=1, source_target_pairs={{0,1},{1,0},{2,3},{3,2},{4,5},{5,4},{6,7},{7,6},{8,9},{9,8},{10,11... | collective-permute-start | bytes 393224 | tf_op jit(solution)/shard_map/ppermute | solution.py:44
  55.5 1.3 %collective-permute-start.19 = (bf16[64,256]{1,0:T(8,128)(2,1)S(1)}, bf16[64,256]{1,0:T(8,128)(2,1)S(1)}, u32[]{:S(2)}, u32[]{:S(2)}) collective-permute-start(bf16[64,256]{1,0:T(8,128)(2,1)S(1)} %get-tuple-element.113), channel_id=1, source_target_pairs={{0,1},{1,0},{2,3},{3,2},{4,5},{5,4},{6,7},{7,6},{8,9},{9,8},{10,11... | collective-permute-start | bytes 98312 | tf_op jit(solution)/shard_map/ppermute | solution.py:44
  56.8 4.3 %collective-permute-start.20 = (bf16[64,512]{1,0:T(8,128)(2,1)S(1)}, bf16[64,512]{1,0:T(8,128)(2,1)S(1)}, u32[]{:S(2)}, u32[]{:S(2)}) collective-permute-start(bf16[64,512]{1,0:T(8,128)(2,1)S(1)} %shard_map.126.own), channel_id=1, source_target_pairs={{0,16},{16,0},{1,17},{17,1},{2,18},{18,2},{3,19},{19,3},{4,20},{20... | collective-permute-start | bytes 196616 | tf_op jit(solution)/shard_map/ppermute | solution.py:480

commit v8 on v7

--- a/solution.py
+++ b/solution.py
@@ -81,13 +81,10 @@
         for side, ref in enumerate((wk_ref, wq_ref)):
             to = slice((2 * k + side) * HD, (2 * k + side + 1) * HD)
             copies.append((ref.at[:, head_cols(mine ^ k)], weights.at[:, to]))
-    rows = a_ref.shape[0]
     for k, out in enumerate(outs):
-        if out.shape[0] > rows:
-            out[rows:, :] = jnp.zeros((out.shape[0] - rows, out.shape[1]), out.dtype)
         for side, ref in enumerate((a_ref, b_ref)):
             to = slice(side * HD, (side + 1) * HD)
-            copies.append((ref.at[:, head_cols(mine ^ k)], out.at[:rows, to]))
+            copies.append((ref.at[:, head_cols(mine ^ k)], out.at[:, to]))
     started = [pltpu.make_async_copy(*pair, sems.at[i]) for i, pair in enumerate(copies)]
     for copy in started:
         copy.start()
@@ -101,10 +98,20 @@
     far_kq[...] = nn(far[...], own).astype(jnp.bfloat16)
 
 
-def project_both_kernel(rows_ref, weights, own_kq, other_kq):
+class Sides:
+    def __init__(self, left, right):
+        self.left, self.right = left, right
+
+    def __getitem__(self, where):
+        rows, cols = where
+        return (self.right if cols.start == HD else self.left)[rows, :]
+
+
+def project_both_kernel(rows_ref, weights, own_kq, other_k, other_q):
     both = nn(rows_ref[...], weights[...]).astype(jnp.bfloat16)
     own_kq[...] = both[:, : 2 * HD]
-    other_kq[...] = both[:, 2 * HD :]
+    other_k[...] = both[:, 2 * HD : 3 * HD]
+    other_q[...] = both[:, 3 * HD :]
 
 
 def upper():
@@ -113,6 +120,8 @@
 
 def edge_kernel(own, skip, *refs):
     *sources, big, small = refs
+    if len(sources) % 2:
+        sources[1:3] = [Sides(*sources[1:3])]
     rows = small.shape[0]
     if big.shape[0] > 2 * rows:
         big[2 * rows :, :] = jnp.zeros((big.shape[0] - 2 * rows, big.shape[1]), big.dtype)
@@ -123,7 +132,6 @@
         to_big = slice((pair - skip) * HD, (pair - skip + 1) * HD)
         for i, at_core in ((0, core), (1, 1 - core)):
             ref = sources[2 * pair + i]
-            ref = ref.at[:rows, :]
             at = pl.ds(pl.multiple_of(at_core * rows, rows), rows)
 
             @pl.when(keys_big)
@@ -294,7 +302,7 @@
 
 
 def inner_kernel(
-    len_ref, shift_ref, keep_ref, a0, a1, a2, a3, b0, b1, b2, b3,
+    len_ref, shift_ref, keep_ref, a0, a1, a2, a3_k, a3_q, b0, b1, b2, b3,
     early_out, early_dq, early_dk, early_dv,
     k_ref, q_ref, v_ref, o_ref, out_t, dq_t, dk, dv,
 ):
@@ -303,7 +311,7 @@
     shift = shift_ref[0]
     base = plane_base(rows)
     me = place()
-    b2, b3 = b2.at[:rows, :], b3.at[:rows, :]
+    a3 = Sides(a3_k, a3_q)
     for i, (kq, vo) in enumerate(((a0, b0), (a1, b1), (a2, b2), (a3, b3))):
         at = pl.ds(pl.multiple_of((me ^ i) * rows, rows), rows)
         k_ref[at, :] = kq[:, :HD]
@@ -515,7 +523,7 @@
     e2 = partner(local, 2)
     vo0, vo1, vo2, vo3, weights = call(
         fetch_kernel,
-        [pair] * 2 + [like(rows + 32, 2 * HD)] * 2 + [like(width, 4 * HD)],
+        [pair] * GROUP + [like(width, 4 * HD)],
         [
             pltpu.with_memory_space_constraint(a, pltpu.HBM)
             for a in (values[0], grad_out[0], w_key, w_query)
@@ -529,7 +537,7 @@
     wide, tall = like(HD, all_rows, jnp.float32), like(all_rows, HD, jnp.float32)
     sums = [wide, wide, tall, tall]
     wide, tall = like(HD, 2 * rows, jnp.float32), like(2 * rows, HD, jnp.float32)
-    kq0, kq1 = call(project_kernel, [pair] * 2, (local, e1, weights), busy=0.1)
+    kq0, kq1 = call(project_kernel, [pair] * 2, (local, e1, weights), busy=1)
     big, small = call(
         functools.partial(edge_kernel, True, 0),
         [like(2 * rows, 2 * HD), pair],
@@ -546,29 +554,30 @@
         scratch=[pltpu.VMEM((2 * rows, 2 * HD), jnp.bfloat16)] * 2,
     )
     vo2, vo3 = partner(after(vo2, *early), 2), partner(after(vo3, *early), 3)
-    kq2, give = call(project_both_kernel, [pair] * 2, (after(e2, own[1], *early), weights), busy=0.1)
-    kq3 = partner(give, 1)
+    half = like(rows, HD)
+    kq2, *give = call(project_both_kernel, [pair, half, half], (after(e2, own[1], *early), weights), busy=1)
+    k3, q3 = partner(give[0], 1), partner(give[1], 1)
     big_kq, _ = call(
         functools.partial(edge_kernel, False, 0),
-        [like(2 * rows + 64, HD), like(rows, HD)],
-        (kq2, kq3),
+        [like(2 * rows + 16, HD), like(rows, HD)],
+        (kq2, k3, q3),
         busy=0.1,
     )
     big_vo, small = call(
         functools.partial(edge_kernel, False, 1),
         [like(2 * rows, HD), pair],
-        (kq2, kq3, after(vo2, own[0], big_kq), vo3),
+        (kq2, k3, q3, after(vo2, own[0], big_kq), vo3),
         busy=2,
     )
     big_kq = around(big_kq, 1, -1)
-    kq3 = after(kq3, big_vo)
+    k3 = after(k3, big_vo)
     own0 = after(own[0], big_kq)
     other = big_kq, around(big_vo, 1, -1), around(small, -1, 1)
     k, q, v, o, *held = call(
         inner_kernel,
         [full] * 4 + sums,
-        (*info, kq0, kq1, kq2, kq3, vo0, vo1, vo2, vo3, *early),
-        specs=[SMEM] * 3 + [VMEM] * 12,
+        (*info, kq0, kq1, kq2, k3, q3, vo0, vo1, vo2, vo3, *early),
+        specs=[SMEM] * 3 + [VMEM] * 13,
         busy=3,
     )
     held = call(

time: 61.9 us -> 61.5 us (level)
  waiting for transfers between devices: 19.6 us -> 18 us
  starting transfers between devices: 24 us -> 25 us
    ppermute x11 -> x12, waiting for transfers between devices: 8.95 us -> 7.78 us  [partner(): return lax.ppermute(value, 'ctx', [(i, i ^ steps) for i in range(count)])]
    ppermute x1, starting transfers between devices: 0.75 us -> 1.58 us  [direct_reduce(): other = lax.ppermute(both, 'dp', [(0, 1), (1, 0)])]
    ppermute x11 -> x12, starting transfers between devices: 6.69 us -> 7.17 us  [partner(): return lax.ppermute(value, 'ctx', [(i, i ^ steps) for i in range(count)])]
  transfers between devices with their start and end apart: 21 -> 22, of which waited for: 12 -> 11; matrix products, arithmetic and copies ran while one was open for 0% -> 0% of each run, Pallas kernels for 25% -> 25%
where the time goes in v8:
time: 61.5 us; the launch traced here: 61.3 us
  starting transfers between devices  25 us (41%)
  waiting for transfers between devices  18 us (29%)
  Pallas kernels  16.7 us (27%)
  between operations  1.47 us (2%)
    pallas_call x17, Pallas kernels, call(): pl.pallas_call(kernel, out_shape=tuple(outs), in_specs=specs or [VMEM] *...  16.7 us
    ppermute x8, starting transfers between devices, around(): return lax.ppermute(value, 'ctx', pairs)  14.5 us
    ppermute x12, waiting for transfers between devices, partner(): return lax.ppermute(value, 'ctx', [(i, i ^ steps) for i in range(count)])  7.78 us
    ppermute x12, starting transfers between devices, partner(): return lax.ppermute(value, 'ctx', [(i, i ^ steps) for i in range(count)])  7.17 us
    ppermute x1, waiting for transfers between devices, direct_reduce(): got = lax.ppermute(give, ('dp', 'ctx'), across)  6.86 us
    ppermute x8, waiting for transfers between devices, around(): return lax.ppermute(value, 'ctx', pairs)  3.41 us
    ppermute x1, starting transfers between devices, direct_reduce(): got = lax.ppermute(give, ('dp', 'ctx'), across)  1.78 us
    ppermute x1, starting transfers between devices, direct_reduce(): other = lax.ppermute(both, 'dp', [(0, 1), (1, 0)])  1.58 us
  transfers between devices with their start and end apart: 22, of which 11 were waited for; matrix products, arithmetic and copies ran while one was open for 0% of the time, Pallas kernels for 25%

profile of v8, /device:TPU:0, one launch (start us, length us, event | category | flops | bytes accessed | tf_op | source)
XLA Modules:
  0.0 61.3 jit_solution(5110939886809475302)
XLA Ops:
  1.1 2.6 %collective-permute-start.1 = (bf16[256,1024]{1,0:T(8,128)(2,1)}, bf16[256,1024]{1,0:T(8,128)(2,1)S(1)}, u32[]{:S(2)}, u32[]{:S(2)}) collective-permute-start(bf16[256,1024]{1,0:T(8,128)(2,1)} %bitcast.6), channel_id=1, source_target_pairs={{0,2},{1,3},{2,0},{3,1},{4,6},{5,7},{6,4},{7,5},{8,10},{9,11},{10,... | collective-permute-start | bytes 1572872 | tf_op jit(solution)/shard_map/ppermute | solution.py:44
  3.7 1.5 %shard_map.111 = (bf16[256,256]{1,0:T(8,128)(2,1)S(1)}, bf16[256,256]{1,0:T(8,128)(2,1)S(1)}, bf16[256,256]{1,0:T(8,128)(2,1)S(1)}, bf16[256,256]{1,0:T(8,128)(2,1)S(1)}, bf16[1024,512]{1,0:T(8,128)(2,1)S(1)}) custom-call(bf16[256,512]{1,0:T(8,128)(2,1)} %bitcast.10, bf16[256,512]{1,0:T(8,128)(2,1)} %bitcast.11, bf16[1024,512]{1,0:T(8,128)(2,1)} %wk_ref.1, ...), custom_call_target="tpu_custom_call" | custom-call | flops 115000000 | tf_op jit(solution)/shard_map/pallas_call | solution.py:24
  5.9 0.7 %collective-permute-done.2.refs_3_.b1 = bf16[256,256]{1,0:T(8,128)(2,1)S(1)} collective-permute-done((bf16[256,256]{1,0:T(8,128)(2,1)S(1)}, bf16[256,256]{1,0:T(8,128)(2,1)S(1)}, u32[]{:S(2)}, u32[]{:S(2)}) %collective-permute-start.2) | collective-permute-done | bytes 131104 | tf_op jit(solution)/shard_map/ppermute | solution.py:44
  6.7 1.6 %collective-permute-start.3 = (bf16[256,256]{1,0:T(8,128)(2,1)S(1)}, bf16[256,256]{1,0:T(8,128)(2,1)S(1)}, u32[]{:S(2)}, u32[]{:S(2)}) collective-permute-start(bf16[256,256]{1,0:T(8,128)(2,1)S(1)} %get-tuple-element.66), channel_id=1, source_target_pairs={{0,4},{1,5},{2,14},{3,15},{4,8},{5,9},{6,2},{7,3},{8,12},{9,13},{1... | collective-permute-start | bytes 393224 | tf_op jit(solution)/shard_map/ppermute | solution.py:53
  8.4 2.2 %collective-permute-start.7 = (bf16[512,256]{1,0:T(8,128)(2,1)S(1)}, bf16[512,256]{1,0:T(8,128)(2,1)S(1)}, u32[]{:S(2)}, u32[]{:S(2)}) collective-permute-start(bf16[512,256]{1,0:T(8,128)(2,1)S(1)} %get-tuple-element.78), channel_id=1, source_target_pairs={{0,12},{1,13},{2,6},{3,7},{4,0},{5,1},{6,10},{7,11},{8,4},{9,5},{1... | collective-permute-start | bytes 786440 | tf_op jit(solution)/shard_map/ppermute | solution.py:53
  11.3 1.9 %shard_map.114 = (f32[128,512]{1,0:T(8,128)S(1)}, f32[128,512]{1,0:T(8,128)S(1)}, f32[512,128]{1,0:T(8,128)S(1)}, f32[512,128]{1,0:T(8,128)S(1)}) custom-call(s32[1,8]{1,0:T(1,128)S(1)} %copy-done, s32[1]{0:T(128)S(6)} %copy.28.shift_ref, s32[1,32]{1,0:T(1,128)S(1)} %copy-done.1, bf16[256,256]{1,0:T(8,128)(2,1)S(1)} %get-tuple-element.67.refs_0_.a0, ...), custom_call_target="tpu_custom_call" | custom-call | flops 115000000 | tf_op jit(solution)/shard_map/pallas_call | solution.py:24
  13.2 1.4 %collective-permute-start.6 = (bf16[256,256]{1,0:T(8,128)(2,1)S(1)}, bf16[256,256]{1,0:T(8,128)(2,1)S(1)}, u32[]{:S(2)}, u32[]{:S(2)}) collective-permute-start(bf16[256,256]{1,0:T(8,128)(2,1)S(1)} %get-tuple-element.77), channel_id=1, source_target_pairs={{0,2},{1,3},{2,0},{3,1},{4,6},{5,7},{6,4},{7,5},{8,10},{9,11},{10,... | collective-permute-start | bytes 393224 | tf_op jit(solution)/shard_map/ppermute | solution.py:44
  14.6 2.0 %collective-permute-done.1.rows_ref.e2 = bf16[256,1024]{1,0:T(8,128)(2,1)S(1)} collective-permute-done((bf16[256,1024]{1,0:T(8,128)(2,1)}, bf16[256,1024]{1,0:T(8,128)(2,1)S(1)}, u32[]{:S(2)}, u32[]{:S(2)}) %collective-permute-start.1) | collective-permute-done | bytes 524320 | tf_op jit(solution)/shard_map/ppermute | solution.py:44
  17.6 0.7 %collective-permute-done.4.refs_1_.a3_k = bf16[256,128]{1,0:T(8,128)(2,1)S(1)} collective-permute-done((bf16[256,128]{1,0:T(8,128)(2,1)S(1)}, bf16[256,128]{1,0:T(8,128)(2,1)S(1)}, u32[]{:S(2)}, u32[]{:S(2)}) %collective-permute-start.4) | collective-permute-done | bytes 65568 | tf_op jit(solution)/shard_map/ppermute | solution.py:44
  18.5 0.7 %shard_map.116 = (bf16[528,128]{1,0:T(8,128)(2,1)S(1)}, bf16[256,128]{1,0:T(8,128)(2,1)}) custom-call(bf16[256,256]{1,0:T(8,128)(2,1)S(1)} %get-tuple-element.73.refs_0_.a2, bf16[256,128]{1,0:T(8,128)(2,1)S(1)} %collective-permute-done.4.refs_1_.a3_k, bf16[256,128]{1,0:T(8,128)(2,1)S(1)} %collective-permute-done.5.refs_2_.a3_q), custom_call_target="tpu_custom_call" | custom-call | flops 115000000 | tf_op jit(solution)/shard_map/pallas_call | solution.py:24
  19.2 2.1 %collective-permute-start.9 = (bf16[528,128]{1,0:T(8,128)(2,1)S(1)}, bf16[528,128]{1,0:T(8,128)(2,1)S(1)}, u32[]{:S(2)}, u32[]{:S(2)}) collective-permute-start(bf16[528,128]{1,0:T(8,128)(2,1)S(1)} %get-tuple-element.79), channel_id=1, source_target_pairs={{0,4},{1,5},{2,14},{3,15},{4,8},{5,9},{6,2},{7,3},{8,12},{9,13},{1... | collective-permute-start | bytes 405512 | tf_op jit(solution)/shard_map/ppermute | solution.py:53
  21.3 0.7 %collective-permute-done.6.refs_3_.b2 = bf16[256,256]{1,0:T(8,128)(2,1)S(1)} collective-permute-done((bf16[256,256]{1,0:T(8,128)(2,1)S(1)}, bf16[256,256]{1,0:T(8,128)(2,1)S(1)}, u32[]{:S(2)}, u32[]{:S(2)}) %collective-permute-start.6) | collective-permute-done | bytes 131104 | tf_op jit(solution)/shard_map/ppermute | solution.py:44
  22.1 1.9 %collective-permute-start.10 = (bf16[512,128]{1,0:T(8,128)(2,1)S(1)}, bf16[512,128]{1,0:T(8,128)(2,1)S(1)}, u32[]{:S(2)}, u32[]{:S(2)}) collective-permute-start(bf16[512,128]{1,0:T(8,128)(2,1)S(1)} %get-tuple-element.83), channel_id=1, source_target_pairs={{0,4},{1,5},{2,14},{3,15},{4,8},{5,9},{6,2},{7,3},{8,12},{9,13},{1... | collective-permute-start | bytes 393224 | tf_op jit(solution)/shard_map/ppermute | solution.py:53
  24.0 2.1 %collective-permute-start.11 = (bf16[256,256]{1,0:T(8,128)(2,1)S(1)}, bf16[256,256]{1,0:T(8,128)(2,1)S(1)}, u32[]{:S(2)}, u32[]{:S(2)}) collective-permute-start(bf16[256,256]{1,0:T(8,128)(2,1)S(1)} %get-tuple-element.89), channel_id=1, source_target_pairs={{0,12},{1,13},{2,6},{3,7},{4,0},{5,1},{6,10},{7,11},{8,4},{9,5},{1... | collective-permute-start | bytes 393224 | tf_op jit(solution)/shard_map/ppermute | solution.py:53
  26.1 3.6 %shard_map.118 = (bf16[1024,128]{1,0:T(8,128)(2,1)S(1)}, bf16[1024,128]{1,0:T(8,128)(2,1)S(1)}, bf16[1024,128]{1,0:T(8,128)(2,1)S(1)}, bf16[1024,128]{1,0:T(8,12...) custom-call(s32[1,8]{1,0:T(1,128)S(1)} %copy-done, ...), custom_call_target="tpu_custom_call" | custom-call | flops 3449999872 | tf_op jit(solution)/shard_map/pallas_call | solution.py:24
  29.7 2.3 %shard_map.119 = (f32[128,1024]{1,0:T(8,128)S(1)}, f32[128,1024]{1,0:T(8,128)S(1)}, f32[1024,128]{1,0:T(8,128)S(1)}, f32[1024,128]{1,0:T(8,128)S(1)}) custom-call(s32[1,8]{1,0:T(1,128)S(1)} %copy-done, s32[1]{0:T(128)S(6)} %copy.28.shift_ref, s32[1,32]{1,0:T(1,128)S(1)} %copy-done.1, ...), custom_call_target="tpu_custom_call", output_to_operand_aliasing={{0}: (9, {}), {1}: (10, {}), {2}: (11, {}), {3}: (12, {})} | custom-call | flops 5750000128 | tf_op jit(solution)/shard_map/pallas_call | solution.py:24
  32.2 1.7 %collective-permute-done.11.small = bf16[256,256]{1,0:T(8,128)(2,1)S(1)} collective-permute-done((bf16[256,256]{1,0:T(8,128)(2,1)S(1)}, bf16[256,256]{1,0:T(8,128)(2,1)S(1)}, u32[]{:S(2)}, u32[]{:S(2)}) %collective-permute-start.11) | collective-permute-done | bytes 131104 | tf_op jit(solution)/shard_map/ppermute | solution.py:53
  33.9 2.9 %shard_map.120 = (f32[128,1024]{1,0:T(8,128)S(1)}, f32[128,1024]{1,0:T(8,128)S(1)}, f32[1024,128]{1,0:T(8,128)S(1)}, f32[1024,128]{1,0:T(8,128)S(1)}, bf16[256,2...) custom-call(s32[1,8]{1,0:T(1,128)S(1)} %copy-done, ...), custom_call_target="tpu_custom_call", output_to_operand_aliasing={{0}: (10, {}), {1}: (11, {}), {2}: (12, {}), {3}: (13, {})} | custom-call | flops 6899999744 | tf_op jit(solution)/shard_map/pallas_call | solution.py:24
  36.8 0.6 shard_map.121
  37.4 1.8 %collective-permute-start.13 = (bf16[1024,128]{1,0:T(8,128)(2,1)S(1)}, bf16[1024,128]{1,0:T(8,128)(2,1)S(1)}, u32[]{:S(2)}, u32[]{:S(2)}) collective-permute-start(bf16[1024,128]{1,0:T(8,128)(2,1)S(1)} %shard_map.121), channel_id=1, source_target_pairs={{0,18},{1,19},{2,16},{3,17},{4,22},{5,23},{6,20},{7,21},{8,26},{9,... | collective-permute-start | bytes 786440 | tf_op jit(solution)/shard_map/ppermute | solution.py:474
  39.1 0.6 shard_map.123.mine
  39.7 6.9 %collective-permute-done.13.other = bf16[1024,128]{1,0:T(8,128)(2,1)S(1)} collective-permute-done((bf16[1024,128]{1,0:T(8,128)(2,1)S(1)}, bf16[1024,128]{1,0:T(8,128)(2,1)S(1)}, u32[]{:S(2)}, u32[]{:S(2)}) %collective-permute-start.13) | collective-permute-done | bytes 262176 | tf_op jit(solution)/shard_map/ppermute | solution.py:474
  46.6 0.6 %collective-permute-start.17 = (bf16[256,128]{1,0:T(8,128)(2,1)S(1)}, bf16[256,128]{1,0:T(8,128)(2,1)S(1)}, u32[]{:S(2)}, u32[]{:S(2)}) collective-permute-start(bf16[256,128]{1,0:T(8,128)(2,1)S(1)} %get-tuple-element.111), channel_id=1, source_target_pairs={{0,4},{1,5},{2,6},{3,7},{4,8},{5,9},{6,10},{7,11},{8,12},{9,13},{1... | collective-permute-start | bytes 196616 | tf_op jit(solution)/shard_map/ppermute | solution.py:53
  47.2 2.4 %collective-permute-start.18 = (bf16[256,128]{1,0:T(8,128)(2,1)S(1)}, bf16[256,128]{1,0:T(8,128)(2,1)S(1)}, u32[]{:S(2)}, u32[]{:S(2)}) collective-permute-start(bf16[256,128]{1,0:T(8,128)(2,1)S(1)} %get-tuple-element.112), channel_id=1, source_target_pairs={{0,8},{1,9},{2,10},{3,11},{4,12},{5,13},{6,14},{7,15},{8,0},{9,1},... | collective-permute-start | bytes 196616 | tf_op jit(solution)/shard_map/ppermute | solution.py:53
  49.6 1.5 %collective-permute-start.19 = (bf16[256,128]{1,0:T(8,128)(2,1)S(1)}, bf16[256,128]{1,0:T(8,128)(2,1)S(1)}, u32[]{:S(2)}, u32[]{:S(2)}) collective-permute-start(bf16[256,128]{1,0:T(8,128)(2,1)S(1)} %get-tuple-element.113), channel_id=1, source_target_pairs={{0,12},{1,13},{2,14},{3,15},{4,0},{5,1},{6,2},{7,3},{8,4},{9,5},{1... | collective-permute-start | bytes 196616 | tf_op jit(solution)/shard_map/ppermute | solution.py:53
  51.1 1.7 %collective-permute-start.15 = (bf16[256,256]{1,0:T(8,128)(2,1)S(1)}, bf16[256,256]{1,0:T(8,128)(2,1)S(1)}, u32[]{:S(2)}, u32[]{:S(2)}) collective-permute-start(bf16[256,256]{1,0:T(8,128)(2,1)S(1)} %get-tuple-element.105), channel_id=1, source_target_pairs={{0,2},{1,3},{2,0},{3,1},{4,6},{5,7},{6,4},{7,5},{8,10},{9,11},{10,... | collective-permute-start | bytes 393224 | tf_op jit(solution)/shard_map/ppermute | solution.py:44
  53.1 1.4 %collective-permute-done.18.refs_2_ = bf16[256,128]{1,0:T(8,128)(2,1)S(1)} collective-permute-done((bf16[256,128]{1,0:T(8,128)(2,1)S(1)}, bf16[256,128]{1,0:T(8,128)(2,1)S(1)}, u32[]{:S(2)}, u32[]{:S(2)}) %collective-permute-start.18) | collective-permute-done | bytes 65568 | tf_op jit(solution)/shard_map/ppermute | solution.py:53
  54.7 1.2 %collective-permute-done.20.other = bf16[64,256]{1,0:T(8,128)(2,1)S(1)} collective-permute-done((bf16[64,256]{1,0:T(8,128)(2,1)S(1)}, bf16[64,256]{1,0:T(8,128)(2,1)S(1)}, u32[]{:S(2)}, u32[]{:S(2)}) %collective-permute-start.20) | collective-permute-done | bytes 32800 | tf_op jit(solution)/shard_map/ppermute | solution.py:44
  55.9 1.6 %collective-permute-start.21 = (bf16[64,512]{1,0:T(8,128)(2,1)S(1)}, bf16[64,512]{1,0:T(8,128)(2,1)S(1)}, u32[]{:S(2)}, u32[]{:S(2)}) collective-permute-start(bf16[64,512]{1,0:T(8,128)(2,1)S(1)} %shard_map.126.own), channel_id=1, source_target_pairs={{0,16},{16,0},{1,17},{17,1},{2,18},{18,2},{3,19},{19,3},{4,20},{20... | collective-permute-start | bytes 196616 | tf_op jit(solution)/shard_map/ppermute | solution.py:488
  57.5 2.2 %collective-permute-done.15.i2 = bf16[256,256]{1,0:T(8,128)(2,1)S(1)} collective-permute-done((bf16[256,256]{1,0:T(8,128)(2,1)S(1)}, bf16[256,256]{1,0:T(8,128)(2,1)S(1)}, u32[]{:S(2)}, u32[]{:S(2)}) %collective-permute-start.15) | collective-permute-done | bytes 131104 | tf_op jit(solution)/shard_map/ppermute | solution.py:44
  59.7 0.9 %shard_map.122 = (bf16[256,512]{1,0:T(8,128)(2,1)}, bf16[256,512]{1,0:T(8,128)(2,1)}) custom-call(bf16[256,256]{1,0:T(8,128)(2,1)S(1)} %get-tuple-element.99.i0, bf16[256,256]{1,0:T(8,128)(2,1)S(1)} %collective-permute-done.14.i1, bf16[256,256]{1,0:T(8,128)(2,1)S(1)} %collective-permute-done.15.i2, bf16[256,256]{1,0:T(8,128)(2,1)S(1)} %collective-permute-done.16.i3), custom_call_target="tpu_custom_call" | custom-call | flops 575000000 | tf_op jit(solution)/shard_map/pallas_call | solution.py:24
  60.6 0.7 %shard_map.127 = (bf16[64,512]{1,0:T(8,128)(2,1)}, bf16[64,512]{1,0:T(8,128)(2,1)}) custom-call(bf16[64,512]{1,0:T(8,128)(2,1)S(1)} %shard_map.126.own, bf16[64,512]{1,0:T(8,128)(2,1)S(1)} %collective-permute-done.21.other), custom_call_target="tpu_custom_call" | custom-call | flops 575000000 | tf_op jit(solution)/shard_map/pallas_call | solution.py:24
  (35 shorter events, 3.2 us)
Async XLA Ops:
  0.6 4.8 %collective-permute-start = (bf16[256,1024]{1,0:T(8,128)(2,1)}, bf16[256,1024]{1,0:T(8,128)(2,1)S(1)}, u32[]{:S(2)}, u32[]{:S(2)}) collective-permute-start(bf16[256,1024]{1,0:T(8,128)(2,1)} %bitcast.5), channel_id=1, source_target_pairs={{0,1},{1,0},{2,3},{3,2},{4,5},{5,4},{6,7},{7,6},{8,9},{9,8},{10,11... | collective-permute-start | bytes 1572872 | tf_op jit(solution)/shard_map/ppermute | solution.py:44
  1.1 15.4 %collective-permute-start.1 = (bf16[256,1024]{1,0:T(8,128)(2,1)}, bf16[256,1024]{1,0:T(8,128)(2,1)S(1)}, u32[]{:S(2)}, u32[]{:S(2)}) collective-permute-start(bf16[256,1024]{1,0:T(8,128)(2,1)} %bitcast.6), channel_id=1, source_target_pairs={{0,2},{1,3},{2,0},{3,1},{4,6},{5,7},{6,4},{7,5},{8,10},{9,11},{10,... | collective-permute-start | bytes 1572872 | tf_op jit(solution)/shard_map/ppermute | solution.py:44
  3.7 1.8 %copy-start.2 = (bf16[1,256,1024]{2,1,0:T(8,128)(2,1)S(1)}, bf16[1,256,1024]{2,1,0:T(8,128)(2,1)}, u32[]{:S(2)}) copy-start(bf16[1,256,1024]{2,1,0:T(8,128)(2,1)} %param.8) | copy-start | bytes 1572868
  5.2 1.4 %collective-permute-start.2 = (bf16[256,256]{1,0:T(8,128)(2,1)S(1)}, bf16[256,256]{1,0:T(8,128)(2,1)S(1)}, u32[]{:S(2)}, u32[]{:S(2)}) collective-permute-start(bf16[256,256]{1,0:T(8,128)(2,1)S(1)} %get-tuple-element.65), channel_id=1, source_target_pairs={{0,1},{1,0},{2,3},{3,2},{4,5},{5,4},{6,7},{7,6},{8,9},{9,8},{10,11... | collective-permute-start | bytes 393224 | tf_op jit(solution)/shard_map/ppermute | solution.py:44
  6.7 9.9 %collective-permute-start.3 = (bf16[256,256]{1,0:T(8,128)(2,1)S(1)}, bf16[256,256]{1,0:T(8,128)(2,1)S(1)}, u32[]{:S(2)}, u32[]{:S(2)}) collective-permute-start(bf16[256,256]{1,0:T(8,128)(2,1)S(1)} %get-tuple-element.66), channel_id=1, source_target_pairs={{0,4},{1,5},{2,14},{3,15},{4,8},{5,9},{6,2},{7,3},{8,12},{9,13},{1... | collective-permute-start | bytes 393224 | tf_op jit(solution)/shard_map/ppermute | solution.py:53
  8.4 2.9 %copy-start = (s32[1,8]{1,0:T(1,128)S(1)}, s32[1,8]{1,0:T(1,128)}, u32[]{:S(2)}) copy-start(s32[1,8]{1,0:T(1,128)} %len_ref.7) | copy-start | bytes 100
  8.4 2.9 %copy-start.1 = (s32[1,32]{1,0:T(1,128)S(1)}, s32[1,32]{1,0:T(1,128)}, u32[]{:S(2)}) copy-start(s32[1,32]{1,0:T(1,128)} %keep_ref.7) | copy-start | bytes 388
  8.4 13.7 %collective-permute-start.7 = (bf16[512,256]{1,0:T(8,128)(2,1)S(1)}, bf16[512,256]{1,0:T(8,128)(2,1)S(1)}, u32[]{:S(2)}, u32[]{:S(2)}) collective-permute-start(bf16[512,256]{1,0:T(8,128)(2,1)S(1)} %get-tuple-element.78), channel_id=1, source_target_pairs={{0,12},{1,13},{2,6},{3,7},{4,0},{5,1},{6,10},{7,11},{8,4},{9,5},{1... | collective-permute-start | bytes 786440 | tf_op jit(solution)/shard_map/ppermute | solution.py:53
  13.2 8.9 %collective-permute-start.8 = (bf16[256,256]{1,0:T(8,128)(2,1)S(1)}, bf16[256,256]{1,0:T(8,128)(2,1)S(1)}, u32[]{:S(2)}, u32[]{:S(2)}) collective-permute-start(bf16[256,256]{1,0:T(8,128)(2,1)S(1)} %get-tuple-element.82), channel_id=1, source_target_pairs={{0,3},{1,2},{2,1},{3,0},{4,7},{5,6},{6,5},{7,4},{8,11},{9,10},{10,... | collective-permute-start | bytes 393224 | tf_op jit(solution)/shard_map/ppermute | solution.py:44
  13.2 8.8 %collective-permute-start.6 = (bf16[256,256]{1,0:T(8,128)(2,1)S(1)}, bf16[256,256]{1,0:T(8,128)(2,1)S(1)}, u32[]{:S(2)}, u32[]{:S(2)}) collective-permute-start(bf16[256,256]{1,0:T(8,128)(2,1)S(1)} %get-tuple-element.77), channel_id=1, source_target_pairs={{0,2},{1,3},{2,0},{3,1},{4,6},{5,7},{6,4},{7,5},{8,10},{9,11},{10,... | collective-permute-start | bytes 393224 | tf_op jit(solution)/shard_map/ppermute | solution.py:44
  17.0 1.3 %collective-permute-start.4 = (bf16[256,128]{1,0:T(8,128)(2,1)S(1)}, bf16[256,128]{1,0:T(8,128)(2,1)S(1)}, u32[]{:S(2)}, u32[]{:S(2)}) collective-permute-start(bf16[256,128]{1,0:T(8,128)(2,1)S(1)} %get-tuple-element.74), channel_id=1, source_target_pairs={{0,1},{1,0},{2,3},{3,2},{4,5},{5,4},{6,7},{7,6},{8,9},{9,8},{10,11... | collective-permute-start | bytes 196616 | tf_op jit(solution)/shard_map/ppermute | solution.py:44
  17.1 1.4 %collective-permute-start.5 = (bf16[256,128]{1,0:T(8,128)(2,1)S(1)}, bf16[256,128]{1,0:T(8,128)(2,1)S(1)}, u32[]{:S(2)}, u32[]{:S(2)}) collective-permute-start(bf16[256,128]{1,0:T(8,128)(2,1)S(1)} %get-tuple-element.75), channel_id=1, source_target_pairs={{0,1},{1,0},{2,3},{3,2},{4,5},{5,4},{6,7},{7,6},{8,9},{9,8},{10,11... | collective-permute-start | bytes 196616 | tf_op jit(solution)/shard_map/ppermute | solution.py:44
  19.2 10.5 %collective-permute-start.9 = (bf16[528,128]{1,0:T(8,128)(2,1)S(1)}, bf16[528,128]{1,0:T(8,128)(2,1)S(1)}, u32[]{:S(2)}, u32[]{:S(2)}) collective-permute-start(bf16[528,128]{1,0:T(8,128)(2,1)S(1)} %get-tuple-element.79), channel_id=1, source_target_pairs={{0,4},{1,5},{2,14},{3,15},{4,8},{5,9},{6,2},{7,3},{8,12},{9,13},{1... | collective-permute-start | bytes 405512 | tf_op jit(solution)/shard_map/ppermute | solution.py:53
  22.1 10.0 %collective-permute-start.10 = (bf16[512,128]{1,0:T(8,128)(2,1)S(1)}, bf16[512,128]{1,0:T(8,128)(2,1)S(1)}, u32[]{:S(2)}, u32[]{:S(2)}) collective-permute-start(bf16[512,128]{1,0:T(8,128)(2,1)S(1)} %get-tuple-element.83), channel_id=1, source_target_pairs={{0,4},{1,5},{2,14},{3,15},{4,8},{5,9},{6,2},{7,3},{8,12},{9,13},{1... | collective-permute-start | bytes 393224 | tf_op jit(solution)/shard_map/ppermute | solution.py:53
  24.0 9.8 %collective-permute-start.11 = (bf16[256,256]{1,0:T(8,128)(2,1)S(1)}, bf16[256,256]{1,0:T(8,128)(2,1)S(1)}, u32[]{:S(2)}, u32[]{:S(2)}) collective-permute-start(bf16[256,256]{1,0:T(8,128)(2,1)S(1)} %get-tuple-element.89), channel_id=1, source_target_pairs={{0,12},{1,13},{2,6},{3,7},{4,0},{5,1},{6,10},{7,11},{8,4},{9,5},{1... | collective-permute-start | bytes 393224 | tf_op jit(solution)/shard_map/ppermute | solution.py:53
  32.1 4.7 %collective-permute-start.12 = (bf16[256,1024]{1,0:T(8,128)(2,1)S(1)}, bf16[256,1024]{1,0:T(8,128)(2,1)S(1)}, u32[]{:S(2)}, u32[]{:S(2)}) collective-permute-start(bf16[256,1024]{1,0:T(8,128)(2,1)S(1)} %collective-permute-done.1.rows_ref.e2), channel_id=1, source_target_pairs={{0,1},{1,0},{2,3},{3,2},{4,5},{5,4},{6,7},{7,6},{8,9},{9,8},{10,11... | collective-permute-start | bytes 1572872 | tf_op jit(solution)/shard_map/ppermute | solution.py:44
  37.4 9.2 %collective-permute-start.13 = (bf16[1024,128]{1,0:T(8,128)(2,1)S(1)}, bf16[1024,128]{1,0:T(8,128)(2,1)S(1)}, u32[]{:S(2)}, u32[]{:S(2)}) collective-permute-start(bf16[1024,128]{1,0:T(8,128)(2,1)S(1)} %shard_map.121), channel_id=1, source_target_pairs={{0,18},{1,19},{2,16},{3,17},{4,22},{5,23},{6,20},{7,21},{8,26},{9,... | collective-permute-start | bytes 786440 | tf_op jit(solution)/shard_map/ppermute | solution.py:474
  46.6 6.5 %collective-permute-start.17 = (bf16[256,128]{1,0:T(8,128)(2,1)S(1)}, bf16[256,128]{1,0:T(8,128)(2,1)S(1)}, u32[]{:S(2)}, u32[]{:S(2)}) collective-permute-start(bf16[256,128]{1,0:T(8,128)(2,1)S(1)} %get-tuple-element.111), channel_id=1, source_target_pairs={{0,4},{1,5},{2,6},{3,7},{4,8},{5,9},{6,10},{7,11},{8,12},{9,13},{1... | collective-permute-start | bytes 196616 | tf_op jit(solution)/shard_map/ppermute | solution.py:53
  47.2 7.3 %collective-permute-start.18 = (bf16[256,128]{1,0:T(8,128)(2,1)S(1)}, bf16[256,128]{1,0:T(8,128)(2,1)S(1)}, u32[]{:S(2)}, u32[]{:S(2)}) collective-permute-start(bf16[256,128]{1,0:T(8,128)(2,1)S(1)} %get-tuple-element.112), channel_id=1, source_target_pairs={{0,8},{1,9},{2,10},{3,11},{4,12},{5,13},{6,14},{7,15},{8,0},{9,1},... | collective-permute-start | bytes 196616 | tf_op jit(solution)/shard_map/ppermute | solution.py:53
  49.6 4.9 %collective-permute-start.19 = (bf16[256,128]{1,0:T(8,128)(2,1)S(1)}, bf16[256,128]{1,0:T(8,128)(2,1)S(1)}, u32[]{:S(2)}, u32[]{:S(2)}) collective-permute-start(bf16[256,128]{1,0:T(8,128)(2,1)S(1)} %get-tuple-element.113), channel_id=1, source_target_pairs={{0,12},{1,13},{2,14},{3,15},{4,0},{5,1},{6,2},{7,3},{8,4},{9,5},{1... | collective-permute-start | bytes 196616 | tf_op jit(solution)/shard_map/ppermute | solution.py:53
  51.1 6.4 %collective-permute-start.16 = (bf16[256,256]{1,0:T(8,128)(2,1)S(1)}, bf16[256,256]{1,0:T(8,128)(2,1)S(1)}, u32[]{:S(2)}, u32[]{:S(2)}) collective-permute-start(bf16[256,256]{1,0:T(8,128)(2,1)S(1)} %get-tuple-element.107), channel_id=1, source_target_pairs={{0,3},{1,2},{2,1},{3,0},{4,7},{5,6},{6,5},{7,4},{8,11},{9,10},{10,... | collective-permute-start | bytes 393224 | tf_op jit(solution)/shard_map/ppermute | solution.py:44
  51.1 8.6 %collective-permute-start.15 = (bf16[256,256]{1,0:T(8,128)(2,1)S(1)}, bf16[256,256]{1,0:T(8,128)(2,1)S(1)}, u32[]{:S(2)}, u32[]{:S(2)}) collective-permute-start(bf16[256,256]{1,0:T(8,128)(2,1)S(1)} %get-tuple-element.105), channel_id=1, source_target_pairs={{0,2},{1,3},{2,0},{3,1},{4,6},{5,7},{6,4},{7,5},{8,10},{9,11},{10,... | collective-permute-start | bytes 393224 | tf_op jit(solution)/shard_map/ppermute | solution.py:44
  53.1 6.7 %collective-permute-start.14 = (bf16[256,256]{1,0:T(8,128)(2,1)S(1)}, bf16[256,256]{1,0:T(8,128)(2,1)S(1)}, u32[]{:S(2)}, u32[]{:S(2)}) collective-permute-start(bf16[256,256]{1,0:T(8,128)(2,1)S(1)} %get-tuple-element.103), channel_id=1, source_target_pairs={{0,1},{1,0},{2,3},{3,2},{4,5},{5,4},{6,7},{7,6},{8,9},{9,8},{10,11... | collective-permute-start | bytes 393224 | tf_op jit(solution)/shard_map/ppermute | solution.py:44
  54.7 1.3 %collective-permute-start.20 = (bf16[64,256]{1,0:T(8,128)(2,1)S(1)}, bf16[64,256]{1,0:T(8,128)(2,1)S(1)}, u32[]{:S(2)}, u32[]{:S(2)}) collective-permute-start(bf16[64,256]{1,0:T(8,128)(2,1)S(1)} %get-tuple-element.115), channel_id=1, source_target_pairs={{0,1},{1,0},{2,3},{3,2},{4,5},{5,4},{6,7},{7,6},{8,9},{9,8},{10,11... | collective-permute-start | bytes 98312 | tf_op jit(solution)/shard_map/ppermute | solution.py:44
  55.9 4.7 %collective-permute-start.21 = (bf16[64,512]{1,0:T(8,128)(2,1)S(1)}, bf16[64,512]{1,0:T(8,128)(2,1)S(1)}, u32[]{:S(2)}, u32[]{:S(2)}) collective-permute-start(bf16[64,512]{1,0:T(8,128)(2,1)S(1)} %shard_map.126.own), channel_id=1, source_target_pairs={{0,16},{16,0},{1,17},{17,1},{2,18},{18,2},{3,19},{19,3},{4,20},{20... | collective-permute-start | bytes 196616 | tf_op jit(solution)/shard_map/ppermute | solution.py:488

commit v9 on v8

--- a/solution.py
+++ b/solution.py
@@ -203,7 +203,7 @@
     own, len_ref, shift_ref, keep_ref, k_ref, q_ref, v_ref, o_ref, big, small,
     out_t, dq_t, dk, dv,
 ):
-    rows = small[0].shape[0]
+    rows = k_ref.shape[0] // GROUP
     span = GROUP - 1
     total = rows * lax.axis_size("ctx")
     shift = shift_ref[0]
@@ -247,13 +247,17 @@
 
     @pl.when(keys_big)
     def _():
-        before(big, 1, range(1, span))
-        behind(small, span - 1, [span - 1])
+        if big:
+            before(big, 1, range(1, span))
+        if small:
+            behind(small, span - 1, [span - 1])
 
     @pl.when(jnp.logical_not(keys_big))
     def _():
-        before(small, 0, [0])
-        behind(big, 0, range(span - 1))
+        if small:
+            before(small, 0, [0])
+        if big:
+            behind(big, 0, range(span - 1))
 
 
 def square(own_row, shift, total, len_ref, keep_ref, pairs, out_t, dq_t, dk, dv, at):
@@ -360,14 +364,23 @@
     )
 
 
+def big_halo_kernel(
+    len_ref, shift_ref, keep_ref, k_ref, q_ref, v_ref, o_ref, big_kq, big_vo, *refs
+):
+    rows = k_ref.shape[0] // GROUP
+    cross_pairs(
+        False, len_ref, shift_ref, keep_ref, k_ref, q_ref, v_ref, o_ref,
+        (big_kq.at[: 2 * rows, :], big_vo), (), *refs[4:],
+    )
+
+
 def outer_kernel(
-    len_ref, shift_ref, keep_ref, k_ref, q_ref, v_ref, o_ref, big_kq, big_vo, small,
-    *refs,
+    len_ref, shift_ref, keep_ref, k_ref, q_ref, v_ref, o_ref, small, *refs
 ):
     out_t, dq_t, dk, dv, s0, s1, s2, s3, dqk = refs[4:]
     cross_pairs(
-        False, len_ref, shift_ref, keep_ref, k_ref, q_ref, v_ref, o_ref,
-        (big_kq, big_vo), (small,), out_t, dq_t, dk, dv,
+        False, len_ref, shift_ref, keep_ref, k_ref, q_ref, v_ref, o_ref, (), (small,),
+        out_t, dq_t, dk, dv,
     )
     rows = small.shape[0]
     me = place()
@@ -588,15 +601,23 @@
         aliases={9: 0, 10: 1, 11: 2, 12: 3},
         busy=5,
     )
+    held = call(
+        big_halo_kernel,
+        sums,
+        (*info, k, q, v, o, *other[:2], *held),
+        specs=[SMEM] * 3 + [VMEM] * 10,
+        aliases={9: 0, 10: 1, 11: 2, 12: 3},
+        busy=4,
+    )
     *_, p0, p1, p2, p3, dqk = call(
         outer_kernel,
         sums + [pair] * GROUP + [like(2 * HD, all_rows)],
-        (*info, k, q, v, o, *other, *held),
-        specs=[SMEM] * 3 + [VMEM] * 11,
-        aliases={10: 0, 11: 1, 12: 2, 13: 3},
-        busy=6,
-    )
-    e3 = partner(after(e2, *held), 1)
+        (*info, k, q, v, o, other[2], *held),
+        specs=[SMEM] * 3 + [VMEM] * 9,
+        aliases={8: 0, 9: 1, 10: 2, 11: 3},
+        busy=2,
+    )
+    e3 = partner(after(e2, kq2), 1)
     share = width // count
     reduce = direct_reduce if paired() else general_reduce
     reached, (grad_wq, grad_wk) = reduce(dqk, (local, e1, e2, e3), share)

time: 61.5 us -> 60.3 us (0.980)
  waiting for transfers between devices: 18 us -> 14.4 us
  starting transfers between devices: 25 us -> 26.7 us
  Pallas kernels: 16.7 us -> 17.5 us
    ppermute x8, waiting for transfers between devices: 3.41 us -> 1.38 us  [around(): return lax.ppermute(value, 'ctx', pairs)]
    ppermute x1, waiting for transfers between devices: 6.86 us -> 5.73 us  [direct_reduce(): got = lax.ppermute(give, ('dp', 'ctx'), across)]
    ppermute x8, starting transfers between devices: 14.5 us -> 15.5 us  [around(): return lax.ppermute(value, 'ctx', pairs)]
    ppermute x12, waiting for transfers between devices: 7.78 us -> 6.85 us  [partner(): return lax.ppermute(value, 'ctx', [(i, i ^ steps) for i in range(count)])]
    pallas_call x17 -> x18, Pallas kernels: 16.7 us -> 17.5 us  [call(): pl.pallas_call(kernel, out_shape=tuple(outs), in_specs=specs or [VMEM] *...]
    ppermute x1, starting transfers between devices: 1.78 us -> 2.45 us  [direct_reduce(): got = lax.ppermute(give, ('dp', 'ctx'), across)]
  transfers between devices with their start and end apart: 22 -> 22, of which waited for: 11 -> 11; matrix products, arithmetic and copies ran while one was open for 0% -> 0% of each run, Pallas kernels for 25% -> 27%
where the time goes in v9:
time: 60.3 us; the launch traced here: 60.1 us
  starting transfers between devices  26.7 us (44%)
  Pallas kernels  17.5 us (29%)
  waiting for transfers between devices  14.4 us (24%)
  between operations  1.48 us (2%)
    pallas_call x18, Pallas kernels, call(): pl.pallas_call(kernel, out_shape=tuple(outs), in_specs=specs or [VMEM] *...  17.5 us
    ppermute x8, starting transfers between devices, around(): return lax.ppermute(value, 'ctx', pairs)  15.5 us
    ppermute x12, starting transfers between devices, partner(): return lax.ppermute(value, 'ctx', [(i, i ^ steps) for i in range(count)])  7.29 us
    ppermute x12, waiting for transfers between devices, partner(): return lax.ppermute(value, 'ctx', [(i, i ^ steps) for i in range(count)])  6.85 us
    ppermute x1, waiting for transfers between devices, direct_reduce(): got = lax.ppermute(give, ('dp', 'ctx'), across)  5.73 us
    ppermute x1, starting transfers between devices, direct_reduce(): got = lax.ppermute(give, ('dp', 'ctx'), across)  2.45 us
    ppermute x1, starting transfers between devices, direct_reduce(): other = lax.ppermute(both, 'dp', [(0, 1), (1, 0)])  1.52 us
    ppermute x8, waiting for transfers between devices, around(): return lax.ppermute(value, 'ctx', pairs)  1.38 us
  transfers between devices with their start and end apart: 22, of which 11 were waited for; matrix products, arithmetic and copies ran while one was open for 0% of the time, Pallas kernels for 27%

profile of v9, /device:TPU:0, one launch (start us, length us, event | category | flops | bytes accessed | tf_op | source)
XLA Modules:
  0.0 60.1 jit_solution(5117581580805741036)
XLA Ops:
  1.1 2.6 %collective-permute-start.1 = (bf16[256,1024]{1,0:T(8,128)(2,1)}, bf16[256,1024]{1,0:T(8,128)(2,1)S(1)}, u32[]{:S(2)}, u32[]{:S(2)}) collective-permute-start(bf16[256,1024]{1,0:T(8,128)(2,1)} %bitcast.6), channel_id=1, source_target_pairs={{0,2},{1,3},{2,0},{3,1},{4,6},{5,7},{6,4},{7,5},{8,10},{9,11},{10,... | collective-permute-start | bytes 1572872 | tf_op jit(solution)/shard_map/ppermute | solution.py:44
  3.7 1.5 %shard_map.111 = (bf16[256,256]{1,0:T(8,128)(2,1)S(1)}, bf16[256,256]{1,0:T(8,128)(2,1)S(1)}, bf16[256,256]{1,0:T(8,128)(2,1)S(1)}, bf16[256,256]{1,0:T(8,128)(2,1)S(1)}, bf16[1024,512]{1,0:T(8,128)(2,1)S(1)}) custom-call(bf16[256,512]{1,0:T(8,128)(2,1)} %bitcast.10, bf16[256,512]{1,0:T(8,128)(2,1)} %bitcast.11, bf16[1024,512]{1,0:T(8,128)(2,1)} %wk_ref.1, ...), custom_call_target="tpu_custom_call" | custom-call | flops 115000000 | tf_op jit(solution)/shard_map/pallas_call | solution.py:24
  5.9 0.7 %collective-permute-done.2.refs_3_.b1 = bf16[256,256]{1,0:T(8,128)(2,1)S(1)} collective-permute-done((bf16[256,256]{1,0:T(8,128)(2,1)S(1)}, bf16[256,256]{1,0:T(8,128)(2,1)S(1)}, u32[]{:S(2)}, u32[]{:S(2)}) %collective-permute-start.2) | collective-permute-done | bytes 131104 | tf_op jit(solution)/shard_map/ppermute | solution.py:44
  6.7 1.6 %collective-permute-start.3 = (bf16[256,256]{1,0:T(8,128)(2,1)S(1)}, bf16[256,256]{1,0:T(8,128)(2,1)S(1)}, u32[]{:S(2)}, u32[]{:S(2)}) collective-permute-start(bf16[256,256]{1,0:T(8,128)(2,1)S(1)} %get-tuple-element.70), channel_id=1, source_target_pairs={{0,4},{1,5},{2,14},{3,15},{4,8},{5,9},{6,2},{7,3},{8,12},{9,13},{1... | collective-permute-start | bytes 393224 | tf_op jit(solution)/shard_map/ppermute | solution.py:53
  8.4 2.2 %collective-permute-start.7 = (bf16[512,256]{1,0:T(8,128)(2,1)S(1)}, bf16[512,256]{1,0:T(8,128)(2,1)S(1)}, u32[]{:S(2)}, u32[]{:S(2)}) collective-permute-start(bf16[512,256]{1,0:T(8,128)(2,1)S(1)} %get-tuple-element.82), channel_id=1, source_target_pairs={{0,12},{1,13},{2,6},{3,7},{4,0},{5,1},{6,10},{7,11},{8,4},{9,5},{1... | collective-permute-start | bytes 786440 | tf_op jit(solution)/shard_map/ppermute | solution.py:53
  11.3 1.9 %shard_map.114 = (f32[128,512]{1,0:T(8,128)S(1)}, f32[128,512]{1,0:T(8,128)S(1)}, f32[512,128]{1,0:T(8,128)S(1)}, f32[512,128]{1,0:T(8,128)S(1)}) custom-call(s32[1,8]{1,0:T(1,128)S(1)} %copy-done, s32[1]{0:T(128)S(6)} %copy.36.shift_ref, s32[1,32]{1,0:T(1,128)S(1)} %copy-done.1, bf16[256,256]{1,0:T(8,128)(2,1)S(1)} %get-tuple-element.71.refs_0_.a0, ...), custom_call_target="tpu_custom_call" | custom-call | flops 115000000 | tf_op jit(solution)/shard_map/pallas_call | solution.py:24
  13.2 1.4 %collective-permute-start.6 = (bf16[256,256]{1,0:T(8,128)(2,1)S(1)}, bf16[256,256]{1,0:T(8,128)(2,1)S(1)}, u32[]{:S(2)}, u32[]{:S(2)}) collective-permute-start(bf16[256,256]{1,0:T(8,128)(2,1)S(1)} %get-tuple-element.81), channel_id=1, source_target_pairs={{0,2},{1,3},{2,0},{3,1},{4,6},{5,7},{6,4},{7,5},{8,10},{9,11},{10,... | collective-permute-start | bytes 393224 | tf_op jit(solution)/shard_map/ppermute | solution.py:44
  14.6 2.0 %collective-permute-done.1.rows_ref.e2 = bf16[256,1024]{1,0:T(8,128)(2,1)S(1)} collective-permute-done((bf16[256,1024]{1,0:T(8,128)(2,1)}, bf16[256,1024]{1,0:T(8,128)(2,1)S(1)}, u32[]{:S(2)}, u32[]{:S(2)}) %collective-permute-start.1) | collective-permute-done | bytes 524320 | tf_op jit(solution)/shard_map/ppermute | solution.py:44
  17.6 0.7 %collective-permute-done.4.refs_1_.a3_k = bf16[256,128]{1,0:T(8,128)(2,1)S(1)} collective-permute-done((bf16[256,128]{1,0:T(8,128)(2,1)S(1)}, bf16[256,128]{1,0:T(8,128)(2,1)S(1)}, u32[]{:S(2)}, u32[]{:S(2)}) %collective-permute-start.4) | collective-permute-done | bytes 65568 | tf_op jit(solution)/shard_map/ppermute | solution.py:44
  18.5 0.7 %shard_map.116 = (bf16[528,128]{1,0:T(8,128)(2,1)S(1)}, bf16[256,128]{1,0:T(8,128)(2,1)}) custom-call(bf16[256,256]{1,0:T(8,128)(2,1)S(1)} %get-tuple-element.77.refs_0_.a2, bf16[256,128]{1,0:T(8,128)(2,1)S(1)} %collective-permute-done.4.refs_1_.a3_k, bf16[256,128]{1,0:T(8,128)(2,1)S(1)} %collective-permute-done.5.refs_2_.a3_q), custom_call_target="tpu_custom_call" | custom-call | flops 115000000 | tf_op jit(solution)/shard_map/pallas_call | solution.py:24
  19.2 2.1 %collective-permute-start.10 = (bf16[528,128]{1,0:T(8,128)(2,1)S(1)}, bf16[528,128]{1,0:T(8,128)(2,1)S(1)}, u32[]{:S(2)}, u32[]{:S(2)}) collective-permute-start(bf16[528,128]{1,0:T(8,128)(2,1)S(1)} %get-tuple-element.83), channel_id=1, source_target_pairs={{0,4},{1,5},{2,14},{3,15},{4,8},{5,9},{6,2},{7,3},{8,12},{9,13},{1... | collective-permute-start | bytes 405512 | tf_op jit(solution)/shard_map/ppermute | solution.py:53
  21.3 0.7 %collective-permute-done.6.refs_3_.b2 = bf16[256,256]{1,0:T(8,128)(2,1)S(1)} collective-permute-done((bf16[256,256]{1,0:T(8,128)(2,1)S(1)}, bf16[256,256]{1,0:T(8,128)(2,1)S(1)}, u32[]{:S(2)}, u32[]{:S(2)}) %collective-permute-start.6) | collective-permute-done | bytes 131104 | tf_op jit(solution)/shard_map/ppermute | solution.py:44
  22.1 1.9 %collective-permute-start.11 = (bf16[512,128]{1,0:T(8,128)(2,1)S(1)}, bf16[512,128]{1,0:T(8,128)(2,1)S(1)}, u32[]{:S(2)}, u32[]{:S(2)}) collective-permute-start(bf16[512,128]{1,0:T(8,128)(2,1)S(1)} %get-tuple-element.87), channel_id=1, source_target_pairs={{0,4},{1,5},{2,14},{3,15},{4,8},{5,9},{6,2},{7,3},{8,12},{9,13},{1... | collective-permute-start | bytes 393224 | tf_op jit(solution)/shard_map/ppermute | solution.py:53
  24.0 2.1 %collective-permute-start.9 = (bf16[256,256]{1,0:T(8,128)(2,1)S(1)}, bf16[256,256]{1,0:T(8,128)(2,1)S(1)}, u32[]{:S(2)}, u32[]{:S(2)}) collective-permute-start(bf16[256,256]{1,0:T(8,128)(2,1)S(1)} %get-tuple-element.93), channel_id=1, source_target_pairs={{0,12},{1,13},{2,6},{3,7},{4,0},{5,1},{6,10},{7,11},{8,4},{9,5},{1... | collective-permute-start | bytes 393224 | tf_op jit(solution)/shard_map/ppermute | solution.py:53
  26.1 3.6 %shard_map.118 = (bf16[1024,128]{1,0:T(8,128)(2,1)S(1)}, bf16[1024,128]{1,0:T(8,128)(2,1)S(1)}, bf16[1024,128]{1,0:T(8,128)(2,1)S(1)}, bf16[1024,128]{1,0:T(8,12...) custom-call(s32[1,8]{1,0:T(1,128)S(1)} %copy-done, ...), custom_call_target="tpu_custom_call" | custom-call | flops 3449999872 | tf_op jit(solution)/shard_map/pallas_call | solution.py:24
  29.7 2.3 %shard_map.119 = (f32[128,1024]{1,0:T(8,128)S(1)}, f32[128,1024]{1,0:T(8,128)S(1)}, f32[1024,128]{1,0:T(8,128)S(1)}, f32[1024,128]{1,0:T(8,128)S(1)}) custom-call(s32[1,8]{1,0:T(1,128)S(1)} %copy-done, s32[1]{0:T(128)S(6)} %copy.36.shift_ref, s32[1,32]{1,0:T(1,128)S(1)} %copy-done.1, ...), custom_call_target="tpu_custom_call", output_to_operand_aliasing={{0}: (9, {}), {1}: (10, {}), {2}: (11, {}), {3}: (12, {})} | custom-call | flops 5750000128 | tf_op jit(solution)/shard_map/pallas_call | solution.py:24
  32.1 2.2 %shard_map.120 = (f32[128,1024]{1,0:T(8,128)S(1)}, f32[128,1024]{1,0:T(8,128)S(1)}, f32[1024,128]{1,0:T(8,128)S(1)}, f32[1024,128]{1,0:T(8,128)S(1)}) custom-call(s32[1,8]{1,0:T(1,128)S(1)} %copy-done, s32[1]{0:T(128)S(6)} %copy.36.shift_ref, s32[1,32]{1,0:T(1,128)S(1)} %copy-done.1, ...), custom_call_target="tpu_custom_call", output_to_operand_aliasing={{0}: (9, {}), {1}: (10, {}), {2}: (11, {}), {3}: (12, {})} | custom-call | flops 4600000000 | tf_op jit(solution)/shard_map/pallas_call | solution.py:24
  34.3 1.4 %shard_map.121 = (f32[128,1024]{1,0:T(8,128)S(1)}, f32[128,1024]{1,0:T(8,128)S(1)}, f32[1024,128]{1,0:T(8,128)S(1)}, f32[1024,128]{1,0:T(8,128)S(1)}, bf16[256,2...) custom-call(s32[1,8]{1,0:T(1,128)S(1)} %copy-done, ...), custom_call_target="tpu_custom_call", output_to_operand_aliasing={{0}: (8, {}), {1}: (9, {}), {2}: (10, {}), {3}: (11, {})} | custom-call | flops 2300000000 | tf_op jit(solution)/shard_map/pallas_call | solution.py:24
  35.7 0.6 shard_map.122
  36.3 2.4 %collective-permute-start.13 = (bf16[1024,128]{1,0:T(8,128)(2,1)S(1)}, bf16[1024,128]{1,0:T(8,128)(2,1)S(1)}, u32[]{:S(2)}, u32[]{:S(2)}) collective-permute-start(bf16[1024,128]{1,0:T(8,128)(2,1)S(1)} %shard_map.122), channel_id=1, source_target_pairs={{0,18},{1,19},{2,16},{3,17},{4,22},{5,23},{6,20},{7,21},{8,26},{9,... | collective-permute-start | bytes 786440 | tf_op jit(solution)/shard_map/ppermute | solution.py:487
  39.3 5.7 %collective-permute-done.13.other = bf16[1024,128]{1,0:T(8,128)(2,1)S(1)} collective-permute-done((bf16[1024,128]{1,0:T(8,128)(2,1)S(1)}, bf16[1024,128]{1,0:T(8,128)(2,1)S(1)}, u32[]{:S(2)}, u32[]{:S(2)}) %collective-permute-start.13) | collective-permute-done | bytes 262176 | tf_op jit(solution)/shard_map/ppermute | solution.py:487
  45.1 0.6 %collective-permute-start.17 = (bf16[256,128]{1,0:T(8,128)(2,1)S(1)}, bf16[256,128]{1,0:T(8,128)(2,1)S(1)}, u32[]{:S(2)}, u32[]{:S(2)}) collective-permute-start(bf16[256,128]{1,0:T(8,128)(2,1)S(1)} %get-tuple-element.119), channel_id=1, source_target_pairs={{0,4},{1,5},{2,6},{3,7},{4,8},{5,9},{6,10},{7,11},{8,12},{9,13},{1... | collective-permute-start | bytes 196616 | tf_op jit(solution)/shard_map/ppermute | solution.py:53
  45.7 3.5 %collective-permute-start.18 = (bf16[256,128]{1,0:T(8,128)(2,1)S(1)}, bf16[256,128]{1,0:T(8,128)(2,1)S(1)}, u32[]{:S(2)}, u32[]{:S(2)}) collective-permute-start(bf16[256,128]{1,0:T(8,128)(2,1)S(1)} %get-tuple-element.120), channel_id=1, source_target_pairs={{0,8},{1,9},{2,10},{3,11},{4,12},{5,13},{6,14},{7,15},{8,0},{9,1},... | collective-permute-start | bytes 196616 | tf_op jit(solution)/shard_map/ppermute | solution.py:53
  49.3 1.3 %collective-permute-start.19 = (bf16[256,128]{1,0:T(8,128)(2,1)S(1)}, bf16[256,128]{1,0:T(8,128)(2,1)S(1)}, u32[]{:S(2)}, u32[]{:S(2)}) collective-permute-start(bf16[256,128]{1,0:T(8,128)(2,1)S(1)} %get-tuple-element.121), channel_id=1, source_target_pairs={{0,12},{1,13},{2,14},{3,15},{4,0},{5,1},{6,2},{7,3},{8,4},{9,5},{1... | collective-permute-start | bytes 196616 | tf_op jit(solution)/shard_map/ppermute | solution.py:53
  50.6 0.9 %collective-permute-start.15 = (bf16[256,256]{1,0:T(8,128)(2,1)S(1)}, bf16[256,256]{1,0:T(8,128)(2,1)S(1)}, u32[]{:S(2)}, u32[]{:S(2)}) collective-permute-start(bf16[256,256]{1,0:T(8,128)(2,1)S(1)} %get-tuple-element.113), channel_id=1, source_target_pairs={{0,2},{1,3},{2,0},{3,1},{4,6},{5,7},{6,4},{7,5},{8,10},{9,11},{10,... | collective-permute-start | bytes 393224 | tf_op jit(solution)/shard_map/ppermute | solution.py:44
  51.6 0.8 %collective-permute-start.14 = (bf16[256,256]{1,0:T(8,128)(2,1)S(1)}, bf16[256,256]{1,0:T(8,128)(2,1)S(1)}, u32[]{:S(2)}, u32[]{:S(2)}) collective-permute-start(bf16[256,256]{1,0:T(8,128)(2,1)S(1)} %get-tuple-element.111), channel_id=1, source_target_pairs={{0,1},{1,0},{2,3},{3,2},{4,5},{5,4},{6,7},{7,6},{8,9},{9,8},{10,11... | collective-permute-start | bytes 393224 | tf_op jit(solution)/shard_map/ppermute | solution.py:44
  52.5 0.8 %collective-permute-done.18.refs_2_ = bf16[256,128]{1,0:T(8,128)(2,1)S(1)} collective-permute-done((bf16[256,128]{1,0:T(8,128)(2,1)S(1)}, bf16[256,128]{1,0:T(8,128)(2,1)S(1)}, u32[]{:S(2)}, u32[]{:S(2)}) %collective-permute-start.18) | collective-permute-done | bytes 65568 | tf_op jit(solution)/shard_map/ppermute | solution.py:53
  53.9 1.2 %collective-permute-done.20.other = bf16[64,256]{1,0:T(8,128)(2,1)S(1)} collective-permute-done((bf16[64,256]{1,0:T(8,128)(2,1)S(1)}, bf16[64,256]{1,0:T(8,128)(2,1)S(1)}, u32[]{:S(2)}, u32[]{:S(2)}) %collective-permute-start.20) | collective-permute-done | bytes 32800 | tf_op jit(solution)/shard_map/ppermute | solution.py:44
  55.1 1.5 %collective-permute-start.21 = (bf16[64,512]{1,0:T(8,128)(2,1)S(1)}, bf16[64,512]{1,0:T(8,128)(2,1)S(1)}, u32[]{:S(2)}, u32[]{:S(2)}) collective-permute-start(bf16[64,512]{1,0:T(8,128)(2,1)S(1)} %shard_map.127.own), channel_id=1, source_target_pairs={{0,16},{16,0},{1,17},{17,1},{2,18},{18,2},{3,19},{19,3},{4,20},{20... | collective-permute-start | bytes 196616 | tf_op jit(solution)/shard_map/ppermute | solution.py:501
  56.7 1.4 %collective-permute-done.15.i2 = bf16[256,256]{1,0:T(8,128)(2,1)S(1)} collective-permute-done((bf16[256,256]{1,0:T(8,128)(2,1)S(1)}, bf16[256,256]{1,0:T(8,128)(2,1)S(1)}, u32[]{:S(2)}, u32[]{:S(2)}) %collective-permute-start.15) | collective-permute-done | bytes 131104 | tf_op jit(solution)/shard_map/ppermute | solution.py:44
  58.1 0.9 %shard_map.123 = (bf16[256,512]{1,0:T(8,128)(2,1)}, bf16[256,512]{1,0:T(8,128)(2,1)}) custom-call(bf16[256,256]{1,0:T(8,128)(2,1)S(1)} %get-tuple-element.107.i0, bf16[256,256]{1,0:T(8,128)(2,1)S(1)} %collective-permute-done.14.i1, bf16[256,256]{1,0:T(8,128)(2,1)S(1)} %collective-permute-done.15.i2, bf16[256,256]{1,0:T(8,128)(2,1)S(1)} %collective-permute-done.16.i3), custom_call_target="tpu_custom_call" | custom-call | flops 575000000 | tf_op jit(solution)/shard_map/pallas_call | solution.py:24
  59.5 0.7 %shard_map.128 = (bf16[64,512]{1,0:T(8,128)(2,1)}, bf16[64,512]{1,0:T(8,128)(2,1)}) custom-call(bf16[64,512]{1,0:T(8,128)(2,1)S(1)} %shard_map.127.own, bf16[64,512]{1,0:T(8,128)(2,1)S(1)} %collective-permute-done.21.other), custom_call_target="tpu_custom_call" | custom-call | flops 575000000 | tf_op jit(solution)/shard_map/pallas_call | solution.py:24
  (36 shorter events, 4.5 us)
Async XLA Ops:
  0.6 4.8 %collective-permute-start = (bf16[256,1024]{1,0:T(8,128)(2,1)}, bf16[256,1024]{1,0:T(8,128)(2,1)S(1)}, u32[]{:S(2)}, u32[]{:S(2)}) collective-permute-start(bf16[256,1024]{1,0:T(8,128)(2,1)} %bitcast.5), channel_id=1, source_target_pairs={{0,1},{1,0},{2,3},{3,2},{4,5},{5,4},{6,7},{7,6},{8,9},{9,8},{10,11... | collective-permute-start | bytes 1572872 | tf_op jit(solution)/shard_map/ppermute | solution.py:44
  1.1 15.4 %collective-permute-start.1 = (bf16[256,1024]{1,0:T(8,128)(2,1)}, bf16[256,1024]{1,0:T(8,128)(2,1)S(1)}, u32[]{:S(2)}, u32[]{:S(2)}) collective-permute-start(bf16[256,1024]{1,0:T(8,128)(2,1)} %bitcast.6), channel_id=1, source_target_pairs={{0,2},{1,3},{2,0},{3,1},{4,6},{5,7},{6,4},{7,5},{8,10},{9,11},{10,... | collective-permute-start | bytes 1572872 | tf_op jit(solution)/shard_map/ppermute | solution.py:44
  3.7 1.8 %copy-start.2 = (bf16[1,256,1024]{2,1,0:T(8,128)(2,1)S(1)}, bf16[1,256,1024]{2,1,0:T(8,128)(2,1)}, u32[]{:S(2)}) copy-start(bf16[1,256,1024]{2,1,0:T(8,128)(2,1)} %param.8) | copy-start | bytes 1572868
  5.2 1.4 %collective-permute-start.2 = (bf16[256,256]{1,0:T(8,128)(2,1)S(1)}, bf16[256,256]{1,0:T(8,128)(2,1)S(1)}, u32[]{:S(2)}, u32[]{:S(2)}) collective-permute-start(bf16[256,256]{1,0:T(8,128)(2,1)S(1)} %get-tuple-element.69), channel_id=1, source_target_pairs={{0,1},{1,0},{2,3},{3,2},{4,5},{5,4},{6,7},{7,6},{8,9},{9,8},{10,11... | collective-permute-start | bytes 393224 | tf_op jit(solution)/shard_map/ppermute | solution.py:44
  6.7 9.9 %collective-permute-start.3 = (bf16[256,256]{1,0:T(8,128)(2,1)S(1)}, bf16[256,256]{1,0:T(8,128)(2,1)S(1)}, u32[]{:S(2)}, u32[]{:S(2)}) collective-permute-start(bf16[256,256]{1,0:T(8,128)(2,1)S(1)} %get-tuple-element.70), channel_id=1, source_target_pairs={{0,4},{1,5},{2,14},{3,15},{4,8},{5,9},{6,2},{7,3},{8,12},{9,13},{1... | collective-permute-start | bytes 393224 | tf_op jit(solution)/shard_map/ppermute | solution.py:53
  8.4 2.9 %copy-start = (s32[1,8]{1,0:T(1,128)S(1)}, s32[1,8]{1,0:T(1,128)}, u32[]{:S(2)}) copy-start(s32[1,8]{1,0:T(1,128)} %len_ref.9) | copy-start | bytes 100
  8.4 2.9 %copy-start.1 = (s32[1,32]{1,0:T(1,128)S(1)}, s32[1,32]{1,0:T(1,128)}, u32[]{:S(2)}) copy-start(s32[1,32]{1,0:T(1,128)} %keep_ref.9) | copy-start | bytes 388
  8.4 13.7 %collective-permute-start.7 = (bf16[512,256]{1,0:T(8,128)(2,1)S(1)}, bf16[512,256]{1,0:T(8,128)(2,1)S(1)}, u32[]{:S(2)}, u32[]{:S(2)}) collective-permute-start(bf16[512,256]{1,0:T(8,128)(2,1)S(1)} %get-tuple-element.82), channel_id=1, source_target_pairs={{0,12},{1,13},{2,6},{3,7},{4,0},{5,1},{6,10},{7,11},{8,4},{9,5},{1... | collective-permute-start | bytes 786440 | tf_op jit(solution)/shard_map/ppermute | solution.py:53
  13.2 8.9 %collective-permute-start.8 = (bf16[256,256]{1,0:T(8,128)(2,1)S(1)}, bf16[256,256]{1,0:T(8,128)(2,1)S(1)}, u32[]{:S(2)}, u32[]{:S(2)}) collective-permute-start(bf16[256,256]{1,0:T(8,128)(2,1)S(1)} %get-tuple-element.86), channel_id=1, source_target_pairs={{0,3},{1,2},{2,1},{3,0},{4,7},{5,6},{6,5},{7,4},{8,11},{9,10},{10,... | collective-permute-start | bytes 393224 | tf_op jit(solution)/shard_map/ppermute | solution.py:44
  13.2 8.8 %collective-permute-start.6 = (bf16[256,256]{1,0:T(8,128)(2,1)S(1)}, bf16[256,256]{1,0:T(8,128)(2,1)S(1)}, u32[]{:S(2)}, u32[]{:S(2)}) collective-permute-start(bf16[256,256]{1,0:T(8,128)(2,1)S(1)} %get-tuple-element.81), channel_id=1, source_target_pairs={{0,2},{1,3},{2,0},{3,1},{4,6},{5,7},{6,4},{7,5},{8,10},{9,11},{10,... | collective-permute-start | bytes 393224 | tf_op jit(solution)/shard_map/ppermute | solution.py:44
  17.0 1.3 %collective-permute-start.4 = (bf16[256,128]{1,0:T(8,128)(2,1)S(1)}, bf16[256,128]{1,0:T(8,128)(2,1)S(1)}, u32[]{:S(2)}, u32[]{:S(2)}) collective-permute-start(bf16[256,128]{1,0:T(8,128)(2,1)S(1)} %get-tuple-element.78), channel_id=1, source_target_pairs={{0,1},{1,0},{2,3},{3,2},{4,5},{5,4},{6,7},{7,6},{8,9},{9,8},{10,11... | collective-permute-start | bytes 196616 | tf_op jit(solution)/shard_map/ppermute | solution.py:44
  17.1 1.4 %collective-permute-start.5 = (bf16[256,128]{1,0:T(8,128)(2,1)S(1)}, bf16[256,128]{1,0:T(8,128)(2,1)S(1)}, u32[]{:S(2)}, u32[]{:S(2)}) collective-permute-start(bf16[256,128]{1,0:T(8,128)(2,1)S(1)} %get-tuple-element.79), channel_id=1, source_target_pairs={{0,1},{1,0},{2,3},{3,2},{4,5},{5,4},{6,7},{7,6},{8,9},{9,8},{10,11... | collective-permute-start | bytes 196616 | tf_op jit(solution)/shard_map/ppermute | solution.py:44
  18.4 17.4 %collective-permute-start.12 = (bf16[256,1024]{1,0:T(8,128)(2,1)S(1)}, bf16[256,1024]{1,0:T(8,128)(2,1)S(1)}, u32[]{:S(2)}, u32[]{:S(2)}) collective-permute-start(bf16[256,1024]{1,0:T(8,128)(2,1)S(1)} %collective-permute-done.1.rows_ref.e2), channel_id=1, source_target_pairs={{0,1},{1,0},{2,3},{3,2},{4,5},{5,4},{6,7},{7,6},{8,9},{9,8},{10,11... | collective-permute-start | bytes 1572872 | tf_op jit(solution)/shard_map/ppermute | solution.py:44
  19.2 10.5 %collective-permute-start.10 = (bf16[528,128]{1,0:T(8,128)(2,1)S(1)}, bf16[528,128]{1,0:T(8,128)(2,1)S(1)}, u32[]{:S(2)}, u32[]{:S(2)}) collective-permute-start(bf16[528,128]{1,0:T(8,128)(2,1)S(1)} %get-tuple-element.83), channel_id=1, source_target_pairs={{0,4},{1,5},{2,14},{3,15},{4,8},{5,9},{6,2},{7,3},{8,12},{9,13},{1... | collective-permute-start | bytes 405512 | tf_op jit(solution)/shard_map/ppermute | solution.py:53
  22.1 9.9 %collective-permute-start.11 = (bf16[512,128]{1,0:T(8,128)(2,1)S(1)}, bf16[512,128]{1,0:T(8,128)(2,1)S(1)}, u32[]{:S(2)}, u32[]{:S(2)}) collective-permute-start(bf16[512,128]{1,0:T(8,128)(2,1)S(1)} %get-tuple-element.87), channel_id=1, source_target_pairs={{0,4},{1,5},{2,14},{3,15},{4,8},{5,9},{6,2},{7,3},{8,12},{9,13},{1... | collective-permute-start | bytes 393224 | tf_op jit(solution)/shard_map/ppermute | solution.py:53
  24.0 10.3 %collective-permute-start.9 = (bf16[256,256]{1,0:T(8,128)(2,1)S(1)}, bf16[256,256]{1,0:T(8,128)(2,1)S(1)}, u32[]{:S(2)}, u32[]{:S(2)}) collective-permute-start(bf16[256,256]{1,0:T(8,128)(2,1)S(1)} %get-tuple-element.93), channel_id=1, source_target_pairs={{0,12},{1,13},{2,6},{3,7},{4,0},{5,1},{6,10},{7,11},{8,4},{9,5},{1... | collective-permute-start | bytes 393224 | tf_op jit(solution)/shard_map/ppermute | solution.py:53
  36.3 8.7 %collective-permute-start.13 = (bf16[1024,128]{1,0:T(8,128)(2,1)S(1)}, bf16[1024,128]{1,0:T(8,128)(2,1)S(1)}, u32[]{:S(2)}, u32[]{:S(2)}) collective-permute-start(bf16[1024,128]{1,0:T(8,128)(2,1)S(1)} %shard_map.122), channel_id=1, source_target_pairs={{0,18},{1,19},{2,16},{3,17},{4,22},{5,23},{6,20},{7,21},{8,26},{9,... | collective-permute-start | bytes 786440 | tf_op jit(solution)/shard_map/ppermute | solution.py:487
  45.1 6.5 %collective-permute-start.17 = (bf16[256,128]{1,0:T(8,128)(2,1)S(1)}, bf16[256,128]{1,0:T(8,128)(2,1)S(1)}, u32[]{:S(2)}, u32[]{:S(2)}) collective-permute-start(bf16[256,128]{1,0:T(8,128)(2,1)S(1)} %get-tuple-element.119), channel_id=1, source_target_pairs={{0,4},{1,5},{2,6},{3,7},{4,8},{5,9},{6,10},{7,11},{8,12},{9,13},{1... | collective-permute-start | bytes 196616 | tf_op jit(solution)/shard_map/ppermute | solution.py:53
  45.7 7.5 %collective-permute-start.18 = (bf16[256,128]{1,0:T(8,128)(2,1)S(1)}, bf16[256,128]{1,0:T(8,128)(2,1)S(1)}, u32[]{:S(2)}, u32[]{:S(2)}) collective-permute-start(bf16[256,128]{1,0:T(8,128)(2,1)S(1)} %get-tuple-element.120), channel_id=1, source_target_pairs={{0,8},{1,9},{2,10},{3,11},{4,12},{5,13},{6,14},{7,15},{8,0},{9,1},... | collective-permute-start | bytes 196616 | tf_op jit(solution)/shard_map/ppermute | solution.py:53
  49.3 4.5 %collective-permute-start.19 = (bf16[256,128]{1,0:T(8,128)(2,1)S(1)}, bf16[256,128]{1,0:T(8,128)(2,1)S(1)}, u32[]{:S(2)}, u32[]{:S(2)}) collective-permute-start(bf16[256,128]{1,0:T(8,128)(2,1)S(1)} %get-tuple-element.121), channel_id=1, source_target_pairs={{0,12},{1,13},{2,14},{3,15},{4,0},{5,1},{6,2},{7,3},{8,4},{9,5},{1... | collective-permute-start | bytes 196616 | tf_op jit(solution)/shard_map/ppermute | solution.py:53
  50.6 6.1 %collective-permute-start.16 = (bf16[256,256]{1,0:T(8,128)(2,1)S(1)}, bf16[256,256]{1,0:T(8,128)(2,1)S(1)}, u32[]{:S(2)}, u32[]{:S(2)}) collective-permute-start(bf16[256,256]{1,0:T(8,128)(2,1)S(1)} %get-tuple-element.115), channel_id=1, source_target_pairs={{0,3},{1,2},{2,1},{3,0},{4,7},{5,6},{6,5},{7,4},{8,11},{9,10},{10,... | collective-permute-start | bytes 393224 | tf_op jit(solution)/shard_map/ppermute | solution.py:44
  50.6 7.5 %collective-permute-start.15 = (bf16[256,256]{1,0:T(8,128)(2,1)S(1)}, bf16[256,256]{1,0:T(8,128)(2,1)S(1)}, u32[]{:S(2)}, u32[]{:S(2)}) collective-permute-start(bf16[256,256]{1,0:T(8,128)(2,1)S(1)} %get-tuple-element.113), channel_id=1, source_target_pairs={{0,2},{1,3},{2,0},{3,1},{4,6},{5,7},{6,4},{7,5},{8,10},{9,11},{10,... | collective-permute-start | bytes 393224 | tf_op jit(solution)/shard_map/ppermute | solution.py:44
  51.6 6.5 %collective-permute-start.14 = (bf16[256,256]{1,0:T(8,128)(2,1)S(1)}, bf16[256,256]{1,0:T(8,128)(2,1)S(1)}, u32[]{:S(2)}, u32[]{:S(2)}) collective-permute-start(bf16[256,256]{1,0:T(8,128)(2,1)S(1)} %get-tuple-element.111), channel_id=1, source_target_pairs={{0,1},{1,0},{2,3},{3,2},{4,5},{5,4},{6,7},{7,6},{8,9},{9,8},{10,11... | collective-permute-start | bytes 393224 | tf_op jit(solution)/shard_map/ppermute | solution.py:44
  53.8 1.3 %collective-permute-start.20 = (bf16[64,256]{1,0:T(8,128)(2,1)S(1)}, bf16[64,256]{1,0:T(8,128)(2,1)S(1)}, u32[]{:S(2)}, u32[]{:S(2)}) collective-permute-start(bf16[64,256]{1,0:T(8,128)(2,1)S(1)} %get-tuple-element.123), channel_id=1, source_target_pairs={{0,1},{1,0},{2,3},{3,2},{4,5},{5,4},{6,7},{7,6},{8,9},{9,8},{10,11... | collective-permute-start | bytes 98312 | tf_op jit(solution)/shard_map/ppermute | solution.py:44
  55.1 4.3 %collective-permute-start.21 = (bf16[64,512]{1,0:T(8,128)(2,1)S(1)}, bf16[64,512]{1,0:T(8,128)(2,1)S(1)}, u32[]{:S(2)}, u32[]{:S(2)}) collective-permute-start(bf16[64,512]{1,0:T(8,128)(2,1)S(1)} %shard_map.127.own), channel_id=1, source_target_pairs={{0,16},{16,0},{1,17},{17,1},{2,18},{18,2},{3,19},{19,3},{4,20},{20... | collective-permute-start | bytes 196616 | tf_op jit(solution)/shard_map/ppermute | solution.py:501

commit v10 on v9

--- a/solution.py
+++ b/solution.py
@@ -572,7 +572,7 @@
     k3, q3 = partner(give[0], 1), partner(give[1], 1)
     big_kq, _ = call(
         functools.partial(edge_kernel, False, 0),
-        [like(2 * rows + 16, HD), like(rows, HD)],
+        [like(2 * rows, HD), like(rows, HD)],
         (kq2, k3, q3),
         busy=0.1,
     )

time: 60.3 us -> 60.2 us (level)
  no operation moved by 1% of the time
where the time goes in v10:
time: 60.2 us; the launch traced here: 60 us
  starting transfers between devices  26.7 us (44%)
  Pallas kernels  17.4 us (29%)
  waiting for transfers between devices  14.4 us (24%)
  between operations  1.48 us (2%)
    pallas_call x18, Pallas kernels, call(): pl.pallas_call(kernel, out_shape=tuple(outs), in_specs=specs or [VMEM] *...  17.4 us
    ppermute x8, starting transfers between devices, around(): return lax.ppermute(value, 'ctx', pairs)  15.5 us
    ppermute x12, starting transfers between devices, partner(): return lax.ppermute(value, 'ctx', [(i, i ^ steps) for i in range(count)])  7.31 us
    ppermute x12, waiting for transfers between devices, partner(): return lax.ppermute(value, 'ctx', [(i, i ^ steps) for i in range(count)])  6.89 us
    ppermute x1, waiting for transfers between devices, direct_reduce(): got = lax.ppermute(give, ('dp', 'ctx'), across)  5.72 us
    ppermute x1, starting transfers between devices, direct_reduce(): got = lax.ppermute(give, ('dp', 'ctx'), across)  2.42 us
    ppermute x1, starting transfers between devices, direct_reduce(): other = lax.ppermute(both, 'dp', [(0, 1), (1, 0)])  1.55 us
    ppermute x8, waiting for transfers between devices, around(): return lax.ppermute(value, 'ctx', pairs)  1.34 us
  transfers between devices with their start and end apart: 22, of which 11 were waited for; matrix products, arithmetic and copies ran while one was open for 0% of the time, Pallas kernels for 27%

profile of v10, /device:TPU:0, one launch (start us, length us, event | category | flops | bytes accessed | tf_op | source)
XLA Modules:
  0.0 60.0 jit_solution(15238701150448809576)
XLA Ops:
  1.1 2.6 %collective-permute-start.1 = (bf16[256,1024]{1,0:T(8,128)(2,1)}, bf16[256,1024]{1,0:T(8,128)(2,1)S(1)}, u32[]{:S(2)}, u32[]{:S(2)}) collective-permute-start(bf16[256,1024]{1,0:T(8,128)(2,1)} %bitcast.6), channel_id=1, source_target_pairs={{0,2},{1,3},{2,0},{3,1},{4,6},{5,7},{6,4},{7,5},{8,10},{9,11},{10,... | collective-permute-start | bytes 1572872 | tf_op jit(solution)/shard_map/ppermute | solution.py:44
  3.7 1.5 %shard_map.111 = (bf16[256,256]{1,0:T(8,128)(2,1)S(1)}, bf16[256,256]{1,0:T(8,128)(2,1)S(1)}, bf16[256,256]{1,0:T(8,128)(2,1)S(1)}, bf16[256,256]{1,0:T(8,128)(2,1)S(1)}, bf16[1024,512]{1,0:T(8,128)(2,1)S(1)}) custom-call(bf16[256,512]{1,0:T(8,128)(2,1)} %bitcast.10, bf16[256,512]{1,0:T(8,128)(2,1)} %bitcast.11, bf16[1024,512]{1,0:T(8,128)(2,1)} %wk_ref.1, ...), custom_call_target="tpu_custom_call" | custom-call | flops 115000000 | tf_op jit(solution)/shard_map/pallas_call | solution.py:24
  5.9 0.7 %collective-permute-done.2.refs_3_.b1 = bf16[256,256]{1,0:T(8,128)(2,1)S(1)} collective-permute-done((bf16[256,256]{1,0:T(8,128)(2,1)S(1)}, bf16[256,256]{1,0:T(8,128)(2,1)S(1)}, u32[]{:S(2)}, u32[]{:S(2)}) %collective-permute-start.2) | collective-permute-done | bytes 131104 | tf_op jit(solution)/shard_map/ppermute | solution.py:44
  6.7 1.6 %collective-permute-start.3 = (bf16[256,256]{1,0:T(8,128)(2,1)S(1)}, bf16[256,256]{1,0:T(8,128)(2,1)S(1)}, u32[]{:S(2)}, u32[]{:S(2)}) collective-permute-start(bf16[256,256]{1,0:T(8,128)(2,1)S(1)} %get-tuple-element.70), channel_id=1, source_target_pairs={{0,4},{1,5},{2,14},{3,15},{4,8},{5,9},{6,2},{7,3},{8,12},{9,13},{1... | collective-permute-start | bytes 393224 | tf_op jit(solution)/shard_map/ppermute | solution.py:53
  8.4 2.2 %collective-permute-start.7 = (bf16[512,256]{1,0:T(8,128)(2,1)S(1)}, bf16[512,256]{1,0:T(8,128)(2,1)S(1)}, u32[]{:S(2)}, u32[]{:S(2)}) collective-permute-start(bf16[512,256]{1,0:T(8,128)(2,1)S(1)} %get-tuple-element.82), channel_id=1, source_target_pairs={{0,12},{1,13},{2,6},{3,7},{4,0},{5,1},{6,10},{7,11},{8,4},{9,5},{1... | collective-permute-start | bytes 786440 | tf_op jit(solution)/shard_map/ppermute | solution.py:53
  11.3 1.9 %shard_map.114 = (f32[128,512]{1,0:T(8,128)S(1)}, f32[128,512]{1,0:T(8,128)S(1)}, f32[512,128]{1,0:T(8,128)S(1)}, f32[512,128]{1,0:T(8,128)S(1)}) custom-call(s32[1,8]{1,0:T(1,128)S(1)} %copy-done, s32[1]{0:T(128)S(6)} %copy.36.shift_ref, s32[1,32]{1,0:T(1,128)S(1)} %copy-done.1, bf16[256,256]{1,0:T(8,128)(2,1)S(1)} %get-tuple-element.71.refs_0_.a0, ...), custom_call_target="tpu_custom_call" | custom-call | flops 115000000 | tf_op jit(solution)/shard_map/pallas_call | solution.py:24
  13.2 1.4 %collective-permute-start.6 = (bf16[256,256]{1,0:T(8,128)(2,1)S(1)}, bf16[256,256]{1,0:T(8,128)(2,1)S(1)}, u32[]{:S(2)}, u32[]{:S(2)}) collective-permute-start(bf16[256,256]{1,0:T(8,128)(2,1)S(1)} %get-tuple-element.81), channel_id=1, source_target_pairs={{0,2},{1,3},{2,0},{3,1},{4,6},{5,7},{6,4},{7,5},{8,10},{9,11},{10,... | collective-permute-start | bytes 393224 | tf_op jit(solution)/shard_map/ppermute | solution.py:44
  14.6 2.0 %collective-permute-done.1.rows_ref.e2 = bf16[256,1024]{1,0:T(8,128)(2,1)S(1)} collective-permute-done((bf16[256,1024]{1,0:T(8,128)(2,1)}, bf16[256,1024]{1,0:T(8,128)(2,1)S(1)}, u32[]{:S(2)}, u32[]{:S(2)}) %collective-permute-start.1) | collective-permute-done | bytes 524320 | tf_op jit(solution)/shard_map/ppermute | solution.py:44
  17.6 0.7 %collective-permute-done.4.refs_1_.a3_k = bf16[256,128]{1,0:T(8,128)(2,1)S(1)} collective-permute-done((bf16[256,128]{1,0:T(8,128)(2,1)S(1)}, bf16[256,128]{1,0:T(8,128)(2,1)S(1)}, u32[]{:S(2)}, u32[]{:S(2)}) %collective-permute-start.4) | collective-permute-done | bytes 65568 | tf_op jit(solution)/shard_map/ppermute | solution.py:44
  18.5 0.7 %shard_map.116 = (bf16[512,128]{1,0:T(8,128)(2,1)S(1)}, bf16[256,128]{1,0:T(8,128)(2,1)}) custom-call(bf16[256,256]{1,0:T(8,128)(2,1)S(1)} %get-tuple-element.77.refs_0_.a2, bf16[256,128]{1,0:T(8,128)(2,1)S(1)} %collective-permute-done.4.refs_1_.a3_k, bf16[256,128]{1,0:T(8,128)(2,1)S(1)} %collective-permute-done.5.refs_2_.a3_q), custom_call_target="tpu_custom_call" | custom-call | flops 115000000 | tf_op jit(solution)/shard_map/pallas_call | solution.py:24
  19.2 2.1 %collective-permute-start.10 = (bf16[512,128]{1,0:T(8,128)(2,1)S(1)}, bf16[512,128]{1,0:T(8,128)(2,1)S(1)}, u32[]{:S(2)}, u32[]{:S(2)}) collective-permute-start(bf16[512,128]{1,0:T(8,128)(2,1)S(1)} %get-tuple-element.83), channel_id=1, source_target_pairs={{0,4},{1,5},{2,14},{3,15},{4,8},{5,9},{6,2},{7,3},{8,12},{9,13},{1... | collective-permute-start | bytes 393224 | tf_op jit(solution)/shard_map/ppermute | solution.py:53
  21.3 0.7 %collective-permute-done.6.refs_3_.b2 = bf16[256,256]{1,0:T(8,128)(2,1)S(1)} collective-permute-done((bf16[256,256]{1,0:T(8,128)(2,1)S(1)}, bf16[256,256]{1,0:T(8,128)(2,1)S(1)}, u32[]{:S(2)}, u32[]{:S(2)}) %collective-permute-start.6) | collective-permute-done | bytes 131104 | tf_op jit(solution)/shard_map/ppermute | solution.py:44
  22.1 1.9 %collective-permute-start.11 = (bf16[512,128]{1,0:T(8,128)(2,1)S(1)}, bf16[512,128]{1,0:T(8,128)(2,1)S(1)}, u32[]{:S(2)}, u32[]{:S(2)}) collective-permute-start(bf16[512,128]{1,0:T(8,128)(2,1)S(1)} %get-tuple-element.87), channel_id=1, source_target_pairs={{0,4},{1,5},{2,14},{3,15},{4,8},{5,9},{6,2},{7,3},{8,12},{9,13},{1... | collective-permute-start | bytes 393224 | tf_op jit(solution)/shard_map/ppermute | solution.py:53
  24.0 2.1 %collective-permute-start.9 = (bf16[256,256]{1,0:T(8,128)(2,1)S(1)}, bf16[256,256]{1,0:T(8,128)(2,1)S(1)}, u32[]{:S(2)}, u32[]{:S(2)}) collective-permute-start(bf16[256,256]{1,0:T(8,128)(2,1)S(1)} %get-tuple-element.93), channel_id=1, source_target_pairs={{0,12},{1,13},{2,6},{3,7},{4,0},{5,1},{6,10},{7,11},{8,4},{9,5},{1... | collective-permute-start | bytes 393224 | tf_op jit(solution)/shard_map/ppermute | solution.py:53
  26.1 3.5 %shard_map.118 = (bf16[1024,128]{1,0:T(8,128)(2,1)S(1)}, bf16[1024,128]{1,0:T(8,128)(2,1)S(1)}, bf16[1024,128]{1,0:T(8,128)(2,1)S(1)}, bf16[1024,128]{1,0:T(8,12...) custom-call(s32[1,8]{1,0:T(1,128)S(1)} %copy-done, ...), custom_call_target="tpu_custom_call" | custom-call | flops 3449999872 | tf_op jit(solution)/shard_map/pallas_call | solution.py:24
  29.7 2.3 %shard_map.119 = (f32[128,1024]{1,0:T(8,128)S(1)}, f32[128,1024]{1,0:T(8,128)S(1)}, f32[1024,128]{1,0:T(8,128)S(1)}, f32[1024,128]{1,0:T(8,128)S(1)}) custom-call(s32[1,8]{1,0:T(1,128)S(1)} %copy-done, s32[1]{0:T(128)S(6)} %copy.36.shift_ref, s32[1,32]{1,0:T(1,128)S(1)} %copy-done.1, ...), custom_call_target="tpu_custom_call", output_to_operand_aliasing={{0}: (9, {}), {1}: (10, {}), {2}: (11, {}), {3}: (12, {})} | custom-call | flops 5750000128 | tf_op jit(solution)/shard_map/pallas_call | solution.py:24
  32.1 2.2 %shard_map.120 = (f32[128,1024]{1,0:T(8,128)S(1)}, f32[128,1024]{1,0:T(8,128)S(1)}, f32[1024,128]{1,0:T(8,128)S(1)}, f32[1024,128]{1,0:T(8,128)S(1)}) custom-call(s32[1,8]{1,0:T(1,128)S(1)} %copy-done, s32[1]{0:T(128)S(6)} %copy.36.shift_ref, s32[1,32]{1,0:T(1,128)S(1)} %copy-done.1, ...), custom_call_target="tpu_custom_call", output_to_operand_aliasing={{0}: (9, {}), {1}: (10, {}), {2}: (11, {}), {3}: (12, {})} | custom-call | flops 4600000000 | tf_op jit(solution)/shard_map/pallas_call | solution.py:24
  34.3 1.4 %shard_map.121 = (f32[128,1024]{1,0:T(8,128)S(1)}, f32[128,1024]{1,0:T(8,128)S(1)}, f32[1024,128]{1,0:T(8,128)S(1)}, f32[1024,128]{1,0:T(8,128)S(1)}, bf16[256,2...) custom-call(s32[1,8]{1,0:T(1,128)S(1)} %copy-done, ...), custom_call_target="tpu_custom_call", output_to_operand_aliasing={{0}: (8, {}), {1}: (9, {}), {2}: (10, {}), {3}: (11, {})} | custom-call | flops 2300000000 | tf_op jit(solution)/shard_map/pallas_call | solution.py:24
  35.7 0.6 shard_map.122
  36.3 2.4 %collective-permute-start.13 = (bf16[1024,128]{1,0:T(8,128)(2,1)S(1)}, bf16[1024,128]{1,0:T(8,128)(2,1)S(1)}, u32[]{:S(2)}, u32[]{:S(2)}) collective-permute-start(bf16[1024,128]{1,0:T(8,128)(2,1)S(1)} %shard_map.122), channel_id=1, source_target_pairs={{0,18},{1,19},{2,16},{3,17},{4,22},{5,23},{6,20},{7,21},{8,26},{9,... | collective-permute-start | bytes 786440 | tf_op jit(solution)/shard_map/ppermute | solution.py:487
  39.3 5.7 %collective-permute-done.13.other = bf16[1024,128]{1,0:T(8,128)(2,1)S(1)} collective-permute-done((bf16[1024,128]{1,0:T(8,128)(2,1)S(1)}, bf16[1024,128]{1,0:T(8,128)(2,1)S(1)}, u32[]{:S(2)}, u32[]{:S(2)}) %collective-permute-start.13) | collective-permute-done | bytes 262176 | tf_op jit(solution)/shard_map/ppermute | solution.py:487
  45.0 0.6 %collective-permute-start.17 = (bf16[256,128]{1,0:T(8,128)(2,1)S(1)}, bf16[256,128]{1,0:T(8,128)(2,1)S(1)}, u32[]{:S(2)}, u32[]{:S(2)}) collective-permute-start(bf16[256,128]{1,0:T(8,128)(2,1)S(1)} %get-tuple-element.119), channel_id=1, source_target_pairs={{0,4},{1,5},{2,6},{3,7},{4,8},{5,9},{6,10},{7,11},{8,12},{9,13},{1... | collective-permute-start | bytes 196616 | tf_op jit(solution)/shard_map/ppermute | solution.py:53
  45.7 3.5 %collective-permute-start.18 = (bf16[256,128]{1,0:T(8,128)(2,1)S(1)}, bf16[256,128]{1,0:T(8,128)(2,1)S(1)}, u32[]{:S(2)}, u32[]{:S(2)}) collective-permute-start(bf16[256,128]{1,0:T(8,128)(2,1)S(1)} %get-tuple-element.120), channel_id=1, source_target_pairs={{0,8},{1,9},{2,10},{3,11},{4,12},{5,13},{6,14},{7,15},{8,0},{9,1},... | collective-permute-start | bytes 196616 | tf_op jit(solution)/shard_map/ppermute | solution.py:53
  49.1 1.3 %collective-permute-start.19 = (bf16[256,128]{1,0:T(8,128)(2,1)S(1)}, bf16[256,128]{1,0:T(8,128)(2,1)S(1)}, u32[]{:S(2)}, u32[]{:S(2)}) collective-permute-start(bf16[256,128]{1,0:T(8,128)(2,1)S(1)} %get-tuple-element.121), channel_id=1, source_target_pairs={{0,12},{1,13},{2,14},{3,15},{4,0},{5,1},{6,2},{7,3},{8,4},{9,5},{1... | collective-permute-start | bytes 196616 | tf_op jit(solution)/shard_map/ppermute | solution.py:53
  50.5 0.9 %collective-permute-start.15 = (bf16[256,256]{1,0:T(8,128)(2,1)S(1)}, bf16[256,256]{1,0:T(8,128)(2,1)S(1)}, u32[]{:S(2)}, u32[]{:S(2)}) collective-permute-start(bf16[256,256]{1,0:T(8,128)(2,1)S(1)} %get-tuple-element.113), channel_id=1, source_target_pairs={{0,2},{1,3},{2,0},{3,1},{4,6},{5,7},{6,4},{7,5},{8,10},{9,11},{10,... | collective-permute-start | bytes 393224 | tf_op jit(solution)/shard_map/ppermute | solution.py:44
  51.5 0.8 %collective-permute-start.14 = (bf16[256,256]{1,0:T(8,128)(2,1)S(1)}, bf16[256,256]{1,0:T(8,128)(2,1)S(1)}, u32[]{:S(2)}, u32[]{:S(2)}) collective-permute-start(bf16[256,256]{1,0:T(8,128)(2,1)S(1)} %get-tuple-element.111), channel_id=1, source_target_pairs={{0,1},{1,0},{2,3},{3,2},{4,5},{5,4},{6,7},{7,6},{8,9},{9,8},{10,11... | collective-permute-start | bytes 393224 | tf_op jit(solution)/shard_map/ppermute | solution.py:44
  52.4 0.8 %collective-permute-done.18.refs_2_ = bf16[256,128]{1,0:T(8,128)(2,1)S(1)} collective-permute-done((bf16[256,128]{1,0:T(8,128)(2,1)S(1)}, bf16[256,128]{1,0:T(8,128)(2,1)S(1)}, u32[]{:S(2)}, u32[]{:S(2)}) %collective-permute-start.18) | collective-permute-done | bytes 65568 | tf_op jit(solution)/shard_map/ppermute | solution.py:53
  53.8 1.2 %collective-permute-done.20.other = bf16[64,256]{1,0:T(8,128)(2,1)S(1)} collective-permute-done((bf16[64,256]{1,0:T(8,128)(2,1)S(1)}, bf16[64,256]{1,0:T(8,128)(2,1)S(1)}, u32[]{:S(2)}, u32[]{:S(2)}) %collective-permute-start.20) | collective-permute-done | bytes 32800 | tf_op jit(solution)/shard_map/ppermute | solution.py:44
  55.0 1.5 %collective-permute-start.21 = (bf16[64,512]{1,0:T(8,128)(2,1)S(1)}, bf16[64,512]{1,0:T(8,128)(2,1)S(1)}, u32[]{:S(2)}, u32[]{:S(2)}) collective-permute-start(bf16[64,512]{1,0:T(8,128)(2,1)S(1)} %shard_map.127.own), channel_id=1, source_target_pairs={{0,16},{16,0},{1,17},{17,1},{2,18},{18,2},{3,19},{19,3},{4,20},{20... | collective-permute-start | bytes 196616 | tf_op jit(solution)/shard_map/ppermute | solution.py:501
  56.5 1.5 %collective-permute-done.15.i2 = bf16[256,256]{1,0:T(8,128)(2,1)S(1)} collective-permute-done((bf16[256,256]{1,0:T(8,128)(2,1)S(1)}, bf16[256,256]{1,0:T(8,128)(2,1)S(1)}, u32[]{:S(2)}, u32[]{:S(2)}) %collective-permute-start.15) | collective-permute-done | bytes 131104 | tf_op jit(solution)/shard_map/ppermute | solution.py:44
  58.0 0.9 %shard_map.123 = (bf16[256,512]{1,0:T(8,128)(2,1)}, bf16[256,512]{1,0:T(8,128)(2,1)}) custom-call(bf16[256,256]{1,0:T(8,128)(2,1)S(1)} %get-tuple-element.107.i0, bf16[256,256]{1,0:T(8,128)(2,1)S(1)} %collective-permute-done.14.i1, bf16[256,256]{1,0:T(8,128)(2,1)S(1)} %collective-permute-done.15.i2, bf16[256,256]{1,0:T(8,128)(2,1)S(1)} %collective-permute-done.16.i3), custom_call_target="tpu_custom_call" | custom-call | flops 575000000 | tf_op jit(solution)/shard_map/pallas_call | solution.py:24
  59.3 0.7 %shard_map.128 = (bf16[64,512]{1,0:T(8,128)(2,1)}, bf16[64,512]{1,0:T(8,128)(2,1)}) custom-call(bf16[64,512]{1,0:T(8,128)(2,1)S(1)} %shard_map.127.own, bf16[64,512]{1,0:T(8,128)(2,1)S(1)} %collective-permute-done.21.other), custom_call_target="tpu_custom_call" | custom-call | flops 575000000 | tf_op jit(solution)/shard_map/pallas_call | solution.py:24
  (36 shorter events, 4.4 us)
Async XLA Ops:
  0.6 4.8 %collective-permute-start = (bf16[256,1024]{1,0:T(8,128)(2,1)}, bf16[256,1024]{1,0:T(8,128)(2,1)S(1)}, u32[]{:S(2)}, u32[]{:S(2)}) collective-permute-start(bf16[256,1024]{1,0:T(8,128)(2,1)} %bitcast.5), channel_id=1, source_target_pairs={{0,1},{1,0},{2,3},{3,2},{4,5},{5,4},{6,7},{7,6},{8,9},{9,8},{10,11... | collective-permute-start | bytes 1572872 | tf_op jit(solution)/shard_map/ppermute | solution.py:44
  1.1 15.4 %collective-permute-start.1 = (bf16[256,1024]{1,0:T(8,128)(2,1)}, bf16[256,1024]{1,0:T(8,128)(2,1)S(1)}, u32[]{:S(2)}, u32[]{:S(2)}) collective-permute-start(bf16[256,1024]{1,0:T(8,128)(2,1)} %bitcast.6), channel_id=1, source_target_pairs={{0,2},{1,3},{2,0},{3,1},{4,6},{5,7},{6,4},{7,5},{8,10},{9,11},{10,... | collective-permute-start | bytes 1572872 | tf_op jit(solution)/shard_map/ppermute | solution.py:44
  3.7 1.8 %copy-start.2 = (bf16[1,256,1024]{2,1,0:T(8,128)(2,1)S(1)}, bf16[1,256,1024]{2,1,0:T(8,128)(2,1)}, u32[]{:S(2)}) copy-start(bf16[1,256,1024]{2,1,0:T(8,128)(2,1)} %param.8) | copy-start | bytes 1572868
  5.2 1.4 %collective-permute-start.2 = (bf16[256,256]{1,0:T(8,128)(2,1)S(1)}, bf16[256,256]{1,0:T(8,128)(2,1)S(1)}, u32[]{:S(2)}, u32[]{:S(2)}) collective-permute-start(bf16[256,256]{1,0:T(8,128)(2,1)S(1)} %get-tuple-element.69), channel_id=1, source_target_pairs={{0,1},{1,0},{2,3},{3,2},{4,5},{5,4},{6,7},{7,6},{8,9},{9,8},{10,11... | collective-permute-start | bytes 393224 | tf_op jit(solution)/shard_map/ppermute | solution.py:44
  6.7 9.9 %collective-permute-start.3 = (bf16[256,256]{1,0:T(8,128)(2,1)S(1)}, bf16[256,256]{1,0:T(8,128)(2,1)S(1)}, u32[]{:S(2)}, u32[]{:S(2)}) collective-permute-start(bf16[256,256]{1,0:T(8,128)(2,1)S(1)} %get-tuple-element.70), channel_id=1, source_target_pairs={{0,4},{1,5},{2,14},{3,15},{4,8},{5,9},{6,2},{7,3},{8,12},{9,13},{1... | collective-permute-start | bytes 393224 | tf_op jit(solution)/shard_map/ppermute | solution.py:53
  8.4 2.9 %copy-start = (s32[1,8]{1,0:T(1,128)S(1)}, s32[1,8]{1,0:T(1,128)}, u32[]{:S(2)}) copy-start(s32[1,8]{1,0:T(1,128)} %len_ref.9) | copy-start | bytes 100
  8.4 2.9 %copy-start.1 = (s32[1,32]{1,0:T(1,128)S(1)}, s32[1,32]{1,0:T(1,128)}, u32[]{:S(2)}) copy-start(s32[1,32]{1,0:T(1,128)} %keep_ref.9) | copy-start | bytes 388
  8.4 13.7 %collective-permute-start.7 = (bf16[512,256]{1,0:T(8,128)(2,1)S(1)}, bf16[512,256]{1,0:T(8,128)(2,1)S(1)}, u32[]{:S(2)}, u32[]{:S(2)}) collective-permute-start(bf16[512,256]{1,0:T(8,128)(2,1)S(1)} %get-tuple-element.82), channel_id=1, source_target_pairs={{0,12},{1,13},{2,6},{3,7},{4,0},{5,1},{6,10},{7,11},{8,4},{9,5},{1... | collective-permute-start | bytes 786440 | tf_op jit(solution)/shard_map/ppermute | solution.py:53
  13.2 8.9 %collective-permute-start.8 = (bf16[256,256]{1,0:T(8,128)(2,1)S(1)}, bf16[256,256]{1,0:T(8,128)(2,1)S(1)}, u32[]{:S(2)}, u32[]{:S(2)}) collective-permute-start(bf16[256,256]{1,0:T(8,128)(2,1)S(1)} %get-tuple-element.86), channel_id=1, source_target_pairs={{0,3},{1,2},{2,1},{3,0},{4,7},{5,6},{6,5},{7,4},{8,11},{9,10},{10,... | collective-permute-start | bytes 393224 | tf_op jit(solution)/shard_map/ppermute | solution.py:44
  13.2 8.8 %collective-permute-start.6 = (bf16[256,256]{1,0:T(8,128)(2,1)S(1)}, bf16[256,256]{1,0:T(8,128)(2,1)S(1)}, u32[]{:S(2)}, u32[]{:S(2)}) collective-permute-start(bf16[256,256]{1,0:T(8,128)(2,1)S(1)} %get-tuple-element.81), channel_id=1, source_target_pairs={{0,2},{1,3},{2,0},{3,1},{4,6},{5,7},{6,4},{7,5},{8,10},{9,11},{10,... | collective-permute-start | bytes 393224 | tf_op jit(solution)/shard_map/ppermute | solution.py:44
  17.0 1.3 %collective-permute-start.4 = (bf16[256,128]{1,0:T(8,128)(2,1)S(1)}, bf16[256,128]{1,0:T(8,128)(2,1)S(1)}, u32[]{:S(2)}, u32[]{:S(2)}) collective-permute-start(bf16[256,128]{1,0:T(8,128)(2,1)S(1)} %get-tuple-element.78), channel_id=1, source_target_pairs={{0,1},{1,0},{2,3},{3,2},{4,5},{5,4},{6,7},{7,6},{8,9},{9,8},{10,11... | collective-permute-start | bytes 196616 | tf_op jit(solution)/shard_map/ppermute | solution.py:44
  17.1 1.4 %collective-permute-start.5 = (bf16[256,128]{1,0:T(8,128)(2,1)S(1)}, bf16[256,128]{1,0:T(8,128)(2,1)S(1)}, u32[]{:S(2)}, u32[]{:S(2)}) collective-permute-start(bf16[256,128]{1,0:T(8,128)(2,1)S(1)} %get-tuple-element.79), channel_id=1, source_target_pairs={{0,1},{1,0},{2,3},{3,2},{4,5},{5,4},{6,7},{7,6},{8,9},{9,8},{10,11... | collective-permute-start | bytes 196616 | tf_op jit(solution)/shard_map/ppermute | solution.py:44
  18.4 17.3 %collective-permute-start.12 = (bf16[256,1024]{1,0:T(8,128)(2,1)S(1)}, bf16[256,1024]{1,0:T(8,128)(2,1)S(1)}, u32[]{:S(2)}, u32[]{:S(2)}) collective-permute-start(bf16[256,1024]{1,0:T(8,128)(2,1)S(1)} %collective-permute-done.1.rows_ref.e2), channel_id=1, source_target_pairs={{0,1},{1,0},{2,3},{3,2},{4,5},{5,4},{6,7},{7,6},{8,9},{9,8},{10,11... | collective-permute-start | bytes 1572872 | tf_op jit(solution)/shard_map/ppermute | solution.py:44
  19.2 10.5 %collective-permute-start.10 = (bf16[512,128]{1,0:T(8,128)(2,1)S(1)}, bf16[512,128]{1,0:T(8,128)(2,1)S(1)}, u32[]{:S(2)}, u32[]{:S(2)}) collective-permute-start(bf16[512,128]{1,0:T(8,128)(2,1)S(1)} %get-tuple-element.83), channel_id=1, source_target_pairs={{0,4},{1,5},{2,14},{3,15},{4,8},{5,9},{6,2},{7,3},{8,12},{9,13},{1... | collective-permute-start | bytes 393224 | tf_op jit(solution)/shard_map/ppermute | solution.py:53
  22.1 9.9 %collective-permute-start.11 = (bf16[512,128]{1,0:T(8,128)(2,1)S(1)}, bf16[512,128]{1,0:T(8,128)(2,1)S(1)}, u32[]{:S(2)}, u32[]{:S(2)}) collective-permute-start(bf16[512,128]{1,0:T(8,128)(2,1)S(1)} %get-tuple-element.87), channel_id=1, source_target_pairs={{0,4},{1,5},{2,14},{3,15},{4,8},{5,9},{6,2},{7,3},{8,12},{9,13},{1... | collective-permute-start | bytes 393224 | tf_op jit(solution)/shard_map/ppermute | solution.py:53
  24.0 10.2 %collective-permute-start.9 = (bf16[256,256]{1,0:T(8,128)(2,1)S(1)}, bf16[256,256]{1,0:T(8,128)(2,1)S(1)}, u32[]{:S(2)}, u32[]{:S(2)}) collective-permute-start(bf16[256,256]{1,0:T(8,128)(2,1)S(1)} %get-tuple-element.93), channel_id=1, source_target_pairs={{0,12},{1,13},{2,6},{3,7},{4,0},{5,1},{6,10},{7,11},{8,4},{9,5},{1... | collective-permute-start | bytes 393224 | tf_op jit(solution)/shard_map/ppermute | solution.py:53
  36.3 8.7 %collective-permute-start.13 = (bf16[1024,128]{1,0:T(8,128)(2,1)S(1)}, bf16[1024,128]{1,0:T(8,128)(2,1)S(1)}, u32[]{:S(2)}, u32[]{:S(2)}) collective-permute-start(bf16[1024,128]{1,0:T(8,128)(2,1)S(1)} %shard_map.122), channel_id=1, source_target_pairs={{0,18},{1,19},{2,16},{3,17},{4,22},{5,23},{6,20},{7,21},{8,26},{9,... | collective-permute-start | bytes 786440 | tf_op jit(solution)/shard_map/ppermute | solution.py:487
  45.0 6.5 %collective-permute-start.17 = (bf16[256,128]{1,0:T(8,128)(2,1)S(1)}, bf16[256,128]{1,0:T(8,128)(2,1)S(1)}, u32[]{:S(2)}, u32[]{:S(2)}) collective-permute-start(bf16[256,128]{1,0:T(8,128)(2,1)S(1)} %get-tuple-element.119), channel_id=1, source_target_pairs={{0,4},{1,5},{2,6},{3,7},{4,8},{5,9},{6,10},{7,11},{8,12},{9,13},{1... | collective-permute-start | bytes 196616 | tf_op jit(solution)/shard_map/ppermute | solution.py:53
  45.7 7.5 %collective-permute-start.18 = (bf16[256,128]{1,0:T(8,128)(2,1)S(1)}, bf16[256,128]{1,0:T(8,128)(2,1)S(1)}, u32[]{:S(2)}, u32[]{:S(2)}) collective-permute-start(bf16[256,128]{1,0:T(8,128)(2,1)S(1)} %get-tuple-element.120), channel_id=1, source_target_pairs={{0,8},{1,9},{2,10},{3,11},{4,12},{5,13},{6,14},{7,15},{8,0},{9,1},... | collective-permute-start | bytes 196616 | tf_op jit(solution)/shard_map/ppermute | solution.py:53
  49.1 4.4 %collective-permute-start.19 = (bf16[256,128]{1,0:T(8,128)(2,1)S(1)}, bf16[256,128]{1,0:T(8,128)(2,1)S(1)}, u32[]{:S(2)}, u32[]{:S(2)}) collective-permute-start(bf16[256,128]{1,0:T(8,128)(2,1)S(1)} %get-tuple-element.121), channel_id=1, source_target_pairs={{0,12},{1,13},{2,14},{3,15},{4,0},{5,1},{6,2},{7,3},{8,4},{9,5},{1... | collective-permute-start | bytes 196616 | tf_op jit(solution)/shard_map/ppermute | solution.py:53
  50.5 6.1 %collective-permute-start.16 = (bf16[256,256]{1,0:T(8,128)(2,1)S(1)}, bf16[256,256]{1,0:T(8,128)(2,1)S(1)}, u32[]{:S(2)}, u32[]{:S(2)}) collective-permute-start(bf16[256,256]{1,0:T(8,128)(2,1)S(1)} %get-tuple-element.115), channel_id=1, source_target_pairs={{0,3},{1,2},{2,1},{3,0},{4,7},{5,6},{6,5},{7,4},{8,11},{9,10},{10,... | collective-permute-start | bytes 393224 | tf_op jit(solution)/shard_map/ppermute | solution.py:44
  50.5 7.5 %collective-permute-start.15 = (bf16[256,256]{1,0:T(8,128)(2,1)S(1)}, bf16[256,256]{1,0:T(8,128)(2,1)S(1)}, u32[]{:S(2)}, u32[]{:S(2)}) collective-permute-start(bf16[256,256]{1,0:T(8,128)(2,1)S(1)} %get-tuple-element.113), channel_id=1, source_target_pairs={{0,2},{1,3},{2,0},{3,1},{4,6},{5,7},{6,4},{7,5},{8,10},{9,11},{10,... | collective-permute-start | bytes 393224 | tf_op jit(solution)/shard_map/ppermute | solution.py:44
  51.5 6.5 %collective-permute-start.14 = (bf16[256,256]{1,0:T(8,128)(2,1)S(1)}, bf16[256,256]{1,0:T(8,128)(2,1)S(1)}, u32[]{:S(2)}, u32[]{:S(2)}) collective-permute-start(bf16[256,256]{1,0:T(8,128)(2,1)S(1)} %get-tuple-element.111), channel_id=1, source_target_pairs={{0,1},{1,0},{2,3},{3,2},{4,5},{5,4},{6,7},{7,6},{8,9},{9,8},{10,11... | collective-permute-start | bytes 393224 | tf_op jit(solution)/shard_map/ppermute | solution.py:44
  53.7 1.3 %collective-permute-start.20 = (bf16[64,256]{1,0:T(8,128)(2,1)S(1)}, bf16[64,256]{1,0:T(8,128)(2,1)S(1)}, u32[]{:S(2)}, u32[]{:S(2)}) collective-permute-start(bf16[64,256]{1,0:T(8,128)(2,1)S(1)} %get-tuple-element.123), channel_id=1, source_target_pairs={{0,1},{1,0},{2,3},{3,2},{4,5},{5,4},{6,7},{7,6},{8,9},{9,8},{10,11... | collective-permute-start | bytes 98312 | tf_op jit(solution)/shard_map/ppermute | solution.py:44
  55.0 4.3 %collective-permute-start.21 = (bf16[64,512]{1,0:T(8,128)(2,1)S(1)}, bf16[64,512]{1,0:T(8,128)(2,1)S(1)}, u32[]{:S(2)}, u32[]{:S(2)}) collective-permute-start(bf16[64,512]{1,0:T(8,128)(2,1)S(1)} %shard_map.127.own), channel_id=1, source_target_pairs={{0,16},{16,0},{1,17},{17,1},{2,18},{18,2},{3,19},{19,3},{4,20},{20... | collective-permute-start | bytes 196616 | tf_op jit(solution)/shard_map/ppermute | solution.py:501
